TPU v7x, 32 devices: a whole 2x2x4 slice. The times are simulated.
32 devices in a mesh: dp: 8 (over y, x, core), mp: 4 (over z).
Axes of the slice: x: 2, y: 2, z: 4, core: 2. Of those that a mesh axis runs over, the one named last changes fastest.
Arguments:
- hidden: bfloat16 [128, 64, 768], P('dp'), may hold values from -6 to 6
- images: bfloat16 [128, 257, 1408], P('dp'), may hold values from -6 to 6
- caption_len: int32 [128], P('dp'), may hold values from 5 to 32, as said below
- cotangent: bfloat16 [128, 64, 768], P('dp'), may hold values from -6 to 6
- attn_in: float32 [4, 768, 768], P(None, 'dp', 'mp'), may hold values from -0.21875 to 0.21875
- attn_in_first: float32 [4, 768, 768], P(None, 'dp', 'mp'), may hold values from -24 to 24
- attn_in_second: float32 [4, 768, 768], P(None, 'dp', 'mp'), may hold values from 1.31072 to 5.24288
- attn_out: float32 [2, 768, 768], P(None, 'mp', 'dp'), may hold values from -0.625 to 0.625
- attn_out_first: float32 [2, 768, 768], P(None, 'mp', 'dp'), may hold values from -12 to 12
- attn_out_second: float32 [2, 768, 768], P(None, 'mp', 'dp'), may hold values from 0.32768 to 1.31072
- cross_key_value_maps: float32 [2, 1408, 768], P(None, 'dp', 'mp'), may hold values from -0.15625 to 0.15625
- cross_kv_first: float32 [2, 1408, 768], P(None, 'dp', 'mp'), may hold values from -6 to 6
- cross_kv_second: float32 [2, 1408, 768], P(None, 'dp', 'mp'), may hold values from 0.08224 to 0.32896
- ffn_up: float32 [2, 768, 3072], P(None, 'dp', 'mp'), may hold values from -0.21875 to 0.21875
- ffn_up_first: float32 [2, 768, 3072], P(None, 'dp', 'mp'), may hold values from -8 to 8
- ffn_up_second: float32 [2, 768, 3072], P(None, 'dp', 'mp'), may hold values from 0.16384 to 0.65536
- ffn_down: float32 [2, 3072, 768], P(None, 'mp', 'dp'), may hold values from -0.109375 to 0.109375
- ffn_down_first: float32 [2, 3072, 768], P(None, 'mp', 'dp'), may hold values from -20 to 20
- ffn_down_second: float32 [2, 3072, 768], P(None, 'mp', 'dp'), may hold values from 1.024 to 4.096
- vec_rep: float32 [12, 768], replicated
- vec_rep_first: float32 [12, 768], replicated, may hold values from -40 to 40
- vec_rep_second: float32 [12, 768], replicated, may hold values from 4.01408 to 16.05632
- query_value_bias_rows: float32 [4, 768], P(None, 'mp'), may hold values from -1.25 to 1.25
- vec_head_first: float32 [4, 768], P(None, 'mp'), may hold values from -24 to 24
- vec_head_second: float32 [4, 768], P(None, 'mp'), may hold values from 1.31072 to 5.24288
- bias_up: float32 [2, 3072], P(None, 'mp'), may hold values from -1.25 to 1.25
- bias_up_first: float32 [2, 3072], P(None, 'mp'), may hold values from -8 to 8
- bias_up_second: float32 [2, 3072], P(None, 'mp'), may hold values from 0.16384 to 0.65536
Outputs:
- layer_out: bfloat16 [128, 64, 768], P('dp')
- grad_hidden: float32 [128, 64, 768], P('dp')
- attn_in_moment: float32 [4, 768, 768], P(None, 'dp', 'mp')
- attn_in_square: float32 [4, 768, 768], P(None, 'dp', 'mp')
- attn_in_next: float32 [4, 768, 768], P(None, 'dp', 'mp')
- attn_out_moment: float32 [2, 768, 768], P(None, 'mp', 'dp')
- attn_out_square: float32 [2, 768, 768], P(None, 'mp', 'dp')
- attn_out_next: float32 [2, 768, 768], P(None, 'mp', 'dp')
- cross_kv_moment: float32 [2, 1408, 768], P(None, 'dp', 'mp')
- cross_kv_square: float32 [2, 1408, 768], P(None, 'dp', 'mp')
- cross_kv_next: float32 [2, 1408, 768], P(None, 'dp', 'mp')
- ffn_up_moment: float32 [2, 768, 3072], P(None, 'dp', 'mp')
- ffn_up_square: float32 [2, 768, 3072], P(None, 'dp', 'mp')
- ffn_up_next: float32 [2, 768, 3072], P(None, 'dp', 'mp')
- ffn_down_moment: float32 [2, 3072, 768], P(None, 'mp', 'dp')
- ffn_down_square: float32 [2, 3072, 768], P(None, 'mp', 'dp')
- ffn_down_next: float32 [2, 3072, 768], P(None, 'mp', 'dp')
- vec_rep_moment: float32 [12, 768], replicated
- vec_rep_square: float32 [12, 768], replicated
- vec_rep_next: float32 [12, 768], replicated
- vec_head_moment: float32 [4, 768], P(None, 'mp')
- vec_head_square: float32 [4, 768], P(None, 'mp')
- vec_head_next: float32 [4, 768], P(None, 'mp')
- bias_up_moment: float32 [2, 3072], P(None, 'mp')
- bias_up_square: float32 [2, 3072], P(None, 'mp')
- bias_up_next: float32 [2, 3072], P(None, 'mp')
Inputs may be any that keep to these rules, and one draw needn't show every extreme that they name: `caption_len`: in the items of one index of dp some item has 32 caption tokens.
All inputs are finite; a program needn't handle non-finite values.
Results may differ from a plain program's by a relative error of at most 0.02.
Values may be sent and summed in bfloat16 or wider, within the bound.
No kernel may reach another device: no remote copies, remote signals or barrier semaphores. Data moves between devices by JAX's collectives and lax.ppermute only.
A program may use at most 192 MiB of HBM per device.

v0:
```python
import math

import jax
import jax.numpy as jnp
from jax import lax
from jax.sharding import PartitionSpec as P

D = 768
HEAD_DIM = 64
F = 3072
E = 1408
NQ = 32
MICRO = 2
STEP_COUNT = 10


NORM_EPS = 1e-06
BETA_ONE = 0.9
BETA_TWO = 0.999
ADAM_EPS = 1e-08
WEIGHT_DECAY = 0.01
MASKED = -1000000000.0


def local_rows(values):
    share = values.shape[0] // lax.axis_size("mp")
    return lax.dynamic_slice_in_dim(values, lax.axis_index("mp") * share, share, 0)


def branch_reduce(term, full):
    return lax.psum_scatter(
        term(jnp.int32(0), full // lax.axis_size("mp") * lax.axis_size("mp")),
        "mp",
        scatter_dimension=0,
        tiled=True,
    )


def input_reduce(term, full):
    return lax.psum_scatter(
        term(jnp.int32(0), full // lax.axis_size("mp") * lax.axis_size("mp")).astype(jnp.bfloat16),
        "mp",
        scatter_dimension=0,
        tiled=True,
    ).astype(jnp.float32)


def rows_forward(values):
    return lax.all_gather(values, "mp", axis=0, tiled=True)


def rows_backward(values):
    return lax.all_gather(values, "mp", axis=0, tiled=True)


def rows_output(values):
    return lax.all_gather(values, "mp", axis=0, tiled=True)


def rows_gradient(values):
    return lax.all_gather(values.astype(jnp.bfloat16), "mp", axis=0, tiled=True).astype(
        values.dtype
    )


def to_pair(values):
    count = values.shape[0]
    width = values.shape[-1]
    return values.reshape(count, 2, NQ, width).transpose(0, 2, 1, 3).reshape(count * NQ, 2, width)


def from_pair(values, count):
    width = values.shape[-1]
    return values.reshape(count, NQ, 2, width).transpose(0, 2, 1, 3).reshape(count, 2 * NQ, width)


def norm_forward(values, gain, shift):
    center = values - jnp.mean(values, axis=-1, keepdims=True)
    spread = jnp.mean(center * center, axis=-1, keepdims=True)
    inverse = lax.rsqrt(spread + NORM_EPS)
    normed = center * inverse
    return (normed * gain + shift, normed, inverse)


def norm_backward(grad_out, normed, inverse, gain):
    scaled = grad_out * gain
    inner = (
        scaled
        - jnp.mean(scaled, axis=-1, keepdims=True)
        - normed * jnp.mean(scaled * normed, axis=-1, keepdims=True)
    )
    grad_gain = jnp.sum(grad_out * normed, axis=0)
    grad_shift = jnp.sum(grad_out, axis=0)
    return (inner * inverse, grad_gain, grad_shift)


def split_heads(values):
    return values.reshape(values.shape[0], values.shape[1], values.shape[2] // HEAD_DIM, HEAD_DIM)


def merge_heads(values):
    return values.reshape(values.shape[0], values.shape[1], values.shape[2] * values.shape[3])


def scores_of(query_heads, key_heads, mask_add):
    raw = jnp.einsum("nqhc,nkhc->nhqk", query_heads, key_heads, preferred_element_type=jnp.float32)
    return raw * HEAD_DIM ** (-0.5) + mask_add


def attend_forward(query_heads, key_heads, value_heads, mask_add):
    scores = scores_of(query_heads, key_heads, mask_add)
    top = jnp.max(scores, axis=-1, keepdims=True)
    expo = jnp.exp(scores - top)
    total = jnp.sum(expo, axis=-1, keepdims=True)
    probs = (expo / total).astype(jnp.bfloat16)
    context = jnp.einsum("nhqk,nkhc->nqhc", probs, value_heads, preferred_element_type=jnp.float32)
    return (context.astype(jnp.bfloat16), top + jnp.log(total))


def attend_backward(query_heads, key_heads, value_heads, mask_add, log_total, grad_context):
    scores = scores_of(query_heads, key_heads, mask_add)
    probs = jnp.exp(scores - log_total)
    grad_probs = jnp.einsum(
        "nqhc,nkhc->nhqk", grad_context, value_heads, preferred_element_type=jnp.float32
    )
    grad_value = jnp.einsum(
        "nhqk,nqhc->nkhc",
        probs.astype(jnp.bfloat16),
        grad_context,
        preferred_element_type=jnp.float32,
    )
    grad_scores = probs * (grad_probs - jnp.sum(probs * grad_probs, axis=-1, keepdims=True))
    grad_scores = grad_scores.astype(jnp.bfloat16)
    scale = HEAD_DIM ** (-0.5)
    grad_query = (
        jnp.einsum("nhqk,nkhc->nqhc", grad_scores, key_heads, preferred_element_type=jnp.float32)
        * scale
    )
    grad_key = (
        jnp.einsum("nhqk,nqhc->nkhc", grad_scores, query_heads, preferred_element_type=jnp.float32)
        * scale
    )
    return (
        grad_query.astype(jnp.bfloat16),
        grad_key.astype(jnp.bfloat16),
        grad_value.astype(jnp.bfloat16),
    )


def row_sum(values):
    return jnp.sum(values.astype(jnp.float32), axis=(0, 1))


def adam_update(weight, first, second, grad, rate):
    first_new = BETA_ONE * first + (1.0 - BETA_ONE) * grad
    second_new = BETA_TWO * second + (1.0 - BETA_TWO) * grad * grad
    first_hat = first_new / (1.0 - BETA_ONE**STEP_COUNT)
    second_hat = second_new / (1.0 - BETA_TWO**STEP_COUNT)
    weight_new = weight - rate * (
        first_hat / (jnp.sqrt(second_hat) + ADAM_EPS) + WEIGHT_DECAY * weight
    )
    return (first_new, second_new, weight_new)


def local(
    hidden,
    images,
    caption_len,
    cotangent,
    attn_in,
    attn_in_first,
    attn_in_second,
    attn_out,
    attn_out_first,
    attn_out_second,
    cross_key_value_maps,
    cross_kv_first,
    cross_kv_second,
    ffn_up,
    ffn_up_first,
    ffn_up_second,
    ffn_down,
    ffn_down_first,
    ffn_down_second,
    vec_rep,
    vec_rep_first,
    vec_rep_second,
    query_value_bias_rows,
    vec_head_first,
    vec_head_second,
    bias_up,
    bias_up_first,
    bias_up_second,
):
    lowered = (
        attn_in.astype(jnp.bfloat16),
        attn_out.astype(jnp.bfloat16),
        cross_key_value_maps.astype(jnp.bfloat16),
        ffn_up.astype(jnp.bfloat16),
        ffn_down.astype(jnp.bfloat16),
    )
    w_in, w_out, key_value_weight, w_up, w_down = (
        lax.all_gather(lowered[0], "dp", axis=1, tiled=True),
        lax.all_gather(lowered[1], "dp", axis=2, tiled=True),
        lax.all_gather(lowered[2], "dp", axis=1, tiled=True),
        lax.all_gather(lowered[3], "dp", axis=1, tiled=True),
        lax.all_gather(lowered[4], "dp", axis=2, tiled=True),
    )
    per_micro = hidden.shape[0] // MICRO
    row_count = hidden.shape[1]
    full = per_micro * NQ
    positions = jnp.arange(row_count)
    third_gain = jnp.stack([vec_rep[8], vec_rep[10]])
    third_shift = jnp.stack([vec_rep[9], vec_rep[11]])
    grads = {
        "inward": jnp.zeros(w_in.shape, jnp.float32),
        "outward": jnp.zeros(w_out.shape, jnp.float32),
        "imagekv": jnp.zeros(key_value_weight.shape, jnp.float32),
        "upward": jnp.zeros(w_up.shape, jnp.float32),
        "downward": jnp.zeros(w_down.shape, jnp.float32),
        "shared": jnp.zeros(vec_rep.shape, jnp.float32),
        "headwise": jnp.zeros(query_value_bias_rows.shape, jnp.float32),
        "hiddenbias": jnp.zeros(bias_up.shape, jnp.float32),
    }
    finished = {}
    outputs = []
    grad_inputs = []
    for micro_index in range(MICRO):
        begin = micro_index * per_micro
        tokens = hidden[begin : begin + per_micro]
        image_feature_rows = images[begin : begin + per_micro]
        lengths_here = caption_len[begin : begin + per_micro]
        tokens_pair = to_pair(tokens.astype(jnp.float32))
        top_pair = to_pair(cotangent[begin : begin + per_micro].astype(jnp.float32))
        valid = (positions[None, :] < NQ) | (positions[None, :] - NQ < lengths_here[:, None])
        mask_add = jnp.where(valid, 0.0, MASKED).astype(jnp.float32)[:, None, None, :]
        qkv_pre = jnp.einsum("nrd,tde->tnre", tokens, w_in[:3], preferred_element_type=jnp.float32)
        self_query = split_heads((qkv_pre[0] + query_value_bias_rows[0]).astype(jnp.bfloat16))
        self_key = split_heads(qkv_pre[1].astype(jnp.bfloat16))
        self_value = split_heads((qkv_pre[2] + query_value_bias_rows[1]).astype(jnp.bfloat16))
        self_context, self_log = attend_forward(self_query, self_key, self_value, mask_add)
        self_flat = merge_heads(self_context)
        self_pair = to_pair(self_flat)

        def self_term(start, rows_here):
            return jnp.einsum(
                "mge,ed->mgd", self_pair, w_out[0], preferred_element_type=jnp.float32
            )

        first_sum = branch_reduce(self_term, full)
        first_out, first_normed, first_inverse = norm_forward(
            local_rows(tokens_pair) + first_sum + vec_rep[0], vec_rep[4], vec_rep[5]
        )
        query_local = first_out[:, 0]
        cross_in = rows_forward(query_local.astype(jnp.bfloat16))
        cross_pre = jnp.dot(cross_in, w_in[3], preferred_element_type=jnp.float32)
        cross_query = split_heads(
            (cross_pre + query_value_bias_rows[2])
            .astype(jnp.bfloat16)
            .reshape(per_micro, NQ, cross_pre.shape[-1])
        )
        key_value_preactivation = jnp.einsum(
            "mcr,krb->kmcb",
            image_feature_rows,
            key_value_weight,
            preferred_element_type=jnp.float32,
        )
        cross_attention_key = split_heads(key_value_preactivation[0].astype(jnp.bfloat16))
        cross_attention_value = split_heads(
            (key_value_preactivation[1] + query_value_bias_rows[3]).astype(jnp.bfloat16)
        )
        no_mask = jnp.float32(0.0)
        cross_context, cross_log = attend_forward(
            cross_query, cross_attention_key, cross_attention_value, no_mask
        )
        cross_flat = merge_heads(cross_context).reshape(full, cross_pre.shape[-1])

        def cross_term(start, rows_here):
            return jnp.dot(cross_flat, w_out[1], preferred_element_type=jnp.float32)

        second_sum = branch_reduce(cross_term, full)
        second_query, second_normed, second_inverse = norm_forward(
            query_local + second_sum + vec_rep[1], vec_rep[6], vec_rep[7]
        )
        second_out = jnp.stack([second_query, first_out[:, 1]], axis=1)
        ffn_in = rows_forward(second_out.astype(jnp.bfloat16))
        up_pre = (
            jnp.einsum("mgd,gdf->mgf", ffn_in, w_up, preferred_element_type=jnp.float32)
            + bias_up[None]
        )
        gelu_value, gelu_pull = jax.vjp(
            lambda values: jax.nn.gelu(values, approximate=False), up_pre
        )
        up_act = gelu_value.astype(jnp.bfloat16)

        def ffn_term(start, rows_here):
            return jnp.einsum("mgf,gfd->mgd", up_act, w_down, preferred_element_type=jnp.float32)

        third_sum = branch_reduce(ffn_term, full)
        third_out, third_normed, third_inverse = norm_forward(
            second_out + third_sum + vec_rep[2:4], third_gain, third_shift
        )
        outputs.append(from_pair(rows_output(third_out.astype(jnp.bfloat16)), per_micro))
        grad_third, gain_third, shift_third = norm_backward(
            local_rows(top_pair), third_normed, third_inverse, third_gain
        )
        grad_ffn_local = grad_third.astype(jnp.bfloat16)
        grads["shared"] = (
            grads["shared"]
            .at[2:4]
            .add(jnp.sum(grad_ffn_local.astype(jnp.float32), axis=0))
            .at[8]
            .add(gain_third[0])
            .at[10]
            .add(gain_third[1])
            .at[9]
            .add(shift_third[0])
            .at[11]
            .add(shift_third[1])
        )
        grad_ffn_out = rows_backward(grad_ffn_local)
        grads["downward"] = grads["downward"] + jnp.einsum(
            "mgf,mgd->gfd", up_act, grad_ffn_out, preferred_element_type=jnp.float32
        )
        grad_act = jnp.einsum(
            "mgd,gfd->mgf", grad_ffn_out, w_down, preferred_element_type=jnp.float32
        )
        grad_pre = gelu_pull(grad_act)[0].astype(jnp.bfloat16)
        grads["hiddenbias"] = grads["hiddenbias"] + jnp.sum(grad_pre.astype(jnp.float32), axis=0)
        grads["upward"] = grads["upward"] + jnp.einsum(
            "mgd,mgf->gdf", ffn_in, grad_pre, preferred_element_type=jnp.float32
        )
        finished["feedforward"] = None

        def up_back_term(start, rows_here):
            return jnp.einsum("mgf,gdf->mgd", grad_pre, w_up, preferred_element_type=jnp.float32)

        grad_second = grad_third + input_reduce(up_back_term, full)
        grad_query_rows, gain_second, shift_second = norm_backward(
            grad_second[:, 0], second_normed, second_inverse, vec_rep[6]
        )
        grad_cross_local = grad_query_rows.astype(jnp.bfloat16)
        grads["shared"] = (
            grads["shared"]
            .at[1]
            .add(jnp.sum(grad_cross_local.astype(jnp.float32), axis=0))
            .at[6]
            .add(gain_second)
            .at[7]
            .add(shift_second)
        )
        grad_cross_out = rows_backward(grad_cross_local)
        grads["outward"] = (
            grads["outward"]
            .at[1]
            .add(
                jnp.einsum(
                    "me,md->ed", cross_flat, grad_cross_out, preferred_element_type=jnp.float32
                )
            )
        )
        cross_back = jnp.einsum(
            "md,ed->me", grad_cross_out, w_out[1], preferred_element_type=jnp.float32
        ).astype(jnp.bfloat16)
        grad_cross_context = split_heads(cross_back.reshape(per_micro, NQ, cross_back.shape[-1]))
        cross_gq, cross_gk, cross_gv = attend_backward(
            cross_query,
            cross_attention_key,
            cross_attention_value,
            no_mask,
            cross_log,
            grad_cross_context,
        )
        cross_gq_flat = merge_heads(cross_gq).reshape(full, cross_back.shape[-1])
        cross_gv_flat = merge_heads(cross_gv)
        grads["headwise"] = (
            grads["headwise"]
            .at[2]
            .add(jnp.sum(cross_gq_flat.astype(jnp.float32), axis=0))
            .at[3]
            .add(row_sum(cross_gv_flat))
        )
        grads["inward"] = (
            grads["inward"]
            .at[3]
            .add(
                jnp.einsum("md,me->de", cross_in, cross_gq_flat, preferred_element_type=jnp.float32)
            )
        )
        image_feature_gradient = jnp.stack([merge_heads(cross_gk), cross_gv_flat])
        grads["imagekv"] = grads["imagekv"] + jnp.einsum(
            "pwg,hpwz->hgz",
            image_feature_rows,
            image_feature_gradient,
            preferred_element_type=jnp.float32,
        )

        def cross_back_term(start, rows_here):
            return jnp.einsum(
                "me,de->md", cross_gq_flat, w_in[3], preferred_element_type=jnp.float32
            )

        grad_first_query = grad_query_rows + input_reduce(cross_back_term, full)
        grad_first = jnp.stack([grad_first_query, grad_second[:, 1]], axis=1)
        grad_first_z, gain_first, shift_first = norm_backward(
            grad_first, first_normed, first_inverse, vec_rep[4]
        )
        grad_self_local = grad_first_z.astype(jnp.bfloat16)
        grads["shared"] = (
            grads["shared"]
            .at[0]
            .add(jnp.sum(grad_self_local.astype(jnp.float32), axis=(0, 1)))
            .at[4]
            .add(jnp.sum(gain_first, axis=0))
            .at[5]
            .add(jnp.sum(shift_first, axis=0))
        )
        grad_self_out = from_pair(rows_backward(grad_self_local), per_micro)
        grads["outward"] = (
            grads["outward"]
            .at[0]
            .add(
                jnp.einsum(
                    "nre,nrd->ed", self_flat, grad_self_out, preferred_element_type=jnp.float32
                )
            )
        )
        grad_self_context = split_heads(
            jnp.einsum(
                "nrd,ed->nre", grad_self_out, w_out[0], preferred_element_type=jnp.float32
            ).astype(jnp.bfloat16)
        )
        self_gq, self_gk, self_gv = attend_backward(
            self_query, self_key, self_value, mask_add, self_log, grad_self_context
        )
        stacked = jnp.stack([merge_heads(self_gq), merge_heads(self_gk), merge_heads(self_gv)])
        grads["headwise"] = (
            grads["headwise"].at[0].add(row_sum(stacked[0])).at[1].add(row_sum(stacked[2]))
        )
        grads["inward"] = (
            grads["inward"]
            .at[:3]
            .add(jnp.einsum("nrd,tnre->tde", tokens, stacked, preferred_element_type=jnp.float32))
        )
        finished["attention"] = None
        head_cols = stacked.shape[-1]
        stacked_pair = (
            stacked.reshape(3, per_micro, 2, NQ, head_cols)
            .transpose(0, 1, 3, 2, 4)
            .reshape(3, full, 2, head_cols)
        )

        def self_back_term(start, rows_here):
            return jnp.einsum(
                "tmge,tde->mgd", stacked_pair, w_in[:3], preferred_element_type=jnp.float32
            )

        grad_local = grad_first_z + input_reduce(self_back_term, full)
        grad_inputs.append(from_pair(rows_gradient(grad_local), per_micro))
    reduced_in, reduced_out, reduced_kv, reduced_up, reduced_down = (
        lax.psum_scatter(grads["inward"], "dp", scatter_dimension=1, tiled=True),
        lax.psum_scatter(grads["outward"], "dp", scatter_dimension=2, tiled=True),
        lax.psum_scatter(grads["imagekv"], "dp", scatter_dimension=1, tiled=True),
        lax.psum_scatter(grads["upward"], "dp", scatter_dimension=1, tiled=True),
        lax.psum_scatter(grads["downward"], "dp", scatter_dimension=2, tiled=True),
    )
    group_count = lax.axis_size("mp")
    mp_place = lax.axis_index("mp")
    head_width = query_value_bias_rows.shape[1]
    bias_width = bias_up.shape[1]
    head_padded = lax.dynamic_update_slice(
        jnp.zeros((query_value_bias_rows.shape[0], head_width * group_count), jnp.float32),
        grads["headwise"],
        (jnp.int32(0), mp_place * head_width),
    )
    bias_padded = lax.dynamic_update_slice(
        jnp.zeros((bias_up.shape[0], bias_width * group_count), jnp.float32),
        grads["hiddenbias"],
        (jnp.int32(0), mp_place * bias_width),
    )
    reduced_rep, head_total, bias_total = lax.psum(
        (grads["shared"], head_padded, bias_padded), ("dp", "mp")
    )
    reduced_head = lax.dynamic_slice_in_dim(head_total, mp_place * head_width, head_width, 1)
    reduced_bias = lax.dynamic_slice_in_dim(bias_total, mp_place * bias_width, bias_width, 1)
    rates = (
        2.0 / math.sqrt(D),
        2.0 / math.sqrt(max(D // 8, 1)),
        2.0 / math.sqrt(E),
        2.0 / math.sqrt(D),
        2.0 / math.sqrt(F),
        0.3,
        0.3,
        0.3,
    )
    weights = (
        attn_in,
        attn_out,
        cross_key_value_maps,
        ffn_up,
        ffn_down,
        vec_rep,
        query_value_bias_rows,
        bias_up,
    )
    firsts = (
        attn_in_first,
        attn_out_first,
        cross_kv_first,
        ffn_up_first,
        ffn_down_first,
        vec_rep_first,
        vec_head_first,
        bias_up_first,
    )
    seconds = (
        attn_in_second,
        attn_out_second,
        cross_kv_second,
        ffn_up_second,
        ffn_down_second,
        vec_rep_second,
        vec_head_second,
        bias_up_second,
    )
    reduced = (
        reduced_in,
        reduced_out,
        reduced_kv,
        reduced_up,
        reduced_down,
        reduced_rep,
        reduced_head,
        reduced_bias,
    )
    results = []
    for weight, first, second, grad, rate in zip(weights, firsts, seconds, reduced, rates):
        results.extend(adam_update(weight, first, second, grad, rate))
    layer_out = jnp.concatenate(outputs, axis=0)
    grad_hidden = jnp.concatenate(grad_inputs, axis=0)
    return (
        layer_out,
        grad_hidden,
        results[0],
        results[1],
        results[2],
        results[3],
        results[4],
        results[5],
        results[6],
        results[7],
        results[8],
        results[9],
        results[10],
        results[11],
        results[12],
        results[13],
        results[14],
        results[15],
        results[16],
        results[17],
        results[18],
        results[19],
        results[20],
        results[21],
        results[22],
        results[23],
    )


def solution(mesh):
    placed = (
        P("dp", None, None),
        P("dp", None, None),
        P("dp"),
        P("dp", None, None),
        P(None, "dp", "mp"),
        P(None, "dp", "mp"),
        P(None, "dp", "mp"),
        P(None, "mp", "dp"),
        P(None, "mp", "dp"),
        P(None, "mp", "dp"),
        P(None, "dp", "mp"),
        P(None, "dp", "mp"),
        P(None, "dp", "mp"),
        P(None, "dp", "mp"),
        P(None, "dp", "mp"),
        P(None, "dp", "mp"),
        P(None, "mp", "dp"),
        P(None, "mp", "dp"),
        P(None, "mp", "dp"),
        P(),
        P(),
        P(),
        P(None, "mp"),
        P(None, "mp"),
        P(None, "mp"),
        P(None, "mp"),
        P(None, "mp"),
        P(None, "mp"),
    )
    return jax.shard_map(
        local,
        mesh=mesh,
        in_specs=placed,
        out_specs=(
            P("dp", None, None),
            P("dp", None, None),
            P(None, "dp", "mp"),
            P(None, "dp", "mp"),
            P(None, "dp", "mp"),
            P(None, "mp", "dp"),
            P(None, "mp", "dp"),
            P(None, "mp", "dp"),
            P(None, "dp", "mp"),
            P(None, "dp", "mp"),
            P(None, "dp", "mp"),
            P(None, "dp", "mp"),
            P(None, "dp", "mp"),
            P(None, "dp", "mp"),
            P(None, "mp", "dp"),
            P(None, "mp", "dp"),
            P(None, "mp", "dp"),
            P(),
            P(),
            P(),
            P(None, "mp"),
            P(None, "mp"),
            P(None, "mp"),
            P(None, "mp"),
            P(None, "mp"),
            P(None, "mp"),
        ),
        check_vma=False,
    )
```

profile of v0, /device:TPU:0, one launch (start us, length us, event | category | flops | bytes accessed | tf_op | source)
XLA Modules:
  0.0 1108.5 jit_solution(9952016935349748506)
XLA Ops:
  13.4 13.9 %all_gather.58 = bf16[2,192,768]{1,0,2:T(2,128)(2,1)S(1)} all-gather(bf16[2,192,96]{1,0,2:T(2,128)(2,1)S(1)} %copy.475), channel_id=1, replica_groups=mesh['dp'=8,'mp'=4] {'dp'}, dimensions={2}, use_global_device_ids=true | all-gather | bytes 663552 | tf_op jit(solution)/shard_map/all_gather | solution.py:204
  30.0 10.0 all-gather.5.cloned.1.call-done
  40.0 2.6 copy.619
  61.2 9.7 fusion.206
  70.9 6.2 fusion.8
  80.6 3.5 fusion.9
  87.6 3.6 copy.498
  92.7 3.2 copy.479
  95.8 3.1 slice.948
  101.1 4.2 reduce-scatter.27.cloned.1.call-done
  105.3 37.0 %reduce-scatter.21.cloned.1.call-done = f32[64,2,768]{2,0,1:T(8,128)} async-done(((f32[256,2,768]{2,0,1:T(8,128)}), f32[64,2,768]{2,0,1:T(8,128)}) %reduce-scatter.21.cloned.1.call-update) | async-done | bytes 393232 | tf_op jit(solution)/shard_map/reduce_scatter | solution.py:31
  145.6 15.1 %all_gather.65 = bf16[256,768]{1,0:T(8,128)(2,1)S(1)} all-gather(bf16[64,768]{1,0:T(8,128)(2,1)S(1)} %fusion.161), channel_id=1, replica_groups=mesh['dp'=8,'mp'=4] {'mp'}, dimensions={0}, use_global_device_ids=true | all-gather | bytes 491520 | tf_op jit(solution)/shard_map/all_gather | solution.py:49
  169.0 17.2 %all_gather.60 = bf16[256,768]{1,0:T(8,128)(2,1)S(1)} all-gather(bf16[64,768]{1,0:T(8,128)(2,1)S(1)} %fusion.160), channel_id=1, replica_groups=mesh['dp'=8,'mp'=4] {'mp'}, dimensions={0}, use_global_device_ids=true | all-gather | bytes 491520 | tf_op jit(solution)/shard_map/all_gather | solution.py:49
  193.4 2.2 fusion.145
  201.0 17.0 %reduce-scatter.23.cloned.1.call-done = f32[64,768]{1,0:T(8,128)} async-done(((f32[256,768]{1,0:T(8,128)}), f32[64,768]{1,0:T(8,128)}) %reduce-scatter.23.cloned.1.call-update) | async-done | bytes 196624 | tf_op jit(solution)/shard_map/reduce_scatter | solution.py:31
  221.6 18.4 %all_gather.61 = bf16[256,2,768]{2,0,1:T(8,128)(2,1)} all-gather(bf16[64,2,768]{2,0,1:T(8,128)(2,1)S(1)} %fusion.140), channel_id=1, replica_groups=mesh['dp'=8,'mp'=4] {'mp'}, dimensions={0}, use_global_device_ids=true | all-gather | bytes 983040 | tf_op jit(solution)/shard_map/all_gather | solution.py:49
  239.9 8.9 all-gather.9.cloned.1.call-done
  248.8 7.7 fusion.36
  256.5 23.8 %all-gather.11.cloned.1.call-done = bf16[2,768,768]{1,2,0:T(8,128)(2,1)} async-done(((bf16[2,768,96]{1,2,0:T(8,128)(2,1)}), bf16[2,768,768]{1,2,0:T(8,128)(2,1)}) %all-gather.11.cloned.1.call-update) | async-done | bytes 2359312 | tf_op jit(solution)/shard_map/all_gather | solution.py:207
  280.3 3.9 convolution_bitcast_fusion.2
  286.3 29.7 %all_gather.66 = bf16[256,2,768]{2,0,1:T(8,128)(2,1)S(1)} all-gather(bf16[64,2,768]{2,0,1:T(8,128)(2,1)S(1)} %fusion.139), channel_id=1, replica_groups=mesh['dp'=8,'mp'=4] {'mp'}, dimensions={0}, use_global_device_ids=true | all-gather | bytes 983040 | tf_op jit(solution)/shard_map/all_gather | solution.py:49
  316.0 7.1 fusion.34
  333.9 34.3 %reduce-scatter.31.cloned.1.call-done = f32[64,2,768]{2,0,1:T(8,128)} async-done(((f32[256,2,768]{2,0,1:T(8,128)}), f32[64,2,768]{2,0,1:T(8,128)}) %reduce-scatter.31.cloned.1.call-update) | async-done | bytes 393232 | tf_op jit(solution)/shard_map/reduce_scatter | solution.py:31
  373.4 18.1 %all_gather.68 = bf16[256,2,768]{2,0,1:T(8,128)(2,1)S(1)} all-gather(bf16[64,2,768]{2,0,1:T(8,128)(2,1)S(1)} %get-tuple-element.670), channel_id=1, replica_groups=mesh['dp'=8,'mp'=4] {'mp'}, dimensions={0}, use_global_device_ids=true | all-gather | bytes 983040 | tf_op jit(solution)/shard_map/all_gather | solution.py:53
  391.6 3.5 convert_reduce_fusion.3
  401.1 27.8 %all_gather.72 = bf16[256,2,768]{2,0,1:T(8,128)(2,1)S(1)} all-gather(bf16[64,2,768]{2,0,1:T(8,128)(2,1)S(1)} %get-tuple-element.663), channel_id=1, replica_groups=mesh['dp'=8,'mp'=4] {'mp'}, dimensions={0}, use_global_device_ids=true | all-gather | bytes 983040 | tf_op jit(solution)/shard_map/all_gather | solution.py:53
  429.0 4.2 convert_reduce_fusion.2
  453.9 4.7 reduce-scatter.39.cloned.1.call-done
  458.6 2.7 convert_add_fusion
  463.7 14.9 %all_gather.69 = bf16[256,768]{1,0:T(8,128)(2,1)S(1)} all-gather(bf16[64,768]{1,0:T(8,128)(2,1)S(1)} %get-tuple-element.667), channel_id=1, replica_groups=mesh['dp'=8,'mp'=4] {'mp'}, dimensions={0}, use_global_device_ids=true | all-gather | bytes 491520 | tf_op jit(solution)/shard_map/all_gather | solution.py:53
  484.1 3.2 convert_reduce_fusion.1
  494.1 14.6 %all_gather.73 = bf16[256,768]{1,0:T(8,128)(2,1)S(1)} all-gather(bf16[64,768]{1,0:T(8,128)(2,1)S(1)} %get-tuple-element.660), channel_id=1, replica_groups=mesh['dp'=8,'mp'=4] {'mp'}, dimensions={0}, use_global_device_ids=true | all-gather | bytes 491520 | tf_op jit(solution)/shard_map/all_gather | solution.py:53
  510.2 2.3 multiply_reduce_fusion
  518.6 2.5 copy.563
  521.1 2.5 copy.562
  523.6 2.5 slice_reduce_fusion.11
  533.2 7.8 fusion.7
  544.8 2.6 copy.566
  551.1 9.6 reduce-scatter.41.cloned.1.call-done
  563.2 17.5 %all_gather.70 = bf16[256,2,768]{2,0,1:T(8,128)(2,1)S(1)} all-gather(bf16[64,2,768]{2,0,1:T(8,128)(2,1)S(1)} %get-tuple-element.665), channel_id=1, replica_groups=mesh['dp'=8,'mp'=4] {'mp'}, dimensions={0}, use_global_device_ids=true | all-gather | bytes 983040 | tf_op jit(solution)/shard_map/all_gather | solution.py:53
  582.4 3.1 multiply_reduce_fusion.3
  587.3 16.6 %all_gather.74 = bf16[256,2,768]{2,0,1:T(8,128)(2,1)S(1)} all-gather(bf16[64,2,768]{2,0,1:T(8,128)(2,1)S(1)} %get-tuple-element.658), channel_id=1, replica_groups=mesh['dp'=8,'mp'=4] {'mp'}, dimensions={0}, use_global_device_ids=true | all-gather | bytes 983040 | tf_op jit(solution)/shard_map/all_gather | solution.py:53
  605.5 3.1 multiply_reduce_fusion.2
  653.3 8.4 fusion.6
  661.7 5.4 copy.568
  691.6 3.3 reshape.1518
  715.3 3.4 fusion.16
  718.7 4.5 copy.607
  723.2 4.7 reshape.1516
  730.5 3.1 convolution_add_fusion
  736.1 3.1 convolution_add_fusion.1
  743.5 19.8 %all_gather.64 = bf16[256,2,768]{2,0,1:T(8,128)(2,1)S(1)} all-gather(bf16[64,2,768]{2,0,1:T(8,128)(2,1)S(1)} %copy-done.140), channel_id=1, replica_groups=mesh['dp'=8,'mp'=4] {'mp'}, dimensions={0}, use_global_device_ids=true | all-gather | bytes 983040 | tf_op jit(solution)/shard_map/all_gather | solution.py:57
  763.4 16.1 %all_gather.67 = bf16[256,2,768]{2,0,1:T(8,128)(2,1)S(1)} all-gather(bf16[64,2,768]{2,0,1:T(8,128)(2,1)} %get-tuple-element.717), channel_id=1, replica_groups=mesh['dp'=8,'mp'=4] {'mp'}, dimensions={0}, use_global_device_ids=true | all-gather | bytes 983040 | tf_op jit(solution)/shard_map/all_gather | solution.py:57
  785.3 62.5 %all-reduce.7.cloned.1.call-done = f32[2,1408,192]{2,0,1:T(2,128)} async-done(((f32[2,1408,192]{2,0,1:T(2,128)}), f32[2,1408,192]{2,0,1:T(2,128)}) %all-reduce.7.cloned.1.call-update) | async-done | bytes 2162704
  848.9 2.2 multiply_subtract_fusion.3
  851.2 22.1 %reduce-scatter.43.cloned.1.call-done = bf16[64,2,768]{2,0,1:T(8,128)(2,1)} async-done(((bf16[256,2,768]{2,0,1:T(8,128)(2,1)}), bf16[64,2,768]{2,0,1:T(8,128)(2,1)}) %reduce-scatter.43.cloned.1.call-update) | async-done | bytes 196624 | tf_op jit(solution)/shard_map/reduce_scatter | solution.py:40
  873.3 24.9 %reduce-scatter.37.cloned.1.call-done = bf16[64,2,768]{2,0,1:T(8,128)(2,1)} async-done(((bf16[256,2,768]{2,0,1:T(8,128)(2,1)}), bf16[64,2,768]{2,0,1:T(8,128)(2,1)}) %reduce-scatter.37.cloned.1.call-update) | async-done | bytes 196624 | tf_op jit(solution)/shard_map/reduce_scatter | solution.py:40
  899.6 18.1 %all_gather.75 = bf16[256,2,768]{2,0,1:T(8,128)(2,1)S(1)} all-gather(bf16[64,2,768]{2,0,1:T(8,128)(2,1)S(1)} %get-tuple-element.741), channel_id=1, replica_groups=mesh['dp'=8,'mp'=4] {'mp'}, dimensions={0}, use_global_device_ids=true | all-gather | bytes 983040 | tf_op jit(solution)/shard_map/all_gather | solution.py:61
  917.8 17.4 %all_gather.71 = bf16[256,2,768]{2,0,1:T(8,128)(2,1)S(1)} all-gather(bf16[64,2,768]{2,0,1:T(8,128)(2,1)S(1)} %get-tuple-element.740), channel_id=1, replica_groups=mesh['dp'=8,'mp'=4] {'mp'}, dimensions={0}, use_global_device_ids=true | all-gather | bytes 983040 | tf_op jit(solution)/shard_map/all_gather | solution.py:61
  940.0 43.5 %reduce-scatter.49.cloned.1.call-done = f32[96,768]{1,0:T(8,128)} async-done(((f32[768,768]{1,0:T(8,128)}), f32[96,768]{1,0:T(8,128)}) %reduce-scatter.49.cloned.1.call-update) | async-done | bytes 294928
  988.2 53.1 %reduce-scatter.47.cloned.1.call-done = f32[2,768,96]{1,2,0:T(8,128)} async-done(((f32[2,768,768]{1,2,0:T(8,128)}), f32[2,768,96]{1,2,0:T(8,128)}) %reduce-scatter.47.cloned.1.call-update) | async-done | bytes 589840 | tf_op jit(solution)/shard_map/reduce_scatter | solution.py:465
  1041.3 2.7 multiply_subtract_fusion
  1044.0 54.7 %reduce-scatter.45.cloned.1.call-done = f32[2,96,768]{2,1,0:T(8,128)} async-done(((f32[2,768,768]{2,1,0:T(8,128)}), f32[2,96,768]{2,1,0:T(8,128)}) %reduce-scatter.45.cloned.1.call-update) | async-done | bytes 589840 | tf_op jit(solution)/shard_map/reduce_scatter | solution.py:464
  1098.7 2.5 multiply_subtract_fusion.1
  (869 shorter events, 268.7 us)
Async XLA Ops:
  7.2 32.8 %all-gather.5.cloned.1.call-start = ((), (), s32[]{:S(2)}) async-start(), calls=%async_computation.16 | async-start | bytes 1769472 | tf_op jit(solution)/shard_map/all_gather | solution.py:203
  9.2 61.7 %all-gather.7.cloned.1.call-start = ((), (), s32[]{:S(2)}) async-start(), calls=%async_computation.18 | async-start | bytes 1622016 | tf_op jit(solution)/shard_map/all_gather | solution.py:205
  11.0 94.3 %reduce-scatter.27.cloned.1.call-start = ((), (), s32[]{:S(2)}) async-start(), calls=%async_computation.23 | async-start | bytes 1966080 | tf_op jit(solution)/shard_map/reduce_scatter | solution.py:31
  29.3 21.9 %copy-start.176 = (f32[3,64]{1,0:T(4,128)}, f32[3,64]{1,0:T(4,128)S(1)}, u32[]{:S(2)}) copy-start(f32[3,64]{1,0:T(4,128)S(1)} %add.783) | copy-start | bytes 2308
  29.4 22.4 %copy-start.200 = (f32[3,64]{1,0:T(4,128)}, f32[3,64]{1,0:T(4,128)S(1)}, u32[]{:S(2)}) copy-start(f32[3,64]{1,0:T(4,128)S(1)} %add.780) | copy-start | bytes 2308
  47.9 94.4 %reduce-scatter.21.cloned.1.call-start = ((), (), s32[]{:S(2)}) async-start(), calls=%async_computation.17 | async-start | bytes 1966080 | tf_op jit(solution)/shard_map/reduce_scatter | solution.py:31
  55.6 145.5 %reduce-scatter.29.cloned.1.call-start = ((), (), s32[]{:S(2)}) async-start(), calls=%async_computation.24 | async-start | bytes 983040 | tf_op jit(solution)/shard_map/reduce_scatter | solution.py:31
  59.0 131.0 %copy-start.203 = (f32[3,64]{1,0:T(4,128)}, f32[3,64]{1,0:T(4,128)S(1)}, u32[]{:S(2)}) copy-start(f32[3,64]{1,0:T(4,128)S(1)} %add.796) | copy-start | bytes 2308
  61.2 83.1 %copy-start.160 = (f32[768]{0:T(1024)}, f32[768]{0:T(1024)S(1)}, u32[]{:S(2)}) copy-start(f32[768]{0:T(1024)S(1)} %get-tuple-element.640) | copy-start | bytes 9220
  61.2 158.6 %copy-start.168 = (f32[768]{0:T(1024)}, f32[768]{0:T(1024)S(1)}, u32[]{:S(2)}) copy-start(f32[768]{0:T(1024)S(1)} %get-tuple-element.636) | copy-start | bytes 9220
  87.5 76.3 %copy-start.4 = (bf16[1,8,257,192]{2,3,1,0:T(8,128)(2,1)}, bf16[1,8,257,192]{2,3,1,0:T(8,128)(2,1)S(1)}, u32[]{:S(2)}) copy-start(bf16[1,8,257,192]{2,3,1,0:T(8,128)(2,1)S(1)} %copy.500) | copy-start | bytes 2368516
  101.1 59.5 %copy-start.16 = (bf16[1,768,192]{1,2,0:T(8,128)(2,1)}, bf16[1,768,192]{1,2,0:T(8,128)(2,1)S(1)}, u32[]{:S(2)}) copy-start(bf16[1,768,192]{1,2,0:T(8,128)(2,1)S(1)} %copy.622) | copy-start | bytes 884740
  168.0 50.0 %reduce-scatter.23.cloned.1.call-start = ((), (), s32[]{:S(2)}) async-start(), calls=%async_computation.19 | async-start | bytes 983040 | tf_op jit(solution)/shard_map/reduce_scatter | solution.py:31
  195.6 53.2 %all-gather.9.cloned.1.call-start = ((), (), s32[]{:S(2)}) async-start(), calls=%async_computation.20 | async-start | bytes 2654208 | tf_op jit(solution)/shard_map/all_gather | solution.py:206
  197.5 82.9 %all-gather.11.cloned.1.call-start = ((), (), s32[]{:S(2)}) async-start(), calls=%async_computation.21 | async-start | bytes 2654208 | tf_op jit(solution)/shard_map/all_gather | solution.py:207
  199.3 134.5 %reduce-scatter.25.cloned.1.call-start = ((), (), s32[]{:S(2)}) async-start(), calls=%async_computation.22 | async-start | bytes 1966080 | tf_op jit(solution)/shard_map/reduce_scatter | solution.py:31
  219.6 36.9 %copy-start.228 = (f32[64]{0:T(128)}, f32[64]{0:T(128)S(1)}, u32[]{:S(2)}) copy-start(f32[64]{0:T(128)S(1)} %broadcast_multiply_fusion.17) | copy-start | bytes 772
  284.2 31.8 %copy-start.237 = (f32[2,768]{1,0:T(2,128)S(1)}, f32[2,768]{1,0:T(2,128)}, u32[]{:S(2)}) copy-start(f32[2,768]{1,0:T(2,128)} %param.129) | copy-start | bytes 18436
  284.2 83.9 %reduce-scatter.31.cloned.1.call-start = ((), (), s32[]{:S(2)}) async-start(), calls=%async_computation.25 | async-start | bytes 1966080 | tf_op jit(solution)/shard_map/reduce_scatter | solution.py:31
  326.1 127.8 %reduce-scatter.33.cloned.1.call-start = ((), (), s32[]{:S(2)}) async-start(), calls=%async_computation.26 | async-start | bytes 983040 | tf_op jit(solution)/shard_map/reduce_scatter | solution.py:40
  370.1 21.4 %copy-start.205 = (f32[64,2]{0,1:T(2,128)}, f32[64,2]{0,1:T(2,128)S(1)}, u32[]{:S(2)}) copy-start(f32[64,2]{0,1:T(2,128)S(1)} %add_rsqrt_fusion) | copy-start | bytes 1540
  370.1 21.4 %copy-start.198 = (f32[64,2]{0,1:T(2,128)}, f32[64,2]{0,1:T(2,128)S(1)}, u32[]{:S(2)}) copy-start(f32[64,2]{0,1:T(2,128)S(1)} %broadcast_multiply_fusion.10) | copy-start | bytes 1540
  370.2 21.4 %copy-start.255 = (f32[256,2,768]{2,0,1:T(8,128)S(1)}, f32[256,2,768]{2,0,1:T(8,128)}, u32[]{:S(2)}) copy-start(f32[256,2,768]{2,0,1:T(8,128)} %get-tuple-element.689) | copy-start | bytes 4718596
  397.7 60.9 %reduce-scatter.39.cloned.1.call-start = ((), (), s32[]{:S(2)}) async-start(), calls=%async_computation.29 | async-start | bytes 983040 | tf_op jit(solution)/shard_map/reduce_scatter | solution.py:40
  397.7 31.2 %copy-start.254 = (f32[256,2,768]{2,0,1:T(8,128)S(1)}, f32[256,2,768]{2,0,1:T(8,128)}, u32[]{:S(2)}) copy-start(f32[256,2,768]{2,0,1:T(8,128)} %get-tuple-element.697) | copy-start | bytes 4718596
  398.5 30.4 %copy-start.220 = (f32[64,2]{0,1:T(2,128)}, f32[64,2]{0,1:T(2,128)S(1)}, u32[]{:S(2)}) copy-start(f32[64,2]{0,1:T(2,128)S(1)} %broadcast_multiply_fusion.2) | copy-start | bytes 1540
  399.2 29.7 %copy-start.221 = (f32[64,2]{0,1:T(2,128)}, f32[64,2]{0,1:T(2,128)S(1)}, u32[]{:S(2)}) copy-start(f32[64,2]{0,1:T(2,128)S(1)} %broadcast_multiply_fusion.3) | copy-start | bytes 1540
  435.8 113.0 %reduce-scatter.35.cloned.1.call-start = ((), (), s32[]{:S(2)}) async-start(), calls=%async_computation.27 | async-start | bytes 491520 | tf_op jit(solution)/shard_map/reduce_scatter | solution.py:40
  518.6 42.1 %reduce-scatter.41.cloned.1.call-start = ((), (), s32[]{:S(2)}) async-start(), calls=%async_computation.30 | async-start | bytes 491520 | tf_op jit(solution)/shard_map/reduce_scatter | solution.py:40
  528.9 252.1 %all-reduce.9.cloned.1.call-start = ((), (), s32[]{:S(2)}) async-start(), calls=%async_computation.37 | async-start | bytes 172032 | tf_op jit(solution)/shard_map/psum | solution.py:481
  550.3 30.4 %copy-start.71 = (f32[64,1,768]{2,0,1:T(8,128)}, f32[64,1,768]{2,0,1:T(8,128)S(1)}, u32[]{:S(2)}) copy-start(f32[64,1,768]{2,0,1:T(8,128)S(1)} %get-tuple-element.723) | copy-start | bytes 589828
  551.1 29.6 %copy-start.214 = (f32[64,2]{0,1:T(2,128)}, f32[64,2]{0,1:T(2,128)S(1)}, u32[]{:S(2)}) copy-start(f32[64,2]{0,1:T(2,128)S(1)} %broadcast_multiply_fusion.4) | copy-start | bytes 1540
  551.1 29.6 %copy-start.216 = (f32[64,2]{0,1:T(2,128)}, f32[64,2]{0,1:T(2,128)S(1)}, u32[]{:S(2)}) copy-start(f32[64,2]{0,1:T(2,128)S(1)} %broadcast_multiply_fusion.5) | copy-start | bytes 1540
  610.5 66.5 %copy-start.40 = (bf16[8,64,3,64]{3,1,2,0:T(8,128)(2,1)}, bf16[8,64,3,64]{3,1,2,0:T(8,128)(2,1)S(1)}, u32[]{:S(2)}) copy-start(bf16[8,64,3,64]{3,1,2,0:T(8,128)(2,1)S(1)} %get-tuple-element.780) | copy-start | bytes 589828
  619.3 30.5 %copy-start.207 = (f32[768]{0:T(1024)S(1)}, f32[768]{0:T(1024)}, u32[]{:S(2)}) copy-start(f32[768]{0:T(1024)} %get-tuple-element.632) | copy-start | bytes 9220
  621.4 45.8 %copy-start.42 = (bf16[8,64,3,64]{3,1,2,0:T(8,128)(2,1)}, bf16[8,64,3,64]{3,1,2,0:T(8,128)(2,1)S(1)}, u32[]{:S(2)}) copy-start(bf16[8,64,3,64]{3,1,2,0:T(8,128)(2,1)S(1)} %get-tuple-element.788) | copy-start | bytes 589828
  653.3 194.5 %all-reduce.7.cloned.1.call-start = ((), (), s32[]{:S(2)}) async-start(), calls=%async_computation.36 | async-start | bytes 5767168
  667.1 206.2 %reduce-scatter.43.cloned.1.call-start = ((), (), s32[]{:S(2)}) async-start(), calls=%async_computation.31 | async-start | bytes 983040 | tf_op jit(solution)/shard_map/reduce_scatter | solution.py:40
  676.7 221.4 %reduce-scatter.37.cloned.1.call-start = ((), (), s32[]{:S(2)}) async-start(), calls=%async_computation.28 | async-start | bytes 983040 | tf_op jit(solution)/shard_map/reduce_scatter | solution.py:40
  685.2 252.6 %reduce-scatter.51.cloned.1.call-start = ((), (), s32[]{:S(2)}) async-start(), calls=%async_computation.35 | async-start | bytes 1327104
  694.9 288.6 %reduce-scatter.49.cloned.1.call-start = ((), (), s32[]{:S(2)}) async-start(), calls=%async_computation.34 | async-start | bytes 2654208
  728.0 313.3 %reduce-scatter.47.cloned.1.call-start = ((), (), s32[]{:S(2)}) async-start(), calls=%async_computation.33 | async-start | bytes 5308416 | tf_op jit(solution)/shard_map/reduce_scatter | solution.py:465
  733.6 365.1 %reduce-scatter.45.cloned.1.call-start = ((), (), s32[]{:S(2)}) async-start(), calls=%async_computation.32 | async-start | bytes 5308416 | tf_op jit(solution)/shard_map/reduce_scatter | solution.py:464
  779.7 69.2 %copy-start.120 = (f32[2,176,192]{2,1,0:T(8,128)S(1)}, f32[2,176,192]{2,1,0:T(8,128)}, u32[]{:S(2)}) copy-start(f32[2,176,192]{2,1,0:T(8,128)} %param.114) | copy-start | bytes 811012
  785.2 112.9 %copy-start.65 = (f32[64,1,768]{2,0,1:T(8,128)S(1)}, f32[64,1,768]{2,0,1:T(8,128)}, u32[]{:S(2)}) copy-start(f32[64,1,768]{2,0,1:T(8,128)} %get-tuple-element.795) | copy-start | bytes 589828
  785.2 112.9 %copy-start.70 = (f32[64,1,768]{2,0,1:T(8,128)S(1)}, f32[64,1,768]{2,0,1:T(8,128)}, u32[]{:S(2)}) copy-start(f32[64,1,768]{2,0,1:T(8,128)} %get-tuple-element.718) | copy-start | bytes 589828
  785.2 112.9 %copy-start.72 = (f32[64,1,768]{2,0,1:T(8,128)S(1)}, f32[64,1,768]{2,0,1:T(8,128)}, u32[]{:S(2)}) copy-start(f32[64,1,768]{2,0,1:T(8,128)} %copy-done.71) | copy-start | bytes 589828
  785.2 112.9 %copy-start.79 = (f32[64,1,768]{2,0,1:T(8,128)S(1)}, f32[64,1,768]{2,0,1:T(8,128)}, u32[]{:S(2)}) copy-start(f32[64,1,768]{2,0,1:T(8,128)} %copy-done.77) | copy-start | bytes 589828
  785.2 112.9 %copy-start.163 = (f32[768]{0:T(1024)S(1)}, f32[768]{0:T(1024)}, u32[]{:S(2)}) copy-start(f32[768]{0:T(1024)} %copy-done.160) | copy-start | bytes 9220
  785.2 112.9 %copy-start.185 = (f32[64,2]{0,1:T(2,128)S(1)}, f32[64,2]{0,1:T(2,128)}, u32[]{:S(2)}) copy-start(f32[64,2]{0,1:T(2,128)} %copy-done.183) | copy-start | bytes 1540
  785.2 112.9 %copy-start.189 = (f32[64,2]{0,1:T(2,128)S(1)}, f32[64,2]{0,1:T(2,128)}, u32[]{:S(2)}) copy-start(f32[64,2]{0,1:T(2,128)} %copy-done.186) | copy-start | bytes 1540
  785.3 112.9 %copy-start.192 = (f32[64,2]{0,1:T(2,128)S(1)}, f32[64,2]{0,1:T(2,128)}, u32[]{:S(2)}) copy-start(f32[64,2]{0,1:T(2,128)} %copy-done.190) | copy-start | bytes 1540
  785.3 112.9 %copy-start.196 = (f32[64,2]{0,1:T(2,128)S(1)}, f32[64,2]{0,1:T(2,128)}, u32[]{:S(2)}) copy-start(f32[64,2]{0,1:T(2,128)} %copy-done.193) | copy-start | bytes 1540
  785.3 112.9 %copy-start.215 = (f32[64,2]{0,1:T(2,128)S(1)}, f32[64,2]{0,1:T(2,128)}, u32[]{:S(2)}) copy-start(f32[64,2]{0,1:T(2,128)} %copy-done.214) | copy-start | bytes 1540
  785.3 112.9 %copy-start.217 = (f32[64,2]{0,1:T(2,128)S(1)}, f32[64,2]{0,1:T(2,128)}, u32[]{:S(2)}) copy-start(f32[64,2]{0,1:T(2,128)} %copy-done.216) | copy-start | bytes 1540
  785.3 112.9 %copy-start.225 = (f32[64,2]{0,1:T(2,128)S(1)}, f32[64,2]{0,1:T(2,128)}, u32[]{:S(2)}) copy-start(f32[64,2]{0,1:T(2,128)} %copy-done.224) | copy-start | bytes 1540
  785.3 112.9 %copy-start.227 = (f32[64,2]{0,1:T(2,128)S(1)}, f32[64,2]{0,1:T(2,128)}, u32[]{:S(2)}) copy-start(f32[64,2]{0,1:T(2,128)} %copy-done.226) | copy-start | bytes 1540
  938.9 46.1 %copy-start.118 = (f32[4,96,192]{1,2,0:T(8,128)S(1)}, f32[4,96,192]{1,2,0:T(8,128)}, u32[]{:S(2)}) copy-start(f32[4,96,192]{1,2,0:T(8,128)} %copy.542) | copy-start | bytes 884740
  938.9 46.1 %copy-start.119 = (f32[4,96,192]{1,2,0:T(8,128)S(1)}, f32[4,96,192]{1,2,0:T(8,128)}, u32[]{:S(2)}) copy-start(f32[4,96,192]{1,2,0:T(8,128)} %copy.555) | copy-start | bytes 884740
  985.3 56.0 %copy-start.98 = (f32[2,768,96]{1,2,0:T(8,128)S(1)}, f32[2,768,96]{1,2,0:T(8,128)}, u32[]{:S(2)}) copy-start(f32[2,768,96]{1,2,0:T(8,128)} %param.120) | copy-start | bytes 1769476
  985.3 56.0 %copy-start.141 = (f32[2,768,96]{1,2,0:T(8,128)S(1)}, f32[2,768,96]{1,2,0:T(8,128)}, u32[]{:S(2)}) copy-start(f32[2,768,96]{1,2,0:T(8,128)} %param.122) | copy-start | bytes 1769476
  988.2 110.5 %copy-start.99 = (f32[2,96,768]{2,1,0:T(8,128)S(1)}, f32[2,96,768]{2,1,0:T(8,128)}, u32[]{:S(2)}) copy-start(f32[2,96,768]{2,1,0:T(8,128)} %param.117) | copy-start | bytes 1769476
  988.2 110.5 %copy-start.142 = (f32[2,96,768]{2,1,0:T(8,128)S(1)}, f32[2,96,768]{2,1,0:T(8,128)}, u32[]{:S(2)}) copy-start(f32[2,96,768]{2,1,0:T(8,128)} %param.119) | copy-start | bytes 1769476
  988.2 110.5 %copy-start.143 = (f32[2,96,768]{2,1,0:T(8,128)S(1)}, f32[2,96,768]{2,1,0:T(8,128)}, u32[]{:S(2)}) copy-start(f32[2,96,768]{2,1,0:T(8,128)} %param.118) | copy-start | bytes 1769476
  (214 other events, 929.5 us)
Sparse Core Ops, SparseCore 0:
  10.5 29.4 all-gather.4
  42.5 25.1 all-gather.6
  69.9 35.3 reduce-scatter.26
  108.0 34.2 reduce-scatter.20
  168.1 24.2 reduce-scatter.28
  195.7 22.2 reduce-scatter.22
  220.5 28.2 all-gather.8
  251.3 29.0 all-gather.10
  284.4 45.4 reduce-scatter.24
  332.0 36.1 reduce-scatter.30
  397.8 32.0 reduce-scatter.32
  435.9 22.5 reduce-scatter.38
  518.7 20.2 reduce-scatter.34
  541.8 18.8 reduce-scatter.40
  653.4 122.4 all-reduce.8
  779.0 68.7 all-reduce.6
  850.0 23.1 reduce-scatter.42
  875.5 22.5 reduce-scatter.36
  901.7 36.0 reduce-scatter.50
  941.0 42.4 reduce-scatter.48
  987.4 53.8 reduce-scatter.46
  1044.7 53.8 reduce-scatter.44
where the time goes:
time: 1120 us; the launch traced here: 1110 us
  waiting for transfers between devices  411 us (37%)
  blocking collectives  275 us (25%)
  local copies, waits for them, and re-layouts  193 us (17%)
  matrix products  120 us (11%)
  other arithmetic  88.4 us (8%)
  between operations  18.3 us (2%)
    all_gather x6, blocking collectives, rows_backward(): return lax.all_gather(values, 'mp', axis=0, tiled=True)  110 us
    unnamed x25, waiting for transfers between devices  107 us
    reduce_scatter x6, waiting for transfers between devices, branch_reduce(): lax.psum_scatter(term(jnp.int32(0), full // lax.axis_size('mp') * lax.axi...  92.6 us
    all_gather x4, blocking collectives, rows_forward(): return lax.all_gather(values, 'mp', axis=0, tiled=True)  80.4 us
    reduce_scatter x6, waiting for transfers between devices, input_reduce(): lax.psum_scatter(term(jnp.int32(0), full // lax.axis_size('mp') * lax.axi...  61.2 us
    reduce_scatter x1, waiting for transfers between devices, local(): lax.psum_scatter(grads['upward'], 'dp', scatter_dimension=1, tiled=True)  54.7 us
    unnamed x534, local copies, waits for them, and re-layouts  53.8 us
    reduce_scatter x1, waiting for transfers between devices, local(): lax.psum_scatter(grads['downward'], 'dp', scatter_dimension=2, tiled=True)  53.1 us
  transfers between devices with their start and end apart: 22, of which 16 were waited for; matrix products, arithmetic and copies ran while one was open for 24% of the time, Pallas kernels for 0%

commit v1 on v0

v1 whole, which is shorter than its diff:
```python
import math

import jax
import jax.numpy as jnp
from jax import lax
from jax.sharding import Mesh
from jax.sharding import PartitionSpec as P

D = 768
HEAD_DIM = 64
F = 3072
E = 1408
NQ = 32
STEP_COUNT = 10

NORM_EPS = 1e-06
BETA_ONE = 0.9
BETA_TWO = 0.999
ADAM_EPS = 1e-08
WEIGHT_DECAY = 0.01
MASKED = -1000000000.0

BF = jnp.bfloat16
F32 = jnp.float32


def swap(values, axis):
    return lax.ppermute(values, axis, [(0, 1), (1, 0)])


def mp_swap(values, distance):
    count = lax.axis_size("mp")
    return lax.ppermute(values, "mp", [(i, i ^ distance) for i in range(count)])


def pick(values, place):
    return lax.dynamic_index_in_dim(values, place, 0, keepdims=False)


def mp_place(pieces):
    me = lax.axis_index("mp")
    total = jnp.zeros((len(pieces),) + pieces[0].shape, pieces[0].dtype)
    for distance, piece in enumerate(pieces):
        total = lax.dynamic_update_index_in_dim(total, piece, me ^ distance, 0)
    return total


def mp_gather(values):
    count = lax.axis_size("mp")
    return mp_place([values] + [mp_swap(values, j) for j in range(1, count)])


def grow(values, axis):
    other = swap(values, axis)
    first = lax.axis_index(axis) == 0
    return jnp.stack([jnp.where(first, values, other), jnp.where(first, other, values)])


def shrink(values, axis):
    me = lax.axis_index(axis)
    sent = pick(values, 1 - me).astype(BF)
    return pick(values, me).astype(F32) + swap(sent, axis).astype(F32)


def tree_gather(values, order):
    for axis in order + ("core",):
        values = grow(values, axis)
    return values


def tree_reduce(values, order):
    for axis in (order + ("core",))[::-1]:
        values = shrink(values, axis)
    return values


def mp_reduce(values):
    count = lax.axis_size("mp")
    me = lax.axis_index("mp")
    total = pick(values, me)
    for j in range(1, count):
        total = total + mp_swap(pick(values, me ^ j).astype(BF), j).astype(F32)
    return total


def axes_to_rows(order):
    bits = len(order)
    natural = [bits - order.index(f"b{k}") for k in range(bits)] + [0]
    return natural


def to_rows(values, order):
    bits = len(order)
    natural = axes_to_rows(order)
    moved = values.transpose(natural + [bits + 2, bits + 1, bits + 3])
    rows = math.prod(moved.shape[: bits + 2])
    return moved.reshape((rows,) + moved.shape[bits + 2 :])


def from_rows(values, order):
    bits = len(order)
    natural = axes_to_rows(order)
    rows = values.shape[0] // 2 ** (bits + 1)
    split = values.reshape((2,) * (bits + 1) + (rows,) + values.shape[1:])
    back = [0] * (bits + 1)
    for place, axis in enumerate(natural):
        back[axis] = place
    return split.transpose(back + [bits + 2, bits + 1, bits + 3])


def split_two(rows):
    width = rows.shape[2] // 2
    halves = rows.reshape(rows.shape[0], rows.shape[1], 2, width)
    return tuple(halves[:, :, i].reshape(rows.shape[0], rows.shape[1] * width) for i in range(2))


def join_two(first, second, count):
    parts = [v.reshape(v.shape[0], count, v.shape[1] // count) for v in (first, second)]
    return jnp.concatenate(parts, axis=2)


def norm_forward(values, gain, shift):
    center = values - jnp.mean(values, axis=-1, keepdims=True)
    spread = jnp.mean(center * center, axis=-1, keepdims=True)
    inverse = lax.rsqrt(spread + NORM_EPS)
    normed = center * inverse
    return (normed * gain + shift, normed, inverse)


def norm_backward(grad_out, normed, inverse, gain):
    scaled = grad_out * gain
    inner = (
        scaled
        - jnp.mean(scaled, axis=-1, keepdims=True)
        - normed * jnp.mean(scaled * normed, axis=-1, keepdims=True)
    )
    grad_gain = jnp.sum(grad_out * normed, axis=0)
    grad_shift = jnp.sum(grad_out, axis=0)
    return (inner * inverse, grad_gain, grad_shift)


def dot(a, b):
    return lax.dot_general(a, b, (((1,), (0,)), ((), ())), preferred_element_type=F32)


def dot_t(a, b):
    return lax.dot_general(a, b, (((1,), (1,)), ((), ())), preferred_element_type=F32)


def t_dot(a, b):
    return lax.dot_general(a, b, (((0,), (0,)), ((), ())), preferred_element_type=F32)


def scores_of(query_heads, key_heads, mask_add):
    raw = jnp.einsum("nqhc,nkhc->nhqk", query_heads, key_heads, preferred_element_type=F32)
    return raw * HEAD_DIM ** (-0.5) + mask_add


def attend_forward(query_heads, key_heads, value_heads, mask_add):
    scores = scores_of(query_heads, key_heads, mask_add)
    top = jnp.max(scores, axis=-1, keepdims=True)
    expo = jnp.exp(scores - top)
    total = jnp.sum(expo, axis=-1, keepdims=True)
    probs = expo / total
    context = jnp.einsum(
        "nhqk,nkhc->nqhc", probs.astype(BF), value_heads, preferred_element_type=F32
    )
    return (context.astype(BF), probs)


def attend_backward(query_heads, key_heads, value_heads, probs, grad_context):
    grad_probs = jnp.einsum(
        "nqhc,nkhc->nhqk", grad_context, value_heads, preferred_element_type=F32
    )
    grad_value = jnp.einsum(
        "nhqk,nqhc->nkhc", probs.astype(BF), grad_context, preferred_element_type=F32
    )
    grad_scores = probs * (grad_probs - jnp.sum(probs * grad_probs, axis=-1, keepdims=True))
    grad_scores = grad_scores.astype(BF)
    scale = HEAD_DIM ** (-0.5)
    grad_query = (
        jnp.einsum("nhqk,nkhc->nqhc", grad_scores, key_heads, preferred_element_type=F32) * scale
    )
    grad_key = (
        jnp.einsum("nhqk,nqhc->nkhc", grad_scores, query_heads, preferred_element_type=F32) * scale
    )
    return (grad_query.astype(BF), grad_key.astype(BF), grad_value.astype(BF))


def column_sum(values):
    return jnp.sum(values.astype(F32), axis=0)


def adam_update(weight, first, second, grad, rate):
    first_new = BETA_ONE * first + (1.0 - BETA_ONE) * grad
    second_new = BETA_TWO * second + (1.0 - BETA_TWO) * grad * grad
    first_hat = first_new / (1.0 - BETA_ONE**STEP_COUNT)
    second_hat = second_new / (1.0 - BETA_TWO**STEP_COUNT)
    weight_new = weight - rate * (
        first_hat / (jnp.sqrt(second_hat) + ADAM_EPS) + WEIGHT_DECAY * weight
    )
    return (first_new, second_new, weight_new)


def local(
    bits,
    hidden,
    images,
    caption_len,
    cotangent,
    attn_in,
    attn_in_first,
    attn_in_second,
    attn_out,
    attn_out_first,
    attn_out_second,
    cross_key_value_maps,
    cross_kv_first,
    cross_kv_second,
    ffn_up,
    ffn_up_first,
    ffn_up_second,
    ffn_down,
    ffn_down_first,
    ffn_down_second,
    vec_rep,
    vec_rep_first,
    vec_rep_second,
    query_value_bias_rows,
    vec_head_first,
    vec_head_second,
    bias_up,
    bias_up_first,
    bias_up_second,
):
    forth = tuple(f"b{k}" for k in range(bits))
    back = forth[::-1]
    every = forth + ("core", "mp")
    mp = lax.axis_size("mp")
    me = lax.axis_index("mp")
    group = me & 1
    pair = me - group
    items = hidden.shape[0] // mp
    row_count = hidden.shape[1]
    rows = items * NQ

    def side(values):
        return jnp.concatenate([values[0], values[1]], axis=1)

    low_in = attn_in.astype(BF)
    low_out = attn_out.astype(BF).transpose(0, 2, 1)
    low_kv = cross_key_value_maps.astype(BF)
    low_up = ffn_up.astype(BF)
    low_down = ffn_down.astype(BF).transpose(0, 2, 1)
    qk_all = mp_gather(side(low_in[:2]))
    vc_all = mp_gather(side(low_in[2:]))
    kv_all = mp_gather(side(low_kv))
    oo_all = mp_gather(side(low_out))

    def group_gather(values):
        mine, other = pick(values, group), pick(values, 1 - group)
        pieces = [mine] + [mp_swap(other if j % 2 else mine, j) for j in range(1, mp)]
        return mp_place(pieces)

    up_all = group_gather(low_up)
    down_all = group_gather(low_down)
    w_query, w_key = split_two(to_rows(tree_gather(qk_all, forth), forth))
    w_value, w_cross = split_two(to_rows(tree_gather(vc_all, back), back))
    w_ck, w_cv = split_two(to_rows(tree_gather(kv_all, forth), forth))
    w_out, w_cout = split_two(to_rows(tree_gather(oo_all, back), back))
    up_rows = to_rows(tree_gather(up_all, forth), forth)
    w_up = up_rows.reshape(up_rows.shape[0], -1)
    down_rows = to_rows(tree_gather(down_all, back), back)
    w_down = down_rows.reshape(down_rows.shape[0], -1)

    head_all = lax.all_gather(query_value_bias_rows, "mp", axis=1, tiled=True)
    bias_all = lax.all_gather(bias_up, "mp", axis=1, tiled=True)

    tokens = lax.dynamic_slice_in_dim(hidden, me * items, items, 0)
    image_rows = lax.dynamic_slice_in_dim(images, me * items, items, 0)
    lengths = lax.dynamic_slice_in_dim(caption_len, me * items, items, 0)
    image_flat = image_rows.reshape(items * image_rows.shape[1], image_rows.shape[2])
    tokens_flat = tokens.reshape(items * row_count, D)
    heads = D // HEAD_DIM

    def split_heads(values, length):
        return values.reshape(items, length, heads, HEAD_DIM)

    def merge(values):
        return values.reshape(-1, D)

    positions = jnp.arange(row_count)
    valid = (positions[None, :] < NQ) | (positions[None, :] - NQ < lengths[:, None])
    mask_add = jnp.where(valid, 0.0, MASKED).astype(F32)[:, None, None, :]
    query = split_heads((dot(tokens_flat, w_query) + head_all[0]).astype(BF), row_count)
    key = split_heads(dot(tokens_flat, w_key).astype(BF), row_count)
    value = split_heads((dot(tokens_flat, w_value) + head_all[1]).astype(BF), row_count)
    context, probs = attend_forward(query, key, value, mask_add)
    context_flat = merge(context)
    first_out, first_normed, first_inverse = norm_forward(
        tokens_flat.astype(F32) + dot_t(context_flat, w_out) + vec_rep[0], vec_rep[4], vec_rep[5]
    )
    first_items = first_out.reshape(items, 2, NQ, D)
    first_query = first_items[:, 0].reshape(rows, D)
    first_low = first_query.astype(BF)
    keys = image_rows.shape[1]
    cross_query = split_heads((dot(first_low, w_cross) + head_all[2]).astype(BF), NQ)
    cross_key = split_heads(dot(image_flat, w_ck).astype(BF), keys)
    cross_value = split_heads((dot(image_flat, w_cv) + head_all[3]).astype(BF), keys)
    cross_context, cross_probs = attend_forward(cross_query, cross_key, cross_value, F32(0.0))
    cross_flat = merge(cross_context)
    second_out, second_normed, second_inverse = norm_forward(
        first_query + dot_t(cross_flat, w_cout) + vec_rep[1], vec_rep[6], vec_rep[7]
    )

    caption_rows = first_items[:, 1].reshape(rows, D)
    is_low = group == 0
    kept = jnp.where(is_low, second_out, caption_rows)
    given = mp_swap(jnp.where(is_low, caption_rows, second_out).astype(BF), 1).astype(F32)
    ffn_rows = jnp.concatenate(
        [jnp.where(is_low, kept, given), jnp.where(is_low, given, kept)], axis=0
    )
    top = lax.dynamic_slice_in_dim(cotangent, pair * items, 2 * items, 0)
    top = top.reshape(2 * items, 2, NQ, D)
    top = lax.dynamic_index_in_dim(top, group, 1, keepdims=False)
    top = top.reshape(2 * rows, D).astype(F32)
    third_bias = pick(vec_rep[2:4], group)
    third_gain = jnp.where(is_low, vec_rep[8], vec_rep[10])
    third_shift = jnp.where(is_low, vec_rep[9], vec_rep[11])
    ffn_low = ffn_rows.astype(BF)
    up_pre = dot(ffn_low, w_up) + pick(bias_all, group)
    gelu_value, gelu_pull = jax.vjp(lambda v: jax.nn.gelu(v, approximate=False), up_pre)
    up_act = gelu_value.astype(BF)
    third_out, third_normed, third_inverse = norm_forward(
        ffn_rows + dot_t(up_act, w_down) + third_bias, third_gain, third_shift
    )
    out_all = mp_gather(third_out.astype(BF))
    layer_out = (
        out_all.reshape(mp // 2, 2, 2, items, NQ, D)
        .transpose(0, 2, 3, 1, 4, 5)
        .reshape(mp * items, row_count, D)
    )
    grad_third, gain_third, shift_third = norm_backward(
        top, third_normed, third_inverse, third_gain
    )
    grad_ffn = grad_third.astype(BF)
    third_bias_sum = column_sum(grad_ffn)
    grad_down = t_dot(grad_ffn, up_act)
    grad_act = dot(grad_ffn, w_down)
    grad_pre = gelu_pull(grad_act)[0].astype(BF)
    bias_sum = column_sum(grad_pre)
    grad_up = t_dot(ffn_low, grad_pre)
    grad_rows = grad_third + dot_t(grad_pre, w_up)
    mine = jnp.where(is_low, grad_rows[:rows], grad_rows[rows:])
    theirs = jnp.where(is_low, grad_rows[rows:], grad_rows[:rows])
    got = mp_swap(theirs.astype(BF), 1).astype(F32)
    grad_second = jnp.where(is_low, mine, got)
    grad_caption = jnp.where(is_low, got, mine)

    grad_cross, gain_second, shift_second = norm_backward(
        grad_second, second_normed, second_inverse, vec_rep[6]
    )
    grad_cross_low = grad_cross.astype(BF)
    second_bias_sum = column_sum(grad_cross_low)
    grad_cout = t_dot(grad_cross_low, cross_flat)
    cross_back = split_heads(dot(grad_cross_low, w_cout).astype(BF), NQ)
    cross_gq, cross_gk, cross_gv = attend_backward(
        cross_query, cross_key, cross_value, cross_probs, cross_back
    )
    cross_gq, cross_gk, cross_gv = merge(cross_gq), merge(cross_gk), merge(cross_gv)
    grad_wcross = t_dot(first_low, cross_gq)
    grad_ck = t_dot(image_flat, cross_gk)
    grad_cv = t_dot(image_flat, cross_gv)
    grad_first_query = grad_cross + dot_t(cross_gq, w_cross)

    grad_first = jnp.stack(
        [grad_first_query.reshape(items, NQ, D), grad_caption.reshape(items, NQ, D)], axis=1
    ).reshape(items * row_count, D)
    grad_self, gain_first, shift_first = norm_backward(
        grad_first, first_normed, first_inverse, vec_rep[4]
    )
    grad_self_low = grad_self.astype(BF)
    first_bias_sum = column_sum(grad_self_low)
    grad_out = t_dot(grad_self_low, context_flat)
    self_back = split_heads(dot(grad_self_low, w_out).astype(BF), row_count)
    self_gq, self_gk, self_gv = attend_backward(query, key, value, probs, self_back)
    self_gq, self_gk, self_gv = merge(self_gq), merge(self_gk), merge(self_gv)
    grad_query = t_dot(tokens_flat, self_gq)
    grad_key = t_dot(tokens_flat, self_gk)
    grad_value = t_dot(tokens_flat, self_gv)
    grad_tokens = (
        grad_self + dot_t(self_gq, w_query) + dot_t(self_gk, w_key) + dot_t(self_gv, w_value)
    )
    grad_hidden = (
        mp_gather(grad_tokens.astype(BF)).reshape(mp * items, row_count, D).astype(F32)
    )

    none = jnp.zeros_like(third_bias_sum)

    def of_group(values):
        return jnp.where(is_low, values, none), jnp.where(is_low, none, values)

    bias_low, bias_high = of_group(third_bias_sum)
    gain_low, gain_high = of_group(gain_third)
    shift_low, shift_high = of_group(shift_third)
    shared = jnp.stack(
        [
            first_bias_sum,
            second_bias_sum,
            bias_low,
            bias_high,
            gain_first,
            shift_first,
            gain_second,
            shift_second,
            gain_low,
            shift_low,
            gain_high,
            shift_high,
        ]
    )
    headwise = jnp.stack(
        [column_sum(self_gq), column_sum(self_gv), column_sum(cross_gq), column_sum(cross_gv)]
    )
    hidden_bias = jnp.stack(
        [
            jnp.where(is_low, bias_sum, jnp.zeros_like(bias_sum)),
            jnp.where(is_low, jnp.zeros_like(bias_sum), bias_sum),
        ]
    )
    reduced_rep, head_total, bias_total = lax.psum((shared, headwise, hidden_bias), every)
    head_width = query_value_bias_rows.shape[1]
    bias_width = bias_up.shape[1]
    reduced_head = lax.dynamic_slice_in_dim(head_total, me * head_width, head_width, 1)
    reduced_bias = lax.dynamic_slice_in_dim(bias_total, me * bias_width, bias_width, 1)

    def reduce_two(first, second, order):
        pieces = from_rows(join_two(first, second, mp), order)
        total = mp_reduce(tree_reduce(pieces, order))
        width = total.shape[1] // 2
        return jnp.stack([total[:, :width], total[:, width:]])

    def reduce_group(values, order):
        pieces = from_rows(values.reshape(values.shape[0], mp, -1), order)
        local_sum = tree_reduce(pieces, order)
        mine = pick(local_sum, me)
        other = jnp.zeros_like(mine)
        for j in range(1, mp):
            got = mp_swap(pick(local_sum, me ^ j).astype(BF), j).astype(F32)
            if j % 2:
                other = other + got
            else:
                mine = mine + got
        return jnp.stack([jnp.where(is_low, mine, other), jnp.where(is_low, other, mine)])

    reduced_down = reduce_group(grad_down, back).transpose(0, 2, 1)
    reduced_up = reduce_group(grad_up, forth)
    reduced_kv = reduce_two(grad_ck, grad_cv, forth)
    reduced_out = reduce_two(grad_out, grad_cout, back).transpose(0, 2, 1)
    reduced_in = jnp.concatenate(
        [reduce_two(grad_query, grad_key, forth), reduce_two(grad_value, grad_wcross, back)]
    )
    rates = (
        2.0 / math.sqrt(D),
        2.0 / math.sqrt(max(D // 8, 1)),
        2.0 / math.sqrt(E),
        2.0 / math.sqrt(D),
        2.0 / math.sqrt(F),
        0.3,
        0.3,
        0.3,
    )
    weights = (
        attn_in,
        attn_out,
        cross_key_value_maps,
        ffn_up,
        ffn_down,
        vec_rep,
        query_value_bias_rows,
        bias_up,
    )
    firsts = (
        attn_in_first,
        attn_out_first,
        cross_kv_first,
        ffn_up_first,
        ffn_down_first,
        vec_rep_first,
        vec_head_first,
        bias_up_first,
    )
    seconds = (
        attn_in_second,
        attn_out_second,
        cross_kv_second,
        ffn_up_second,
        ffn_down_second,
        vec_rep_second,
        vec_head_second,
        bias_up_second,
    )
    reduced = (
        reduced_in,
        reduced_out,
        reduced_kv,
        reduced_up,
        reduced_down,
        reduced_rep,
        reduced_head,
        reduced_bias,
    )
    results = []
    for weight, first, second, grad, rate in zip(weights, firsts, seconds, reduced, rates):
        results.extend(adam_update(weight, first, second, grad, rate))
    return (layer_out, grad_hidden, *results)


def solution(mesh):
    dp, mp = mesh.devices.shape
    bits = (dp // 2).bit_length() - 1
    names = tuple(f"b{k}" for k in range(bits)) + ("core",)
    fine = Mesh(mesh.devices.reshape((2,) * (bits + 1) + (mp,)), names + ("mp",))
    split = P(names)
    inward = P(None, names, "mp")
    outward = P(None, "mp", names)
    head = P(None, "mp")
    placed = (
        (split,) * 4
        + (inward,) * 3
        + (outward,) * 3
        + (inward,) * 6
        + (outward,) * 3
        + (P(),) * 3
        + (head,) * 6
    )
    out_placed = (
        (split,) * 2
        + (inward,) * 3
        + (outward,) * 3
        + (inward,) * 6
        + (outward,) * 3
        + (P(),) * 3
        + (head,) * 6
    )
    return jax.shard_map(
        lambda *arrays: local(bits, *arrays),
        mesh=fine,
        in_specs=placed,
        out_specs=out_placed,
        check_vma=False,
    )
```

time: 1120 us -> 1040 us (0.929)
  blocking collectives: 275 us -> 28.1 us
  local copies, waits for them, and re-layouts: 193 us -> 415 us
  waiting for transfers between devices: 411 us -> 257 us
  starting transfers between devices: 2.06 us -> 113 us
  matrix products: 120 us -> 88.7 us
  other arithmetic: 88.4 us -> 110 us
    reduce_scatter x14 -> x0, waiting for transfers between devices: 262 us -> none  [the longest x6 92.6 us: branch_reduce(): lax.psum_scatter(term(jnp.int32(0), full // lax.axis_size('mp') * lax.axi...]
    all_gather x15 -> x2, blocking collectives: 275 us -> 28.1 us  [the longest x1 14.5 us: local(): bias_all = lax.all_gather(bias_up, 'mp', axis=1, tiled=True)]
    ppermute x0 -> x80, waiting for transfers between devices: none -> 140 us  [the longest x36 87.1 us: swap(): return lax.ppermute(values, axis, [(0, 1), (1, 0)])]
    psum x1, waiting for transfers between devices: 0.01 us -> 117 us  [local(): lax.psum((shared, headwise, hidden_bias), every)]
    ppermute x0 -> x80, starting transfers between devices: none -> 113 us  [the longest x44 82 us: mp_swap(): return lax.ppermute(values, 'mp', [(i, i ^ distance) for i in range(count)])]
    unnamed x25 -> x1, waiting for transfers between devices: 107 us -> 0.02 us
    slice x30 -> x16, local copies, waits for them, and re-layouts: 40.6 us -> 116 us  [the longest x12 115 us: split_two(): halves[:, :, i].reshape(rows.shape[0], rows.shape[1] * width)]
    reshape x4 -> x22, local copies, waits for them, and re-layouts: 5.37 us -> 59 us  [the longest x11 35.5 us: split_heads(): return values.reshape(items, length, heads, HEAD_DIM)]
  transfers between devices with their start and end apart: 22 -> 81, of which waited for: 16 -> 31; matrix products, arithmetic and copies ran while one was open for 24% -> 55% of each run, Pallas kernels for 0% -> 0%
where the time goes in v1:
time: 1040 us; the launch traced here: 1030 us
  local copies, waits for them, and re-layouts  415 us (40%)
  waiting for transfers between devices  257 us (25%)
  starting transfers between devices  113 us (11%)
  other arithmetic  110 us (11%)
  matrix products  88.7 us (9%)
  blocking collectives  28.1 us (3%)
  between operations  17.2 us (2%)
    psum x1, waiting for transfers between devices, local(): lax.psum((shared, headwise, hidden_bias), every)  117 us
    slice x12, local copies, waits for them, and re-layouts, split_two(): halves[:, :, i].reshape(rows.shape[0], rows.shape[1] * width)  115 us
    ppermute x36, waiting for transfers between devices, swap(): return lax.ppermute(values, axis, [(0, 1), (1, 0)])  87.1 us
    ppermute x44, starting transfers between devices, mp_swap(): return lax.ppermute(values, 'mp', [(i, i ^ distance) for i in range(count)])  82 us
    ppermute x44, waiting for transfers between devices, mp_swap(): return lax.ppermute(values, 'mp', [(i, i ^ distance) for i in range(count)])  52.9 us
    dynamic_update_slice x26, local copies, waits for them, and re-layouts, mp_place(): total = lax.dynamic_update_index_in_dim(total, piece, me ^ distance, 0)  47.6 us
    another operation x31, other arithmetic, grow(): jnp.stack([jnp.where(first, values, other), jnp.where(first, other, value...  41.7 us
    another operation x4, local copies, waits for them, and re-layouts, split_two(): halves = rows.reshape(rows.shape[0], rows.shape[1], 2, width)  37 us
  transfers between devices with their start and end apart: 81, of which 31 were waited for; matrix products, arithmetic and copies ran while one was open for 55% of the time, Pallas kernels for 0%

profile of v1, /device:TPU:0, one launch (start us, length us, event | category | flops | bytes accessed | tf_op | source)
XLA Modules:
  0.0 1028.4 jit_solution(8822847632198504369)
XLA Ops:
  27.2 4.2 reshape.433
  31.5 4.3 reshape.462
  38.0 13.6 %all-gather = f32[4,192,4]{1,2,0:T(4,128)S(1)} all-gather(f32[1,192,4]{1,2,0:T(4,128)S(1)} %bitcast.697), channel_id=1, replica_groups=mesh['b0'=2,'b1'=2,'core'=2,'mp'=4] {'mp'}, dimensions={0}, use_global_device_ids=true | all-gather | bytes 15360 | tf_op jit(solution)/shard_map/all_gather | solution.py:276
  54.5 14.5 %all_gather.7 = f32[2,3072]{1,0:T(2,128)} all-gather(f32[2,768]{1,0:T(2,128)} %param.53), channel_id=1, replica_groups=mesh['b0'=2,'b1'=2,'core'=2,'mp'=4] {'mp'}, dimensions={1}, use_global_device_ids=true | all-gather | bytes 30720 | tf_op jit(solution)/shard_map/all_gather | solution.py:277
  95.6 4.9 collective-permute-done.7
  101.6 6.0 collective-permute-done.1
  124.5 4.6 collective-permute-done.14
  131.6 5.3 collective-permute-start.32
  175.8 4.3 dynamic_update_slice.119
  192.3 4.1 collective-permute-done.28
  198.2 10.8 %collective-permute-done.16 = bf16[2,4,96,384]{3,2,1,0:T(8,128)(2,1)S(1)} collective-permute-done((bf16[2,4,96,384]{3,2,1,0:T(8,128)(2,1)S(1)}, bf16[2,4,96,384]{3,2,1,0:T(8,128)(2,1)S(1)}, u32[]{:S(2)}, u32[]{:S(2)}) %collective-permute-start.16) | collective-permute-done | bytes 589856 | tf_op jit(solution)/shard_map/ppermute | solution.py:28
  211.6 5.4 collective-permute-done.4
  218.4 4.9 collective-permute-done.22
  225.4 4.2 collective-permute-done.35
  243.5 7.9 reshape_reshape.26
  251.5 9.4 fusion.148
  260.8 8.2 copy.311
  272.8 7.9 reshape_reshape.25
  280.7 9.4 fusion.150
  290.1 6.7 copy.295
  301.4 6.7 copy.297
  314.2 7.9 reshape_reshape.24
  322.1 9.8 fusion.149
  331.9 8.1 copy.289
  356.0 8.3 copy.318
  367.2 8.1 copy.325
  380.6 13.2 %reshape_reshape.27 = bf16[1408,4,2,192]{3,2,0,1:T(2,128)(2,1)} reshape(bf16[2,2,2,176,4,384]{5,3,2,1,0,4:T(8,128)(2,1)} %maximum_bitcast_fusion.1) | data formatting | bytes 8650752 | tf_op jit(solution)/shard_map/reshape;reshape | solution.py:113
  393.8 12.8 %fusion.147 = (bf16[1408,4,1,192]{3,2,0,1:T(2,128)(2,1)}, bf16[1408,4,1,192]{3,2,0,1:T(2,128)(2,1)}) fusion(bf16[1408,4,2,192]{3,2,0,1:T(2,128)(2,1)} %reshape_reshape.27), kind=kLoop, calls=%fused_computation.470 | loop fusion | bytes 8650752 | tf_op jit(solution)/shard_map/slice | solution.py:114
  406.6 13.8 %copy.319 = bf16[1408,4,1,192]{0,3,1,2:T(8,128)(2,1)} copy(bf16[1408,4,1,192]{3,2,0,1:T(2,128)(2,1)} %get-tuple-element.172) | data formatting | bytes 4325376 | tf_op jit(solution)/shard_map/slice | solution.py:114
  420.4 6.3 convolution_convert_fusion
  426.7 6.1 reshape.466
  432.8 6.6 copy.322
  439.5 13.9 %copy.316 = bf16[1408,4,1,192]{0,3,1,2:T(8,128)(2,1)} copy(bf16[1408,4,1,192]{3,2,0,1:T(2,128)(2,1)} %get-tuple-element.173) | data formatting | bytes 4325376 | tf_op jit(solution)/shard_map/slice | solution.py:114
  462.2 5.9 reshape.465
  468.2 6.6 copy.323
  482.2 5.4 collective-permute-done.24
  488.5 4.3 select_bitcast_fusion.1
  497.8 4.5 select_bitcast_fusion.3
  508.4 8.2 multiply_convert_fusion.1
  519.1 5.1 fusion.128
  528.2 5.0 fusion.113
  542.3 12.5 %reshape_reshape.31 = f32[2,2,2,96,4,768]{5,4,3,2,1,0:T(4,128)} reshape(f32[768,3072]{1,0:T(8,128)} %fusion.128) | data formatting | bytes 18874368 | tf_op jit(solution)/shard_map/reshape;reshape | solution.py:104
  563.7 12.9 %reshape_reshape.30 = f32[2,2,2,96,4,768]{5,4,3,2,1,0:T(4,128)} reshape(f32[768,3072]{1,0:T(8,128)} %fusion.113) | data formatting | bytes 18874368 | tf_op jit(solution)/shard_map/reshape;reshape | solution.py:104
  588.8 4.8 convert_reduce_fusion
  607.6 4.6 convert_reduce_fusion.2
  636.7 4.9 copy.369
  641.6 4.7 reshape.451
  646.3 4.9 copy.371
  651.2 5.0 reshape.452
  656.3 5.7 fusion.162
  669.2 9.1 copy.372
  686.2 6.1 copy.363
  698.7 6.0 copy.355
  710.5 6.3 copy.358
  721.8 117.1 %all-reduce.3.cloned.1.call-done = (f32[12,768]{1,0:T(8,128)}, f32[4,768]{1,0:T(4,128)}, f32[2,3072]{1,0:T(2,128)}) async-done(((f32[12,768]{1,0:T(8,128)}, f32[4,768]{1,0:T(4,128)}, f32[2,3072]{1,0:T(2,128)}), (f32[12,768]{1,0:T(8,128)}, f32[4,768]{1,0:T(4,128)}, f32[2,3072]{1,0:T(2,128)})) %all-reduce.3.cloned.1.call-update) | async-done | bytes 73744 | tf_op jit(solution)/shard_map/psum | solution.py:431
  844.4 4.9 collective-permute-start.43
  854.7 4.7 collective-permute-done.43
  871.1 11.6 %collective-permute-done.57 = bf16[2,4,96,384]{3,2,0,1:T(8,128)(2,1)S(1)} collective-permute-done((bf16[2,4,96,384]{3,2,0,1:T(8,128)(2,1)S(1)}, bf16[2,4,96,384]{3,2,0,1:T(8,128)(2,1)S(1)}, u32[]{:S(2)}, u32[]{:S(2)}) %collective-permute-start.57) | collective-permute-done | bytes 589856 | tf_op jit(solution)/shard_map/ppermute | solution.py:28
  885.3 10.1 collective-permute-done.51
  897.2 9.0 collective-permute-start.59
  941.7 18.8 %collective-permute-done.63 = bf16[2,4,176,384]{3,2,0,1:T(8,128)(2,1)S(1)} collective-permute-done((bf16[2,4,176,384]{3,2,0,1:T(8,128)(2,1)S(1)}, bf16[2,4,176,384]{3,2,0,1:T(8,128)(2,1)S(1)}, u32[]{:S(2)}, u32[]{:S(2)}) %collective-permute-start.63) | collective-permute-done | bytes 1081376 | tf_op jit(solution)/shard_map/ppermute | solution.py:28
  971.2 4.8 collective-permute-done.64
  990.3 5.5 collective-permute-done.76
  1003.2 9.3 collective-permute-done.77
  (773 shorter events, 420.6 us)
Async XLA Ops:
  7.2 831.6 %all-reduce.3.cloned.1.call-start = ((), (), s32[]{:S(2)}) async-start(), calls=%async_computation | async-start | bytes 172032 | tf_op jit(solution)/shard_map/psum | solution.py:431
  9.3 130.7 %collective-permute-start.31 = (bf16[96,768]{1,0:T(8,128)(2,1)}, bf16[96,768]{1,0:T(8,128)(2,1)}, u32[]{:S(2)}, u32[]{:S(2)}) collective-permute-start(bf16[96,768]{1,0:T(8,128)(2,1)} %get-tuple-element.247), channel_id=1, source_target_pairs={{0,1},{1,0},{2,3},{3,2},{4,5},{5,4},{6,7},{7,6},{8,9},{9,8},{10,11... | collective-permute-start | bytes 442376 | tf_op jit(solution)/shard_map/ppermute | solution.py:33
  12.3 132.2 %collective-permute-start.33 = (bf16[96,768]{1,0:T(8,128)(2,1)}, bf16[96,768]{1,0:T(8,128)(2,1)}, u32[]{:S(2)}, u32[]{:S(2)}) collective-permute-start(bf16[96,768]{1,0:T(8,128)(2,1)} %get-tuple-element.247), channel_id=1, source_target_pairs={{0,3},{1,2},{2,1},{3,0},{4,7},{5,6},{6,5},{7,4},{8,11},{9,10},{10,... | collective-permute-start | bytes 442376 | tf_op jit(solution)/shard_map/ppermute | solution.py:33
  16.4 93.7 %collective-permute-start.12 = (bf16[96,384]{0,1:T(8,128)(2,1)}, bf16[96,384]{0,1:T(8,128)(2,1)}, u32[]{:S(2)}, u32[]{:S(2)}) collective-permute-start(bf16[96,384]{0,1:T(8,128)(2,1)} %get-tuple-element.265), channel_id=1, source_target_pairs={{0,1},{1,0},{2,3},{3,2},{4,5},{5,4},{6,7},{7,6},{8,9},{9,8},{10,11... | collective-permute-start | bytes 221192 | tf_op jit(solution)/shard_map/ppermute | solution.py:33
  17.1 94.1 %collective-permute-start.13 = (bf16[96,384]{0,1:T(8,128)(2,1)}, bf16[96,384]{0,1:T(8,128)(2,1)}, u32[]{:S(2)}, u32[]{:S(2)}) collective-permute-start(bf16[96,384]{0,1:T(8,128)(2,1)} %get-tuple-element.265), channel_id=1, source_target_pairs={{0,2},{1,3},{2,0},{3,1},{4,6},{5,7},{6,4},{7,5},{8,10},{9,11},{10,... | collective-permute-start | bytes 221192 | tf_op jit(solution)/shard_map/ppermute | solution.py:33
  19.9 69.1 %collective-permute-start.6 = (bf16[96,384]{1,0:T(8,128)(2,1)}, bf16[96,384]{1,0:T(8,128)(2,1)}, u32[]{:S(2)}, u32[]{:S(2)}) collective-permute-start(bf16[96,384]{1,0:T(8,128)(2,1)} %get-tuple-element.169), channel_id=1, source_target_pairs={{0,1},{1,0},{2,3},{3,2},{4,5},{5,4},{6,7},{7,6},{8,9},{9,8},{10,11... | collective-permute-start | bytes 221192 | tf_op jit(solution)/shard_map/ppermute | solution.py:33
  110.2 21.5 %collective-permute-start.18 = (bf16[176,384]{1,0:T(8,128)(2,1)}, bf16[176,384]{1,0:T(8,128)(2,1)S(1)}, u32[]{:S(2)}, u32[]{:S(2)}) collective-permute-start(bf16[176,384]{1,0:T(8,128)(2,1)} %get-tuple-element.167), channel_id=1, source_target_pairs={{0,1},{1,0},{2,3},{3,2},{4,5},{5,4},{6,7},{7,6},{8,9},{9,8},{10,11... | collective-permute-start | bytes 405512 | tf_op jit(solution)/shard_map/ppermute | solution.py:33
  111.2 25.8 %collective-permute-start.19 = (bf16[176,384]{1,0:T(8,128)(2,1)}, bf16[176,384]{1,0:T(8,128)(2,1)S(1)}, u32[]{:S(2)}, u32[]{:S(2)}) collective-permute-start(bf16[176,384]{1,0:T(8,128)(2,1)} %get-tuple-element.167), channel_id=1, source_target_pairs={{0,2},{1,3},{2,0},{3,1},{4,6},{5,7},{6,4},{7,5},{8,10},{9,11},{10,... | collective-permute-start | bytes 405512 | tf_op jit(solution)/shard_map/ppermute | solution.py:33
  129.1 9.5 collective-permute-start.20
  131.6 10.9 %collective-permute-start.32 = (bf16[96,768]{1,0:T(8,128)(2,1)S(1)}, bf16[96,768]{1,0:T(8,128)(2,1)S(1)}, u32[]{:S(2)}, u32[]{:S(2)}) collective-permute-start(bf16[96,768]{1,0:T(8,128)(2,1)S(1)} %copy-done.85), channel_id=1, source_target_pairs={{0,2},{1,3},{2,0},{3,1},{4,6},{5,7},{6,4},{7,5},{8,10},{9,11},{10,... | collective-permute-start | bytes 442376 | tf_op jit(solution)/shard_map/ppermute | solution.py:33
  137.0 43.1 %collective-permute-start.15 = (bf16[4,96,384]{2,1,0:T(8,128)(2,1)}, bf16[4,96,384]{2,1,0:T(8,128)(2,1)}, u32[]{:S(2)}, u32[]{:S(2)}) collective-permute-start(bf16[4,96,384]{2,1,0:T(8,128)(2,1)} %constant_dynamic-update-slice_fusion), channel_id=1, source_target_pairs={{0,8},{8,0},{1,9},{9,1},{2,10},{10,2},{3,11},{11,3},{4,12},{12,4},... | collective-permute-start | bytes 884744 | tf_op jit(solution)/shard_map/ppermute | solution.py:28
  138.6 8.7 collective-permute-start.25
  139.9 25.0 %collective-permute-start.27 = (bf16[96,768]{1,0:T(8,128)(2,1)}, bf16[96,768]{1,0:T(8,128)(2,1)}, u32[]{:S(2)}, u32[]{:S(2)}) collective-permute-start(bf16[96,768]{1,0:T(8,128)(2,1)} %get-tuple-element.249), channel_id=1, source_target_pairs={{0,3},{1,2},{2,1},{3,0},{4,7},{5,6},{6,5},{7,4},{8,11},{9,10},{10,... | collective-permute-start | bytes 442376 | tf_op jit(solution)/shard_map/ppermute | solution.py:33
  144.5 37.3 %collective-permute-start.9 = (bf16[4,96,384]{2,1,0:T(8,128)(2,1)}, bf16[4,96,384]{2,1,0:T(8,128)(2,1)}, u32[]{:S(2)}, u32[]{:S(2)}) collective-permute-start(bf16[4,96,384]{2,1,0:T(8,128)(2,1)} %bitcast_dynamic-update-slice_fusion.12), channel_id=1, source_target_pairs={{0,16},{16,0},{1,17},{17,1},{2,18},{18,2},{3,19},{19,3},{4,20},{20... | collective-permute-start | bytes 884744 | tf_op jit(solution)/shard_map/ppermute | solution.py:28
  147.2 37.4 %collective-permute-start.3 = (bf16[4,96,384]{2,1,0:T(8,128)(2,1)}, bf16[4,96,384]{2,1,0:T(8,128)(2,1)}, u32[]{:S(2)}, u32[]{:S(2)}) collective-permute-start(bf16[4,96,384]{2,1,0:T(8,128)(2,1)} %bitcast_dynamic-update-slice_fusion.16), channel_id=1, source_target_pairs={{0,8},{8,0},{1,9},{9,1},{2,10},{10,2},{3,11},{11,3},{4,12},{12,4},... | collective-permute-start | bytes 884744 | tf_op jit(solution)/shard_map/ppermute | solution.py:28
  150.3 36.2 %collective-permute-start.21 = (bf16[4,176,384]{2,1,0:T(8,128)(2,1)S(1)}, bf16[4,176,384]{2,1,0:T(8,128)(2,1)}, u32[]{:S(2)}, u32[]{:S(2)}) collective-permute-start(bf16[4,176,384]{2,1,0:T(8,128)(2,1)S(1)} %bitcast_dynamic-update-slice_fusion.8), channel_id=1, source_target_pairs={{0,16},{16,0},{1,17},{17,1},{2,18},{18,2},{3,19},{19,3},{4,20},{20... | collective-permute-start | bytes 1622024 | tf_op jit(solution)/shard_map/ppermute | solution.py:28
  164.9 23.4 %collective-permute-start.34 = (bf16[4,96,768]{2,0,1:T(4,128)(2,1)S(1)}, bf16[4,96,768]{2,0,1:T(4,128)(2,1)}, u32[]{:S(2)}, u32[]{:S(2)}) collective-permute-start(bf16[4,96,768]{2,0,1:T(4,128)(2,1)S(1)} %dynamic_update_slice.123), channel_id=1, source_target_pairs={{0,8},{8,0},{1,9},{9,1},{2,10},{10,2},{3,11},{11,3},{4,12},{12,4},... | collective-permute-start | bytes 1769480 | tf_op jit(solution)/shard_map/ppermute | solution.py:28
  180.1 16.3 %collective-permute-start.28 = (bf16[4,96,768]{2,0,1:T(4,128)(2,1)S(1)}, bf16[4,96,768]{2,0,1:T(4,128)(2,1)S(1)}, u32[]{:S(2)}, u32[]{:S(2)}) collective-permute-start(bf16[4,96,768]{2,0,1:T(4,128)(2,1)S(1)} %dynamic_update_slice.119), channel_id=1, source_target_pairs={{0,16},{16,0},{1,17},{17,1},{2,18},{18,2},{3,19},{19,3},{4,20},{20... | collective-permute-start | bytes 1769480 | tf_op jit(solution)/shard_map/ppermute | solution.py:28
  181.9 27.2 %collective-permute-start.16 = (bf16[2,4,96,384]{3,2,1,0:T(8,128)(2,1)S(1)}, bf16[2,4,96,384]{3,2,1,0:T(8,128)(2,1)S(1)}, u32[]{:S(2)}, u32[]{:S(2)}) collective-permute-start(bf16[2,4,96,384]{3,2,1,0:T(8,128)(2,1)S(1)} %pad_maximum_fusion.18), channel_id=1, source_target_pairs={{0,16},{16,0},{1,17},{17,1},{2,18},{18,2},{3,19},{19,3},{4,20},{20... | collective-permute-start | bytes 1769480 | tf_op jit(solution)/shard_map/ppermute | solution.py:28
  184.6 25.4 %collective-permute-start.10 = (bf16[2,4,96,384]{3,2,0,1:T(8,128)(2,1)S(1)}, bf16[2,4,96,384]{3,2,0,1:T(8,128)(2,1)S(1)}, u32[]{:S(2)}, u32[]{:S(2)}) collective-permute-start(bf16[2,4,96,384]{3,2,0,1:T(8,128)(2,1)S(1)} %pad_maximum_fusion.17), channel_id=1, source_target_pairs={{0,8},{8,0},{1,9},{9,1},{2,10},{10,2},{3,11},{11,3},{4,12},{12,4},... | collective-permute-start | bytes 1769480 | tf_op jit(solution)/shard_map/ppermute | solution.py:28
  186.4 30.6 %collective-permute-start.4 = (bf16[2,4,96,384]{3,2,1,0:T(8,128)(2,1)S(1)}, bf16[2,4,96,384]{3,2,1,0:T(8,128)(2,1)S(1)}, u32[]{:S(2)}, u32[]{:S(2)}) collective-permute-start(bf16[2,4,96,384]{3,2,1,0:T(8,128)(2,1)S(1)} %pad_maximum_fusion.16), channel_id=1, source_target_pairs={{0,16},{16,0},{1,17},{17,1},{2,18},{18,2},{3,19},{19,3},{4,20},{20... | collective-permute-start | bytes 1769480 | tf_op jit(solution)/shard_map/ppermute | solution.py:28
  188.3 35.0 %collective-permute-start.22 = (bf16[2,4,176,384]{3,2,0,1:T(8,128)(2,1)S(1)}, bf16[2,4,176,384]{3,2,0,1:T(8,128)(2,1)S(1)}, u32[]{:S(2)}, u32[]{:S(2)}) collective-permute-start(bf16[2,4,176,384]{3,2,0,1:T(8,128)(2,1)S(1)} %pad_maximum_fusion.13), channel_id=1, source_target_pairs={{0,8},{8,0},{1,9},{9,1},{2,10},{10,2},{3,11},{11,3},{4,12},{12,4},... | collective-permute-start | bytes 3244040 | tf_op jit(solution)/shard_map/ppermute | solution.py:28
  196.4 33.2 %collective-permute-start.35 = (bf16[2,4,96,768]{3,1,2,0:T(4,128)(2,1)S(1)}, bf16[2,4,96,768]{3,1,2,0:T(4,128)(2,1)S(1)}, u32[]{:S(2)}, u32[]{:S(2)}) collective-permute-start(bf16[2,4,96,768]{3,1,2,0:T(4,128)(2,1)S(1)} %pad_maximum_fusion.12), channel_id=1, source_target_pairs={{0,16},{16,0},{1,17},{17,1},{2,18},{18,2},{3,19},{19,3},{4,20},{20... | collective-permute-start | bytes 3538952 | tf_op jit(solution)/shard_map/ppermute | solution.py:28
  209.0 26.9 %collective-permute-start.29 = (bf16[2,4,96,768]{3,1,2,0:T(4,128)(2,1)S(1)}, bf16[2,4,96,768]{3,1,2,0:T(4,128)(2,1)S(1)}, u32[]{:S(2)}, u32[]{:S(2)}) collective-permute-start(bf16[2,4,96,768]{3,1,2,0:T(4,128)(2,1)S(1)} %pad_maximum_fusion.11), channel_id=1, source_target_pairs={{0,8},{8,0},{1,9},{9,1},{2,10},{10,2},{3,11},{11,3},{4,12},{12,4},... | collective-permute-start | bytes 3538952 | tf_op jit(solution)/shard_map/ppermute | solution.py:28
  210.0 30.8 %collective-permute-start.17 = (bf16[2,2,4,96,384]{4,3,1,0,2:T(8,128)(2,1)S(1)}, bf16[2,2,4,96,384]{4,3,1,0,2:T(8,128)(2,1)S(1)}, u32[]{:S(2)}, u32[]{:S(2)}) collective-permute-start(bf16[2,2,4,96,384]{4,3,1,0,2:T(8,128)(2,1)S(1)} %copy.385), channel_id=1, source_target_pairs={{0,4},{4,0},{1,5},{5,1},{2,6},{6,2},{3,7},{7,3},{8,12},{12,8},{9,1... | collective-permute-start | bytes 3538952 | tf_op jit(solution)/shard_map/ppermute | solution.py:28
  217.0 52.0 %collective-permute-start.11 = (bf16[2,2,4,96,384]{4,3,1,0,2:T(8,128)(2,1)}, bf16[2,2,4,96,384]{4,3,1,0,2:T(8,128)(2,1)}, u32[]{:S(2)}, u32[]{:S(2)}) collective-permute-start(bf16[2,2,4,96,384]{4,3,1,0,2:T(8,128)(2,1)} %pad_maximum_fusion.9), channel_id=1, source_target_pairs={{0,4},{4,0},{1,5},{5,1},{2,6},{6,2},{3,7},{7,3},{8,12},{12,8},{9,1... | collective-permute-start | bytes 3538952 | tf_op jit(solution)/shard_map/ppermute | solution.py:28
  223.3 86.9 %collective-permute-start.5 = (bf16[2,2,4,96,384]{4,3,2,1,0:T(8,128)(2,1)}, bf16[2,2,4,96,384]{4,3,2,1,0:T(8,128)(2,1)}, u32[]{:S(2)}, u32[]{:S(2)}) collective-permute-start(bf16[2,2,4,96,384]{4,3,2,1,0:T(8,128)(2,1)} %pad_maximum_fusion.8), channel_id=1, source_target_pairs={{0,4},{4,0},{1,5},{5,1},{2,6},{6,2},{3,7},{7,3},{8,12},{12,8},{9,1... | collective-permute-start | bytes 3538952 | tf_op jit(solution)/shard_map/ppermute | solution.py:28
  229.6 145.7 %collective-permute-start.23 = (bf16[2,2,4,176,384]{4,3,0,1,2:T(8,128)(2,1)}, bf16[2,2,4,176,384]{4,3,0,1,2:T(8,128)(2,1)}, u32[]{:S(2)}, u32[]{:S(2)}) collective-permute-start(bf16[2,2,4,176,384]{4,3,0,1,2:T(8,128)(2,1)} %pad_maximum_fusion.7), channel_id=1, source_target_pairs={{0,4},{4,0},{1,5},{5,1},{2,6},{6,2},{3,7},{7,3},{8,12},{12,8},{9,1... | collective-permute-start | bytes 6488072 | tf_op jit(solution)/shard_map/ppermute | solution.py:28
  236.0 252.5 %collective-permute-start.36 = (bf16[2,2,4,96,768]{4,2,3,1,0:T(4,128)(2,1)}, bf16[2,2,4,96,768]{4,2,3,1,0:T(4,128)(2,1)}, u32[]{:S(2)}, u32[]{:S(2)}) collective-permute-start(bf16[2,2,4,96,768]{4,2,3,1,0:T(4,128)(2,1)} %pad_maximum_fusion.6), channel_id=1, source_target_pairs={{0,4},{4,0},{1,5},{5,1},{2,6},{6,2},{3,7},{7,3},{8,12},{12,8},{9,1... | collective-permute-start | bytes 7077896 | tf_op jit(solution)/shard_map/ppermute | solution.py:28
  240.9 256.4 %collective-permute-start.30 = (bf16[2,2,4,96,768]{4,2,3,1,0:T(4,128)(2,1)}, bf16[2,2,4,96,768]{4,2,3,1,0:T(4,128)(2,1)}, u32[]{:S(2)}, u32[]{:S(2)}) collective-permute-start(bf16[2,2,4,96,768]{4,2,3,1,0:T(4,128)(2,1)} %pad_maximum_fusion.5), channel_id=1, source_target_pairs={{0,4},{4,0},{1,5},{5,1},{2,6},{6,2},{3,7},{7,3},{8,12},{12,8},{9,1... | collective-permute-start | bytes 7077896 | tf_op jit(solution)/shard_map/ppermute | solution.py:28
  535.5 307.7 %collective-permute-start.37 = (bf16[256,768]{1,0:T(8,128)(2,1)}, bf16[256,768]{1,0:T(8,128)(2,1)}, u32[]{:S(2)}, u32[]{:S(2)}) collective-permute-start(bf16[256,768]{1,0:T(8,128)(2,1)} %get-tuple-element.163), channel_id=1, source_target_pairs={{0,1},{1,0},{2,3},{3,2},{4,5},{5,4},{6,7},{7,6},{8,9},{9,8},{10,11... | collective-permute-start | bytes 1179656 | tf_op jit(solution)/shard_map/ppermute | solution.py:33
  535.7 308.7 %collective-permute-start.38 = (bf16[256,768]{1,0:T(8,128)(2,1)}, bf16[256,768]{1,0:T(8,128)(2,1)}, u32[]{:S(2)}, u32[]{:S(2)}) collective-permute-start(bf16[256,768]{1,0:T(8,128)(2,1)} %get-tuple-element.163), channel_id=1, source_target_pairs={{0,2},{1,3},{2,0},{3,1},{4,6},{5,7},{6,4},{7,5},{8,10},{9,11},{10,... | collective-permute-start | bytes 1179656 | tf_op jit(solution)/shard_map/ppermute | solution.py:33
  538.3 316.2 %collective-permute-start.39 = (bf16[256,768]{1,0:T(8,128)(2,1)}, bf16[256,768]{1,0:T(8,128)(2,1)}, u32[]{:S(2)}, u32[]{:S(2)}) collective-permute-start(bf16[256,768]{1,0:T(8,128)(2,1)} %get-tuple-element.163), channel_id=1, source_target_pairs={{0,3},{1,2},{2,1},{3,0},{4,7},{5,6},{6,5},{7,4},{8,11},{9,10},{10,... | collective-permute-start | bytes 1179656 | tf_op jit(solution)/shard_map/ppermute | solution.py:33
  539.9 45.6 %collective-permute-start.40 = (bf16[128,768]{1,0:T(8,128)(2,1)S(1)}, bf16[128,768]{1,0:T(8,128)(2,1)S(1)}, u32[]{:S(2)}, u32[]{:S(2)}) collective-permute-start(bf16[128,768]{1,0:T(8,128)(2,1)S(1)} %select_convert_fusion), channel_id=1, source_target_pairs={{0,1},{1,0},{2,3},{3,2},{4,5},{5,4},{6,7},{7,6},{8,9},{9,8},{10,11... | collective-permute-start | bytes 589832 | tf_op jit(solution)/shard_map/ppermute | solution.py:33
  629.9 220.4 %collective-permute-start.41 = (bf16[256,768]{1,0:T(8,128)(2,1)}, bf16[256,768]{1,0:T(8,128)(2,1)}, u32[]{:S(2)}, u32[]{:S(2)}) collective-permute-start(bf16[256,768]{1,0:T(8,128)(2,1)} %get-tuple-element.293), channel_id=1, source_target_pairs={{0,1},{1,0},{2,3},{3,2},{4,5},{5,4},{6,7},{7,6},{8,9},{9,8},{10,11... | collective-permute-start | bytes 1179656 | tf_op jit(solution)/shard_map/ppermute | solution.py:33
  631.9 220.5 %collective-permute-start.42 = (bf16[256,768]{1,0:T(8,128)(2,1)}, bf16[256,768]{1,0:T(8,128)(2,1)}, u32[]{:S(2)}, u32[]{:S(2)}) collective-permute-start(bf16[256,768]{1,0:T(8,128)(2,1)} %get-tuple-element.293), channel_id=1, source_target_pairs={{0,2},{1,3},{2,0},{3,1},{4,6},{5,7},{6,4},{7,5},{8,10},{9,11},{10,... | collective-permute-start | bytes 1179656 | tf_op jit(solution)/shard_map/ppermute | solution.py:33
  843.2 22.9 %collective-permute-start.56 = (bf16[2,2,4,96,384]{4,3,1,0,2:T(8,128)(2,1)}, bf16[2,2,4,96,384]{4,3,1,0,2:T(8,128)(2,1)S(1)}, u32[]{:S(2)}, u32[]{:S(2)}) collective-permute-start(bf16[2,2,4,96,384]{4,3,1,0,2:T(8,128)(2,1)} %fusion.35), channel_id=1, source_target_pairs={{0,4},{4,0},{1,5},{5,1},{2,6},{6,2},{3,7},{7,3},{8,12},{12,8},{9,1... | collective-permute-start | bytes 3538952 | tf_op jit(solution)/shard_map/ppermute | solution.py:28
  844.4 15.0 %collective-permute-start.43 = (bf16[256,768]{1,0:T(8,128)(2,1)}, bf16[256,768]{1,0:T(8,128)(2,1)S(1)}, u32[]{:S(2)}, u32[]{:S(2)}) collective-permute-start(bf16[256,768]{1,0:T(8,128)(2,1)} %get-tuple-element.293), channel_id=1, source_target_pairs={{0,3},{1,2},{2,1},{3,0},{4,7},{5,6},{6,5},{7,4},{8,11},{9,10},{10,... | collective-permute-start | bytes 1179656 | tf_op jit(solution)/shard_map/ppermute | solution.py:33
  850.4 17.6 %collective-permute-start.44 = (bf16[2,2,4,96,384]{4,3,0,1,2:T(8,128)(2,1)S(1)}, bf16[2,2,4,96,384]{4,3,0,1,2:T(8,128)(2,1)S(1)}, u32[]{:S(2)}, u32[]{:S(2)}) collective-permute-start(bf16[2,2,4,96,384]{4,3,0,1,2:T(8,128)(2,1)S(1)} %fusion.34), channel_id=1, source_target_pairs={{0,4},{4,0},{1,5},{5,1},{2,6},{6,2},{3,7},{7,3},{8,12},{12,8},{9,1... | collective-permute-start | bytes 3538952 | tf_op jit(solution)/shard_map/ppermute | solution.py:28
  852.4 16.7 %collective-permute-start.50 = (bf16[2,2,4,96,384]{4,3,2,1,0:T(8,128)(2,1)}, bf16[2,2,4,96,384]{4,3,2,1,0:T(8,128)(2,1)S(1)}, u32[]{:S(2)}, u32[]{:S(2)}) collective-permute-start(bf16[2,2,4,96,384]{4,3,2,1,0:T(8,128)(2,1)} %fusion.38), channel_id=1, source_target_pairs={{0,4},{4,0},{1,5},{5,1},{2,6},{6,2},{3,7},{7,3},{8,12},{12,8},{9,1... | collective-permute-start | bytes 3538952 | tf_op jit(solution)/shard_map/ppermute | solution.py:28
  854.5 80.6 %collective-permute-start.74 = (bf16[2,2,4,96,768]{4,3,2,1,0:T(8,128)(2,1)S(1)}, bf16[2,2,4,96,768]{4,3,2,1,0:T(8,128)(2,1)}, u32[]{:S(2)}, u32[]{:S(2)}) collective-permute-start(bf16[2,2,4,96,768]{4,3,2,1,0:T(8,128)(2,1)S(1)} %bitcast.674), channel_id=1, source_target_pairs={{0,4},{4,0},{1,5},{5,1},{2,6},{6,2},{3,7},{7,3},{8,12},{12,8},{9,1... | collective-permute-start | bytes 7077896 | tf_op jit(solution)/shard_map/ppermute | solution.py:28
  859.4 73.6 %collective-permute-start.62 = (bf16[2,2,4,176,384]{4,3,0,1,2:T(8,128)(2,1)}, bf16[2,2,4,176,384]{4,3,0,1,2:T(8,128)(2,1)S(1)}, u32[]{:S(2)}, u32[]{:S(2)}) collective-permute-start(bf16[2,2,4,176,384]{4,3,0,1,2:T(8,128)(2,1)} %fusion.15), channel_id=1, source_target_pairs={{0,4},{4,0},{1,5},{5,1},{2,6},{6,2},{3,7},{7,3},{8,12},{12,8},{9,1... | collective-permute-start | bytes 6488072 | tf_op jit(solution)/shard_map/ppermute | solution.py:28
  866.5 16.2 %collective-permute-start.57 = (bf16[2,4,96,384]{3,2,0,1:T(8,128)(2,1)S(1)}, bf16[2,4,96,384]{3,2,0,1:T(8,128)(2,1)S(1)}, u32[]{:S(2)}, u32[]{:S(2)}) collective-permute-start(bf16[2,4,96,384]{3,2,0,1:T(8,128)(2,1)S(1)} %fusion.55), channel_id=1, source_target_pairs={{0,16},{16,0},{1,17},{17,1},{2,18},{18,2},{3,19},{19,3},{4,20},{20... | collective-permute-start | bytes 1769480 | tf_op jit(solution)/shard_map/ppermute | solution.py:28
  868.4 16.0 %collective-permute-start.45 = (bf16[2,4,96,384]{3,2,0,1:T(8,128)(2,1)S(1)}, bf16[2,4,96,384]{3,2,0,1:T(8,128)(2,1)S(1)}, u32[]{:S(2)}, u32[]{:S(2)}) collective-permute-start(bf16[2,4,96,384]{3,2,0,1:T(8,128)(2,1)S(1)} %fusion.53), channel_id=1, source_target_pairs={{0,8},{8,0},{1,9},{9,1},{2,10},{10,2},{3,11},{11,3},{4,12},{12,4},... | collective-permute-start | bytes 1769480 | tf_op jit(solution)/shard_map/ppermute | solution.py:28
  869.6 25.8 %collective-permute-start.51 = (bf16[2,4,96,384]{3,2,1,0:T(8,128)(2,1)S(1)}, bf16[2,4,96,384]{3,2,1,0:T(8,128)(2,1)S(1)}, u32[]{:S(2)}, u32[]{:S(2)}) collective-permute-start(bf16[2,4,96,384]{3,2,1,0:T(8,128)(2,1)S(1)} %fusion.54), channel_id=1, source_target_pairs={{0,16},{16,0},{1,17},{17,1},{2,18},{18,2},{3,19},{19,3},{4,20},{20... | collective-permute-start | bytes 1769480 | tf_op jit(solution)/shard_map/ppermute | solution.py:28
  882.9 14.1 %collective-permute-start.58 = (bf16[4,96,384]{2,1,0:T(8,128)(2,1)S(1)}, bf16[4,96,384]{2,1,0:T(8,128)(2,1)S(1)}, u32[]{:S(2)}, u32[]{:S(2)}) collective-permute-start(bf16[4,96,384]{2,1,0:T(8,128)(2,1)S(1)} %fusion.77), channel_id=1, source_target_pairs={{0,8},{8,0},{1,9},{9,1},{2,10},{10,2},{3,11},{11,3},{4,12},{12,4},... | collective-permute-start | bytes 884744 | tf_op jit(solution)/shard_map/ppermute | solution.py:28
  884.7 21.6 %collective-permute-start.46 = (bf16[4,96,384]{2,1,0:T(8,128)(2,1)S(1)}, bf16[4,96,384]{2,1,0:T(8,128)(2,1)S(1)}, u32[]{:S(2)}, u32[]{:S(2)}) collective-permute-start(bf16[4,96,384]{2,1,0:T(8,128)(2,1)S(1)} %fusion.75), channel_id=1, source_target_pairs={{0,16},{16,0},{1,17},{17,1},{2,18},{18,2},{3,19},{19,3},{4,20},{20... | collective-permute-start | bytes 884744 | tf_op jit(solution)/shard_map/ppermute | solution.py:28
  895.5 14.7 %collective-permute-start.52 = (bf16[4,96,384]{2,1,0:T(8,128)(2,1)S(1)}, bf16[4,96,384]{2,1,0:T(8,128)(2,1)S(1)}, u32[]{:S(2)}, u32[]{:S(2)}) collective-permute-start(bf16[4,96,384]{2,1,0:T(8,128)(2,1)S(1)} %fusion.76), channel_id=1, source_target_pairs={{0,8},{8,0},{1,9},{9,1},{2,10},{10,2},{3,11},{11,3},{4,12},{12,4},... | collective-permute-start | bytes 884744 | tf_op jit(solution)/shard_map/ppermute | solution.py:28
  897.2 15.7 %collective-permute-start.59 = (bf16[96,384]{1,0:T(8,128)(2,1)S(1)}, bf16[96,384]{1,0:T(8,128)(2,1)S(1)}, u32[]{:S(2)}, u32[]{:S(2)}) collective-permute-start(bf16[96,384]{1,0:T(8,128)(2,1)S(1)} %get-tuple-element.231), channel_id=1, source_target_pairs={{0,1},{1,0},{2,3},{3,2},{4,5},{5,4},{6,7},{7,6},{8,9},{9,8},{10,11... | collective-permute-start | bytes 221192 | tf_op jit(solution)/shard_map/ppermute | solution.py:33
  919.5 19.9 %collective-permute-start.68 = (bf16[2,2,4,96,768]{4,3,2,1,0:T(8,128)(2,1)S(1)}, bf16[2,2,4,96,768]{4,3,2,1,0:T(8,128)(2,1)S(1)}, u32[]{:S(2)}, u32[]{:S(2)}) collective-permute-start(bf16[2,2,4,96,768]{4,3,2,1,0:T(8,128)(2,1)S(1)} %bitcast.673), channel_id=1, source_target_pairs={{0,4},{4,0},{1,5},{5,1},{2,6},{6,2},{3,7},{7,3},{8,12},{12,8},{9,1... | collective-permute-start | bytes 7077896 | tf_op jit(solution)/shard_map/ppermute | solution.py:28
  933.6 26.9 %collective-permute-start.63 = (bf16[2,4,176,384]{3,2,0,1:T(8,128)(2,1)S(1)}, bf16[2,4,176,384]{3,2,0,1:T(8,128)(2,1)S(1)}, u32[]{:S(2)}, u32[]{:S(2)}) collective-permute-start(bf16[2,4,176,384]{3,2,0,1:T(8,128)(2,1)S(1)} %fusion.41), channel_id=1, source_target_pairs={{0,8},{8,0},{1,9},{9,1},{2,10},{10,2},{3,11},{11,3},{4,12},{12,4},... | collective-permute-start | bytes 3244040 | tf_op jit(solution)/shard_map/ppermute | solution.py:28
  938.1 29.1 %collective-permute-start.75 = (bf16[2,4,96,768]{3,2,1,0:T(8,128)(2,1)S(1)}, bf16[2,4,96,768]{3,2,1,0:T(8,128)(2,1)}, u32[]{:S(2)}, u32[]{:S(2)}) collective-permute-start(bf16[2,4,96,768]{3,2,1,0:T(8,128)(2,1)S(1)} %fusion.37), channel_id=1, source_target_pairs={{0,16},{16,0},{1,17},{17,1},{2,18},{18,2},{3,19},{19,3},{4,20},{20... | collective-permute-start | bytes 3538952 | tf_op jit(solution)/shard_map/ppermute | solution.py:28
  940.8 45.1 %collective-permute-start.69 = (bf16[2,4,96,768]{3,2,1,0:T(8,128)(2,1)S(1)}, bf16[2,4,96,768]{3,2,1,0:T(8,128)(2,1)}, u32[]{:S(2)}, u32[]{:S(2)}) collective-permute-start(bf16[2,4,96,768]{3,2,1,0:T(8,128)(2,1)S(1)} %fusion.36), channel_id=1, source_target_pairs={{0,8},{8,0},{1,9},{9,1},{2,10},{10,2},{3,11},{11,3},{4,12},{12,4},... | collective-permute-start | bytes 3538952 | tf_op jit(solution)/shard_map/ppermute | solution.py:28
  962.2 13.8 %collective-permute-start.64 = (bf16[4,176,384]{2,1,0:T(8,128)(2,1)}, bf16[4,176,384]{2,1,0:T(8,128)(2,1)}, u32[]{:S(2)}, u32[]{:S(2)}) collective-permute-start(bf16[4,176,384]{2,1,0:T(8,128)(2,1)} %fusion.67), channel_id=1, source_target_pairs={{0,16},{16,0},{1,17},{17,1},{2,18},{18,2},{3,19},{19,3},{4,20},{20... | collective-permute-start | bytes 1622024 | tf_op jit(solution)/shard_map/ppermute | solution.py:28
  969.7 26.1 %collective-permute-start.76 = (bf16[4,96,768]{2,1,0:T(8,128)(2,1)S(1)}, bf16[4,96,768]{2,1,0:T(8,128)(2,1)S(1)}, u32[]{:S(2)}, u32[]{:S(2)}) collective-permute-start(bf16[4,96,768]{2,1,0:T(8,128)(2,1)S(1)} %fusion.57), channel_id=1, source_target_pairs={{0,8},{8,0},{1,9},{9,1},{2,10},{10,2},{3,11},{11,3},{4,12},{12,4},... | collective-permute-start | bytes 1769480 | tf_op jit(solution)/shard_map/ppermute | solution.py:28
  977.3 11.7 %collective-permute-start.65 = (bf16[176,384]{1,0:T(8,128)(2,1)S(1)}, bf16[176,384]{1,0:T(8,128)(2,1)S(1)}, u32[]{:S(2)}, u32[]{:S(2)}) collective-permute-start(bf16[176,384]{1,0:T(8,128)(2,1)S(1)} %get-tuple-element.218), channel_id=1, source_target_pairs={{0,1},{1,0},{2,3},{3,2},{4,5},{5,4},{6,7},{7,6},{8,9},{9,8},{10,11... | collective-permute-start | bytes 405512 | tf_op jit(solution)/shard_map/ppermute | solution.py:33
  977.3 11.6 %collective-permute-start.66 = (bf16[176,384]{1,0:T(8,128)(2,1)S(1)}, bf16[176,384]{1,0:T(8,128)(2,1)S(1)}, u32[]{:S(2)}, u32[]{:S(2)}) collective-permute-start(bf16[176,384]{1,0:T(8,128)(2,1)S(1)} %get-tuple-element.220), channel_id=1, source_target_pairs={{0,2},{1,3},{2,0},{3,1},{4,6},{5,7},{6,4},{7,5},{8,10},{9,11},{10,... | collective-permute-start | bytes 405512 | tf_op jit(solution)/shard_map/ppermute | solution.py:33
  979.8 9.1 collective-permute-start.67
  987.5 13.0 %collective-permute-start.70 = (bf16[4,96,768]{2,1,0:T(8,128)(2,1)S(1)}, bf16[4,96,768]{2,1,0:T(8,128)(2,1)S(1)}, u32[]{:S(2)}, u32[]{:S(2)}) collective-permute-start(bf16[4,96,768]{2,1,0:T(8,128)(2,1)S(1)} %fusion.56), channel_id=1, source_target_pairs={{0,16},{16,0},{1,17},{17,1},{2,18},{18,2},{3,19},{19,3},{4,20},{20... | collective-permute-start | bytes 1769480 | tf_op jit(solution)/shard_map/ppermute | solution.py:28
  996.0 16.5 %collective-permute-start.77 = (bf16[96,768]{1,0:T(8,128)(2,1)S(1)}, bf16[96,768]{1,0:T(8,128)(2,1)S(1)}, u32[]{:S(2)}, u32[]{:S(2)}) collective-permute-start(bf16[96,768]{1,0:T(8,128)(2,1)S(1)} %get-tuple-element.202), channel_id=1, source_target_pairs={{0,2},{1,3},{2,0},{3,1},{4,6},{5,7},{6,4},{7,5},{8,10},{9,11},{10,... | collective-permute-start | bytes 442376 | tf_op jit(solution)/shard_map/ppermute | solution.py:33
  996.1 18.0 %collective-permute-start.78 = (bf16[96,768]{1,0:T(8,128)(2,1)S(1)}, bf16[96,768]{1,0:T(8,128)(2,1)S(1)}, u32[]{:S(2)}, u32[]{:S(2)}) collective-permute-start(bf16[96,768]{1,0:T(8,128)(2,1)S(1)} %get-tuple-element.204), channel_id=1, source_target_pairs={{0,1},{1,0},{2,3},{3,2},{4,5},{5,4},{6,7},{7,6},{8,9},{9,8},{10,11... | collective-permute-start | bytes 442376 | tf_op jit(solution)/shard_map/ppermute | solution.py:33
  998.5 15.5 %collective-permute-start.79 = (bf16[96,768]{1,0:T(8,128)(2,1)S(1)}, bf16[96,768]{1,0:T(8,128)(2,1)S(1)}, u32[]{:S(2)}, u32[]{:S(2)}) collective-permute-start(bf16[96,768]{1,0:T(8,128)(2,1)S(1)} %get-tuple-element.203), channel_id=1, source_target_pairs={{0,3},{1,2},{2,1},{3,0},{4,7},{5,6},{6,5},{7,4},{8,11},{9,10},{10,... | collective-permute-start | bytes 442376 | tf_op jit(solution)/shard_map/ppermute | solution.py:33
  1000.6 17.0 %collective-permute-start.71 = (bf16[96,768]{1,0:T(8,128)(2,1)S(1)}, bf16[96,768]{1,0:T(8,128)(2,1)S(1)}, u32[]{:S(2)}, u32[]{:S(2)}) collective-permute-start(bf16[96,768]{1,0:T(8,128)(2,1)S(1)} %get-tuple-element.205), channel_id=1, source_target_pairs={{0,2},{1,3},{2,0},{3,1},{4,6},{5,7},{6,4},{7,5},{8,10},{9,11},{10,... | collective-permute-start | bytes 442376 | tf_op jit(solution)/shard_map/ppermute | solution.py:33
  1000.7 16.9 %collective-permute-start.72 = (bf16[96,768]{1,0:T(8,128)(2,1)S(1)}, bf16[96,768]{1,0:T(8,128)(2,1)S(1)}, u32[]{:S(2)}, u32[]{:S(2)}) collective-permute-start(bf16[96,768]{1,0:T(8,128)(2,1)S(1)} %get-tuple-element.207), channel_id=1, source_target_pairs={{0,1},{1,0},{2,3},{3,2},{4,5},{5,4},{6,7},{7,6},{8,9},{9,8},{10,11... | collective-permute-start | bytes 442376 | tf_op jit(solution)/shard_map/ppermute | solution.py:33
  (177 other events, 3105.5 us)
Sparse Core Ops, SparseCore 0:
  719.0 119.7 all-reduce.2

commit v2 on v1

v2 whole, which is shorter than its diff:
```python
import functools
import math

import jax
import jax.numpy as jnp
from jax import lax
from jax.experimental import pallas as pl
from jax.experimental.pallas import tpu as pltpu
from jax.sharding import Mesh
from jax.sharding import PartitionSpec as P

D = 768
HEAD_DIM = 64
F = 3072
E = 1408
NQ = 32
STEP_COUNT = 10

NORM_EPS = 1e-06
BETA_ONE = 0.9
BETA_TWO = 0.999
ADAM_EPS = 1e-08
WEIGHT_DECAY = 0.01
MASKED = -1000000000.0

BF = jnp.bfloat16
F32 = jnp.float32
SCALE = HEAD_DIM ** (-0.5)
MIB = 1 << 20


def dot(a, b):
    return lax.dot_general(a, b, (((1,), (0,)), ((), ())), preferred_element_type=F32)


def dot_t(a, b):
    return lax.dot_general(a, b, (((1,), (1,)), ((), ())), preferred_element_type=F32)


def t_dot(a, b):
    return lax.dot_general(a, b, (((0,), (0,)), ((), ())), preferred_element_type=F32)


def swap(values, axis):
    return lax.ppermute(values, axis, [(0, 1), (1, 0)])


def mp_swap(values, distance):
    count = lax.axis_size("mp")
    return lax.ppermute(values, "mp", [(i, i ^ distance) for i in range(count)])


class Plan:
    def __init__(self, bits, mp, items, dp):
        self.bits = bits
        self.mp = mp
        self.dp = dp
        self.items = items
        self.rows = items * 2 * NQ
        self.half = items * NQ
        self.width = D // mp
        self.forth = tuple(f"b{k}" for k in range(bits))
        self.back = self.forth[::-1]

    def direct(self, rows):
        return rows % 16 == 0

    def bit(self, axis):
        return 1 if axis == "core" else 2 << (self.bits - 1 - int(axis[1:]))

    def masks(self, order):
        found = [0]
        for axis in order + ("core",):
            found = found + [m | self.bit(axis) for m in found]
        return found

    def dp_index(self):
        place = lax.axis_index("core")
        for axis in self.forth:
            place = place + self.bit(axis) * lax.axis_index(axis)
        return place


def mp_collect(own, sent):
    return [own] + [mp_swap(sent(j), j) for j in range(1, lax.axis_size("mp"))]


def tree_gather(plan, stacked, order):
    if plan.direct(stacked.shape[1]):
        pieces = [stacked]
        for axis in order + ("core",):
            pieces = pieces + [swap(p, axis) for p in pieces]
        return pieces
    near = jnp.arange(plan.mp) ^ lax.axis_index("mp")
    values = jnp.take(stacked, near, axis=0)[None]
    for axis in order + ("core",):
        values = jnp.concatenate([values, swap(values, axis)])
    back = [0] * plan.dp
    for k, mask in enumerate(plan.masks(order)):
        back[mask] = k
    natural = jnp.take(jnp.array(back), jnp.arange(plan.dp) ^ plan.dp_index())
    values = jnp.take(values, natural, axis=0).transpose(1, 0, 2, 3)
    return [values.reshape(plan.mp, -1, values.shape[-1])]


def tree_halves(plan, grads, rows, order):
    if plan.direct(rows):
        return grads
    (natural,) = grads
    blocks = natural.reshape(plan.mp, plan.dp, rows, natural.shape[-1])
    near = jnp.arange(plan.mp) ^ lax.axis_index("mp")
    places = jnp.array(plan.masks(order)) ^ plan.dp_index()
    blocks = jnp.take(jnp.take(blocks, near, axis=0), places, axis=1).transpose(1, 0, 2, 3)
    return blocks[: plan.dp // 2], blocks[plan.dp // 2 :]


def tree_reduce(halves, order):
    kept, sent = halves
    for axis in (order + ("core",))[::-1]:
        got = swap(sent, axis)
        half = got.shape[0] // 2
        if half == 0:
            return (kept.astype(F32) + got.astype(F32))[0]
        kept, sent = (
            (kept[:half].astype(F32) + got[:half].astype(F32)).astype(BF),
            (kept[half:].astype(F32) + got[half:].astype(F32)).astype(BF),
        )


def norm_parts(values):
    center = values - jnp.mean(values, axis=-1, keepdims=True)
    spread = jnp.mean(center * center, axis=-1, keepdims=True)
    inverse = lax.rsqrt(spread + NORM_EPS)
    return center * inverse, inverse


def norm_backward(grad_out, normed, inverse, gain):
    scaled = grad_out * gain
    inner = (
        scaled
        - jnp.mean(scaled, axis=-1, keepdims=True)
        - normed * jnp.mean(scaled * normed, axis=-1, keepdims=True)
    )
    return inner * inverse


def column_sum(values):
    return jnp.sum(values.astype(F32), axis=0, keepdims=True)


def halves_of(values, items):
    split = values.reshape(items, 2 * NQ, values.shape[-1])
    parts = split[:, :NQ], split[:, NQ:]
    return tuple(p.reshape(items * NQ, values.shape[-1]) for p in parts)


def join_halves(query, caption, items):
    width = query.shape[-1]
    parts = [v.reshape(items, NQ, width) for v in (query, caption)]
    return jnp.concatenate(parts, axis=1).reshape(items * 2 * NQ, width)


def wide(first, second):
    return jnp.concatenate([first, second], axis=1)


def after(values, width):
    return jnp.concatenate([jnp.zeros_like(values), values], axis=1)


def before(values, width):
    return jnp.concatenate([values, jnp.zeros_like(values)], axis=1)


def head_lanes(width):
    lane = lax.broadcasted_iota(jnp.int32, (1, width), 1)
    return [lane // HEAD_DIM == h for h in range(width // HEAD_DIM)]


def only(values, lanes):
    return jnp.where(lanes, values, jnp.zeros_like(values))


def softmax(scores):
    expo = jnp.exp(scores - jnp.max(scores, axis=-1, keepdims=True))
    return expo * (1.0 / jnp.sum(expo, axis=-1, keepdims=True))


def fetch(plan, pieces, order, target, sem):
    if len(pieces) == 1:
        pltpu.make_async_copy(pieces[0], target, sem).start()
        return
    rows = pieces[0].shape[1]
    me, place = lax.axis_index("mp"), plan.dp_index()
    for mask, piece in zip(plan.masks(order), pieces):
        begin = pl.multiple_of((place ^ mask) * rows, 16)
        for j in range(plan.mp):
            pltpu.make_async_copy(
                piece.at[j], target.at[me ^ j, pl.ds(begin, rows), :], sem
            ).start()


def settle(target, sem):
    pltpu.make_async_copy(target, target, sem).wait()


def spread(plan, source, outs, order, sem):
    if len(outs) == 1:
        pltpu.make_async_copy(source, outs[0], sem).start()
        return
    rows = outs[0].shape[2]
    me, place = lax.axis_index("mp"), plan.dp_index()
    half = plan.dp // 2
    for k, mask in enumerate(plan.masks(order)):
        begin = pl.multiple_of((place ^ mask) * rows, 16)
        for j in range(plan.mp):
            pltpu.make_async_copy(
                source.at[me ^ j, pl.ds(begin, rows), :], outs[k // half].at[k % half, j], sem
            ).start()


def gradient_shapes(plan, rows, total, width):
    if plan.direct(rows):
        return [jax.ShapeDtypeStruct((plan.dp // 2, plan.mp, rows, width), BF)] * 2
    return [jax.ShapeDtypeStruct((plan.mp, total, width), BF)]


def call(kernel, ins, places, outs, out_places, scratch, limit, flops, moved):
    return pl.pallas_call(
        kernel,
        out_shape=outs,
        in_specs=[pl.BlockSpec(memory_space=p) for p in places],
        out_specs=[pl.BlockSpec(memory_space=p) for p in out_places],
        scratch_shapes=scratch,
        compiler_params=pltpu.CompilerParams(vmem_limit_bytes=limit * MIB),
        cost_estimate=pl.CostEstimate(flops=flops, bytes_accessed=moved, transcendentals=0),
    )(*ins)


ANY, VMEM, SMEM = pl.ANY, pltpu.VMEM, pltpu.SMEM
DMA = pltpu.SemaphoreType.DMA


def self_mask(plan, lengths, me):
    count = plan.rows
    row = lax.broadcasted_iota(jnp.int32, (count, count), 0)
    col = lax.broadcasted_iota(jnp.int32, (count, count), 1)
    span = 2 * NQ
    limit = jnp.zeros((count, count), jnp.int32)
    for i in range(plan.items):
        limit = jnp.where(col // span == i, lengths[me * plan.items + i], limit)
    inside = col % span
    valid = (row // span == col // span) & ((inside < NQ) | (inside - NQ < limit))
    return jnp.where(valid, 0.0, MASKED).astype(F32)


def load_tokens(plan, hidden, target, sem):
    me = lax.axis_index("mp")
    return pltpu.make_async_copy(hidden.at[pl.ds(me * plan.items, plan.items)], target, sem)


def self_forward(plan, lengths, hidden, vec, heads, qk, vc, oo):
    counts = len(qk), len(vc), len(oo)
    mp, rows, half, width = plan.mp, plan.rows, plan.half, plan.width

    def kernel(lengths, hidden, vec, heads, *rest):
        qk = rest[: counts[0]]
        vc = rest[counts[0] : counts[0] + counts[1]]
        oo = rest[counts[0] + counts[1] : sum(counts)]
        qk_out, v_out, context_out, z_out, cross_out = rest[sum(counts) : sum(counts) + 5]
        tokens, w_qk, w_vc, w_oo, sems = rest[sum(counts) + 5 :]
        me = lax.axis_index("mp")
        loaded = load_tokens(plan, hidden, tokens, sems.at[0])
        loaded.start()
        fetch(plan, qk, plan.forth, w_qk, sems.at[1])
        fetch(plan, vc, plan.back, w_vc, sems.at[2])
        fetch(plan, oo, plan.back, w_oo, sems.at[3])
        mask = self_mask(plan, lengths, me)
        lanes = head_lanes(width)
        loaded.wait()
        x = tokens[...].reshape(rows, D)
        settle(w_qk, sems.at[1])
        settle(w_vc, sems.at[2])
        settle(w_oo, sems.at[3])
        total = x.astype(F32) + vec[0:1, :]
        for z in range(mp):
            both = (dot(x, w_qk[z]) + heads[me ^ z, 0:1, :]).astype(BF)
            qk_out[z] = both
            q, k = both[:, :width], both[:, width:]
            v = (dot(x, w_vc[z]) + heads[me ^ z, 1:2, :]).astype(BF)[:, :width]
            v_out[z] = v
            context = jnp.zeros((rows, width), F32)
            for lane in lanes:
                probs = softmax(dot_t(only(q, lane), k) * SCALE + mask)
                context = context + only(dot(probs.astype(BF), v), lane)
            context = context.astype(BF)
            context_out[z] = context
            total = total + dot_t(before(context, width), w_oo[z])
        z_out[...] = total
        normed, _ = norm_parts(total)
        first = normed * vec[4:5, :] + vec[5:6, :]
        u = halves_of(first, plan.items)[0].astype(BF)
        for z in range(mp):
            cross = (dot(u, w_vc[z]) + heads[me ^ z, 1:2, :]).astype(BF)
            cross_out[z] = cross[:, width:]

    outs = [
        jax.ShapeDtypeStruct((mp, rows, 2 * width), BF),
        jax.ShapeDtypeStruct((mp, rows, width), BF),
        jax.ShapeDtypeStruct((mp, rows, width), BF),
        jax.ShapeDtypeStruct((rows, D), F32),
        jax.ShapeDtypeStruct((mp, half, width), BF),
    ]
    return call(
        kernel,
        (lengths, hidden, vec, heads, *qk, *vc, *oo),
        [SMEM, ANY, VMEM, VMEM] + [ANY] * sum(counts),
        outs,
        [VMEM] * 5,
        [
            pltpu.VMEM((plan.items, 2 * NQ, D), BF),
            pltpu.VMEM((mp, D, 2 * width), BF),
            pltpu.VMEM((mp, D, 2 * width), BF),
            pltpu.VMEM((mp, D, 2 * width), BF),
            DMA((4,)),
        ],
        32,
        3 * 10**9,
        9 * 10**6,
    )


def image_maps(plan, images, heads, kv):
    count = len(kv)
    mp, items, width = plan.mp, plan.items, plan.width
    keys = images.shape[1]
    padded = -(-keys // 128) * 128

    def kernel(images, heads, *rest):
        kv = rest[:count]
        out = rest[count]
        held, w_kv, sems = rest[count + 1 :]
        me = lax.axis_index("mp")
        loaded = load_tokens(plan, images, held, sems.at[0])
        loaded.start()
        fetch(plan, kv, plan.forth, w_kv, sems.at[1])
        loaded.wait()
        settle(w_kv, sems.at[1])
        for i in range(items):
            for z in range(mp):
                both = (dot(held[i], w_kv[z]) + heads[me ^ z, 2:3, :]).astype(BF)
                out[i, z, 0:keys, :] = both
                out[i, z, keys:padded, :] = jnp.zeros((padded - keys, 2 * width), BF)

    return call(
        kernel,
        (images, heads, *kv),
        [ANY, VMEM] + [ANY] * count,
        [jax.ShapeDtypeStruct((items, mp, padded, 2 * width), BF)],
        [VMEM],
        [
            pltpu.VMEM((items, keys, images.shape[2]), BF),
            pltpu.VMEM((mp, images.shape[2], 2 * width), BF),
            DMA((2,)),
        ],
        32,
        5 * 10**9,
        12 * 10**6,
    )[0]


def key_mask(plan, keys, padded):
    lane = lax.broadcasted_iota(jnp.int32, (1, padded), 1)
    return jnp.where(lane < keys, 0.0, MASKED).astype(F32)


def spread_heads(values, lanes):
    return jnp.concatenate([only(values, lane) for lane in lanes], axis=0)


def gather_heads(values, lanes):
    total = None
    for h, lane in enumerate(lanes):
        part = only(values[h * NQ : (h + 1) * NQ], lane)
        total = part if total is None else total + part
    return total


def cross_forward(plan, keys, vec, z_first, cross, kv, oo):
    count = len(oo)
    mp, rows, half, width, items = plan.mp, plan.rows, plan.half, plan.width, plan.items
    padded = kv.shape[2]

    def kernel(vec, z_first, cross, kv, *rest):
        oo = rest[:count]
        context_out, z_out, kept, given = rest[count : count + 4]
        w_oo, sems = rest[count + 4 :]
        group = lax.axis_index("mp") & 1
        fetch(plan, oo, plan.back, w_oo, sems.at[0])
        lanes = head_lanes(width)
        mask = key_mask(plan, keys, padded)
        normed, _ = norm_parts(z_first[...])
        u, caption = halves_of(normed * vec[4:5, :] + vec[5:6, :], items)
        for z in range(mp):
            for i in range(items):
                span = slice(i * NQ, (i + 1) * NQ)
                q = spread_heads(cross[z, span, :], lanes)
                both = kv[i, z]
                probs = softmax(dot_t(q, both[:, :width]) * SCALE + mask)
                context = gather_heads(dot(probs.astype(BF), both[:, width:]), lanes)
                context_out[z, span, :] = context.astype(BF)
        settle(w_oo, sems.at[0])
        total = u + vec[1:2, :]
        for z in range(mp):
            total = total + dot_t(after(context_out[z], width), w_oo[z])
        z_out[...] = total
        normed, _ = norm_parts(total)
        second = normed * vec[6:7, :] + vec[7:8, :]
        low = group == 0
        kept[...] = jnp.where(low, second, caption)
        given[...] = jnp.where(low, caption, second).astype(BF)

    outs = [
        jax.ShapeDtypeStruct((mp, half, width), BF),
        jax.ShapeDtypeStruct((half, D), F32),
        jax.ShapeDtypeStruct((half, D), F32),
        jax.ShapeDtypeStruct((half, D), BF),
    ]
    return call(
        kernel,
        (vec, z_first, cross, kv, *oo),
        [VMEM] * 4 + [ANY] * count,
        outs,
        [VMEM] * 4,
        [pltpu.VMEM((mp, D, 2 * width), BF), DMA((1,))],
        32,
        2 * 10**9,
        8 * 10**6,
    )


def feed_forward(plan, vec, heads, kept, got, cotangent, up, down, shard_rows):
    counts = len(up), len(down)
    mp, half, items = plan.mp, plan.half, plan.items
    hidden_width = F // mp
    shapes = gradient_shapes(plan, shard_rows, D, hidden_width)
    grads = len(shapes)

    def kernel(vec, heads, kept, got, cotangent, *rest):
        up, down = rest[: counts[0]], rest[counts[0] : sum(counts)]
        rest = rest[sum(counts) :]
        layer, kept_back, given_back, sums, bias_sums = rest[:5]
        up_out, down_out = rest[5 : 5 + grads], rest[5 + grads : 5 + 2 * grads]
        (top, w_up, w_down, act, up_grad, down_grad, sems) = rest[5 + 2 * grads :]
        me = lax.axis_index("mp")
        group = me & 1
        fetch(plan, up, plan.forth, w_up, sems.at[0])
        fetch(plan, down, plan.back, w_down, sems.at[1])
        tops = []
        for s in range(2):
            first = (me ^ s) * items
            tops.append(
                pltpu.make_async_copy(
                    cotangent.at[
                        pl.ds(first, items), pl.ds(pl.multiple_of(group * NQ, NQ), NQ), :
                    ],
                    top.at[s],
                    sems.at[2 + s],
                )
            )
            tops[-1].start()
        x = jnp.concatenate([kept[...], got[...].astype(F32)], axis=0)
        low = x.astype(BF)
        settle(w_up, sems.at[0])
        settle(w_down, sems.at[1])
        total = x + vec[pl.ds(2 + group, 1), :]
        for z in range(mp):
            bias = wide(
                heads[me ^ z, pl.ds(3 + 2 * group, 1), :], heads[me ^ z, pl.ds(4 + 2 * group, 1), :]
            )
            pre = dot(low, w_up[z]) + bias
            act[z] = pre
            value = 0.5 * pre * (1.0 + lax.erf(pre * (0.5**0.5)))
            total = total + dot_t(value.astype(BF), w_down[z])
        normed, inverse = norm_parts(total)
        gain = vec[pl.ds(8 + 2 * group, 1), :]
        third = normed * gain + vec[pl.ds(9 + 2 * group, 1), :]
        layer[...] = third.astype(BF).reshape(2, items, NQ, D)
        for t in tops:
            t.wait()
        grad = top[...].reshape(2 * half, D).astype(F32)
        back = norm_backward(grad, normed, inverse, gain)
        branch = back.astype(BF)
        sums[0:1, :] = column_sum(branch)
        sums[1:2, :] = column_sum(grad * normed)
        sums[2:3, :] = column_sum(grad)
        low_t = low.T
        branch_t = branch.T
        for z in range(mp):
            pre = act[z]
            cdf = 0.5 * (1.0 + lax.erf(pre * (0.5**0.5)))
            value = (pre * cdf).astype(BF)
            slope = cdf + pre * jnp.exp(-0.5 * pre * pre) * (1.0 / math.sqrt(2.0 * math.pi))
            pull = (dot(branch, w_down[z]) * slope).astype(BF)
            bias_sums[pl.ds(z, 1), :] = column_sum(pull)
            down_grad[z] = dot(branch_t, value).astype(BF)
            up_grad[z] = dot(low_t, pull).astype(BF)
            back = back + dot_t(pull, w_up[z])
        spread(plan, down_grad, down_out, plan.back, sems.at[4])
        spread(plan, up_grad, up_out, plan.forth, sems.at[5])
        kept_back[...] = back[:half]
        given_back[...] = back[half:].astype(BF)
        settle(down_grad, sems.at[4])
        settle(up_grad, sems.at[5])

    outs = [
        jax.ShapeDtypeStruct((2, items, NQ, D), BF),
        jax.ShapeDtypeStruct((half, D), F32),
        jax.ShapeDtypeStruct((half, D), BF),
        jax.ShapeDtypeStruct((3, D), F32),
        jax.ShapeDtypeStruct((mp, hidden_width), F32),
        *shapes,
        *shapes,
    ]
    found = call(
        kernel,
        (vec, heads, kept, got, cotangent, *up, *down),
        [VMEM] * 4 + [ANY] * (1 + sum(counts)),
        outs,
        [VMEM] * 5 + [ANY] * (2 * grads),
        [
            pltpu.VMEM((2, items, NQ, D), BF),
            pltpu.VMEM((mp, D, hidden_width), BF),
            pltpu.VMEM((mp, D, hidden_width), BF),
            pltpu.VMEM((mp, 2 * half, hidden_width), F32),
            pltpu.VMEM((mp, D, hidden_width), BF),
            pltpu.VMEM((mp, D, hidden_width), BF),
            DMA((6,)),
        ],
        48,
        8 * 10**9,
        20 * 10**6,
    )
    return (*found[:5], found[5 : 5 + grads], found[5 + grads :])


def cross_backward(plan, keys, vec, z_first, z_second, kept, got, cross, kv, vc, oo):
    counts = len(vc), len(oo)
    mp, rows, half, width, items = plan.mp, plan.rows, plan.half, plan.width, plan.items
    padded = kv.shape[2]

    def kernel(vec, z_first, z_second, kept, got, cross, kv, *rest):
        vc, oo = rest[: counts[0]], rest[counts[0] : sum(counts)]
        kv_back, query_back, branch_out, first_back, sums = rest[sum(counts) : sum(counts) + 5]
        w_vc, w_oo, sems = rest[sum(counts) + 5 :]
        low = (lax.axis_index("mp") & 1) == 0
        fetch(plan, oo, plan.back, w_oo, sems.at[0])
        fetch(plan, vc, plan.back, w_vc, sems.at[1])
        lanes = head_lanes(width)
        mask = key_mask(plan, keys, padded)
        other = got[...].astype(F32)
        grad = jnp.where(low, kept[...], other)
        caption = jnp.where(low, other, kept[...])
        normed, inverse = norm_parts(z_second[...])
        back = norm_backward(grad, normed, inverse, vec[6:7, :])
        branch = back.astype(BF)
        branch_out[...] = branch
        sums[0:1, :] = column_sum(branch)
        sums[1:2, :] = column_sum(grad * normed)
        sums[2:3, :] = column_sum(grad)
        settle(w_oo, sems.at[0])
        settle(w_vc, sems.at[1])
        for z in range(mp):
            context_back = dot(branch, w_oo[z]).astype(BF)[:, width:]
            value_sum = jnp.zeros((1, width), F32)
            for i in range(items):
                span = slice(i * NQ, (i + 1) * NQ)
                q = spread_heads(cross[z, span, :], lanes)
                g = spread_heads(context_back[span], lanes)
                both = kv[i, z]
                k, v = both[:, :width], both[:, width:]
                probs = softmax(dot_t(q, k) * SCALE + mask)
                pulled = dot_t(g, v)
                scored = probs * (pulled - jnp.sum(probs * pulled, axis=-1, keepdims=True))
                scored = scored.astype(BF)
                value_back = t_dot(probs.astype(BF), g).astype(BF)
                key_back = (t_dot(scored, q) * SCALE).astype(BF)
                kv_back[i, z] = wide(key_back, value_back)
                value_sum = value_sum + column_sum(value_back)
                query_back[z, span, :] = (gather_heads(dot(scored, k), lanes) * SCALE).astype(BF)
            sums[6:7, z * width : (z + 1) * width] = column_sum(query_back[z])
            sums[7:8, z * width : (z + 1) * width] = value_sum
            back = back + dot_t(after(query_back[z], width), w_vc[z])
        first_grad = join_halves(back, caption, items)
        normed, inverse = norm_parts(z_first[...])
        first = norm_backward(first_grad, normed, inverse, vec[4:5, :])
        first_back[...] = first
        sums[3:4, :] = column_sum(first_grad * normed)
        sums[4:5, :] = column_sum(first_grad)
        sums[5:6, :] = column_sum(first.astype(BF))

    outs = [
        jax.ShapeDtypeStruct((items, mp, padded, 2 * width), BF),
        jax.ShapeDtypeStruct((mp, half, width), BF),
        jax.ShapeDtypeStruct((half, D), BF),
        jax.ShapeDtypeStruct((rows, D), F32),
        jax.ShapeDtypeStruct((8, D), F32),
    ]
    return call(
        kernel,
        (vec, z_first, z_second, kept, got, cross, kv, *vc, *oo),
        [VMEM] * 7 + [ANY] * sum(counts),
        outs,
        [VMEM] * 5,
        [
            pltpu.VMEM((mp, D, 2 * width), BF),
            pltpu.VMEM((mp, D, 2 * width), BF),
            DMA((2,)),
        ],
        40,
        4 * 10**9,
        16 * 10**6,
    )


def image_gradient(plan, images, kv_back, shard_rows):
    mp, items, width = plan.mp, plan.items, plan.width
    keys, features = images.shape[1:]
    shapes = gradient_shapes(plan, shard_rows, features, 2 * width)
    even = keys // 128 * 128

    def kernel(images, kv_back, *rest):
        outs = rest[: len(shapes)]
        held, turned, grad, sems = rest[len(shapes) :]
        loaded = load_tokens(plan, images, held, sems.at[0])
        loaded.start()
        loaded.wait()
        for i in range(items):
            turned[:, i * even : (i + 1) * even] = held[i, 0:even, :].T
        for z in range(mp):
            total = jnp.zeros((features, 2 * width), F32)
            for i in range(items):
                total = total + dot(
                    turned[:, i * even : (i + 1) * even], kv_back[i, z, 0:even, :]
                )
            for i in range(items):
                if keys > even:
                    total = total + t_dot(held[i, even:keys, :], kv_back[i, z, even:keys, :])
            grad[z] = total.astype(BF)
        spread(plan, grad, outs, plan.forth, sems.at[1])
        settle(grad, sems.at[1])

    return call(
        kernel,
        (images, kv_back),
        [ANY, VMEM],
        shapes,
        [ANY] * len(shapes),
        [
            pltpu.VMEM((items, keys, features), BF),
            pltpu.VMEM((features, items * even), BF),
            pltpu.VMEM((mp, features, 2 * width), BF),
            DMA((2,)),
        ],
        48,
        5 * 10**9,
        12 * 10**6,
    )


def self_backward(plan, lengths, hidden, vec, z_first, first_back, branch, cross_context, query_back, qk_all, v_all, context_all, qk, vc, oo, shard_rows):
    counts = len(qk), len(vc), len(oo)
    mp, rows, half, width, items = plan.mp, plan.rows, plan.half, plan.width, plan.items
    shapes = gradient_shapes(plan, shard_rows, D, 2 * width)
    grads = len(shapes)

    def kernel(lengths, hidden, vec, z_first, first_back, branch, cross_context, query_back, qk_all, v_all, context_all, *rest):
        qk = rest[: counts[0]]
        vc = rest[counts[0] : counts[0] + counts[1]]
        oo = rest[counts[0] + counts[1] : sum(counts)]
        rest = rest[sum(counts) :]
        token_back, sums = rest[:2]
        qk_out = rest[2 : 2 + grads]
        vc_out = rest[2 + grads : 2 + 2 * grads]
        oo_out = rest[2 + 2 * grads : 2 + 3 * grads]
        tokens, w_qk, w_vc, w_oo, g_qk, g_vc, g_oo, sems = rest[2 + 3 * grads :]
        me = lax.axis_index("mp")
        loaded = load_tokens(plan, hidden, tokens, sems.at[0])
        loaded.start()
        fetch(plan, oo, plan.back, w_oo, sems.at[3])
        fetch(plan, qk, plan.forth, w_qk, sems.at[1])
        fetch(plan, vc, plan.back, w_vc, sems.at[2])
        mask = self_mask(plan, lengths, me)
        lanes = head_lanes(width)
        total = first_back[...]
        self_branch = total.astype(BF)
        branches_t = jnp.concatenate([self_branch, branch[...]], axis=0).T
        normed, _ = norm_parts(z_first[...])
        u = halves_of(normed * vec[4:5, :] + vec[5:6, :], items)[0].astype(BF)
        loaded.wait()
        inputs_t = jnp.concatenate([tokens[...].reshape(rows, D), u], axis=0).T
        settle(w_oo, sems.at[3])
        settle(w_qk, sems.at[1])
        settle(w_vc, sems.at[2])
        for z in range(mp):
            contexts = jnp.concatenate(
                [before(context_all[z], width), after(cross_context[z], width)], axis=0
            )
            g_oo[z] = dot(branches_t, contexts).astype(BF)
            pulled = dot(self_branch, w_oo[z]).astype(BF)[:, :width]
            q, k, v = qk_all[z][:, :width], qk_all[z][:, width:], v_all[z]
            query_grad = jnp.zeros((rows, width), F32)
            key_grad = jnp.zeros((rows, width), F32)
            value_grad = jnp.zeros((rows, width), F32)
            for lane in lanes:
                q_h, g_h = only(q, lane), only(pulled, lane)
                probs = softmax(dot_t(q_h, k) * SCALE + mask)
                wanted = dot_t(g_h, v)
                scored = probs * (wanted - jnp.sum(probs * wanted, axis=-1, keepdims=True))
                scored = scored.astype(BF)
                value_grad = value_grad + t_dot(probs.astype(BF), g_h)
                query_grad = query_grad + only(dot(scored, k), lane)
                key_grad = key_grad + t_dot(scored, q_h)
            query_grad = (query_grad * SCALE).astype(BF)
            value_grad = value_grad.astype(BF)
            sums[0:1, z * width : (z + 1) * width] = column_sum(query_grad)
            sums[1:2, z * width : (z + 1) * width] = column_sum(value_grad)
            both = wide(query_grad, (key_grad * SCALE).astype(BF))
            value_wide = before(value_grad, width)
            total = total + dot_t(both, w_qk[z]) + dot_t(value_wide, w_vc[z])
            g_qk[z] = dot(inputs_t[:, :rows], both).astype(BF)
            maps = jnp.concatenate([value_wide, after(query_back[z], width)], axis=0)
            g_vc[z] = dot(inputs_t, maps).astype(BF)
        token_back[...] = total.astype(BF)
        spread(plan, g_oo, oo_out, plan.back, sems.at[4])
        spread(plan, g_qk, qk_out, plan.forth, sems.at[5])
        spread(plan, g_vc, vc_out, plan.back, sems.at[6])
        settle(g_oo, sems.at[4])
        settle(g_qk, sems.at[5])
        settle(g_vc, sems.at[6])

    outs = [
        jax.ShapeDtypeStruct((rows, D), BF),
        jax.ShapeDtypeStruct((2, D), F32),
        *shapes,
        *shapes,
        *shapes,
    ]
    found = call(
        kernel,
        (lengths, hidden, vec, z_first, first_back, branch, cross_context, query_back, qk_all, v_all, context_all, *qk, *vc, *oo),
        [SMEM, ANY] + [VMEM] * 9 + [ANY] * sum(counts),
        outs,
        [VMEM] * 2 + [ANY] * (3 * grads),
        [pltpu.VMEM((items, 2 * NQ, D), BF)]
        + [pltpu.VMEM((mp, D, 2 * width), BF)] * 6
        + [DMA((7,))],
        48,
        6 * 10**9,
        24 * 10**6,
    )
    return (
        found[0],
        found[1],
        found[2 : 2 + grads],
        found[2 + grads : 2 + 2 * grads],
        found[2 + 2 * grads :],
    )


def place_layer(plan, pieces):
    mp, items = plan.mp, plan.items

    def kernel(*refs):
        out, sems = refs[mp], refs[mp + 1]
        me = lax.axis_index("mp")
        copies = []
        for j in range(mp):
            source = me ^ j
            group = source & 1
            for s in range(2):
                copies.append(
                    pltpu.make_async_copy(
                        refs[j].at[s],
                        out.at[
                            pl.ds((source ^ s) * items, items),
                            pl.ds(pl.multiple_of(group * NQ, NQ), NQ),
                            :,
                        ],
                        sems.at[2 * j + s],
                    )
                )
                copies[-1].start()
        for c in copies:
            c.wait()

    return call(
        kernel,
        pieces,
        [VMEM] * mp,
        [jax.ShapeDtypeStruct((mp * items, 2 * NQ, D), BF)],
        [ANY],
        [DMA((2 * mp,))],
        16,
        0,
        4 * 10**6,
    )[0]


def place_gradient(plan, pieces):
    mp, items = plan.mp, plan.items

    def kernel(*refs):
        out = refs[mp]
        me = lax.axis_index("mp")
        for j in range(mp):
            values = refs[j][...].astype(F32).reshape(items, 2 * NQ, D)
            out[pl.ds((me ^ j) * items, items)] = values

    return call(
        kernel,
        pieces,
        [VMEM] * mp,
        [jax.ShapeDtypeStruct((mp * items, 2 * NQ, D), F32)],
        [VMEM],
        [],
        24,
        0,
        6 * 10**6,
    )[0]


def adam_update(weight, first, second, grad, rate):
    first_new = BETA_ONE * first + (1.0 - BETA_ONE) * grad
    second_new = BETA_TWO * second + (1.0 - BETA_TWO) * grad * grad
    first_hat = first_new / (1.0 - BETA_ONE**STEP_COUNT)
    second_hat = second_new / (1.0 - BETA_TWO**STEP_COUNT)
    weight_new = weight - rate * (
        first_hat / (jnp.sqrt(second_hat) + ADAM_EPS) + WEIGHT_DECAY * weight
    )
    return (first_new, second_new, weight_new)


def local(
    bits,
    hidden,
    images,
    caption_len,
    cotangent,
    attn_in,
    attn_in_first,
    attn_in_second,
    attn_out,
    attn_out_first,
    attn_out_second,
    cross_key_value_maps,
    cross_kv_first,
    cross_kv_second,
    ffn_up,
    ffn_up_first,
    ffn_up_second,
    ffn_down,
    ffn_down_first,
    ffn_down_second,
    vec_rep,
    vec_rep_first,
    vec_rep_second,
    query_value_bias_rows,
    vec_head_first,
    vec_head_second,
    bias_up,
    bias_up_first,
    bias_up_second,
):
    mp = lax.axis_size("mp")
    me = lax.axis_index("mp")
    plan = Plan(bits, mp, hidden.shape[0] // mp, 2 ** (bits + 1))
    forth, back = plan.forth, plan.back
    group = me & 1
    low = group == 0
    keys = images.shape[1]

    def side(values):
        return jnp.concatenate([values[0], values[1]], axis=1)

    none = jnp.zeros_like(query_value_bias_rows[0])
    bias_rows = query_value_bias_rows
    packed = jnp.concatenate(
        [
            jnp.concatenate([bias_rows[0], none])[None],
            jnp.concatenate([bias_rows[1], bias_rows[2]])[None],
            jnp.concatenate([none, bias_rows[3]])[None],
            bias_up.reshape(-1, 2 * plan.width),
            jnp.zeros((1, 2 * plan.width), F32),
        ]
    )
    heads = jnp.stack(mp_collect(packed, lambda j: packed))

    low_in = attn_in.astype(BF)
    first_shard = jnp.stack([side(low_in[:2]), side(low_in[2:])])
    first_set = mp_collect(first_shard, lambda j: first_shard)
    qk = tree_gather(plan, jnp.stack([p[0] for p in first_set]), forth)
    vc = tree_gather(plan, jnp.stack([p[1] for p in first_set]), back)

    kv_rows = cross_key_value_maps.shape[1]
    second_shard = jnp.concatenate(
        [
            side(cross_key_value_maps.astype(BF)),
            side(attn_out.astype(BF).transpose(0, 2, 1)),
        ]
    )
    second_set = mp_collect(second_shard, lambda j: second_shard)
    oo = tree_gather(plan, jnp.stack([p[kv_rows:] for p in second_set]), back)
    kv = tree_gather(plan, jnp.stack([p[:kv_rows] for p in second_set]), forth)

    third_shard = jnp.stack(
        [ffn_up.astype(BF), ffn_down.astype(BF).transpose(0, 2, 1)], axis=1
    )
    own = lax.dynamic_index_in_dim(third_shard, group, 0, keepdims=False)
    other = lax.dynamic_index_in_dim(third_shard, 1 - group, 0, keepdims=False)
    third_set = mp_collect(own, lambda j: other if j % 2 else own)
    up = tree_gather(plan, jnp.stack([p[0] for p in third_set]), forth)
    down = tree_gather(plan, jnp.stack([p[1] for p in third_set]), back)

    qk_all, v_all, context_all, z_first, cross = self_forward(
        plan, caption_len, hidden, vec_rep, heads, qk, vc, oo
    )
    kv_all = image_maps(plan, images, heads, kv)
    cross_context, z_second, kept, given = cross_forward(
        plan, keys, vec_rep, z_first, cross, kv_all, oo
    )
    got = mp_swap(given, 1)
    layer, kept_back, given_back, third_sums, bias_sums, up_grad, down_grad = feed_forward(
        plan, vec_rep, heads, kept, got, cotangent, up, down, ffn_up.shape[1]
    )
    got_back = mp_swap(given_back, 1)
    layer_out = place_layer(plan, mp_collect(layer, lambda j: layer))
    kv_back, query_back, branch, first_back, cross_sums = cross_backward(
        plan, keys, vec_rep, z_first, z_second, kept_back, got_back, cross, kv_all, vc, oo
    )
    kv_grad = image_gradient(plan, images, kv_back, kv_rows)
    token_back, self_sums, qk_grad, vc_grad, oo_grad = self_backward(
        plan,
        caption_len,
        hidden,
        vec_rep,
        z_first,
        first_back,
        branch,
        cross_context,
        query_back,
        qk_all,
        v_all,
        context_all,
        qk,
        vc,
        oo,
        attn_in.shape[1],
    )
    grad_hidden = place_gradient(plan, mp_collect(token_back, lambda j: token_back))

    zero = jnp.zeros_like(third_sums)
    sums_low, sums_high = jnp.where(low, third_sums, zero), jnp.where(low, zero, third_sums)
    bias_flat = bias_sums.reshape(-1, D)
    bias_zero = jnp.zeros_like(bias_flat)
    vectors = jnp.concatenate(
        [
            cross_sums[5:6],
            cross_sums[0:1],
            sums_low[0:1],
            sums_high[0:1],
            cross_sums[3:5],
            cross_sums[1:3],
            sums_low[1:3],
            sums_high[1:3],
            self_sums,
            cross_sums[6:8],
            jnp.where(low, bias_flat, bias_zero),
            jnp.where(low, bias_zero, bias_flat),
        ]
    )
    for axis in ("core",) + forth:
        vectors = vectors + swap(vectors, axis)
    distance = 1
    while distance < mp:
        vectors = vectors + mp_swap(vectors, distance)
        distance *= 2
    reduced_rep = vectors[:12]
    head_width = query_value_bias_rows.shape[1]
    bias_width = bias_up.shape[1]
    reduced_head = lax.dynamic_slice_in_dim(vectors[12:16], me * head_width, head_width, 1)
    reduced_bias = lax.dynamic_slice_in_dim(
        vectors[16:].reshape(2, -1), me * bias_width, bias_width, 1
    )

    def finish(trees):
        totals = [
            tree_reduce(tree_halves(plan, grads, rows, order), order)
            for grads, rows, order in trees
        ]
        return mp_collect(
            [t[0] for t in totals],
            lambda j: jnp.concatenate([t[j].astype(BF) for t in totals]),
        )

    def split_columns(values):
        width = values.shape[1] // 2
        return jnp.stack([values[:, :width], values[:, width:]])

    def add_all(pieces, rows):
        own, rest = pieces[0], pieces[1:]
        bounds = [0]
        for r in rows:
            bounds.append(bounds[-1] + r)
        return [
            own[k] + sum(p[bounds[k] : bounds[k + 1]].astype(F32) for p in rest)
            for k in range(len(rows))
        ]

    ffn_rows = ffn_up.shape[1]
    attn_rows = attn_in.shape[1]
    third = finish([(up_grad, ffn_rows, forth), (down_grad, ffn_rows, back)])
    mine = [third[0][k] for k in range(2)]
    theirs = [jnp.zeros_like(m) for m in mine]
    for j in range(1, mp):
        for k in range(2):
            part = third[j][k * ffn_rows : (k + 1) * ffn_rows].astype(F32)
            if j % 2:
                theirs[k] = theirs[k] + part
            else:
                mine[k] = mine[k] + part
    reduced_up, reduced_down = (
        jnp.stack([jnp.where(low, m, t), jnp.where(low, t, m)]) for m, t in zip(mine, theirs)
    )
    reduced_down = reduced_down.transpose(0, 2, 1)
    kv_total = add_all(finish([(kv_grad, kv_rows, forth)]), [kv_rows])[0]
    reduced_kv = split_columns(kv_total)
    oo_total, qk_total, vc_total = add_all(
        finish(
            [
                (oo_grad, attn_rows, back),
                (qk_grad, attn_rows, forth),
                (vc_grad, attn_rows, back),
            ]
        ),
        [attn_rows] * 3,
    )
    reduced_out = split_columns(oo_total).transpose(0, 2, 1)
    reduced_in = jnp.concatenate([split_columns(qk_total), split_columns(vc_total)])
    rates = (
        2.0 / math.sqrt(D),
        2.0 / math.sqrt(max(D // 8, 1)),
        2.0 / math.sqrt(E),
        2.0 / math.sqrt(D),
        2.0 / math.sqrt(F),
        0.3,
        0.3,
        0.3,
    )
    weights = (
        attn_in,
        attn_out,
        cross_key_value_maps,
        ffn_up,
        ffn_down,
        vec_rep,
        query_value_bias_rows,
        bias_up,
    )
    firsts = (
        attn_in_first,
        attn_out_first,
        cross_kv_first,
        ffn_up_first,
        ffn_down_first,
        vec_rep_first,
        vec_head_first,
        bias_up_first,
    )
    seconds = (
        attn_in_second,
        attn_out_second,
        cross_kv_second,
        ffn_up_second,
        ffn_down_second,
        vec_rep_second,
        vec_head_second,
        bias_up_second,
    )
    reduced = (
        reduced_in,
        reduced_out,
        reduced_kv,
        reduced_up,
        reduced_down,
        reduced_rep,
        reduced_head,
        reduced_bias,
    )
    results = []
    for weight, first, second, grad, rate in zip(weights, firsts, seconds, reduced, rates):
        results.extend(adam_update(weight, first, second, grad, rate))
    return (layer_out, grad_hidden, *results)


def solution(mesh):
    dp, mp = mesh.devices.shape
    bits = (dp // 2).bit_length() - 1
    names = tuple(f"b{k}" for k in range(bits)) + ("core",)
    fine = Mesh(mesh.devices.reshape((2,) * (bits + 1) + (mp,)), names + ("mp",))
    split = P(names)
    inward = P(None, names, "mp")
    outward = P(None, "mp", names)
    head = P(None, "mp")
    stored = (inward,) * 3 + (outward,) * 3 + (inward,) * 6 + (outward,) * 3 + (P(),) * 3 + (head,) * 6
    return jax.shard_map(
        functools.partial(local, bits),
        mesh=fine,
        in_specs=(split,) * 4 + stored,
        out_specs=(split,) * 2 + stored,
        check_vma=False,
    )
```

time: 1040 us -> 539 us (0.52)
  local copies, waits for them, and re-layouts: 415 us -> 43.3 us
  Pallas kernels: 0 us -> 132 us
  matrix products: 88.7 us -> 0 us
  other arithmetic: 110 us -> 28.3 us
  waiting for transfers between devices: 257 us -> 222 us
  blocking collectives: 28.1 us -> 0 us
  between operations: 17.2 us -> 3.18 us
    pallas_call x0 -> x9, Pallas kernels: none -> 132 us  [call(): pl.pallas_call(kernel, out_shape=outs, in_specs=[pl.BlockSpec(memory_spac...]
    psum x1 -> x0, waiting for transfers between devices: 117 us -> none  [local(): lax.psum((shared, headwise, hidden_bias), every)]
    slice x16, local copies, waits for them, and re-layouts: 116 us -> 3.11 us  [the longest x1 0.6 us: local(): vectors[12:16]]
    dot_general x40 -> x0, matrix products: 88.7 us -> none  [the longest x10 26.5 us: dot(): lax.dot_general(a, b, (((1,), (0,)), ((), ())), preferred_element_type=F32)]
    another operation x30 -> x10, local copies, waits for them, and re-layouts: 77.7 us -> 0.43 us  [the longest x4 0.36 us: split_columns(): return jnp.stack([values[:, :width], values[:, width:]])]
    reshape x22 -> x2, local copies, waits for them, and re-layouts: 59 us -> 0.64 us  [the longest x1 0.63 us: local(): vectors[16:].reshape(2, -1)]
    dynamic_update_slice x26 -> x0, local copies, waits for them, and re-layouts: 47.6 us -> none  [mp_place(): total = lax.dynamic_update_index_in_dim(total, piece, me ^ distance, 0)]
    ppermute x44 -> x31, waiting for transfers between devices: 52.9 us -> 100 us  [mp_swap(): return lax.ppermute(values, 'mp', [(i, i ^ distance) for i in range(count)])]
  transfers between devices with their start and end apart: 81 -> 94, of which waited for: 31 -> 31; matrix products, arithmetic and copies ran while one was open for 55% -> 7% of each run, Pallas kernels for 0% -> 21%
where the time goes in v2:
time: 539 us; the launch traced here: 534 us
  waiting for transfers between devices  222 us (41%)
  Pallas kernels  132 us (24%)
  starting transfers between devices  106 us (20%)
  local copies, waits for them, and re-layouts  43.3 us (8%)
  other arithmetic  28.3 us (5%)
    pallas_call x9, Pallas kernels, call(): pl.pallas_call(kernel, out_shape=outs, in_specs=[pl.BlockSpec(memory_spac...  132 us
    ppermute x63, waiting for transfers between devices, swap(): return lax.ppermute(values, axis, [(0, 1), (1, 0)])  121 us
    ppermute x31, waiting for transfers between devices, mp_swap(): return lax.ppermute(values, 'mp', [(i, i ^ distance) for i in range(count)])  100 us
    ppermute x31, starting transfers between devices, mp_swap(): return lax.ppermute(values, 'mp', [(i, i ^ distance) for i in range(count)])  62.2 us
    ppermute x63, starting transfers between devices, swap(): return lax.ppermute(values, axis, [(0, 1), (1, 0)])  43.4 us
    unnamed x277, local copies, waits for them, and re-layouts  38 us
  transfers between devices with their start and end apart: 94, of which 31 were waited for; matrix products, arithmetic and copies ran while one was open for 7% of the time, Pallas kernels for 21%

profile of v2, /device:TPU:0, one launch (start us, length us, event | category | flops | bytes accessed | tf_op | source)
XLA Modules:
  0.0 533.8 jit_solution(3936895904846948275)
XLA Ops:
  2.0 3.1 collective-permute-start.3
  5.1 2.6 collective-permute-start.4
  8.7 3.9 collective-permute-start.22
  14.4 13.7 %collective-permute-done.4 = bf16[2,96,384]{2,1,0:T(8,128)(2,1)S(1)} collective-permute-done((bf16[2,96,384]{2,1,0:T(8,128)(2,1)S(1)}, bf16[2,96,384]{2,1,0:T(8,128)(2,1)S(1)}, u32[]{:S(2)}, u32[]{:S(2)}) %collective-permute-start.4) | collective-permute-done | bytes 147488 | tf_op jit(solution)/shard_map/ppermute | solution.py:50
  28.1 4.5 collective-permute-start.1
  32.8 1.6 collective-permute-start.2
  34.5 5.1 collective-permute-done.21
  39.6 2.5 collective-permute-start.40
  46.3 6.1 %collective-permute-done.38 = bf16[2,96,768]{2,1,0:T(8,128)(2,1)S(1)} collective-permute-done((bf16[2,96,768]{2,1,0:T(8,128)(2,1)S(1)}, bf16[2,96,768]{2,1,0:T(8,128)(2,1)S(1)}, u32[]{:S(2)}, u32[]{:S(2)}) %collective-permute-start.38) | collective-permute-done | bytes 294944 | tf_op jit(solution)/shard_map/ppermute | solution.py:50
  54.0 13.2 %collective-permute-done.39 = bf16[2,96,768]{2,1,0:T(8,128)(2,1)S(1)} collective-permute-done((bf16[2,96,768]{2,1,0:T(8,128)(2,1)S(1)}, bf16[2,96,768]{2,1,0:T(8,128)(2,1)S(1)}, u32[]{:S(2)}, u32[]{:S(2)}) %collective-permute-start.39) | collective-permute-done | bytes 294944 | tf_op jit(solution)/shard_map/ppermute | solution.py:50
  71.2 5.8 %collective-permute-done.7.rest_2_ = bf16[4,96,384]{2,1,0:T(8,128)(2,1)S(1)} collective-permute-done((bf16[4,96,384]{2,1,0:T(8,128)(2,1)S(1)}, bf16[4,96,384]{2,1,0:T(8,128)(2,1)S(1)}, u32[]{:S(2)}, u32[]{:S(2)}) %collective-permute-start.7) | collective-permute-done | bytes 294944 | tf_op jit(solution)/shard_map/ppermute | solution.py:45
  78.5 4.4 collective-permute-done.23.rest_17_.rest_1_.rest_9_
  82.9 1.6 collective-permute-start.8
  84.6 1.6 collective-permute-start.30
  87.3 5.6 %collective-permute-done.8.rest_3_ = bf16[4,96,384]{2,1,0:T(8,128)(2,1)S(1)} collective-permute-done((bf16[4,96,384]{2,1,0:T(8,128)(2,1)S(1)}, bf16[4,96,384]{2,1,0:T(8,128)(2,1)S(1)}, u32[]{:S(2)}, u32[]{:S(2)}) %collective-permute-start.8) | collective-permute-done | bytes 294944 | tf_op jit(solution)/shard_map/ppermute | solution.py:45
  93.0 1.6 collective-permute-start.41
  95.9 3.8 collective-permute-done.30.rest_1_
  99.8 4.2 collective-permute-done.31.rest_2_
  104.1 1.6 collective-permute-start.48
  105.6 12.3 %collective-permute-done.25.rest_19_.rest_3_.rest_11_ = bf16[4,96,384]{2,1,0:T(8,128)(2,1)S(1)} collective-permute-done((bf16[4,96,384]{2,1,0:T(8,128)(2,1)S(1)}, bf16[4,96,384]{2,1,0:T(8,128)(2,1)S(1)}, u32[]{:S(2)}, u32[]{:S(2)}) %collective-permute-start.25) | collective-permute-done | bytes 294944 | tf_op jit(solution)/shard_map/ppermute | solution.py:45
  122.0 12.3 %collective-permute-done.42.rest_2_ = bf16[4,96,768]{2,1,0:T(8,128)(2,1)} collective-permute-done((bf16[4,96,768]{2,1,0:T(8,128)(2,1)S(1)}, bf16[4,96,768]{2,1,0:T(8,128)(2,1)}, u32[]{:S(2)}, u32[]{:S(2)}) %collective-permute-start.42) | collective-permute-done | bytes 589856 | tf_op jit(solution)/shard_map/ppermute | solution.py:45
  138.8 7.0 %collective-permute-done.32.rest_3_ = bf16[4,176,384]{2,1,0:T(8,128)(2,1)S(1)} collective-permute-done((bf16[4,176,384]{2,1,0:T(8,128)(2,1)S(1)}, bf16[4,176,384]{2,1,0:T(8,128)(2,1)S(1)}, u32[]{:S(2)}, u32[]{:S(2)}) %collective-permute-start.32) | collective-permute-done | bytes 540704 | tf_op jit(solution)/shard_map/ppermute | solution.py:45
  146.3 8.1 %copy.55.images = bf16[16,257,1408]{2,1,0:T(8,128)(2,1)S(1)} copy(bf16[16,257,1408]{2,0,1:T(8,128)(2,1)} %param.29) | data formatting | bytes 23158784 | tf_op args[1]
  154.6 18.6 %shard_map.467 = (bf16[4,256,384]{2,1,0:T(8,128)(2,1)S(1)}, bf16[4,256,192]{2,1,0:T(8,128)(2,1)S(1)}, bf16[4,256,192]{2,1,0:T(8,128)(2,1)S(1)}, f32[256,768]{1,0:T(8,128)S(1)}, bf16[4,128,192]{2,1,0:T(8,128)(2,1)S(1)}) custom-call(s32[16]{0:T(128)S(1)} %copy-done.80, bf16[16,64,768]{2,1,0:T(8,128)(2,1)S(1)} %copy-done.37, f32[12,768]{1,0:T(8,128)S(1)} %copy-done.29, ...), custom_call_target="tpu_custom_call" | custom-call | flops 3000000000 | bytes 9000000 | tf_op jit(solution)/shard_map/pallas_call | solution.py:229
  177.8 13.3 %shard_map.468.kv = bf16[4,4,384,384]{3,2,1,0:T(8,128)(2,1)S(1)} custom-call(bf16[16,257,1408]{2,1,0:T(8,128)(2,1)S(1)} %copy.55.images, f32[4,8,384]{2,1,0:T(8,128)S(1)} %pad_maximum_fusion.16.heads, bf16[4,176,384]{2,1,0:T(8,128)(2,1)S(1)} %pad_maximum_fusion.3.rest_0_, bf16[4,176,384]{2,1,0:T(8,128)(2,1)S(1)} %collective-permute-done.30.rest_1_, ...), custom_call_target="tpu_custom_call" | custom-call | flops 5000000000 | bytes 12000000 | tf_op jit(solution)/shard_map/pallas_call | solution.py:229
  191.2 4.3 copy-done
  195.5 10.7 %shard_map.469 = (bf16[4,128,192]{2,1,0:T(8,128)(2,1)S(1)}, f32[128,768]{1,0:T(8,128)S(1)}, f32[128,768]{1,0:T(8,128)S(1)}, bf16[128,768]{1,0:T(8,128)(2,1)S(1)}) custom-call(f32[12,768]{1,0:T(8,128)S(1)} %copy-done.29, f32[256,768]{1,0:T(8,128)S(1)} %get-tuple-element.59.z_first, bf16[4,128,192]{2,1,0:T(8,128)(2,1)S(1)} %get-tuple-element.60.cross, ...), custom_call_target="tpu_custom_call" | custom-call | flops 2000000000 | bytes 8000000 | tf_op jit(solution)/shard_map/pallas_call | solution.py:229
  209.2 7.2 %collective-permute-done.37.got = bf16[128,768]{1,0:T(8,128)(2,1)S(1)} collective-permute-done((bf16[128,768]{1,0:T(8,128)(2,1)S(1)}, bf16[128,768]{1,0:T(8,128)(2,1)S(1)}, u32[]{:S(2)}, u32[]{:S(2)}) %collective-permute-start.37) | collective-permute-done | bytes 196640 | tf_op jit(solution)/shard_map/ppermute | solution.py:50
  222.5 17.6 %shard_map.470 = (bf16[2,4,32,768]{3,2,1,0:T(8,128)(2,1)S(1)}, f32[128,768]{1,0:T(8,128)S(1)}, bf16[128,768]{1,0:T(8,128)(2,1)S(1)}, f32[3,768]{1,0:T(4,128)S(1)...) custom-call(f32[12,768]{1,0:T(8,128)S(1)} %copy-done.30, ...), custom_call_target="tpu_custom_call" | custom-call | flops 8000000000 | bytes 20000000 | tf_op jit(solution)/shard_map/pallas_call | solution.py:229
  242.7 2.9 collective-permute-start.56
  246.5 19.3 %collective-permute-done.58.got = bf16[128,768]{1,0:T(8,128)(2,1)S(1)} collective-permute-done((bf16[128,768]{1,0:T(8,128)(2,1)S(1)}, bf16[128,768]{1,0:T(8,128)(2,1)S(1)}, u32[]{:S(2)}, u32[]{:S(2)}) %collective-permute-start.58) | collective-permute-done | bytes 196640 | tf_op jit(solution)/shard_map/ppermute | solution.py:50
  266.0 22.1 %shard_map.472 = (bf16[4,4,384,384]{3,2,1,0:T(8,128)(2,1)S(1)}, bf16[4,128,192]{2,1,0:T(8,128)(2,1)S(1)}, bf16[128,768]{1,0:T(8,128)(2,1)S(1)}, f32[256,768]{1,0:T(8,128)S(1)}, f32[8,768]{1,0:T(8,128)S(1)}) custom-call(f32[12,768]{1,0:T(8,128)S(1)} %copy-done.31, f32[256,768]{1,0:T(8,128)S(1)} %copy-done.3, f32[128,768]{1,0:T(8,128)S(1)} %copy-done.45, ...), custom_call_target="tpu_custom_call" | custom-call | flops 4000000000 | bytes 16000000 | tf_op jit(solution)/shard_map/pallas_call | solution.py:229
  288.2 2.1 copy-done.81
  291.3 25.2 %shard_map.473 = (bf16[256,768]{1,0:T(8,128)(2,1)}, f32[2,768]{1,0:T(2,128)S(1)}, bf16[4,4,96,384]{3,2,1,0:T(8,128)(2,1)}, bf16[4,4,96,384]{3,2,1,0:T(8,128)(2,1...) custom-call(s32[16]{0:T(128)S(1)} %copy-done.80, ...), custom_call_target="tpu_custom_call" | custom-call | flops 6000000000 | bytes 24000000 | tf_op jit(solution)/shard_map/pallas_call | solution.py:229
  318.0 1.6 collective-permute-start.90
  319.6 2.8 collective-permute-done.90
  323.1 3.8 collective-permute-done.91
  329.1 2.6 collective-permute-start.57
  334.1 1.6 collective-permute-start.93
  335.7 21.1 %shard_map.475 = (bf16[4,4,176,384]{3,2,1,0:T(8,128)(2,1)S(1)}, bf16[4,4,176,384]{3,2,1,0:T(8,128)(2,1)S(1)}) custom-call(bf16[16,257,1408]{2,1,0:T(8,128)(2,1)} %copy-done, bf16[4,4,384,384]{3,2,1,0:T(8,128)(2,1)} %copy-done.81), custom_call_target="tpu_custom_call" | custom-call | flops 5000000000 | bytes 12000000 | tf_op jit(solution)/shard_map/pallas_call | solution.py:229
  357.0 7.5 %collective-permute-start.59 = (bf16[256,768]{1,0:T(8,128)(2,1)S(1)}, bf16[256,768]{1,0:T(8,128)(2,1)S(1)}, u32[]{:S(2)}, u32[]{:S(2)}) collective-permute-start(bf16[256,768]{1,0:T(8,128)(2,1)S(1)} %copy-done.6), channel_id=1, source_target_pairs={{0,1},{1,0},{2,3},{3,2},{4,5},{5,4},{6,7},{7,6},{8,9},{9,8},{10,11... | collective-permute-start | bytes 1179656 | tf_op jit(solution)/shard_map/ppermute | solution.py:50
  369.8 2.8 collective-permute-start.61
  372.6 2.0 add_convert_fusion.13
  374.6 1.6 collective-permute-start.66
  376.2 1.7 add_convert_fusion.15
  378.6 1.7 add_convert_fusion.11
  382.3 13.3 %collective-permute-done.60.refs_2_ = bf16[256,768]{1,0:T(8,128)(2,1)S(1)} collective-permute-done((bf16[256,768]{1,0:T(8,128)(2,1)S(1)}, bf16[256,768]{1,0:T(8,128)(2,1)S(1)}, u32[]{:S(2)}, u32[]{:S(2)}) %collective-permute-start.60) | collective-permute-done | bytes 393248 | tf_op jit(solution)/shard_map/ppermute | solution.py:50
  396.1 1.9 shard_map.474
  399.3 2.4 collective-permute-done.69
  403.3 4.3 collective-permute-done.67
  409.0 6.7 %collective-permute-done.70 = bf16[1,4,96,384]{3,2,1,0:T(8,128)(2,1)S(1)} collective-permute-done((bf16[1,4,96,384]{3,2,1,0:T(8,128)(2,1)S(1)}, bf16[1,4,96,384]{3,2,1,0:T(8,128)(2,1)S(1)}, u32[]{:S(2)}, u32[]{:S(2)}) %collective-permute-start.70) | collective-permute-done | bytes 294944 | tf_op jit(solution)/shard_map/ppermute | solution.py:45
  415.9 8.3 %collective-permute-start.71 = (bf16[288,384]{1,0:T(8,128)(2,1)S(1)}, bf16[288,384]{1,0:T(8,128)(2,1)S(1)}, u32[]{:S(2)}, u32[]{:S(2)}) collective-permute-start(bf16[288,384]{1,0:T(8,128)(2,1)S(1)} %pad_maximum_fusion.12), channel_id=1, source_target_pairs={{0,1},{1,0},{2,3},{3,2},{4,5},{5,4},{6,7},{7,6},{8,9},{9,8},{10,11... | collective-permute-start | bytes 663560 | tf_op jit(solution)/shard_map/ppermute | solution.py:50
  424.3 2.4 collective-permute-start.73
  428.6 1.6 collective-permute-start.75
  432.6 9.3 %collective-permute-done.72 = bf16[288,384]{1,0:T(8,128)(2,1)S(1)} collective-permute-done((bf16[288,384]{1,0:T(8,128)(2,1)S(1)}, bf16[288,384]{1,0:T(8,128)(2,1)S(1)}, u32[]{:S(2)}, u32[]{:S(2)}) %collective-permute-start.72) | collective-permute-done | bytes 221216 | tf_op jit(solution)/shard_map/ppermute | solution.py:50
  443.4 33.4 %collective-permute-done.75 = bf16[2,4,176,384]{3,2,1,0:T(8,128)(2,1)S(1)} collective-permute-done((bf16[2,4,176,384]{3,2,1,0:T(8,128)(2,1)S(1)}, bf16[2,4,176,384]{3,2,1,0:T(8,128)(2,1)S(1)}, u32[]{:S(2)}, u32[]{:S(2)}) %collective-permute-start.75) | collective-permute-done | bytes 1081376 | tf_op jit(solution)/shard_map/ppermute | solution.py:45
  477.0 1.6 collective-permute-start.76
  481.8 10.4 %collective-permute-done.76 = bf16[1,4,176,384]{3,2,1,0:T(8,128)(2,1)S(1)} collective-permute-done((bf16[1,4,176,384]{3,2,1,0:T(8,128)(2,1)S(1)}, bf16[1,4,176,384]{3,2,1,0:T(8,128)(2,1)S(1)}, u32[]{:S(2)}, u32[]{:S(2)}) %collective-permute-start.76) | collective-permute-done | bytes 540704 | tf_op jit(solution)/shard_map/ppermute | solution.py:45
  496.2 2.4 collective-permute-start.79
  501.2 2.8 collective-permute-done.78
  508.9 5.3 %collective-permute-start.86 = (bf16[192,768]{1,0:T(8,128)(2,1)S(1)}, bf16[192,768]{1,0:T(8,128)(2,1)S(1)}, u32[]{:S(2)}, u32[]{:S(2)}) collective-permute-start(bf16[192,768]{1,0:T(8,128)(2,1)S(1)} %pad_maximum_fusion.9), channel_id=1, source_target_pairs={{0,2},{1,3},{2,0},{3,1},{4,6},{5,7},{6,4},{7,5},{8,10},{9,11},{10,... | collective-permute-start | bytes 884744 | tf_op jit(solution)/shard_map/ppermute | solution.py:50
  515.0 2.4 collective-permute-start.88
  518.7 5.8 %collective-permute-done.86 = bf16[192,768]{1,0:T(8,128)(2,1)S(1)} collective-permute-done((bf16[192,768]{1,0:T(8,128)(2,1)S(1)}, bf16[192,768]{1,0:T(8,128)(2,1)S(1)}, u32[]{:S(2)}, u32[]{:S(2)}) %collective-permute-start.86) | collective-permute-done | bytes 294944 | tf_op jit(solution)/shard_map/ppermute | solution.py:50
  524.5 3.9 collective-permute-done.88
  (515 shorter events, 92.2 us)
Async XLA Ops:
  5.1 23.0 %collective-permute-start.4 = (bf16[2,96,384]{2,1,0:T(8,128)(2,1)S(1)}, bf16[2,96,384]{2,1,0:T(8,128)(2,1)S(1)}, u32[]{:S(2)}, u32[]{:S(2)}) collective-permute-start(bf16[2,96,384]{2,1,0:T(8,128)(2,1)S(1)} %pad_maximum_fusion.15), channel_id=1, source_target_pairs={{0,2},{1,3},{2,0},{3,1},{4,6},{5,7},{6,4},{7,5},{8,10},{9,11},{10,... | collective-permute-start | bytes 442376 | tf_op jit(solution)/shard_map/ppermute | solution.py:50
  7.7 20.4 %collective-permute-start.5 = (bf16[2,96,384]{2,1,0:T(8,128)(2,1)S(1)}, bf16[2,96,384]{2,1,0:T(8,128)(2,1)S(1)}, u32[]{:S(2)}, u32[]{:S(2)}) collective-permute-start(bf16[2,96,384]{2,1,0:T(8,128)(2,1)S(1)} %pad_maximum_fusion.15), channel_id=1, source_target_pairs={{0,3},{1,2},{2,1},{3,0},{4,7},{5,6},{6,5},{7,4},{8,11},{9,10},{10,... | collective-permute-start | bytes 442376 | tf_op jit(solution)/shard_map/ppermute | solution.py:50
  8.7 24.1 %collective-permute-start.22 = (bf16[272,384]{1,0:T(8,128)(2,1)S(1)}, bf16[272,384]{1,0:T(8,128)(2,1)S(1)}, u32[]{:S(2)}, u32[]{:S(2)}) collective-permute-start(bf16[272,384]{1,0:T(8,128)(2,1)S(1)} %maximum_maximum_fusion), channel_id=1, source_target_pairs={{0,3},{1,2},{2,1},{3,0},{4,7},{5,6},{6,5},{7,4},{8,11},{9,10},{10,... | collective-permute-start | bytes 626696 | tf_op jit(solution)/shard_map/ppermute | solution.py:50
  12.6 27.0 %collective-permute-start.21 = (bf16[272,384]{1,0:T(8,128)(2,1)S(1)}, bf16[272,384]{1,0:T(8,128)(2,1)S(1)}, u32[]{:S(2)}, u32[]{:S(2)}) collective-permute-start(bf16[272,384]{1,0:T(8,128)(2,1)S(1)} %maximum_maximum_fusion), channel_id=1, source_target_pairs={{0,2},{1,3},{2,0},{3,1},{4,6},{5,7},{6,4},{7,5},{8,10},{9,11},{10,... | collective-permute-start | bytes 626696 | tf_op jit(solution)/shard_map/ppermute | solution.py:50
  13.6 26.0 %collective-permute-start.20 = (bf16[272,384]{1,0:T(8,128)(2,1)S(1)}, bf16[272,384]{1,0:T(8,128)(2,1)S(1)}, u32[]{:S(2)}, u32[]{:S(2)}) collective-permute-start(bf16[272,384]{1,0:T(8,128)(2,1)S(1)} %maximum_maximum_fusion), channel_id=1, source_target_pairs={{0,1},{1,0},{2,3},{3,2},{4,5},{5,4},{6,7},{7,6},{8,9},{9,8},{10,11... | collective-permute-start | bytes 626696 | tf_op jit(solution)/shard_map/ppermute | solution.py:50
  28.1 14.1 %collective-permute-start = (f32[8,384]{1,0:T(8,128)S(1)}, f32[8,384]{1,0:T(8,128)S(1)}, u32[]{:S(2)}, u32[]{:S(2)}) collective-permute-start(f32[8,384]{1,0:T(8,128)S(1)} %concatenate.54), channel_id=1, source_target_pairs={{0,1},{1,0},{2,3},{3,2},{4,5},{5,4},{6,7},{7,6},{8,9},{9,8},{10,11... | collective-permute-start | bytes 36872 | tf_op jit(solution)/shard_map/ppermute | solution.py:50
  28.1 15.1 %collective-permute-start.1 = (f32[8,384]{1,0:T(8,128)S(1)}, f32[8,384]{1,0:T(8,128)S(1)}, u32[]{:S(2)}, u32[]{:S(2)}) collective-permute-start(f32[8,384]{1,0:T(8,128)S(1)} %concatenate.54), channel_id=1, source_target_pairs={{0,2},{1,3},{2,0},{3,1},{4,6},{5,7},{6,4},{7,5},{8,10},{9,11},{10,... | collective-permute-start | bytes 36872 | tf_op jit(solution)/shard_map/ppermute | solution.py:50
  39.6 27.6 %collective-permute-start.40 = (bf16[2,96,768]{2,1,0:T(8,128)(2,1)S(1)}, bf16[2,96,768]{2,1,0:T(8,128)(2,1)S(1)}, u32[]{:S(2)}, u32[]{:S(2)}) collective-permute-start(bf16[2,96,768]{2,1,0:T(8,128)(2,1)S(1)} %get-tuple-element.182), channel_id=1, source_target_pairs={{0,3},{1,2},{2,1},{3,0},{4,7},{5,6},{6,5},{7,4},{8,11},{9,10},{10,... | collective-permute-start | bytes 884744 | tf_op jit(solution)/shard_map/ppermute | solution.py:50
  42.2 25.0 %collective-permute-start.39 = (bf16[2,96,768]{2,1,0:T(8,128)(2,1)S(1)}, bf16[2,96,768]{2,1,0:T(8,128)(2,1)S(1)}, u32[]{:S(2)}, u32[]{:S(2)}) collective-permute-start(bf16[2,96,768]{2,1,0:T(8,128)(2,1)S(1)} %bitcast.167), channel_id=1, source_target_pairs={{0,2},{1,3},{2,0},{3,1},{4,6},{5,7},{6,4},{7,5},{8,10},{9,11},{10,... | collective-permute-start | bytes 884744 | tf_op jit(solution)/shard_map/ppermute | solution.py:50
  43.3 25.4 %collective-permute-start.13 = (bf16[4,96,384]{2,1,0:T(8,128)(2,1)S(1)}, bf16[4,96,384]{2,1,0:T(8,128)(2,1)S(1)}, u32[]{:S(2)}, u32[]{:S(2)}) collective-permute-start(bf16[4,96,384]{2,1,0:T(8,128)(2,1)S(1)} %pad_maximum_fusion.7.rest_8_.rest_0_), channel_id=1, source_target_pairs={{0,8},{8,0},{1,9},{9,1},{2,10},{10,2},{3,11},{11,3},{4,12},{12,4},... | collective-permute-start | bytes 884744 | tf_op jit(solution)/shard_map/ppermute | solution.py:45
  44.7 24.2 %collective-permute-start.14 = (bf16[4,96,384]{2,1,0:T(8,128)(2,1)S(1)}, bf16[4,96,384]{2,1,0:T(8,128)(2,1)S(1)}, u32[]{:S(2)}, u32[]{:S(2)}) collective-permute-start(bf16[4,96,384]{2,1,0:T(8,128)(2,1)S(1)} %pad_maximum_fusion.7.rest_8_.rest_0_), channel_id=1, source_target_pairs={{0,16},{16,0},{1,17},{17,1},{2,18},{18,2},{3,19},{19,3},{4,20},{20... | collective-permute-start | bytes 884744 | tf_op jit(solution)/shard_map/ppermute | solution.py:45
  52.4 17.1 %collective-permute-start.6 = (bf16[4,96,384]{2,1,0:T(8,128)(2,1)S(1)}, bf16[4,96,384]{2,1,0:T(8,128)(2,1)S(1)}, u32[]{:S(2)}, u32[]{:S(2)}) collective-permute-start(bf16[4,96,384]{2,1,0:T(8,128)(2,1)S(1)} %pad_maximum_fusion.6.rest_0_), channel_id=1, source_target_pairs={{0,16},{16,0},{1,17},{17,1},{2,18},{18,2},{3,19},{19,3},{4,20},{20... | collective-permute-start | bytes 884744 | tf_op jit(solution)/shard_map/ppermute | solution.py:45
  68.9 14.0 %collective-permute-start.23 = (bf16[4,96,384]{2,1,0:T(8,128)(2,1)S(1)}, bf16[4,96,384]{2,1,0:T(8,128)(2,1)S(1)}, u32[]{:S(2)}, u32[]{:S(2)}) collective-permute-start(bf16[4,96,384]{2,1,0:T(8,128)(2,1)S(1)} %pad_maximum_fusion.8.rest_16_.rest_0_.rest_8_), channel_id=1, source_target_pairs={{0,8},{8,0},{1,9},{9,1},{2,10},{10,2},{3,11},{11,3},{4,12},{12,4},... | collective-permute-start | bytes 884744 | tf_op jit(solution)/shard_map/ppermute | solution.py:45
  69.5 13.5 %collective-permute-start.24 = (bf16[4,96,384]{2,1,0:T(8,128)(2,1)S(1)}, bf16[4,96,384]{2,1,0:T(8,128)(2,1)S(1)}, u32[]{:S(2)}, u32[]{:S(2)}) collective-permute-start(bf16[4,96,384]{2,1,0:T(8,128)(2,1)S(1)} %pad_maximum_fusion.8.rest_16_.rest_0_.rest_8_), channel_id=1, source_target_pairs={{0,16},{16,0},{1,17},{17,1},{2,18},{18,2},{3,19},{19,3},{4,20},{20... | collective-permute-start | bytes 884744 | tf_op jit(solution)/shard_map/ppermute | solution.py:45
  84.6 15.2 %collective-permute-start.30 = (bf16[4,176,384]{2,1,0:T(8,128)(2,1)S(1)}, bf16[4,176,384]{2,1,0:T(8,128)(2,1)S(1)}, u32[]{:S(2)}, u32[]{:S(2)}) collective-permute-start(bf16[4,176,384]{2,1,0:T(8,128)(2,1)S(1)} %pad_maximum_fusion.3.rest_0_), channel_id=1, source_target_pairs={{0,16},{16,0},{1,17},{17,1},{2,18},{18,2},{3,19},{19,3},{4,20},{20... | collective-permute-start | bytes 1622024 | tf_op jit(solution)/shard_map/ppermute | solution.py:45
  86.2 17.8 %collective-permute-start.31 = (bf16[4,176,384]{2,1,0:T(8,128)(2,1)S(1)}, bf16[4,176,384]{2,1,0:T(8,128)(2,1)S(1)}, u32[]{:S(2)}, u32[]{:S(2)}) collective-permute-start(bf16[4,176,384]{2,1,0:T(8,128)(2,1)S(1)} %pad_maximum_fusion.3.rest_0_), channel_id=1, source_target_pairs={{0,8},{8,0},{1,9},{9,1},{2,10},{10,2},{3,11},{11,3},{4,12},{12,4},... | collective-permute-start | bytes 1622024 | tf_op jit(solution)/shard_map/ppermute | solution.py:45
  86.8 17.3 %collective-permute-start.33 = (bf16[4,176,384]{2,1,0:T(8,128)(2,1)S(1)}, bf16[4,176,384]{2,1,0:T(8,128)(2,1)S(1)}, u32[]{:S(2)}, u32[]{:S(2)}) collective-permute-start(bf16[4,176,384]{2,1,0:T(8,128)(2,1)S(1)} %pad_maximum_fusion.3.rest_0_), channel_id=1, source_target_pairs={{0,4},{4,0},{1,5},{5,1},{2,6},{6,2},{3,7},{7,3},{8,12},{12,8},{9,1... | collective-permute-start | bytes 1622024 | tf_op jit(solution)/shard_map/ppermute | solution.py:45
  93.0 27.0 %collective-permute-start.41 = (bf16[4,96,768]{2,1,0:T(8,128)(2,1)S(1)}, bf16[4,96,768]{2,1,0:T(8,128)(2,1)S(1)}, u32[]{:S(2)}, u32[]{:S(2)}) collective-permute-start(bf16[4,96,768]{2,1,0:T(8,128)(2,1)S(1)} %pad_maximum_fusion.rest_0_), channel_id=1, source_target_pairs={{0,16},{16,0},{1,17},{17,1},{2,18},{18,2},{3,19},{19,3},{4,20},{20... | collective-permute-start | bytes 1769480 | tf_op jit(solution)/shard_map/ppermute | solution.py:45
  94.6 23.4 %collective-permute-start.25 = (bf16[4,96,384]{2,1,0:T(8,128)(2,1)S(1)}, bf16[4,96,384]{2,1,0:T(8,128)(2,1)S(1)}, u32[]{:S(2)}, u32[]{:S(2)}) collective-permute-start(bf16[4,96,384]{2,1,0:T(8,128)(2,1)S(1)} %collective-permute-done.23.rest_17_.rest_1_.rest_9_), channel_id=1, source_target_pairs={{0,16},{16,0},{1,17},{17,1},{2,18},{18,2},{3,19},{19,3},{4,20},{20... | collective-permute-start | bytes 884744 | tf_op jit(solution)/shard_map/ppermute | solution.py:45
  99.8 18.7 %collective-permute-start.27 = (bf16[4,96,384]{2,1,0:T(8,128)(2,1)S(1)}, bf16[4,96,384]{2,1,0:T(8,128)(2,1)S(1)}, u32[]{:S(2)}, u32[]{:S(2)}) collective-permute-start(bf16[4,96,384]{2,1,0:T(8,128)(2,1)S(1)} %collective-permute-done.23.rest_17_.rest_1_.rest_9_), channel_id=1, source_target_pairs={{0,4},{4,0},{1,5},{5,1},{2,6},{6,2},{3,7},{7,3},{8,12},{12,8},{9,1... | collective-permute-start | bytes 884744 | tf_op jit(solution)/shard_map/ppermute | solution.py:45
  104.0 16.1 %collective-permute-start.28 = (bf16[4,96,384]{2,1,0:T(8,128)(2,1)S(1)}, bf16[4,96,384]{2,1,0:T(8,128)(2,1)S(1)}, u32[]{:S(2)}, u32[]{:S(2)}) collective-permute-start(bf16[4,96,384]{2,1,0:T(8,128)(2,1)S(1)} %collective-permute-done.24.rest_18_.rest_2_.rest_10_), channel_id=1, source_target_pairs={{0,4},{4,0},{1,5},{5,1},{2,6},{6,2},{3,7},{7,3},{8,12},{12,8},{9,1... | collective-permute-start | bytes 884744 | tf_op jit(solution)/shard_map/ppermute | solution.py:45
  104.1 16.4 %collective-permute-start.48 = (bf16[4,96,768]{2,1,0:T(8,128)(2,1)S(1)}, bf16[4,96,768]{2,1,0:T(8,128)(2,1)S(1)}, u32[]{:S(2)}, u32[]{:S(2)}) collective-permute-start(bf16[4,96,768]{2,1,0:T(8,128)(2,1)S(1)} %pad_maximum_fusion.1.rest_8_), channel_id=1, source_target_pairs={{0,8},{8,0},{1,9},{9,1},{2,10},{10,2},{3,11},{11,3},{4,12},{12,4},... | collective-permute-start | bytes 1769480 | tf_op jit(solution)/shard_map/ppermute | solution.py:45
  117.9 16.4 %collective-permute-start.42 = (bf16[4,96,768]{2,1,0:T(8,128)(2,1)S(1)}, bf16[4,96,768]{2,1,0:T(8,128)(2,1)}, u32[]{:S(2)}, u32[]{:S(2)}) collective-permute-start(bf16[4,96,768]{2,1,0:T(8,128)(2,1)S(1)} %pad_maximum_fusion.rest_0_), channel_id=1, source_target_pairs={{0,8},{8,0},{1,9},{9,1},{2,10},{10,2},{3,11},{11,3},{4,12},{12,4},... | collective-permute-start | bytes 1769480 | tf_op jit(solution)/shard_map/ppermute | solution.py:45
  118.5 15.8 %collective-permute-start.49 = (bf16[4,96,768]{2,1,0:T(8,128)(2,1)S(1)}, bf16[4,96,768]{2,1,0:T(8,128)(2,1)}, u32[]{:S(2)}, u32[]{:S(2)}) collective-permute-start(bf16[4,96,768]{2,1,0:T(8,128)(2,1)S(1)} %pad_maximum_fusion.1.rest_8_), channel_id=1, source_target_pairs={{0,16},{16,0},{1,17},{17,1},{2,18},{18,2},{3,19},{19,3},{4,20},{20... | collective-permute-start | bytes 1769480 | tf_op jit(solution)/shard_map/ppermute | solution.py:45
  120.0 14.8 %collective-permute-start.44 = (bf16[4,96,768]{2,1,0:T(8,128)(2,1)S(1)}, bf16[4,96,768]{2,1,0:T(8,128)(2,1)S(1)}, u32[]{:S(2)}, u32[]{:S(2)}) collective-permute-start(bf16[4,96,768]{2,1,0:T(8,128)(2,1)S(1)} %pad_maximum_fusion.rest_0_), channel_id=1, source_target_pairs={{0,4},{4,0},{1,5},{5,1},{2,6},{6,2},{3,7},{7,3},{8,12},{12,8},{9,1... | collective-permute-start | bytes 1769480 | tf_op jit(solution)/shard_map/ppermute | solution.py:45
  120.0 15.6 %collective-permute-start.51 = (bf16[4,96,768]{2,1,0:T(8,128)(2,1)S(1)}, bf16[4,96,768]{2,1,0:T(8,128)(2,1)S(1)}, u32[]{:S(2)}, u32[]{:S(2)}) collective-permute-start(bf16[4,96,768]{2,1,0:T(8,128)(2,1)S(1)} %pad_maximum_fusion.1.rest_8_), channel_id=1, source_target_pairs={{0,4},{4,0},{1,5},{5,1},{2,6},{6,2},{3,7},{7,3},{8,12},{12,8},{9,1... | collective-permute-start | bytes 1769480 | tf_op jit(solution)/shard_map/ppermute | solution.py:45
  120.5 25.3 %collective-permute-start.32 = (bf16[4,176,384]{2,1,0:T(8,128)(2,1)S(1)}, bf16[4,176,384]{2,1,0:T(8,128)(2,1)S(1)}, u32[]{:S(2)}, u32[]{:S(2)}) collective-permute-start(bf16[4,176,384]{2,1,0:T(8,128)(2,1)S(1)} %collective-permute-done.30.rest_1_), channel_id=1, source_target_pairs={{0,8},{8,0},{1,9},{9,1},{2,10},{10,2},{3,11},{11,3},{4,12},{12,4},... | collective-permute-start | bytes 1622024 | tf_op jit(solution)/shard_map/ppermute | solution.py:45
  136.7 39.3 %collective-permute-start.43 = (bf16[4,96,768]{2,1,0:T(8,128)(2,1)S(1)}, bf16[4,96,768]{2,1,0:T(8,128)(2,1)}, u32[]{:S(2)}, u32[]{:S(2)}) collective-permute-start(bf16[4,96,768]{2,1,0:T(8,128)(2,1)S(1)} %collective-permute-done.41.rest_1_), channel_id=1, source_target_pairs={{0,8},{8,0},{1,9},{9,1},{2,10},{10,2},{3,11},{11,3},{4,12},{12,4},... | collective-permute-start | bytes 1769480 | tf_op jit(solution)/shard_map/ppermute | solution.py:45
  137.2 39.2 %collective-permute-start.50 = (bf16[4,96,768]{2,1,0:T(8,128)(2,1)S(1)}, bf16[4,96,768]{2,1,0:T(8,128)(2,1)}, u32[]{:S(2)}, u32[]{:S(2)}) collective-permute-start(bf16[4,96,768]{2,1,0:T(8,128)(2,1)S(1)} %collective-permute-done.48.rest_9_), channel_id=1, source_target_pairs={{0,16},{16,0},{1,17},{17,1},{2,18},{18,2},{3,19},{19,3},{4,20},{20... | collective-permute-start | bytes 1769480 | tf_op jit(solution)/shard_map/ppermute | solution.py:45
  138.8 37.7 %collective-permute-start.45 = (bf16[4,96,768]{2,1,0:T(8,128)(2,1)S(1)}, bf16[4,96,768]{2,1,0:T(8,128)(2,1)S(1)}, u32[]{:S(2)}, u32[]{:S(2)}) collective-permute-start(bf16[4,96,768]{2,1,0:T(8,128)(2,1)S(1)} %collective-permute-done.41.rest_1_), channel_id=1, source_target_pairs={{0,4},{4,0},{1,5},{5,1},{2,6},{6,2},{3,7},{7,3},{8,12},{12,8},{9,1... | collective-permute-start | bytes 1769480 | tf_op jit(solution)/shard_map/ppermute | solution.py:45
  145.8 30.0 %collective-permute-start.35 = (bf16[4,176,384]{2,1,0:T(8,128)(2,1)S(1)}, bf16[4,176,384]{2,1,0:T(8,128)(2,1)S(1)}, u32[]{:S(2)}, u32[]{:S(2)}) collective-permute-start(bf16[4,176,384]{2,1,0:T(8,128)(2,1)S(1)} %collective-permute-done.31.rest_2_), channel_id=1, source_target_pairs={{0,4},{4,0},{1,5},{5,1},{2,6},{6,2},{3,7},{7,3},{8,12},{12,8},{9,1... | collective-permute-start | bytes 1622024 | tf_op jit(solution)/shard_map/ppermute | solution.py:45
  145.8 31.9 %collective-permute-start.36 = (bf16[4,176,384]{2,1,0:T(8,128)(2,1)S(1)}, bf16[4,176,384]{2,1,0:T(8,128)(2,1)S(1)}, u32[]{:S(2)}, u32[]{:S(2)}) collective-permute-start(bf16[4,176,384]{2,1,0:T(8,128)(2,1)S(1)} %collective-permute-done.32.rest_3_), channel_id=1, source_target_pairs={{0,4},{4,0},{1,5},{5,1},{2,6},{6,2},{3,7},{7,3},{8,12},{12,8},{9,1... | collective-permute-start | bytes 1622024 | tf_op jit(solution)/shard_map/ppermute | solution.py:45
  175.8 32.6 %collective-permute-start.52 = (bf16[4,96,768]{2,1,0:T(8,128)(2,1)S(1)}, bf16[4,96,768]{2,1,0:T(8,128)(2,1)S(1)}, u32[]{:S(2)}, u32[]{:S(2)}) collective-permute-start(bf16[4,96,768]{2,1,0:T(8,128)(2,1)S(1)} %collective-permute-done.48.rest_9_), channel_id=1, source_target_pairs={{0,4},{4,0},{1,5},{5,1},{2,6},{6,2},{3,7},{7,3},{8,12},{12,8},{9,1... | collective-permute-start | bytes 1769480 | tf_op jit(solution)/shard_map/ppermute | solution.py:45
  176.0 33.3 %collective-permute-start.46 = (bf16[4,96,768]{2,1,0:T(8,128)(2,1)}, bf16[4,96,768]{2,1,0:T(8,128)(2,1)}, u32[]{:S(2)}, u32[]{:S(2)}) collective-permute-start(bf16[4,96,768]{2,1,0:T(8,128)(2,1)} %collective-permute-done.42.rest_2_), channel_id=1, source_target_pairs={{0,4},{4,0},{1,5},{5,1},{2,6},{6,2},{3,7},{7,3},{8,12},{12,8},{9,1... | collective-permute-start | bytes 1769480 | tf_op jit(solution)/shard_map/ppermute | solution.py:45
  176.4 32.8 %collective-permute-start.53 = (bf16[4,96,768]{2,1,0:T(8,128)(2,1)}, bf16[4,96,768]{2,1,0:T(8,128)(2,1)}, u32[]{:S(2)}, u32[]{:S(2)}) collective-permute-start(bf16[4,96,768]{2,1,0:T(8,128)(2,1)} %collective-permute-done.49.rest_10_), channel_id=1, source_target_pairs={{0,4},{4,0},{1,5},{5,1},{2,6},{6,2},{3,7},{7,3},{8,12},{12,8},{9,1... | collective-permute-start | bytes 1769480 | tf_op jit(solution)/shard_map/ppermute | solution.py:45
  177.3 39.8 %collective-permute-start.47 = (bf16[4,96,768]{2,1,0:T(8,128)(2,1)}, bf16[4,96,768]{2,1,0:T(8,128)(2,1)}, u32[]{:S(2)}, u32[]{:S(2)}) collective-permute-start(bf16[4,96,768]{2,1,0:T(8,128)(2,1)} %collective-permute-done.43.rest_3_), channel_id=1, source_target_pairs={{0,4},{4,0},{1,5},{5,1},{2,6},{6,2},{3,7},{7,3},{8,12},{12,8},{9,1... | collective-permute-start | bytes 1769480 | tf_op jit(solution)/shard_map/ppermute | solution.py:45
  177.7 39.4 %collective-permute-start.54 = (bf16[4,96,768]{2,1,0:T(8,128)(2,1)}, bf16[4,96,768]{2,1,0:T(8,128)(2,1)}, u32[]{:S(2)}, u32[]{:S(2)}) collective-permute-start(bf16[4,96,768]{2,1,0:T(8,128)(2,1)} %collective-permute-done.50.rest_11_), channel_id=1, source_target_pairs={{0,4},{4,0},{1,5},{5,1},{2,6},{6,2},{3,7},{7,3},{8,12},{12,8},{9,1... | collective-permute-start | bytes 1769480 | tf_op jit(solution)/shard_map/ppermute | solution.py:45
  242.5 89.7 %collective-permute-start.55 = (bf16[2,4,32,768]{3,2,1,0:T(8,128)(2,1)S(1)}, bf16[2,4,32,768]{3,2,1,0:T(8,128)(2,1)S(1)}, u32[]{:S(2)}, u32[]{:S(2)}) collective-permute-start(bf16[2,4,32,768]{3,2,1,0:T(8,128)(2,1)S(1)} %get-tuple-element.63.refs_0_), channel_id=1, source_target_pairs={{0,1},{1,0},{2,3},{3,2},{4,5},{5,4},{6,7},{7,6},{8,9},{9,8},{10,11... | collective-permute-start | bytes 1179656 | tf_op jit(solution)/shard_map/ppermute | solution.py:50
  242.7 90.7 %collective-permute-start.56 = (bf16[2,4,32,768]{3,2,1,0:T(8,128)(2,1)S(1)}, bf16[2,4,32,768]{3,2,1,0:T(8,128)(2,1)S(1)}, u32[]{:S(2)}, u32[]{:S(2)}) collective-permute-start(bf16[2,4,32,768]{3,2,1,0:T(8,128)(2,1)S(1)} %get-tuple-element.63.refs_0_), channel_id=1, source_target_pairs={{0,2},{1,3},{2,0},{3,1},{4,6},{5,7},{6,4},{7,5},{8,10},{9,11},{10,... | collective-permute-start | bytes 1179656 | tf_op jit(solution)/shard_map/ppermute | solution.py:50
  245.7 20.1 %collective-permute-start.58 = (bf16[128,768]{1,0:T(8,128)(2,1)S(1)}, bf16[128,768]{1,0:T(8,128)(2,1)S(1)}, u32[]{:S(2)}, u32[]{:S(2)}) collective-permute-start(bf16[128,768]{1,0:T(8,128)(2,1)S(1)} %get-tuple-element.66), channel_id=1, source_target_pairs={{0,1},{1,0},{2,3},{3,2},{4,5},{5,4},{6,7},{7,6},{8,9},{9,8},{10,11... | collective-permute-start | bytes 589832 | tf_op jit(solution)/shard_map/ppermute | solution.py:50
  316.8 53.1 %collective-permute-start.65 = (bf16[4,4,96,384]{3,2,1,0:T(8,128)(2,1)}, bf16[4,4,96,384]{3,2,1,0:T(8,128)(2,1)}, u32[]{:S(2)}, u32[]{:S(2)}) collective-permute-start(bf16[4,4,96,384]{3,2,1,0:T(8,128)(2,1)} %get-tuple-element.78), channel_id=1, source_target_pairs={{0,4},{4,0},{1,5},{5,1},{2,6},{6,2},{3,7},{7,3},{8,12},{12,8},{9,1... | collective-permute-start | bytes 3538952 | tf_op jit(solution)/shard_map/ppermute | solution.py:45
  329.1 27.8 %collective-permute-start.57 = (bf16[2,4,32,768]{3,2,1,0:T(8,128)(2,1)S(1)}, bf16[2,4,32,768]{3,2,1,0:T(8,128)(2,1)S(1)}, u32[]{:S(2)}, u32[]{:S(2)}) collective-permute-start(bf16[2,4,32,768]{3,2,1,0:T(8,128)(2,1)S(1)} %get-tuple-element.63.refs_0_), channel_id=1, source_target_pairs={{0,3},{1,2},{2,1},{3,0},{4,7},{5,6},{6,5},{7,4},{8,11},{9,10},{10,... | collective-permute-start | bytes 1179656 | tf_op jit(solution)/shard_map/ppermute | solution.py:50
  332.1 42.5 %collective-permute-start.62 = (bf16[4,4,96,384]{3,2,1,0:T(8,128)(2,1)}, bf16[4,4,96,384]{3,2,1,0:T(8,128)(2,1)}, u32[]{:S(2)}, u32[]{:S(2)}) collective-permute-start(bf16[4,4,96,384]{3,2,1,0:T(8,128)(2,1)} %get-tuple-element.76), channel_id=1, source_target_pairs={{0,4},{4,0},{1,5},{5,1},{2,6},{6,2},{3,7},{7,3},{8,12},{12,8},{9,1... | collective-permute-start | bytes 3538952 | tf_op jit(solution)/shard_map/ppermute | solution.py:45
  332.9 45.1 %collective-permute-start.68 = (bf16[4,4,96,384]{3,2,1,0:T(8,128)(2,1)}, bf16[4,4,96,384]{3,2,1,0:T(8,128)(2,1)}, u32[]{:S(2)}, u32[]{:S(2)}) collective-permute-start(bf16[4,4,96,384]{3,2,1,0:T(8,128)(2,1)} %get-tuple-element.80), channel_id=1, source_target_pairs={{0,4},{4,0},{1,5},{5,1},{2,6},{6,2},{3,7},{7,3},{8,12},{12,8},{9,1... | collective-permute-start | bytes 3538952 | tf_op jit(solution)/shard_map/ppermute | solution.py:45
  334.1 31.5 %collective-permute-start.93 = (f32[24,768]{1,0:T(8,128)S(1)}, f32[24,768]{1,0:T(8,128)S(1)}, u32[]{:S(2)}, u32[]{:S(2)}) collective-permute-start(f32[24,768]{1,0:T(8,128)S(1)} %add.367), channel_id=1, source_target_pairs={{0,2},{1,3},{2,0},{3,1},{4,6},{5,7},{6,4},{7,5},{8,10},{9,11},{10,... | collective-permute-start | bytes 221192 | tf_op jit(solution)/shard_map/ppermute | solution.py:50
  357.0 23.3 %collective-permute-start.59 = (bf16[256,768]{1,0:T(8,128)(2,1)S(1)}, bf16[256,768]{1,0:T(8,128)(2,1)S(1)}, u32[]{:S(2)}, u32[]{:S(2)}) collective-permute-start(bf16[256,768]{1,0:T(8,128)(2,1)S(1)} %copy-done.6), channel_id=1, source_target_pairs={{0,1},{1,0},{2,3},{3,2},{4,5},{5,4},{6,7},{7,6},{8,9},{9,8},{10,11... | collective-permute-start | bytes 1179656 | tf_op jit(solution)/shard_map/ppermute | solution.py:50
  365.7 29.9 %collective-permute-start.60 = (bf16[256,768]{1,0:T(8,128)(2,1)S(1)}, bf16[256,768]{1,0:T(8,128)(2,1)S(1)}, u32[]{:S(2)}, u32[]{:S(2)}) collective-permute-start(bf16[256,768]{1,0:T(8,128)(2,1)S(1)} %copy-done.6), channel_id=1, source_target_pairs={{0,2},{1,3},{2,0},{3,1},{4,6},{5,7},{6,4},{7,5},{8,10},{9,11},{10,... | collective-permute-start | bytes 1179656 | tf_op jit(solution)/shard_map/ppermute | solution.py:50
  369.8 25.7 %collective-permute-start.61 = (bf16[256,768]{1,0:T(8,128)(2,1)S(1)}, bf16[256,768]{1,0:T(8,128)(2,1)S(1)}, u32[]{:S(2)}, u32[]{:S(2)}) collective-permute-start(bf16[256,768]{1,0:T(8,128)(2,1)S(1)} %copy-done.6), channel_id=1, source_target_pairs={{0,3},{1,2},{2,1},{3,0},{4,7},{5,6},{6,5},{7,4},{8,11},{9,10},{10,... | collective-permute-start | bytes 1179656 | tf_op jit(solution)/shard_map/ppermute | solution.py:50
  374.6 23.4 %collective-permute-start.66 = (bf16[2,4,96,384]{3,2,1,0:T(8,128)(2,1)S(1)}, bf16[2,4,96,384]{3,2,1,0:T(8,128)(2,1)S(1)}, u32[]{:S(2)}, u32[]{:S(2)}) collective-permute-start(bf16[2,4,96,384]{3,2,1,0:T(8,128)(2,1)S(1)} %get-tuple-element.161), channel_id=1, source_target_pairs={{0,16},{16,0},{1,17},{17,1},{2,18},{18,2},{3,19},{19,3},{4,20},{20... | collective-permute-start | bytes 1769480 | tf_op jit(solution)/shard_map/ppermute | solution.py:45
  377.9 20.7 %collective-permute-start.63 = (bf16[2,4,96,384]{3,2,1,0:T(8,128)(2,1)S(1)}, bf16[2,4,96,384]{3,2,1,0:T(8,128)(2,1)S(1)}, u32[]{:S(2)}, u32[]{:S(2)}) collective-permute-start(bf16[2,4,96,384]{3,2,1,0:T(8,128)(2,1)S(1)} %get-tuple-element.163), channel_id=1, source_target_pairs={{0,8},{8,0},{1,9},{9,1},{2,10},{10,2},{3,11},{11,3},{4,12},{12,4},... | collective-permute-start | bytes 1769480 | tf_op jit(solution)/shard_map/ppermute | solution.py:45
  380.3 21.5 %collective-permute-start.69 = (bf16[2,4,96,384]{3,2,1,0:T(8,128)(2,1)S(1)}, bf16[2,4,96,384]{3,2,1,0:T(8,128)(2,1)S(1)}, u32[]{:S(2)}, u32[]{:S(2)}) collective-permute-start(bf16[2,4,96,384]{3,2,1,0:T(8,128)(2,1)S(1)} %get-tuple-element.165), channel_id=1, source_target_pairs={{0,16},{16,0},{1,17},{17,1},{2,18},{18,2},{3,19},{19,3},{4,20},{20... | collective-permute-start | bytes 1769480 | tf_op jit(solution)/shard_map/ppermute | solution.py:45
  395.6 28.7 %collective-permute-start.80 = (bf16[4,4,96,768]{3,2,1,0:T(8,128)(2,1)S(1)}, bf16[4,4,96,768]{3,2,1,0:T(8,128)(2,1)S(1)}, u32[]{:S(2)}, u32[]{:S(2)}) collective-permute-start(bf16[4,4,96,768]{3,2,1,0:T(8,128)(2,1)S(1)} %copy-done.131), channel_id=1, source_target_pairs={{0,4},{4,0},{1,5},{5,1},{2,6},{6,2},{3,7},{7,3},{8,12},{12,8},{9,1... | collective-permute-start | bytes 7077896 | tf_op jit(solution)/shard_map/ppermute | solution.py:45
  395.6 33.0 %collective-permute-start.83 = (bf16[4,4,96,768]{3,2,1,0:T(8,128)(2,1)S(1)}, bf16[4,4,96,768]{3,2,1,0:T(8,128)(2,1)S(1)}, u32[]{:S(2)}, u32[]{:S(2)}) collective-permute-start(bf16[4,4,96,768]{3,2,1,0:T(8,128)(2,1)S(1)} %copy-done.130), channel_id=1, source_target_pairs={{0,4},{4,0},{1,5},{5,1},{2,6},{6,2},{3,7},{7,3},{8,12},{12,8},{9,1... | collective-permute-start | bytes 7077896 | tf_op jit(solution)/shard_map/ppermute | solution.py:45
  398.0 29.4 %collective-permute-start.74 = (bf16[4,4,176,384]{3,2,1,0:T(8,128)(2,1)S(1)}, bf16[4,4,176,384]{3,2,1,0:T(8,128)(2,1)S(1)}, u32[]{:S(2)}, u32[]{:S(2)}) collective-permute-start(bf16[4,4,176,384]{3,2,1,0:T(8,128)(2,1)S(1)} %copy-done.36), channel_id=1, source_target_pairs={{0,4},{4,0},{1,5},{5,1},{2,6},{6,2},{3,7},{7,3},{8,12},{12,8},{9,1... | collective-permute-start | bytes 6488072 | tf_op jit(solution)/shard_map/ppermute | solution.py:45
  415.9 15.3 %collective-permute-start.71 = (bf16[288,384]{1,0:T(8,128)(2,1)S(1)}, bf16[288,384]{1,0:T(8,128)(2,1)S(1)}, u32[]{:S(2)}, u32[]{:S(2)}) collective-permute-start(bf16[288,384]{1,0:T(8,128)(2,1)S(1)} %pad_maximum_fusion.12), channel_id=1, source_target_pairs={{0,1},{1,0},{2,3},{3,2},{4,5},{5,4},{6,7},{7,6},{8,9},{9,8},{10,11... | collective-permute-start | bytes 663560 | tf_op jit(solution)/shard_map/ppermute | solution.py:50
  424.2 17.7 %collective-permute-start.72 = (bf16[288,384]{1,0:T(8,128)(2,1)S(1)}, bf16[288,384]{1,0:T(8,128)(2,1)S(1)}, u32[]{:S(2)}, u32[]{:S(2)}) collective-permute-start(bf16[288,384]{1,0:T(8,128)(2,1)S(1)} %pad_maximum_fusion.13), channel_id=1, source_target_pairs={{0,2},{1,3},{2,0},{3,1},{4,6},{5,7},{6,4},{7,5},{8,10},{9,11},{10,... | collective-permute-start | bytes 663560 | tf_op jit(solution)/shard_map/ppermute | solution.py:50
  424.3 17.6 %collective-permute-start.73 = (bf16[288,384]{1,0:T(8,128)(2,1)S(1)}, bf16[288,384]{1,0:T(8,128)(2,1)S(1)}, u32[]{:S(2)}, u32[]{:S(2)}) collective-permute-start(bf16[288,384]{1,0:T(8,128)(2,1)S(1)} %pad_maximum_fusion.14), channel_id=1, source_target_pairs={{0,3},{1,2},{2,1},{3,0},{4,7},{5,6},{6,5},{7,4},{8,11},{9,10},{10,... | collective-permute-start | bytes 663560 | tf_op jit(solution)/shard_map/ppermute | solution.py:50
  427.4 51.2 %collective-permute-start.81 = (bf16[2,4,96,768]{3,2,1,0:T(8,128)(2,1)S(1)}, bf16[2,4,96,768]{3,2,1,0:T(8,128)(2,1)S(1)}, u32[]{:S(2)}, u32[]{:S(2)}) collective-permute-start(bf16[2,4,96,768]{3,2,1,0:T(8,128)(2,1)S(1)} %get-tuple-element.157), channel_id=1, source_target_pairs={{0,8},{8,0},{1,9},{9,1},{2,10},{10,2},{3,11},{11,3},{4,12},{12,4},... | collective-permute-start | bytes 3538952 | tf_op jit(solution)/shard_map/ppermute | solution.py:45
  428.6 48.3 %collective-permute-start.75 = (bf16[2,4,176,384]{3,2,1,0:T(8,128)(2,1)S(1)}, bf16[2,4,176,384]{3,2,1,0:T(8,128)(2,1)S(1)}, u32[]{:S(2)}, u32[]{:S(2)}) collective-permute-start(bf16[2,4,176,384]{3,2,1,0:T(8,128)(2,1)S(1)} %get-tuple-element.159), channel_id=1, source_target_pairs={{0,8},{8,0},{1,9},{9,1},{2,10},{10,2},{3,11},{11,3},{4,12},{12,4},... | collective-permute-start | bytes 3244040 | tf_op jit(solution)/shard_map/ppermute | solution.py:45
  431.1 49.1 %collective-permute-start.84 = (bf16[2,4,96,768]{3,2,1,0:T(8,128)(2,1)S(1)}, bf16[2,4,96,768]{3,2,1,0:T(8,128)(2,1)S(1)}, u32[]{:S(2)}, u32[]{:S(2)}) collective-permute-start(bf16[2,4,96,768]{3,2,1,0:T(8,128)(2,1)S(1)} %get-tuple-element.155), channel_id=1, source_target_pairs={{0,16},{16,0},{1,17},{17,1},{2,18},{18,2},{3,19},{19,3},{4,20},{20... | collective-permute-start | bytes 3538952 | tf_op jit(solution)/shard_map/ppermute | solution.py:45
  477.0 15.3 %collective-permute-start.76 = (bf16[1,4,176,384]{3,2,1,0:T(8,128)(2,1)S(1)}, bf16[1,4,176,384]{3,2,1,0:T(8,128)(2,1)S(1)}, u32[]{:S(2)}, u32[]{:S(2)}) collective-permute-start(bf16[1,4,176,384]{3,2,1,0:T(8,128)(2,1)S(1)} %add_convert_fusion.16), channel_id=1, source_target_pairs={{0,16},{16,0},{1,17},{17,1},{2,18},{18,2},{3,19},{19,3},{4,20},{20... | collective-permute-start | bytes 1622024 | tf_op jit(solution)/shard_map/ppermute | solution.py:45
  479.7 26.2 %collective-permute-start.82 = (bf16[1,4,96,768]{3,2,1,0:T(8,128)(2,1)}, bf16[1,4,96,768]{3,2,1,0:T(8,128)(2,1)}, u32[]{:S(2)}, u32[]{:S(2)}) collective-permute-start(bf16[1,4,96,768]{3,2,1,0:T(8,128)(2,1)} %add_convert_fusion.8), channel_id=1, source_target_pairs={{0,16},{16,0},{1,17},{17,1},{2,18},{18,2},{3,19},{19,3},{4,20},{20... | collective-permute-start | bytes 1769480 | tf_op jit(solution)/shard_map/ppermute | solution.py:45
  481.3 26.2 %collective-permute-start.85 = (bf16[1,4,96,768]{3,2,1,0:T(8,128)(2,1)}, bf16[1,4,96,768]{3,2,1,0:T(8,128)(2,1)}, u32[]{:S(2)}, u32[]{:S(2)}) collective-permute-start(bf16[1,4,96,768]{3,2,1,0:T(8,128)(2,1)} %add_convert_fusion.6), channel_id=1, source_target_pairs={{0,8},{8,0},{1,9},{9,1},{2,10},{10,2},{3,11},{11,3},{4,12},{12,4},... | collective-permute-start | bytes 1769480 | tf_op jit(solution)/shard_map/ppermute | solution.py:45
  508.9 15.5 %collective-permute-start.86 = (bf16[192,768]{1,0:T(8,128)(2,1)S(1)}, bf16[192,768]{1,0:T(8,128)(2,1)S(1)}, u32[]{:S(2)}, u32[]{:S(2)}) collective-permute-start(bf16[192,768]{1,0:T(8,128)(2,1)S(1)} %pad_maximum_fusion.9), channel_id=1, source_target_pairs={{0,2},{1,3},{2,0},{3,1},{4,6},{5,7},{6,4},{7,5},{8,10},{9,11},{10,... | collective-permute-start | bytes 884744 | tf_op jit(solution)/shard_map/ppermute | solution.py:50
  (165 other events, 3990.6 us)

commit v3 on v2

v3 whole, which is shorter than its diff:
```python
import functools
import math

import jax
import jax.numpy as jnp
from jax import lax
from jax.experimental import pallas as pl
from jax.experimental.layout import Layout, with_layout_constraint
from jax.experimental.pallas import tpu as pltpu
from jax.sharding import Mesh
from jax.sharding import PartitionSpec as P

D = 768
HEAD_DIM = 64
F = 3072
E = 1408
NQ = 32
STEP_COUNT = 10

NORM_EPS = 1e-06
BETA_ONE = 0.9
BETA_TWO = 0.999
ADAM_EPS = 1e-08
WEIGHT_DECAY = 0.01
MASKED = -1000000000.0

BF = jnp.bfloat16
F32 = jnp.float32
SCALE = HEAD_DIM ** (-0.5)
MIB = 1 << 20


def dot(a, b):
    return lax.dot_general(a, b, (((1,), (0,)), ((), ())), preferred_element_type=F32)


def dot_t(a, b):
    return lax.dot_general(a, b, (((1,), (1,)), ((), ())), preferred_element_type=F32)


def t_dot(a, b):
    return lax.dot_general(a, b, (((0,), (0,)), ((), ())), preferred_element_type=F32)


def swap(values, axis):
    return lax.ppermute(values, axis, [(0, 1), (1, 0)])


def mp_swap(values, distance):
    count = lax.axis_size("mp")
    return lax.ppermute(values, "mp", [(i, i ^ distance) for i in range(count)])


class Plan:
    def __init__(self, bits, mp, items, dp):
        self.bits = bits
        self.mp = mp
        self.dp = dp
        self.items = items
        self.rows = items * 2 * NQ
        self.half = items * NQ
        self.width = D // mp
        self.forth = tuple(f"b{k}" for k in range(bits))
        self.back = self.forth[::-1]
        self.distances = [1 << k for k in range(mp.bit_length() - 1)]

    def bit(self, axis):
        return 1 if axis == "core" else 2 << (self.bits - 1 - int(axis[1:]))

    def masks(self, order):
        found = [0]
        for axis in order + ("core",):
            found = found + [m | self.bit(axis) for m in found]
        return found

    def dp_index(self):
        place = lax.axis_index("core")
        for axis in self.forth:
            place = place + self.bit(axis) * lax.axis_index(axis)
        return place


class Part:
    def __init__(self, tree, low, count, place):
        self.tree, self.low, self.count, self.place = tree, low, count, place


def hold(*values):
    return lax.optimization_barrier(values)


def mp_double(values, distance):
    return jnp.concatenate([values, mp_swap(values, distance)])


def mp_direct(plan, own, sent):
    return [own] + [mp_swap(sent(j), j) for j in range(1, plan.mp)]


def two_trees(pieces, rows):
    return (
        jnp.concatenate([p[None, :rows] for p in pieces]),
        jnp.concatenate([p[None, rows:] for p in pieces]),
    )


def send_pair(plan, pair, k):
    return swap(pair[0], plan.forth[k]), swap(pair[1], plan.back[k])


def send_cores(pair):
    return tuple(swap(v, "core") for v in pair)


def join_pair(pair, got):
    return tuple(jnp.concatenate([v, g]) for v, g in zip(pair, got))


def as_quarters(pair, got, cores, got_cores):
    return tuple(zip(pair, got, cores, got_cores))


def as_trees(plan, cores):
    return {"a": (cores[0], plan.forth), "b": (cores[1], plan.back)}


def line_pairs(plan):
    return [(1, 2), (2, 1)], [(0, 1), (3, 2)], [(1, 0), (2, 3)]


def mp_middle(plan, values):
    if plan.mp != 4:
        return mp_swap(values, 2)
    return lax.ppermute(values, "mp", line_pairs(plan)[0])


def mp_outward(plan, got):
    if plan.mp != 4:
        return got
    return lax.ppermute(got, "mp", line_pairs(plan)[2])


def from_line(plan, across, far, j):
    if plan.mp != 4:
        return across[j - 2]
    me = lax.axis_index("mp")
    return jnp.where((me == 0) | (me == 3), far[j - 2], across[3 - j])


def mp_inward(plan, state):
    kept, sent = state
    if plan.mp != 4:
        return state
    got = lax.ppermute(sent, "mp", line_pairs(plan)[1])
    return kept, add_low(sent, got[::-1])


def mp_across(plan, state):
    kept, sent = state
    if plan.mp != 4:
        return mp_halve(state, 2)
    got = lax.ppermute(sent, "mp", line_pairs(plan)[0])
    return add_low(kept[:1], got[1:]), add_low(kept[1:], got[:1])


def natural_tree(plan, halves, order):
    values = jnp.concatenate(halves)
    values = values.reshape((plan.dp, values.shape[0] // plan.dp) + values.shape[1:])
    back = [0] * plan.dp
    for k, mask in enumerate(plan.masks(order)):
        back[mask] = k
    places = jnp.take(jnp.array(back), jnp.arange(plan.dp) ^ plan.dp_index())
    return jnp.take(values, places, axis=0)


def assemble(plan, trees, parts):
    found = []
    for part in parts:
        halves, order = trees[part.tree]
        natural = natural_tree(plan, halves, order)
        found.append(natural[:, :, part.low : part.low + part.count])
    whole = jnp.concatenate(found, axis=2).transpose(1, 0, 2, 3)
    return whole.reshape(whole.shape[0], -1, whole.shape[-1])


def by_distance(plan, matrices, segments, order):
    places = jnp.array(plan.masks(order)) ^ plan.dp_index()
    found = []
    for name, part in segments:
        blocks = matrices[name]
        blocks = blocks.reshape(blocks.shape[0], plan.dp, -1, blocks.shape[-1])
        blocks = jnp.take(blocks, places, axis=1).transpose(1, 0, 2, 3)
        found.append(blocks[:, :, part.place : part.place + part.count])
    whole = jnp.concatenate(found, axis=2)
    whole = whole.reshape((-1,) + whole.shape[2:])
    return whole[: whole.shape[0] // 2], whole[whole.shape[0] // 2 :]


def add_low(first, second):
    return (first.astype(F32) + second.astype(F32)).astype(BF)


def shrink_send(halves, axes):
    return tuple(swap(sent, axis) for (_, sent), axis in zip(halves, axes))


def shrink_add(halves, found):
    sums = []
    for (kept, _), got in zip(halves, found):
        half = got.shape[0] // 2
        sums.append((add_low(kept[:half], got[:half]), add_low(kept[half:], got[half:])))
    return tuple(sums)


def join_trees(halves):
    return tuple(jnp.concatenate([h[k] for h in halves], axis=1) for k in range(2))


def mp_halve(state, distance):
    kept, sent = state
    got = mp_swap(sent, distance)
    half = got.shape[0] // 2
    return add_low(kept[:half], got[:half]), add_low(kept[half:], got[half:])


def mp_scatter(plan, state):
    kept, sent = state
    pieces = [kept[0]]
    for j in range(1, plan.mp):
        values = kept if j < plan.mp // 2 else sent
        pieces.append(mp_swap(values[j % (plan.mp // 2)], j))
    return pieces


def mp_last(state):
    kept, sent = state
    return kept[0].astype(F32), mp_swap(sent[0], 1).astype(F32)


def norm_parts(values):
    center = values - jnp.mean(values, axis=-1, keepdims=True)
    spread = jnp.mean(center * center, axis=-1, keepdims=True)
    inverse = lax.rsqrt(spread + NORM_EPS)
    return center * inverse, inverse


def norm_backward(grad_out, normed, inverse, gain):
    scaled = grad_out * gain
    inner = (
        scaled
        - jnp.mean(scaled, axis=-1, keepdims=True)
        - normed * jnp.mean(scaled * normed, axis=-1, keepdims=True)
    )
    return inner * inverse


def column_sum(values):
    return jnp.sum(values.astype(F32), axis=0, keepdims=True)


def halves_of(values, items):
    split = values.reshape(items, 2 * NQ, values.shape[-1])
    parts = split[:, :NQ], split[:, NQ:]
    return tuple(p.reshape(items * NQ, values.shape[-1]) for p in parts)


def join_halves(query, caption, items):
    width = query.shape[-1]
    parts = [v.reshape(items, NQ, width) for v in (query, caption)]
    return jnp.concatenate(parts, axis=1).reshape(items * 2 * NQ, width)


def wide(first, second):
    return jnp.concatenate([first, second], axis=1)


def after(values, width):
    return jnp.concatenate([jnp.zeros_like(values), values], axis=1)


def before(values, width):
    return jnp.concatenate([values, jnp.zeros_like(values)], axis=1)


def head_lanes(width):
    lane = lax.broadcasted_iota(jnp.int32, (1, width), 1)
    return [lane // HEAD_DIM == h for h in range(width // HEAD_DIM)]


def only(values, lanes):
    return jnp.where(lanes, values, jnp.zeros_like(values))


def softmax(scores):
    expo = jnp.exp(scores - jnp.max(scores, axis=-1, keepdims=True))
    return expo * (1.0 / jnp.sum(expo, axis=-1, keepdims=True))


def fetch(plan, refs, parts, trees, target, sem):
    if trees is None:
        pltpu.make_async_copy(refs[0], target, sem).start()
        return
    place = plan.dp_index()
    block = sum(p.count for p in parts)
    for part in parts:
        found, order = trees[part.tree]
        for k, mask in enumerate(plan.masks(order)):
            quarter, index = divmod(k, plan.dp // len(found))
            begin = pl.multiple_of((place ^ mask) * block + part.place, 16)
            pieces = refs[found[quarter]].at[pl.ds(index * plan.mp, plan.mp)]
            pltpu.make_async_copy(
                pieces.at[:, pl.ds(part.low, part.count), :],
                target.at[:, pl.ds(begin, part.count), :],
                sem,
            ).start()


def fetch_whole(matrix, target, sem):
    pltpu.make_async_copy(matrix, target, sem).start()


def settle(target, sem):
    pltpu.make_async_copy(target, target, sem).wait()


def spread(plan, source, parts, outs, sem):
    if parts is None:
        pltpu.make_async_copy(source, outs, sem).start()
        return
    place = plan.dp_index()
    block = sum(p.count for p in parts)
    for part in parts:
        halves, order = outs[part.tree]
        for k, mask in enumerate(plan.masks(order)):
            half, index = divmod(k, plan.dp // 2)
            begin = pl.multiple_of((place ^ mask) * block + part.place, 16)
            pieces = halves[half].at[pl.ds(index * plan.mp, plan.mp)]
            pltpu.make_async_copy(
                source.at[:, pl.ds(begin, part.count), :],
                pieces.at[:, pl.ds(part.low, part.count), :],
                sem,
            ).start()


class Weights:
    def __init__(self, plan, trees, matrices):
        self.plan, self.matrices = plan, matrices
        self.direct = all(p.count % 16 == 0 for parts in matrices.values() for p in parts)
        if self.direct:
            self.trees = trees
        else:
            self.whole = {n: assemble(plan, trees, parts) for n, parts in matrices.items()}

    def operands(self, names):
        arrays, found = [], {}
        if not self.direct:
            for name in names:
                found[name] = (len(arrays), self.matrices[name], None)
                arrays.append(self.whole[name])
            return arrays, found
        seen = {}
        for name in names:
            for part in self.matrices[name]:
                if part.tree not in seen:
                    halves, order = self.trees[part.tree]
                    seen[part.tree] = (range(len(arrays), len(arrays) + len(halves)), order)
                    arrays.extend(halves)
            found[name] = (0, self.matrices[name], seen)
        return arrays, found


def gather_operands(sets):
    arrays, starts = [], {}
    for weights, names in sets:
        more, found = weights.operands(names)
        base = len(arrays)
        for name, (place, parts, trees) in found.items():
            starts[name] = functools.partial(
                lambda refs, target, sem, base, place, parts, trees, plan: fetch(
                    plan, refs[base + place :], parts, trees, target, sem
                )
                if trees is None
                else fetch(plan, refs[base:], parts, trees, target, sem),
                base=base,
                place=place,
                parts=parts,
                trees=trees,
                plan=weights.plan,
            )
        arrays.extend(more)
    return arrays, starts


class Gradients:
    def __init__(self, plan, trees, matrices, over):
        self.plan, self.trees, self.matrices, self.over = plan, trees, matrices, over
        self.direct = all(p.count % 16 == 0 for parts, _ in matrices.values() for p in parts)

    def shapes(self):
        found = []
        if self.direct:
            for _, rows, columns in self.trees.values():
                shape = (self.plan.dp // 2 * self.over, rows, columns)
                found += [jax.ShapeDtypeStruct(shape, BF)] * 2
            return found
        for parts, rows in self.matrices.values():
            columns = self.trees[parts[0].tree][2]
            found.append(jax.ShapeDtypeStruct((self.over, rows, columns), BF))
        return found

    def write(self, name, source, refs, sem):
        parts = self.matrices[name][0]
        if self.direct:
            outs = {
                tree: (refs[2 * k : 2 * k + 2], order)
                for k, (tree, (order, _, _)) in enumerate(self.trees.items())
            }
            spread(self.plan, source, parts, outs, sem)
        else:
            spread(self.plan, source, None, refs[list(self.matrices).index(name)], sem)

    def halves(self, arrays):
        if self.direct:
            return {t: tuple(arrays[2 * k : 2 * k + 2]) for k, t in enumerate(self.trees)}
        named = dict(zip(self.matrices, arrays))
        found = {}
        for tree, (order, _, _) in self.trees.items():
            segments = [
                (name, part)
                for name, (parts, _) in self.matrices.items()
                for part in parts
                if part.tree == tree
            ]
            segments.sort(key=lambda s: s[1].low)
            found[tree] = by_distance(self.plan, named, segments, order)
        return found


def call(kernel, ins, places, outs, out_places, scratch, limit):
    return pl.pallas_call(
        kernel,
        out_shape=outs,
        in_specs=[pl.BlockSpec(memory_space=p) for p in places],
        out_specs=[pl.BlockSpec(memory_space=p) for p in out_places],
        scratch_shapes=scratch,
        compiler_params=pltpu.CompilerParams(vmem_limit_bytes=limit * MIB),
        cost_estimate=pl.CostEstimate(flops=1000, bytes_accessed=1000, transcendentals=0),
    )(*ins)


ANY, HBM, VMEM, SMEM = pl.ANY, pltpu.HBM, pltpu.VMEM, pltpu.SMEM
DMA = pltpu.SemaphoreType.DMA


def self_mask(plan, lengths, me):
    count = plan.rows
    row = lax.broadcasted_iota(jnp.int32, (count, count), 0)
    col = lax.broadcasted_iota(jnp.int32, (count, count), 1)
    span = 2 * NQ
    limit = jnp.zeros((count, count), jnp.int32)
    for i in range(plan.items):
        limit = jnp.where(col // span == i, lengths[me * plan.items + i], limit)
    inside = col % span
    valid = (row // span == col // span) & ((inside < NQ) | (inside - NQ < limit))
    return jnp.where(valid, 0.0, MASKED).astype(F32)


def load_tokens(plan, hidden, target, sem):
    me = lax.axis_index("mp")
    return pltpu.make_async_copy(hidden.at[pl.ds(me * plan.items, plan.items)], target, sem)


def distance_shapes(plan):
    shape = (plan.half, plan.width)
    return [
        jax.ShapeDtypeStruct(shape, BF),
        jax.ShapeDtypeStruct(shape, BF),
        jax.ShapeDtypeStruct((plan.mp - 2,) + shape, BF),
    ]


def put_distance(refs, j, values):
    if j < 2:
        refs[j][...] = values
    else:
        refs[2][j - 2] = values


def get_distance(refs, j, span=slice(None)):
    return refs[j][span, :] if j < 2 else refs[2][j - 2, span, :]


def self_forward(plan, lengths, hidden, vec, heads, sets):
    arrays, starts = gather_operands(sets)
    count = len(arrays)
    mp, rows, half, width, items = plan.mp, plan.rows, plan.half, plan.width, plan.items

    def kernel(lengths, hidden, vec, heads, *rest):
        refs = rest[:count]
        qk_out, v_out, context_out, z_out = rest[count : count + 4]
        cross = rest[count + 4 : count + 7]
        wholes = rest[count + 7 : count + 10]
        tokens, w_qk, w_vc, w_oo, sems = rest[count + 10 :]
        me = lax.axis_index("mp")
        loaded = load_tokens(plan, hidden, tokens, sems.at[0])
        loaded.start()
        starts["qk"](refs, w_qk, sems.at[1])
        starts["vc"](refs, w_vc, sems.at[2])
        starts["oo"](refs, w_oo, sems.at[3])
        mask = self_mask(plan, lengths, me)
        lanes = head_lanes(width)
        loaded.wait()
        x = tokens[...].reshape(rows, D)
        total = x.astype(F32) + vec[0:1, :]
        kept = []
        for k, matrix in enumerate((w_qk, w_vc, w_oo)):
            settle(matrix, sems.at[1 + k])
            kept.append(pltpu.make_async_copy(matrix, wholes[k], sems.at[4 + k]))
            kept[-1].start()
        for j in range(mp):
            both = (dot(x, w_qk[j]) + heads[j, 0:1, :]).astype(BF)
            qk_out[j] = both
            q, k = both[:, :width], both[:, width:]
            v = (dot(x, w_vc[j]) + heads[j, 1:2, :]).astype(BF)[:, :width]
            v_out[j] = v
            context = jnp.zeros((rows, width), F32)
            for lane in lanes:
                probs = softmax(dot_t(only(q, lane), k) * SCALE + mask)
                context = context + only(dot(probs.astype(BF), v), lane)
            context = context.astype(BF)
            context_out[j] = context
            total = total + dot_t(before(context, width), w_oo[j])
        z_out[...] = total
        normed, _ = norm_parts(total)
        u = halves_of(normed * vec[4:5, :] + vec[5:6, :], items)[0].astype(BF)
        for j in range(mp):
            maps = (dot(u, w_vc[j]) + heads[j, 1:2, :]).astype(BF)
            put_distance(cross, j, maps[:, width:])
        for copy in kept:
            copy.wait()

    whole = jax.ShapeDtypeStruct((mp, D, 2 * width), BF)
    outs = [
        jax.ShapeDtypeStruct((mp, rows, 2 * width), BF),
        jax.ShapeDtypeStruct((mp, rows, width), BF),
        jax.ShapeDtypeStruct((mp, rows, width), BF),
        jax.ShapeDtypeStruct((rows, D), F32),
        *distance_shapes(plan),
        whole,
        whole,
        whole,
    ]
    found = call(
        kernel,
        (lengths, hidden, vec, heads, *arrays),
        [SMEM, HBM, VMEM, VMEM] + [ANY] * count,
        outs,
        [VMEM] * 7 + [HBM] * 3,
        [
            pltpu.VMEM((items, 2 * NQ, D), BF),
            *[pltpu.VMEM((mp, D, 2 * width), BF)] * 3,
            DMA((7,)),
        ],
        28,
    )
    return (*found[:4], found[4:7], found[7:])


def load_images(images, held, sems):
    count = images.shape[0]
    cut = -(-count // 4)
    found = []
    for k in range(0, count, cut):
        span = pl.ds(k, min(cut, count - k))
        found.append(pltpu.make_async_copy(images.at[span], held.at[span], sems.at[k // cut]))
        found[-1].start()
    return found, cut


def image_maps(plan, images, bias, maps):
    items, keys, features = images.shape
    width = plan.width
    padded = -(-keys // 128) * 128

    def kernel(images, bias, maps, out, held, w_kv, sems, w_sem):
        weights = pltpu.make_async_copy(maps, w_kv, w_sem.at[0])
        weights.start()
        loaded, cut = load_images(images, held, sems)
        weights.wait()
        for n, copy in enumerate(loaded):
            copy.wait()

            def step(i, carry):
                both = (dot(held[i], w_kv[...]) + bias[2:3, :]).astype(BF)
                out[i, 0:keys, :] = both
                out[i, keys:padded, :] = jnp.zeros((padded - keys, 2 * width), BF)
                return carry

            lax.fori_loop(n * cut, min(items, (n + 1) * cut), step, 0)

    return call(
        kernel,
        (images, bias, maps),
        [ANY, VMEM, ANY],
        [jax.ShapeDtypeStruct((items, padded, 2 * width), BF)],
        [VMEM],
        [
            pltpu.VMEM((items, keys, features), BF),
            pltpu.VMEM((features, 2 * width), BF),
            DMA((4,)),
            DMA((1,)),
        ],
        28,
    )[0]


def key_mask(plan, keys, padded):
    lane = lax.broadcasted_iota(jnp.int32, (1, padded), 1)
    return jnp.where(lane < keys, 0.0, MASKED).astype(F32)


def spread_heads(values, lanes):
    return jnp.concatenate([only(values, lane) for lane in lanes], axis=0)


def gather_heads(values, lanes):
    total = None
    for h, lane in enumerate(lanes):
        part = only(values[h * NQ : (h + 1) * NQ], lane)
        total = part if total is None else total + part
    return total


def cross_attend(plan, keys, queries, kv):
    mp, half, width, items = plan.mp, plan.half, plan.width, plan.items
    padded = kv.shape[1]

    def kernel(*refs):
        queries, kv, contexts = refs[:3], refs[3], refs[4:]
        me = lax.axis_index("mp")
        lanes = head_lanes(width)
        mask = key_mask(plan, keys, padded)
        for j in range(mp):
            rows = []
            for i in range(items):
                q = spread_heads(get_distance(queries, j, slice(i * NQ, (i + 1) * NQ)), lanes)
                both = kv[(me ^ j) * items + i]
                probs = softmax(dot_t(q, both[:, :width]) * SCALE + mask)
                rows.append(gather_heads(dot(probs.astype(BF), both[:, width:]), lanes))
            put_distance(contexts, j, jnp.concatenate(rows, axis=0).astype(BF))

    return call(
        kernel,
        (*queries, kv),
        [VMEM] * 4,
        distance_shapes(plan),
        [VMEM] * 3,
        [],
        24,
    )


def cross_output(plan, vec, z_first, contexts, whole_oo):
    mp, half, width, items = plan.mp, plan.half, plan.width, plan.items

    def kernel(vec, z_first, *rest):
        contexts, whole_oo = rest[:3], rest[3]
        z_out, kept, given, w_oo, sems = rest[4:]
        me = lax.axis_index("mp")
        fetch_whole(whole_oo, w_oo, sems.at[0])
        normed, _ = norm_parts(z_first[...])
        query, caption = halves_of(normed * vec[4:5, :] + vec[5:6, :], items)
        total = query + vec[1:2, :]
        settle(w_oo, sems.at[0])
        for j in range(mp):
            total = total + dot_t(after(get_distance(contexts, j), width), w_oo[j])
        z_out[...] = total
        normed, _ = norm_parts(total)
        second = normed * vec[6:7, :] + vec[7:8, :]
        low = (me & 1) == 0
        kept[...] = jnp.where(low, second, caption)
        given[...] = jnp.where(low, caption, second).astype(BF)

    return call(
        kernel,
        (vec, z_first, *contexts, whole_oo),
        [VMEM] * 5 + [HBM],
        [
            jax.ShapeDtypeStruct((half, D), F32),
            jax.ShapeDtypeStruct((half, D), F32),
            jax.ShapeDtypeStruct((half, D), BF),
        ],
        [VMEM] * 3,
        [pltpu.VMEM((mp, D, 2 * width), BF), DMA((1,))],
        16,
    )


def feed_forward(plan, vec, heads, kept, got, cotangent, sets, gradients):
    arrays, starts = gather_operands(sets)
    count = len(arrays)
    mp, half, items = plan.mp, plan.half, plan.items
    hidden_width = F // mp
    shapes = gradients.shapes()

    def kernel(vec, heads, kept, got, cotangent, *rest):
        refs, rest = rest[:count], rest[count:]
        layer, kept_back, given_back, sums, bias_sums = rest[:5]
        grad_out = rest[5 : 5 + len(shapes)]
        top, w_up, w_down, slope, act, up_grad, down_grad, w_sems, sems = rest[5 + len(shapes) :]
        me = lax.axis_index("mp")
        group = me & 1
        starts["up"](refs, w_up, w_sems.at[0])
        starts["down"](refs, w_down, w_sems.at[1])
        tops = []
        for s in range(2):
            first = (me ^ s) * items
            tops.append(
                pltpu.make_async_copy(
                    cotangent.at[
                        pl.ds(first, items), pl.ds(pl.multiple_of(group * NQ, NQ), NQ), :
                    ],
                    top.at[s],
                    sems.at[2 + s],
                )
            )
            tops[-1].start()
        x = jnp.concatenate([kept[...], got[...].astype(F32)], axis=0)
        low = x.astype(BF)
        low_t = low.T
        total = x + vec[pl.ds(2 + group, 1), :]
        settle(w_up, w_sems.at[0])
        for z in range(mp):
            bias = wide(
                heads[z, pl.ds(3 + 2 * group, 1), :], heads[z, pl.ds(4 + 2 * group, 1), :]
            )
            pre = dot(low, w_up[z]) + bias
            cdf = 0.5 + 0.5 * lax.erf(pre * (0.5**0.5))
            value = (pre * cdf).astype(BF)
            act[z] = value
            slope[z] = cdf + pre * jnp.exp(-0.5 * pre * pre) * (1.0 / math.sqrt(2.0 * math.pi))
            if z == 0:
                settle(w_down, w_sems.at[1])
            total = total + dot_t(value, w_down[z])
        normed, inverse = norm_parts(total)
        gain = vec[pl.ds(8 + 2 * group, 1), :]
        third = normed * gain + vec[pl.ds(9 + 2 * group, 1), :]
        layer[...] = third.astype(BF).reshape(2, items, NQ, D)
        for t in tops:
            t.wait()
        grad = top[...].reshape(2 * half, D).astype(F32)
        back = norm_backward(grad, normed, inverse, gain)
        branch = back.astype(BF)
        sums[0:1, :] = column_sum(branch)
        sums[1:2, :] = column_sum(grad * normed)
        sums[2:3, :] = column_sum(grad)
        branch_t = branch.T
        for z in range(mp):
            down_grad[z] = dot(branch_t, act[z]).astype(BF)
        gradients.write("down", down_grad, grad_out, sems.at[0])
        for z in range(mp):
            pull = (dot(branch, w_down[z]) * slope[z]).astype(BF)
            bias_sums[pl.ds(me ^ z, 1), :] = column_sum(pull)
            up_grad[z] = dot(low_t, pull).astype(BF)
            back = back + dot_t(pull, w_up[z])
        gradients.write("up", up_grad, grad_out, sems.at[1])
        kept_back[...] = back[:half]
        given_back[...] = back[half:].astype(BF)
        settle(down_grad, sems.at[0])
        settle(up_grad, sems.at[1])

    outs = [
        jax.ShapeDtypeStruct((2, items, NQ, D), BF),
        jax.ShapeDtypeStruct((half, D), F32),
        jax.ShapeDtypeStruct((half, D), BF),
        jax.ShapeDtypeStruct((3, D), F32),
        jax.ShapeDtypeStruct((mp, hidden_width), F32),
        *shapes,
    ]
    found = call(
        kernel,
        (vec, heads, kept, got, cotangent, *arrays),
        [VMEM] * 4 + [HBM] + [ANY] * count,
        outs,
        [VMEM] * 5 + [HBM] * len(shapes),
        [
            pltpu.VMEM((2, items, NQ, D), BF),
            pltpu.VMEM((mp, D, hidden_width), BF),
            pltpu.VMEM((mp, D, hidden_width), BF),
            pltpu.VMEM((mp, 2 * half, hidden_width), F32),
            pltpu.VMEM((mp, 2 * half, hidden_width), BF),
            pltpu.VMEM((mp, D, hidden_width), BF),
            pltpu.VMEM((mp, D, hidden_width), BF),
            DMA((2,)),
            DMA((4,)),
        ],
        48,
    )
    return (*found[:5], gradients.halves(found[5:]))


def cross_output_backward(plan, vec, z_second, kept, got, whole_oo):
    mp, half, width = plan.mp, plan.half, plan.width

    def kernel(vec, z_second, kept, got, whole_oo, *rest):
        back_out, branch_out, caption, sums = rest[:4]
        context_back = rest[4:7]
        w_oo, sems = rest[7:]
        low = (lax.axis_index("mp") & 1) == 0
        fetch_whole(whole_oo, w_oo, sems.at[0])
        other = got[...].astype(F32)
        grad = jnp.where(low, kept[...], other)
        caption[...] = jnp.where(low, other, kept[...])
        normed, inverse = norm_parts(z_second[...])
        back = norm_backward(grad, normed, inverse, vec[6:7, :])
        branch = back.astype(BF)
        back_out[...] = back
        branch_out[...] = branch
        sums[0:1, :] = column_sum(branch)
        sums[1:2, :] = column_sum(grad * normed)
        sums[2:3, :] = column_sum(grad)
        settle(w_oo, sems.at[0])
        for j in range(mp):
            put_distance(context_back, j, dot(branch, w_oo[j]).astype(BF)[:, width:])

    found = call(
        kernel,
        (vec, z_second, kept, got, whole_oo),
        [VMEM] * 4 + [HBM],
        [
            jax.ShapeDtypeStruct((half, D), F32),
            jax.ShapeDtypeStruct((half, D), BF),
            jax.ShapeDtypeStruct((half, D), F32),
            jax.ShapeDtypeStruct((3, D), F32),
            *distance_shapes(plan),
        ],
        [VMEM] * 7,
        [pltpu.VMEM((mp, D, 2 * width), BF), DMA((1,))],
        16,
    )
    return (*found[:4], found[4:])


def cross_attend_backward(plan, keys, queries, context_back, kv):
    mp, half, width, items = plan.mp, plan.half, plan.width, plan.items
    padded = kv.shape[1]

    def kernel(*refs):
        queries, context_back, kv = refs[:3], refs[3:6], refs[6]
        kv_back, value_sum, query_back = refs[7], refs[8], refs[9:]
        me = lax.axis_index("mp")
        lanes = head_lanes(width)
        mask = key_mask(plan, keys, padded)
        total = jnp.zeros((1, width), F32)
        for j in range(mp):
            rows = []
            for i in range(items):
                span = slice(i * NQ, (i + 1) * NQ)
                item = (me ^ j) * items + i
                q = spread_heads(get_distance(queries, j, span), lanes)
                g = spread_heads(get_distance(context_back, j, span), lanes)
                both = kv[item]
                k, v = both[:, :width], both[:, width:]
                probs = softmax(dot_t(q, k) * SCALE + mask)
                pulled = dot_t(g, v)
                scored = probs * (pulled - jnp.sum(probs * pulled, axis=-1, keepdims=True))
                scored = scored.astype(BF)
                value_back = t_dot(probs.astype(BF), g).astype(BF)
                key_back = (t_dot(scored, q) * SCALE).astype(BF)
                kv_back[item] = wide(key_back, value_back)
                total = total + column_sum(value_back)
                rows.append(gather_heads(dot(scored, k), lanes) * SCALE)
            put_distance(query_back, j, jnp.concatenate(rows, axis=0).astype(BF))
        value_sum[...] = total

    found = call(
        kernel,
        (*queries, *context_back, kv),
        [VMEM] * 7,
        [
            jax.ShapeDtypeStruct((mp * items, padded, 2 * width), BF),
            jax.ShapeDtypeStruct((1, width), F32),
            *distance_shapes(plan),
        ],
        [VMEM] * 5,
        [],
        28,
    )
    return found[0], found[1], found[2:]


def put_columns(target, row, found, me, width):
    for z in range(len(found)):
        total = jnp.zeros((1, width), F32)
        for j, values in enumerate(found):
            total = jnp.where((me ^ j) == z, values, total)
        target[row : row + 1, z * width : (z + 1) * width] = total


def cross_input_backward(plan, vec, z_first, back, caption, query_back, whole_vc):
    mp, rows, half, width, items = plan.mp, plan.rows, plan.half, plan.width, plan.items

    def kernel(vec, z_first, back, caption, *rest):
        query_back, whole_vc = rest[:3], rest[3]
        first_back, sums, w_vc, sems = rest[4:]
        me = lax.axis_index("mp")
        fetch_whole(whole_vc, w_vc, sems.at[0])
        total = back[...]
        found = [column_sum(get_distance(query_back, j)) for j in range(mp)]
        put_columns(sums, 3, found, me, width)
        settle(w_vc, sems.at[0])
        for j in range(mp):
            total = total + dot_t(after(get_distance(query_back, j), width), w_vc[j])
        first_grad = join_halves(total, caption[...], items)
        normed, inverse = norm_parts(z_first[...])
        first = norm_backward(first_grad, normed, inverse, vec[4:5, :])
        first_back[...] = first
        sums[0:1, :] = column_sum(first_grad * normed)
        sums[1:2, :] = column_sum(first_grad)
        sums[2:3, :] = column_sum(first.astype(BF))

    return call(
        kernel,
        (vec, z_first, back, caption, *query_back, whole_vc),
        [VMEM] * 7 + [HBM],
        [
            jax.ShapeDtypeStruct((rows, D), F32),
            jax.ShapeDtypeStruct((4, D), F32),
        ],
        [VMEM] * 2,
        [pltpu.VMEM((mp, D, 2 * width), BF), DMA((1,))],
        20,
    )


def image_gradient(plan, images, kv_back):
    items, keys, features = images.shape
    width = plan.width
    even = keys // 128 * 128

    def kernel(images, kv_back, out, held, turned, sems):
        loaded, cut = load_images(images, held, sems)
        total = jnp.zeros((2 * width, features), F32)
        for i in range(items):
            turned[i] = kv_back[i, 0:even, :].T
        for i in range(items):
            if i % cut == 0:
                loaded[i // cut].wait()
            total = total + dot(turned[i], held[i, 0:even, :])
        if keys > even:
            left = jnp.concatenate([held[i, even:keys, :] for i in range(items)], axis=0)
            right = jnp.concatenate([kv_back[i, even:keys, :] for i in range(items)], axis=0)
            total = total + t_dot(right, left)
        out[...] = total.astype(BF).T

    return call(
        kernel,
        (images, kv_back),
        [HBM, VMEM],
        [jax.ShapeDtypeStruct((features, 2 * width), BF)],
        [VMEM],
        [
            pltpu.VMEM((items, keys, features), BF),
            pltpu.VMEM((items, 2 * width, even), BF),
            DMA((4,)),
        ],
        40,
    )[0]


def self_backward(plan, lengths, saved, found_sums, wholes):
    mp, rows, width = plan.mp, plan.rows, plan.width
    count = len(saved) + len(found_sums)
    vectors_rows = 16 + 2 * mp * (F // mp // D)

    def kernel(lengths, *rest):
        vec, first_back, qk_all, v_all = rest[:4]
        first_sums, cross_sums, third_sums, bias_sums, value_sum = rest[4:count]
        wholes, rest = rest[count : count + 3], rest[count + 3 :]
        token_back, vectors, maps_back, value_maps = rest[:4]
        w_qk, w_vc, w_oo, w_sems = rest[4:]
        me = lax.axis_index("mp")
        for k, target in enumerate((w_qk, w_vc, w_oo)):
            fetch_whole(wholes[k], target, w_sems.at[k])
        mask = self_mask(plan, lengths, me)
        lanes = head_lanes(width)
        group = me & 1
        vectors[...] = jnp.zeros((vectors_rows, D), F32)
        vectors[0:1, :] = first_sums[2:3, :]
        vectors[1:2, :] = cross_sums[0:1, :]
        vectors[pl.ds(2 + group, 1), :] = third_sums[0:1, :]
        vectors[4:6, :] = first_sums[0:2, :]
        vectors[6:8, :] = cross_sums[1:3, :]
        vectors[pl.ds(8 + 2 * group, 1), :] = third_sums[1:2, :]
        vectors[pl.ds(9 + 2 * group, 1), :] = third_sums[2:3, :]
        vectors[14:15, :] = first_sums[3:4, :]
        for z in range(mp):
            span = slice(z * width, (z + 1) * width)
            vectors[15:16, span] = jnp.where(me == z, value_sum[...], 0.0)
        for g in range(2):
            vectors[16 + g * mp : 16 + (g + 1) * mp, :] = jnp.where(
                group == g, bias_sums[...], 0.0
            )
        total = first_back[...]
        self_branch = total.astype(BF)
        settle(w_oo, w_sems.at[2])
        query_sums, value_sums = [], []
        for z in range(mp):
            pulled = dot(self_branch, w_oo[z]).astype(BF)[:, :width]
            q, k, v = qk_all[z][:, :width], qk_all[z][:, width:], v_all[z]
            query_grad = jnp.zeros((rows, width), F32)
            key_grad = jnp.zeros((rows, width), F32)
            value_grad = jnp.zeros((rows, width), F32)
            for lane in lanes:
                q_h, g_h = only(q, lane), only(pulled, lane)
                probs = softmax(dot_t(q_h, k) * SCALE + mask)
                wanted = dot_t(g_h, v)
                scored = probs * (wanted - jnp.sum(probs * wanted, axis=-1, keepdims=True))
                scored = scored.astype(BF)
                value_grad = value_grad + t_dot(probs.astype(BF), g_h)
                query_grad = query_grad + only(dot(scored, k), lane)
                key_grad = key_grad + t_dot(scored, q_h)
            query_grad = (query_grad * SCALE).astype(BF)
            value_grad = value_grad.astype(BF)
            query_sums.append(column_sum(query_grad))
            value_sums.append(column_sum(value_grad))
            both = wide(query_grad, (key_grad * SCALE).astype(BF))
            maps_back[z] = both
            value_maps[z] = value_grad
            if z == 0:
                settle(w_qk, w_sems.at[0])
                settle(w_vc, w_sems.at[1])
            total = total + dot_t(both, w_qk[z]) + dot_t(before(value_grad, width), w_vc[z])
        put_columns(vectors, 12, query_sums, me, width)
        put_columns(vectors, 13, value_sums, me, width)
        token_back[...] = total.astype(BF)

    return call(
        kernel,
        (lengths, *saved, *found_sums, *wholes),
        [SMEM] + [VMEM] * count + [HBM] * 3,
        [
            jax.ShapeDtypeStruct((rows, D), BF),
            jax.ShapeDtypeStruct((vectors_rows, D), F32),
            jax.ShapeDtypeStruct((mp, rows, 2 * width), BF),
            jax.ShapeDtypeStruct((mp, rows, width), BF),
        ],
        [VMEM] * 4,
        [pltpu.VMEM((mp, D, 2 * width), BF)] * 3 + [DMA((3,))],
        32,
    )


def output_gradient(plan, first_back, branch, context_all, contexts, gradients):
    mp, width = plan.mp, plan.width
    shapes = gradients.shapes()

    def kernel(first_back, branch, context_all, *rest):
        cross_context, grad_out = rest[:3], rest[3 : 3 + len(shapes)]
        g_oo, sems = rest[3 + len(shapes) :]
        branches_t = jnp.concatenate([first_back[...].astype(BF), branch[...]], axis=0).T
        for z in range(mp):
            contexts = jnp.concatenate(
                [
                    before(context_all[z], width),
                    after(get_distance(cross_context, z), width),
                ],
                axis=0,
            )
            g_oo[z] = dot(branches_t, contexts).astype(BF)
        gradients.write("oo", g_oo, grad_out, sems.at[0])
        settle(g_oo, sems.at[0])

    found = call(
        kernel,
        (first_back, branch, context_all, *contexts),
        [VMEM] * 6,
        shapes,
        [HBM] * len(shapes),
        [pltpu.VMEM((mp, D, 2 * width), BF), DMA((1,))],
        24,
    )
    return gradients.halves(found)


def self_gradient(plan, hidden, saved, gradients):
    mp, rows, half, width, items = plan.mp, plan.rows, plan.half, plan.width, plan.items
    shapes = gradients.shapes()
    count = len(saved)

    def kernel(hidden, *rest):
        vec, z_first, maps_back, value_maps = rest[:4]
        query_back = rest[4:7]
        grad_out = rest[count : count + len(shapes)]
        tokens, g_qk, g_vc, sems = rest[count + len(shapes) :]
        loaded = load_tokens(plan, hidden, tokens, sems.at[0])
        loaded.start()
        normed, _ = norm_parts(z_first[...])
        u = halves_of(normed * vec[4:5, :] + vec[5:6, :], items)[0].astype(BF)
        loaded.wait()
        inputs_t = jnp.concatenate([tokens[...].reshape(rows, D), u], axis=0).T
        for z in range(mp):
            g_qk[z] = dot(inputs_t[:, :rows], maps_back[z]).astype(BF)
        gradients.write("qk", g_qk, grad_out, sems.at[1])
        for z in range(mp):
            maps = jnp.concatenate(
                [before(value_maps[z], width), after(get_distance(query_back, z), width)], axis=0
            )
            g_vc[z] = dot(inputs_t, maps).astype(BF)
        gradients.write("vc", g_vc, grad_out, sems.at[2])
        settle(g_qk, sems.at[1])
        settle(g_vc, sems.at[2])

    found = call(
        kernel,
        (hidden, *saved),
        [HBM] + [VMEM] * count,
        shapes,
        [HBM] * len(shapes),
        [pltpu.VMEM((items, 2 * NQ, D), BF)]
        + [pltpu.VMEM((mp, D, 2 * width), BF)] * 2
        + [DMA((3,))],
        24,
    )
    return gradients.halves(found)


def place_layer(plan, two, across, far):
    mp, items = plan.mp, plan.items

    def kernel(two, across, far, out):
        me = lax.axis_index("mp")
        for j in range(mp):
            source = me ^ j
            values = two[j] if j < 2 else from_line(plan, across, far, j)
            for s in range(2):
                out[
                    pl.ds((source ^ s) * items, items),
                    pl.ds(pl.multiple_of((source & 1) * NQ, NQ), NQ),
                    :,
                ] = values[s]

    return call(
        kernel,
        (two, across, far),
        [VMEM] * 3,
        [jax.ShapeDtypeStruct((mp * items, 2 * NQ, D), BF)],
        [VMEM],
        [],
        16,
    )[0]


def place_gradient(plan, two, across, far):
    mp, items = plan.mp, plan.items

    def kernel(two, across, far, out):
        me = lax.axis_index("mp")
        for j in range(mp):
            values = two[j] if j < 2 else from_line(plan, across, far, j)
            values = values.astype(F32).reshape(items, 2 * NQ, D)
            out[pl.ds((me ^ j) * items, items)] = values

    return call(
        kernel,
        (two, across, far),
        [VMEM] * 3,
        [jax.ShapeDtypeStruct((mp * items, 2 * NQ, D), F32)],
        [VMEM],
        [],
        24,
    )[0]


def adam_update(weight, first, second, grad, rate):
    first_new = BETA_ONE * first + (1.0 - BETA_ONE) * grad
    second_new = BETA_TWO * second + (1.0 - BETA_TWO) * grad * grad
    first_hat = first_new / (1.0 - BETA_ONE**STEP_COUNT)
    second_hat = second_new / (1.0 - BETA_TWO**STEP_COUNT)
    weight_new = weight - rate * (
        first_hat / (jnp.sqrt(second_hat) + ADAM_EPS) + WEIGHT_DECAY * weight
    )
    return (first_new, second_new, weight_new)


def local(
    bits,
    hidden,
    images,
    caption_len,
    cotangent,
    attn_in,
    attn_in_first,
    attn_in_second,
    attn_out,
    attn_out_first,
    attn_out_second,
    cross_key_value_maps,
    cross_kv_first,
    cross_kv_second,
    ffn_up,
    ffn_up_first,
    ffn_up_second,
    ffn_down,
    ffn_down_first,
    ffn_down_second,
    vec_rep,
    vec_rep_first,
    vec_rep_second,
    query_value_bias_rows,
    vec_head_first,
    vec_head_second,
    bias_up,
    bias_up_first,
    bias_up_second,
):
    mp = lax.axis_size("mp")
    me = lax.axis_index("mp")
    plan = Plan(bits, mp, hidden.shape[0] // mp, 2 ** (bits + 1))
    forth, back = plan.forth, plan.back
    low = (me & 1) == 0
    keys = images.shape[1]
    attn_rows, kv_rows, ffn_rows = attn_in.shape[1], cross_key_value_maps.shape[1], ffn_up.shape[1]
    oo_first = attn_rows // 32 * 16 or attn_rows // 2
    oo_second = attn_rows - oo_first

    def side(values):
        return jnp.concatenate([values[0], values[1]], axis=1)

    none = jnp.zeros_like(query_value_bias_rows[0])
    bias_rows = query_value_bias_rows
    packed = jnp.concatenate(
        [
            jnp.concatenate([bias_rows[0], none])[None],
            jnp.concatenate([bias_rows[1], bias_rows[2]])[None],
            jnp.concatenate([none, bias_rows[3]])[None],
            bias_up.reshape(-1, 2 * plan.width),
            jnp.zeros((1, 2 * plan.width), F32),
        ]
    )

    def three(values):
        found = []
        for _ in range(3):
            part = lax.reduce_precision(values, 8, 7)
            found.append(part.astype(BF))
            values = values - part
        return jnp.concatenate(found)

    low_in = attn_in.astype(BF)
    low_oo = side(attn_out.astype(BF).transpose(0, 2, 1))
    low_kv = side(cross_key_value_maps.astype(BF))
    attn_first, attn_second = attn_rows + oo_first, attn_rows + oo_second
    first_shard = jnp.concatenate(
        [
            side(low_in[:2]),
            low_oo[:oo_first],
            side(low_in[2:]),
            low_oo[oo_first:],
            three(packed),
        ]
    )
    group = me & 1
    low_ffn = jnp.concatenate([ffn_up.astype(BF), ffn_down.astype(BF).transpose(0, 2, 1)], axis=1)
    third_own = lax.dynamic_index_in_dim(low_ffn, group, 0, keepdims=False)
    third_other = lax.dynamic_index_in_dim(low_ffn, 1 - group, 0, keepdims=False)
    early, last = range(plan.bits - 1), range(plan.bits - 1, plan.bits)

    wide_columns, hidden_columns = 2 * plan.width, F // mp
    attn_parts = {
        "qk": [Part("a", 0, attn_rows, 0)],
        "vc": [Part("b", 0, attn_rows, 0)],
        "oo": [Part("a", attn_rows, oo_first, 0), Part("b", attn_rows, oo_second, oo_first)],
    }
    attn_gradients = Gradients(
        plan,
        {"a": (forth, attn_rows, wide_columns), "b": (back, attn_rows, wide_columns)},
        {"qk": (attn_parts["qk"], D), "vc": (attn_parts["vc"], D)},
        mp,
    )
    out_gradients = Gradients(
        plan,
        {"a": (forth, oo_first, wide_columns), "b": (back, oo_second, wide_columns)},
        {"oo": ([Part("a", 0, oo_first, 0), Part("b", 0, oo_second, oo_first)], D)},
        mp,
    )
    ffn_gradients = Gradients(
        plan,
        {"a": (forth, ffn_rows, hidden_columns), "b": (back, ffn_rows, hidden_columns)},
        {"up": ([Part("a", 0, ffn_rows, 0)], D), "down": ([Part("b", 0, ffn_rows, 0)], D)},
        mp,
    )

    first = mp_direct(plan, first_shard, lambda j: first_shard)
    maps = lax.all_gather(low_kv, forth + ("core",), axis=0, tiled=True)
    images = with_layout_constraint(images, Layout(major_to_minor=(0, 1, 2)))
    first, images, third_own, third_other = hold(first, images, third_own, third_other)
    packed_rows = packed.shape[0]
    heads = jnp.stack([p[attn_first + attn_second :].astype(F32) for p in first])
    heads = heads.reshape(mp, 3, packed_rows, heads.shape[-1]).sum(axis=1)
    first = (
        jnp.stack([p[:attn_first] for p in first]),
        jnp.stack([p[attn_first : attn_first + attn_second] for p in first]),
    )
    near = mp_swap(third_other, 1)
    for k in early:
        got = send_pair(plan, first, k)
        if k < plan.bits - 2:
            first = join_pair(first, got)
    got, near = hold(got, near)
    first = join_pair(first, got)
    third = jnp.stack([third_own, near])
    got = send_pair(plan, first, plan.bits - 1)
    first_cores = send_cores(first)
    for distance in plan.distances[1:]:
        if distance > 2:
            third = mp_double(third, distance)
    far_up = mp_swap(third[:, :ffn_rows], 2)
    kv_all = image_maps(plan, images, packed, maps)
    got, first_cores, kv_all, far_up = hold(got, first_cores, kv_all, far_up)
    got_cores = send_cores(got)
    far_down = mp_swap(third[:, ffn_rows:], 2)

    def before_last(values, order):
        for axis in order[:-2]:
            values = jnp.concatenate([values, swap(values, axis)])
        return values, swap(values, order[-2])

    up, up_got = before_last(jnp.concatenate([third[:, :ffn_rows], far_up]), forth)
    (got_cores,) = hold(got_cores)
    attn_set = Weights(
        plan, as_trees(plan, as_quarters(first, got, first_cores, got_cores)), attn_parts
    )
    qk_all, v_all, context_all, z_first, cross, wholes = self_forward(
        plan, caption_len, hidden, vec_rep, heads, [(attn_set, ["qk", "vc", "oo"])]
    )
    whole_qk, whole_vc, whole_oo = wholes

    def exchange(values):
        own, near, others = values
        got = mp_swap(others, 2)
        for distance in plan.distances[2:]:
            got = mp_swap(got, distance)
        passed = mp_swap(jnp.stack([near, got[1]]), 1)
        return own, passed[0], jnp.stack([got[0], passed[1]])

    far_down, cross, up_got = hold(far_down, cross, up_got)
    up = jnp.concatenate([up, up_got])
    down, down_got = before_last(jnp.concatenate([third[:, ffn_rows:], far_down]), back)
    queries = exchange(cross)
    (queries,) = hold(queries)
    contexts = cross_attend(plan, keys, queries, kv_all)
    contexts, down_got = hold(contexts, down_got)
    down = jnp.concatenate([down, down_got])
    half = up.shape[0] // 2
    up_last, down_last = swap(up[:half], forth[-1]), swap(down[:half], back[-1])
    contexts = exchange(contexts)
    contexts, down, up, up_last, down_last = hold(contexts, down, up, up_last, down_last)
    up_last = jnp.concatenate([up_last, swap(up[half:], forth[-1])])
    down_last = jnp.concatenate([down_last, swap(down[half:], back[-1])])
    up_core, down_core = send_cores((up, down))
    z_second, kept, given = cross_output(plan, vec_rep, z_first, contexts, whole_oo)
    kept, given = hold(kept, given)
    ffn_got = mp_swap(given, 1)
    up_last, down_last, up_core, down_core, ffn_got, kept = hold(
        up_last, down_last, up_core, down_core, ffn_got, kept
    )
    up_last_core, down_last_core = send_cores((up_last, down_last))
    up_last_core, down_last_core, ffn_got, kept = hold(
        up_last_core, down_last_core, ffn_got, kept
    )
    ffn_set = Weights(
        plan,
        as_trees(
            plan,
            (
                (up, up_last, up_core, up_last_core),
                (down, down_last, down_core, down_last_core),
            ),
        ),
        {"up": [Part("a", 0, ffn_rows, 0)], "down": [Part("b", 0, ffn_rows, 0)]},
    )
    layer, kept_back, given_back, third_sums, bias_sums, ffn_halves = feed_forward(
        plan,
        vec_rep,
        heads,
        kept,
        ffn_got,
        cotangent,
        [(ffn_set, ["up", "down"])],
        ffn_gradients,
    )
    cores = ("core", "core")
    ffn_state = ffn_halves["a"], ffn_halves["b"]
    got_back = mp_swap(given_back, 1)
    got = shrink_send(ffn_state, cores)
    got_back, got, kept_back, layer = hold(got_back, got, kept_back, layer)
    layer_near = mp_swap(layer, 1)
    ffn_state = shrink_add(ffn_state, got)
    for k in range(plan.bits - 1, 1, -1):
        ffn_state = shrink_add(ffn_state, shrink_send(ffn_state, (forth[k], back[k])))
    got = shrink_send(ffn_state, (forth[1], back[1]))
    cross_back, branch, caption_back, cross_sums, context_back = cross_output_backward(
        plan, vec_rep, z_second, kept_back, got_back, whole_oo
    )
    (context_back,) = hold(context_back)
    context_back = exchange(context_back)
    context_back, layer_near = hold(context_back, layer_near)
    layer_two = jnp.stack([layer, layer_near])
    layer_across = mp_middle(plan, layer_two)
    kv_back, value_sum, query_back = cross_attend_backward(
        plan, keys, queries, context_back, kv_all
    )
    query_back, got = hold(query_back, got)
    ffn_state = shrink_add(ffn_state, got)
    got = shrink_send(ffn_state, (forth[0], back[0]))
    query_back = exchange(query_back)
    query_back, got, layer_across = hold(query_back, got, layer_across)
    ffn_state = join_trees(shrink_add(ffn_state, got))
    for distance in plan.distances[:1:-1]:
        ffn_state = mp_halve(ffn_state, distance)
    first_back, first_sums = cross_input_backward(
        plan, vec_rep, z_first, cross_back, caption_back, query_back, whole_vc
    )
    out_halves = output_gradient(plan, first_back, branch, context_all, contexts, out_gradients)
    ffn_state, first_back, out_halves = hold(ffn_state, first_back, out_halves)
    middle = ffn_rows if ffn_state[1].shape[0] == 2 else 0
    ffn_got_up = mp_swap(ffn_state[1][:, :middle], 2)
    layer_far = mp_outward(plan, layer_across)
    out_state = out_halves["a"], out_halves["b"]
    out_got = shrink_send(out_state, cores)
    token_back, vectors, maps_back, value_maps = self_backward(
        plan,
        caption_len,
        (vec_rep, first_back, qk_all, v_all),
        (first_sums, cross_sums, third_sums, bias_sums, value_sum),
        wholes,
    )
    token_back, maps_back, vectors, ffn_got_up, out_got = hold(
        token_back, maps_back, vectors, ffn_got_up, out_got
    )
    near = mp_swap(token_back, 1)
    ffn_got_down = mp_swap(ffn_state[1][:, middle:], 2)
    out_state = shrink_add(out_state, out_got)
    for k in range(plan.bits - 1, 1, -1):
        out_state = shrink_add(out_state, shrink_send(out_state, (forth[k], back[k])))
    out_got = shrink_send(out_state, (forth[1], back[1]))
    attn_halves = self_gradient(
        plan,
        hidden,
        (vec_rep, z_first, maps_back, value_maps, *query_back),
        attn_gradients,
    )
    near, layer_far, vectors, attn_halves, kv_back, ffn_got_down, out_got = hold(
        near, layer_far, vectors, attn_halves, kv_back, ffn_got_down, out_got
    )
    attn_state = attn_halves["a"], attn_halves["b"]
    attn_got = shrink_send(attn_state, cores)
    vector_got = swap(vectors, "core")
    tokens_two = jnp.stack([token_back, near])
    across = mp_middle(plan, tokens_two)
    out_state = shrink_add(out_state, out_got)
    out_got = shrink_send(out_state, (forth[0], back[0]))
    attn_got, vector_got, kv_back, out_got = hold(attn_got, vector_got, kv_back, out_got)
    vectors = vectors + vector_got
    attn_state = shrink_add(attn_state, attn_got)
    for k in range(plan.bits - 1, 1, -1):
        attn_state = shrink_add(attn_state, shrink_send(attn_state, (forth[k], back[k])))
    attn_got = shrink_send(attn_state, (forth[1], back[1]))
    out_state = join_trees(shrink_add(out_state, out_got))
    for distance in plan.distances[:1:-1]:
        out_state = mp_halve(out_state, distance)
    out_got = mp_swap(out_state[1], 2)
    vector_got = mp_swap(vectors, 1)
    kv_grad = image_gradient(plan, images, kv_back)
    attn_got, kv_grad, vector_got, across, out_got = hold(
        attn_got, kv_grad, vector_got, across, out_got
    )
    kv_total = lax.psum_scatter(
        kv_grad, forth + ("core",), scatter_dimension=0, tiled=True
    ).astype(F32)
    vectors = vectors + vector_got
    vector_got = mp_swap(vectors, 2)
    tokens_far = mp_outward(plan, across)
    attn_state = shrink_add(attn_state, attn_got)
    attn_got = shrink_send(attn_state, (forth[0], back[0]))
    layer_out = place_layer(plan, layer_two, layer_across, layer_far)

    def add_halves(state, got):
        half = got.shape[0] // 2
        return add_low(state[0][:half], got[:half]), add_low(state[0][half:], got[half:])

    ffn_got = jnp.concatenate([ffn_got_up, ffn_got_down], axis=1)
    mine, theirs = mp_last(add_halves(ffn_state, ffn_got))
    out_state = add_halves(out_state, out_got)
    attn_got, vector_got, mine, theirs, tokens_far = hold(
        attn_got, vector_got, mine, theirs, tokens_far
    )
    vectors = vectors + vector_got
    for distance in plan.distances[2:]:
        vectors = vectors + mp_swap(vectors, distance)
    for axis in forth[1:]:
        vectors = vectors + swap(vectors, axis)
    attn_pieces = mp_scatter(plan, join_trees(shrink_add(attn_state, attn_got)))
    vector_got = swap(vectors, forth[0])
    out_total = sum(mp_last(out_state))
    attn_pieces, vector_got = hold(attn_pieces, vector_got)
    vectors = vectors + vector_got
    attn_total = sum(p.astype(F32) for p in attn_pieces)
    grad_hidden = place_gradient(plan, tokens_two, across, tokens_far)
    reduced_rep = vectors[:12]
    head_width = query_value_bias_rows.shape[1]
    bias_width = bias_up.shape[1]
    reduced_head = lax.dynamic_slice_in_dim(vectors[12:16], me * head_width, head_width, 1)
    reduced_bias = lax.dynamic_slice_in_dim(
        vectors[16:].reshape(2, -1), me * bias_width, bias_width, 1
    )

    def split_columns(values):
        width = values.shape[1] // 2
        return jnp.stack([values[:, :width], values[:, width:]])

    both = jnp.stack([jnp.where(low, mine, theirs), jnp.where(low, theirs, mine)])
    reduced_up, reduced_down = both[:, :ffn_rows], both[:, ffn_rows:].transpose(0, 2, 1)
    reduced_out = split_columns(out_total).transpose(0, 2, 1)
    reduced_in = jnp.concatenate(
        [split_columns(attn_total[:attn_rows]), split_columns(attn_total[attn_rows:])]
    )
    reduced_kv = split_columns(kv_total)
    rates = (
        2.0 / math.sqrt(D),
        2.0 / math.sqrt(max(D // 8, 1)),
        2.0 / math.sqrt(E),
        2.0 / math.sqrt(D),
        2.0 / math.sqrt(F),
        0.3,
        0.3,
        0.3,
    )
    weights = (
        attn_in,
        attn_out,
        cross_key_value_maps,
        ffn_up,
        ffn_down,
        vec_rep,
        query_value_bias_rows,
        bias_up,
    )
    firsts = (
        attn_in_first,
        attn_out_first,
        cross_kv_first,
        ffn_up_first,
        ffn_down_first,
        vec_rep_first,
        vec_head_first,
        bias_up_first,
    )
    seconds = (
        attn_in_second,
        attn_out_second,
        cross_kv_second,
        ffn_up_second,
        ffn_down_second,
        vec_rep_second,
        vec_head_second,
        bias_up_second,
    )
    reduced = (
        reduced_in,
        reduced_out,
        reduced_kv,
        reduced_up,
        reduced_down,
        reduced_rep,
        reduced_head,
        reduced_bias,
    )
    results = []
    for weight, first, second, grad, rate in zip(weights, firsts, seconds, reduced, rates):
        results.extend(adam_update(weight, first, second, grad, rate))
    return (layer_out, grad_hidden, *results)


def solution(mesh):
    dp, mp = mesh.devices.shape
    bits = (dp // 2).bit_length() - 1
    names = tuple(f"b{k}" for k in range(bits)) + ("core",)
    fine = Mesh(mesh.devices.reshape((2,) * (bits + 1) + (mp,)), names + ("mp",))
    split = P(names)
    inward = P(None, names, "mp")
    outward = P(None, "mp", names)
    head = P(None, "mp")
    stored = (inward,) * 3 + (outward,) * 3 + (inward,) * 6 + (outward,) * 3 + (P(),) * 3 + (head,) * 6
    return jax.shard_map(
        functools.partial(local, bits),
        mesh=fine,
        in_specs=(split,) * 4 + stored,
        out_specs=(split,) * 2 + stored,
        check_vma=False,
    )
```

time: 539 us -> 379 us (0.70)
  waiting for transfers between devices: 222 us -> 133 us
  Pallas kernels: 132 us -> 83.4 us
  starting transfers between devices: 106 us -> 70.8 us
  between operations: 3.18 us -> 16.1 us
  local copies, waits for them, and re-layouts: 43.3 us -> 37.4 us
    ppermute x63 -> x39, waiting for transfers between devices: 121 us -> 21.6 us  [swap(): return lax.ppermute(values, axis, [(0, 1), (1, 0)])]
    pallas_call x9 -> x14, Pallas kernels: 132 us -> 83.4 us  [call(): pl.pallas_call(kernel, out_shape=outs, in_specs=[pl.BlockSpec(memory_spac...]
    ppermute x31 -> x28, starting transfers between devices: 62.2 us -> 36.4 us  [mp_swap(): return lax.ppermute(values, 'mp', [(i, i ^ distance) for i in range(count)])]
    ppermute x63 -> x39, starting transfers between devices: 43.4 us -> 29.7 us  [swap(): return lax.ppermute(values, axis, [(0, 1), (1, 0)])]
    ppermute x0 -> x4, waiting for transfers between devices: none -> 7.5 us  [the longest x2 7.49 us: mp_outward(): return lax.ppermute(got, 'mp', line_pairs(plan)[2])]
    convert_element_type x13 -> x22, other arithmetic: 9.82 us -> 16.3 us  [the longest x18 13.5 us: add_low(): return (first.astype(F32) + second.astype(F32)).astype(BF)]
    ppermute x31 -> x28, waiting for transfers between devices: 100 us -> 104 us  [mp_swap(): return lax.ppermute(values, 'mp', [(i, i ^ distance) for i in range(count)])]
    unnamed x277 -> x158, local copies, waits for them, and re-layouts: 38 us -> 35 us
  transfers between devices with their start and end apart: 94 -> 73, of which waited for: 31 -> 29; matrix products, arithmetic and copies ran while one was open for 7% -> 12% of each run, Pallas kernels for 21% -> 17%
where the time goes in v3:
time: 379 us; the launch traced here: 374 us
  waiting for transfers between devices  133 us (35%)
  Pallas kernels  83.4 us (22%)
  starting transfers between devices  70.8 us (19%)
  local copies, waits for them, and re-layouts  37.4 us (10%)
  other arithmetic  33.4 us (9%)
  between operations  16.1 us (4%)
    ppermute x28, waiting for transfers between devices, mp_swap(): return lax.ppermute(values, 'mp', [(i, i ^ distance) for i in range(count)])  104 us
    pallas_call x14, Pallas kernels, call(): pl.pallas_call(kernel, out_shape=outs, in_specs=[pl.BlockSpec(memory_spac...  83.4 us
    ppermute x28, starting transfers between devices, mp_swap(): return lax.ppermute(values, 'mp', [(i, i ^ distance) for i in range(count)])  36.4 us
    unnamed x158, local copies, waits for them, and re-layouts  35 us
    ppermute x39, starting transfers between devices, swap(): return lax.ppermute(values, axis, [(0, 1), (1, 0)])  29.7 us
    ppermute x39, waiting for transfers between devices, swap(): return lax.ppermute(values, axis, [(0, 1), (1, 0)])  21.6 us
    convert_element_type x18, other arithmetic, add_low(): return (first.astype(F32) + second.astype(F32)).astype(BF)  13.5 us
    sub x8, other arithmetic, adam_update(): weight - rate * (first_hat / (jnp.sqrt(second_hat) + ADAM_EPS) + WEIGHT_D...  8.2 us
  transfers between devices with their start and end apart: 73, of which 29 were waited for; matrix products, arithmetic and copies ran while one was open for 12% of the time, Pallas kernels for 17%

profile of v3, /device:TPU:0, one launch (start us, length us, event | category | flops | bytes accessed | tf_op | source)
XLA Modules:
  0.0 374.0 jit_solution(5322879799550129253)
XLA Ops:
  10.8 3.1 collective-permute-start
  13.9 2.6 collective-permute-start.1
  17.4 11.4 %copy.55.images = bf16[16,257,1408]{2,1,0:T(8,128)(2,1)} copy(bf16[16,257,1408]{2,0,1:T(8,128)(2,1)} %param.29) | data formatting | bytes 23158784 | tf_op args[1]
  29.0 4.8 %collective-permute-done.1 = bf16[312,384]{1,0:T(8,128)(2,1)S(1)} collective-permute-done((bf16[312,384]{1,0:T(8,128)(2,1)S(1)}, bf16[312,384]{1,0:T(8,128)(2,1)S(1)}, u32[]{:S(2)}, u32[]{:S(2)}) %collective-permute-start.1) | collective-permute-done | bytes 239648 | tf_op jit(solution)/shard_map/ppermute | solution.py:51
  34.0 1.6 collective-permute-start.3
  35.7 1.6 collective-permute-start.4
  37.3 4.3 %collective-permute-start.5 = (bf16[192,768]{1,0:T(8,128)(2,1)S(1)}, bf16[192,768]{1,0:T(8,128)(2,1)S(1)}, u32[]{:S(2)}, u32[]{:S(2)}) collective-permute-start(bf16[192,768]{1,0:T(8,128)(2,1)S(1)} %get-tuple-element.201), channel_id=1, source_target_pairs={{0,1},{1,0},{2,3},{3,2},{4,5},{5,4},{6,7},{7,6},{8,9},{9,8},{10,11... | collective-permute-start | bytes 884744 | tf_op jit(solution)/shard_map/ppermute | solution.py:51
  41.7 5.1 %collective-permute-done.5 = bf16[192,768]{1,0:T(8,128)(2,1)S(1)} collective-permute-done((bf16[192,768]{1,0:T(8,128)(2,1)S(1)}, bf16[192,768]{1,0:T(8,128)(2,1)S(1)}, u32[]{:S(2)}, u32[]{:S(2)}) %collective-permute-start.5) | collective-permute-done | bytes 294944 | tf_op jit(solution)/shard_map/ppermute | solution.py:51
  47.9 1.6 collective-permute-start.7
  50.8 5.1 %collective-permute-start.11 = (bf16[2,96,768]{2,1,0:T(8,128)(2,1)S(1)}, bf16[2,96,768]{2,1,0:T(8,128)(2,1)S(1)}, u32[]{:S(2)}, u32[]{:S(2)}) collective-permute-start(bf16[2,96,768]{2,1,0:T(8,128)(2,1)S(1)} %get-tuple-element.455), channel_id=1, source_target_pairs={{0,2},{1,3},{2,0},{3,1},{4,6},{5,7},{6,4},{7,5},{8,10},{9,11},{10,... | collective-permute-start | bytes 884744 | tf_op jit(solution)/shard_map/ppermute | solution.py:51
  55.9 4.4 %copy-done = bf16[16,257,1408]{2,1,0:T(8,128)(2,1)S(1)} copy-done((bf16[16,257,1408]{2,1,0:T(8,128)(2,1)S(1)}, bf16[16,257,1408]{2,1,0:T(8,128)(2,1)}, u32[]{:S(2)}) %copy-start) | copy-done | bytes 11579416
  61.5 11.1 %shard_map.467.refs_3_.refs_6_ = bf16[16,384,384]{2,1,0:T(8,128)(2,1)S(1)} custom-call(bf16[16,257,1408]{2,1,0:T(8,128)(2,1)S(1)} %copy-done, f32[8,384]{1,0:T(8,128)S(1)} %concatenate.90.bias, bf16[1408,384]{1,0:T(8,128)(2,1)S(1)} %copy-done.10), custom_call_target="tpu_custom_call" | custom-call | flops 1000 | bytes 1000 | tf_op jit(solution)/shard_map/pallas_call | solution.py:440
  73.4 1.5 collective-permute-start.14
  74.9 1.6 collective-permute-start.6
  78.1 10.6 %shard_map.468 = (bf16[4,256,384]{2,1,0:T(8,128)(2,1)S(1)}, bf16[4,256,192]{2,1,0:T(8,128)(2,1)S(1)}, bf16[4,256,192]{2,1,0:T(8,128)(2,1)S(1)}, f32[256,768]{1,0...) custom-call(s32[16]{0:T(128)S(1)} %copy-done.29, ...), custom_call_target="tpu_custom_call" | custom-call | flops 1000 | bytes 1000 | tf_op jit(solution)/shard_map/pallas_call | solution.py:440
  92.0 6.6 %collective-permute-done.15 = bf16[2,128,192]{2,1,0:T(8,128)(2,1)S(1)} collective-permute-done((bf16[2,128,192]{2,1,0:T(8,128)(2,1)S(1)}, bf16[2,128,192]{2,1,0:T(8,128)(2,1)S(1)}, u32[]{:S(2)}, u32[]{:S(2)}) %collective-permute-start.15) | collective-permute-done | bytes 98336 | tf_op jit(solution)/shard_map/ppermute | solution.py:51
  100.7 3.4 collective-permute-done.16
  104.2 6.1 %shard_map.469 = (bf16[128,192]{1,0:T(8,128)(2,1)S(1)}, bf16[128,192]{1,0:T(8,128)(2,1)S(1)}, bf16[2,128,192]{2,1,0:T(8,128)(2,1)S(1)}) custom-call(bf16[128,192]{1,0:T(8,128)(2,1)S(1)} %get-tuple-element.219.refs_0_, bf16[128,192]{1,0:T(8,128)(2,1)S(1)} %get-tuple-element.220.refs_1_, bf16[2,128,192]{2,1,0:T(8,128)(2,1)S(1)} %pad_maximum_fusion.21.refs_2_, ...), custom_call_target="tpu_custom_call" | custom-call | flops 1000 | bytes 1000 | tf_op jit(solution)/shard_map/pallas_call | solution.py:440
  110.6 8.1 %collective-permute-done.18 = bf16[2,128,192]{2,1,0:T(8,128)(2,1)S(1)} collective-permute-done((bf16[2,128,192]{2,1,0:T(8,128)(2,1)S(1)}, bf16[2,128,192]{2,1,0:T(8,128)(2,1)S(1)}, u32[]{:S(2)}, u32[]{:S(2)}) %collective-permute-start.18) | collective-permute-done | bytes 98336 | tf_op jit(solution)/shard_map/ppermute | solution.py:51
  119.0 5.2 %collective-permute-done.19 = bf16[2,128,192]{2,1,0:T(8,128)(2,1)S(1)} collective-permute-done((bf16[2,128,192]{2,1,0:T(8,128)(2,1)S(1)}, bf16[2,128,192]{2,1,0:T(8,128)(2,1)S(1)}, u32[]{:S(2)}, u32[]{:S(2)}) %collective-permute-start.19) | collective-permute-done | bytes 98336 | tf_op jit(solution)/shard_map/ppermute | solution.py:51
  127.0 1.5 shard_map.470
  128.9 11.4 %collective-permute-done.22 = bf16[4,96,768]{2,1,0:T(8,128)(2,1)S(1)} collective-permute-done((bf16[4,96,768]{2,1,0:T(8,128)(2,1)S(1)}, bf16[4,96,768]{2,1,0:T(8,128)(2,1)S(1)}, u32[]{:S(2)}, u32[]{:S(2)}) %collective-permute-start.22) | collective-permute-done | bytes 589856 | tf_op jit(solution)/shard_map/ppermute | solution.py:46
  141.5 3.2 collective-permute-done.27.rest_3_
  145.7 14.4 %shard_map.471 = (bf16[2,4,32,768]{3,2,1,0:T(8,128)(2,1)S(1)}, f32[128,768]{1,0:T(8,128)S(1)}, bf16[128,768]{1,0:T(8,128)(2,1)S(1)}, f32[3,768]{1,0:T(4,128)S(1)...) custom-call(f32[12,768]{1,0:T(8,128)S(1)} %copy-done.5, ...), custom_call_target="tpu_custom_call" | custom-call | flops 1000 | bytes 1000 | tf_op jit(solution)/shard_map/pallas_call | solution.py:440
  161.0 6.7 %collective-permute-done.29.got = bf16[128,768]{1,0:T(8,128)(2,1)S(1)} collective-permute-done((bf16[128,768]{1,0:T(8,128)(2,1)S(1)}, bf16[128,768]{1,0:T(8,128)(2,1)S(1)}, u32[]{:S(2)}, u32[]{:S(2)}) %collective-permute-start.29) | collective-permute-done | bytes 196640 | tf_op jit(solution)/shard_map/ppermute | solution.py:51
  168.3 2.5 add_convert_fusion.1
  170.8 1.5 collective-permute-start.35
  174.8 8.4 %collective-permute-done.32 = bf16[2,128,192]{2,1,0:T(8,128)(2,1)S(1)} collective-permute-done((bf16[2,128,192]{2,1,0:T(8,128)(2,1)S(1)}, bf16[2,128,192]{2,1,0:T(8,128)(2,1)S(1)}, u32[]{:S(2)}, u32[]{:S(2)}) %collective-permute-start.32) | collective-permute-done | bytes 98336 | tf_op jit(solution)/shard_map/ppermute | solution.py:51
  183.4 2.0 collective-permute-start.34
  185.4 4.3 %collective-permute-done.33 = bf16[2,128,192]{2,1,0:T(8,128)(2,1)S(1)} collective-permute-done((bf16[2,128,192]{2,1,0:T(8,128)(2,1)S(1)}, bf16[2,128,192]{2,1,0:T(8,128)(2,1)S(1)}, u32[]{:S(2)}, u32[]{:S(2)}) %collective-permute-start.33) | collective-permute-done | bytes 98336 | tf_op jit(solution)/shard_map/ppermute | solution.py:51
  189.8 7.4 %collective-permute-done.34 = bf16[2,4,32,768]{3,2,1,0:T(8,128)(2,1)S(1)} collective-permute-done((bf16[2,4,32,768]{3,2,1,0:T(8,128)(2,1)S(1)}, bf16[2,4,32,768]{3,2,1,0:T(8,128)(2,1)S(1)}, u32[]{:S(2)}, u32[]{:S(2)}) %collective-permute-start.34) | collective-permute-done | bytes 393248 | tf_op jit(solution)/shard_map/ppermute | solution.py:51
  198.2 10.0 %shard_map.473 = (bf16[16,384,384]{2,1,0:T(8,128)(2,1)S(1)}, f32[1,192]{1,0:T(1,128)S(1)}, bf16[128,192]{1,0:T(8,128)(2,1)S(1)}, bf16[128,192]{1,0:T(8,128)(2,1)S(1)}, bf16[2,128,192]{2,1,0:T(8,128)(2,1)S(1)}) custom-call(bf16[128,192]{1,0:T(8,128)(2,1)S(1)} %copy-done.26, bf16[128,192]{1,0:T(8,128)(2,1)S(1)} %copy-done.18, ...), custom_call_target="tpu_custom_call" | custom-call | flops 1000 | bytes 1000 | tf_op jit(solution)/shard_map/pallas_call | solution.py:440
  208.2 2.1 copy-done.3
  210.3 2.9 collective-permute-start.37
  213.5 1.6 collective-permute-start.39
  216.0 7.4 %collective-permute-done.37 = bf16[2,128,192]{2,1,0:T(8,128)(2,1)S(1)} collective-permute-done((bf16[2,128,192]{2,1,0:T(8,128)(2,1)S(1)}, bf16[2,128,192]{2,1,0:T(8,128)(2,1)S(1)}, u32[]{:S(2)}, u32[]{:S(2)}) %collective-permute-start.37) | collective-permute-done | bytes 98336 | tf_op jit(solution)/shard_map/ppermute | solution.py:51
  223.6 5.0 %collective-permute-done.38 = bf16[2,128,192]{2,1,0:T(8,128)(2,1)S(1)} collective-permute-done((bf16[2,128,192]{2,1,0:T(8,128)(2,1)S(1)}, bf16[2,128,192]{2,1,0:T(8,128)(2,1)S(1)}, u32[]{:S(2)}, u32[]{:S(2)}) %collective-permute-start.38) | collective-permute-done | bytes 98336 | tf_op jit(solution)/shard_map/ppermute | solution.py:51
  231.3 2.2 shard_map.475
  234.5 1.5 collective-permute-start.46
  236.0 2.7 collective-permute-start.47
  238.7 9.4 %shard_map.476 = (bf16[256,768]{1,0:T(8,128)(2,1)S(1)}, f32[24,768]{1,0:T(8,128)S(1)}, bf16[4,256,384]{2,1,0:T(8,128)(2,1)S(1)}, bf16[4,256,192]{2,1,0:T(8,128)(2,1)S(1)}) custom-call(s32[16]{0:T(128)S(1)} %copy-done.29, f32[12,768]{1,0:T(8,128)S(1)} %copy-done.5, f32[256,768]{1,0:T(8,128)S(1)} %get-tuple-element.302.first_back.rest_1_, ...), custom_call_target="tpu_custom_call" | custom-call | flops 1000 | bytes 1000 | tf_op jit(solution)/shard_map/pallas_call | solution.py:440
  248.2 7.4 %collective-permute-done.42 = bf16[2,96,768]{2,1,0:T(8,128)(2,1)S(1)} collective-permute-done((bf16[2,96,768]{2,1,0:T(8,128)(2,1)S(1)}, bf16[2,96,768]{2,1,0:T(8,128)(2,1)S(1)}, u32[]{:S(2)}, u32[]{:S(2)}) %collective-permute-start.42) | collective-permute-done | bytes 294944 | tf_op jit(solution)/shard_map/ppermute | solution.py:51
  255.8 1.5 collective-permute-start.48
  258.2 3.3 shard_map.477
  261.8 7.5 %collective-permute-done.46.far = bf16[2,2,4,32,768]{4,3,2,1,0:T(8,128)(2,1)S(1)} collective-permute-done((bf16[2,2,4,32,768]{4,3,2,1,0:T(8,128)(2,1)S(1)}, bf16[2,2,4,32,768]{4,3,2,1,0:T(8,128)(2,1)S(1)}, u32[]{:S(2)}, u32[]{:S(2)}) %collective-permute-start.46) | collective-permute-done | bytes 786464 | tf_op jit(solution)/shard_map/ppermute | solution.py:140
  269.3 7.3 %collective-permute-done.45 = bf16[256,768]{1,0:T(8,128)(2,1)S(1)} collective-permute-done((bf16[256,768]{1,0:T(8,128)(2,1)S(1)}, bf16[256,768]{1,0:T(8,128)(2,1)S(1)}, u32[]{:S(2)}, u32[]{:S(2)}) %collective-permute-start.45) | collective-permute-done | bytes 393248 | tf_op jit(solution)/shard_map/ppermute | solution.py:51
  289.6 1.6 collective-permute-start.59
  292.7 1.7 copy.57
  294.4 1.7 copy.56
  298.6 1.8 convert_element_type.521
  300.4 2.3 copy-done.4
  302.7 8.9 %shard_map.479 = bf16[1408,384]{1,0:T(8,128)(2,1)} custom-call(bf16[16,257,1408]{2,1,0:T(8,128)(2,1)} %copy.55.images, bf16[16,384,384]{2,1,0:T(8,128)(2,1)S(1)} %copy-done.4), custom_call_target="tpu_custom_call" | custom-call | flops 1000 | bytes 1000 | tf_op jit(solution)/shard_map/pallas_call | solution.py:440
  311.7 2.1 add_convert_fusion.13
  317.1 2.8 collective-permute-start.70
  319.9 2.0 add_convert_fusion.12
  324.0 13.8 %collective-permute-done.70 = bf16[96,384]{1,0:T(8,128)(2,1)S(1)} collective-permute-done((bf16[96,384]{1,0:T(8,128)(2,1)S(1)}, bf16[96,384]{1,0:T(8,128)(2,1)S(1)}, u32[]{:S(2)}, u32[]{:S(2)}) %collective-permute-start.70) | collective-permute-done | bytes 73760 | tf_op jit(solution)/shard_map/ppermute | solution.py:51
  339.8 1.8 copy.60
  341.5 1.7 copy.61
  346.5 2.4 collective-permute-start.66
  348.9 2.0 collective-permute-start.67
  353.3 1.5 multiply_subtract_fusion.1
  354.8 1.5 collective-permute-done.68
  357.3 1.5 multiply_subtract_fusion
  358.8 1.9 shard_map.480
  (370 shorter events, 69.7 us)
Async XLA Ops:
  7.2 48.7 %all-gather.2.cloned.1.call-start = ((), (), s32[]{:S(2)}) async-start(), calls=%async_computation.1 | async-start | bytes 1216512 | tf_op jit(solution)/shard_map/all_gather | solution.py:1295
  10.8 18.2 %collective-permute-start = (bf16[312,384]{1,0:T(8,128)(2,1)S(1)}, bf16[312,384]{1,0:T(8,128)(2,1)S(1)}, u32[]{:S(2)}, u32[]{:S(2)}) collective-permute-start(bf16[312,384]{1,0:T(8,128)(2,1)S(1)} %constant_dynamic-update-slice_fusion), channel_id=1, source_target_pairs={{0,1},{1,0},{2,3},{3,2},{4,5},{5,4},{6,7},{7,6},{8,9},{9,8},{10,11... | collective-permute-start | bytes 718856 | tf_op jit(solution)/shard_map/ppermute | solution.py:51
  13.9 19.9 %collective-permute-start.1 = (bf16[312,384]{1,0:T(8,128)(2,1)S(1)}, bf16[312,384]{1,0:T(8,128)(2,1)S(1)}, u32[]{:S(2)}, u32[]{:S(2)}) collective-permute-start(bf16[312,384]{1,0:T(8,128)(2,1)S(1)} %constant_dynamic-update-slice_fusion), channel_id=1, source_target_pairs={{0,2},{1,3},{2,0},{3,1},{4,6},{5,7},{6,4},{7,5},{8,10},{9,11},{10,... | collective-permute-start | bytes 718856 | tf_op jit(solution)/shard_map/ppermute | solution.py:51
  16.5 17.3 %collective-permute-start.2 = (bf16[312,384]{1,0:T(8,128)(2,1)S(1)}, bf16[312,384]{1,0:T(8,128)(2,1)S(1)}, u32[]{:S(2)}, u32[]{:S(2)}) collective-permute-start(bf16[312,384]{1,0:T(8,128)(2,1)S(1)} %constant_dynamic-update-slice_fusion), channel_id=1, source_target_pairs={{0,3},{1,2},{2,1},{3,0},{4,7},{5,6},{6,5},{7,4},{8,11},{9,10},{10,... | collective-permute-start | bytes 718856 | tf_op jit(solution)/shard_map/ppermute | solution.py:51
  17.3 347.0 %reduce-scatter.2.cloned.1.call-start = ((), (), s32[]{:S(2)}) async-start(), calls=%async_computation.2 | async-start | bytes 1216512 | tf_op jit(solution)/shard_map/reduce_scatter | solution.py:1479
  34.0 12.8 %collective-permute-start.3 = (bf16[4,144,384]{2,1,0:T(8,128)(2,1)S(1)}, bf16[4,144,384]{2,1,0:T(8,128)(2,1)S(1)}, u32[]{:S(2)}, u32[]{:S(2)}) collective-permute-start(bf16[4,144,384]{2,1,0:T(8,128)(2,1)S(1)} %pad_maximum_fusion.11), channel_id=1, source_target_pairs={{0,16},{16,0},{1,17},{17,1},{2,18},{18,2},{3,19},{19,3},{4,20},{20... | collective-permute-start | bytes 1327112 | tf_op jit(solution)/shard_map/ppermute | solution.py:46
  35.7 12.1 %collective-permute-start.4 = (bf16[4,144,384]{2,1,0:T(8,128)(2,1)S(1)}, bf16[4,144,384]{2,1,0:T(8,128)(2,1)S(1)}, u32[]{:S(2)}, u32[]{:S(2)}) collective-permute-start(bf16[4,144,384]{2,1,0:T(8,128)(2,1)S(1)} %pad_maximum_fusion.12), channel_id=1, source_target_pairs={{0,8},{8,0},{1,9},{9,1},{2,10},{10,2},{3,11},{11,3},{4,12},{12,4},... | collective-permute-start | bytes 1327112 | tf_op jit(solution)/shard_map/ppermute | solution.py:46
  37.3 9.6 %collective-permute-start.5 = (bf16[192,768]{1,0:T(8,128)(2,1)S(1)}, bf16[192,768]{1,0:T(8,128)(2,1)S(1)}, u32[]{:S(2)}, u32[]{:S(2)}) collective-permute-start(bf16[192,768]{1,0:T(8,128)(2,1)S(1)} %get-tuple-element.201), channel_id=1, source_target_pairs={{0,1},{1,0},{2,3},{3,2},{4,5},{5,4},{6,7},{7,6},{8,9},{9,8},{10,11... | collective-permute-start | bytes 884744 | tf_op jit(solution)/shard_map/ppermute | solution.py:51
  47.9 24.8 %collective-permute-start.7 = (bf16[8,144,384]{2,1,0:T(8,128)(2,1)S(1)}, bf16[8,144,384]{2,1,0:T(8,128)(2,1)}, u32[]{:S(2)}, u32[]{:S(2)}) collective-permute-start(bf16[8,144,384]{2,1,0:T(8,128)(2,1)S(1)} %constant_dynamic-update-slice_fusion.5.rest_0_), channel_id=1, source_target_pairs={{0,8},{8,0},{1,9},{9,1},{2,10},{10,2},{3,11},{11,3},{4,12},{12,4},... | collective-permute-start | bytes 2654216 | tf_op jit(solution)/shard_map/ppermute | solution.py:46
  49.5 23.2 %collective-permute-start.8 = (bf16[8,144,384]{2,1,0:T(8,128)(2,1)S(1)}, bf16[8,144,384]{2,1,0:T(8,128)(2,1)}, u32[]{:S(2)}, u32[]{:S(2)}) collective-permute-start(bf16[8,144,384]{2,1,0:T(8,128)(2,1)S(1)} %constant_dynamic-update-slice_fusion.10.rest_4_), channel_id=1, source_target_pairs={{0,16},{16,0},{1,17},{17,1},{2,18},{18,2},{3,19},{19,3},{4,20},{20... | collective-permute-start | bytes 2654216 | tf_op jit(solution)/shard_map/ppermute | solution.py:46
  50.2 22.5 %collective-permute-start.9 = (bf16[8,144,384]{2,1,0:T(8,128)(2,1)S(1)}, bf16[8,144,384]{2,1,0:T(8,128)(2,1)}, u32[]{:S(2)}, u32[]{:S(2)}) collective-permute-start(bf16[8,144,384]{2,1,0:T(8,128)(2,1)S(1)} %constant_dynamic-update-slice_fusion.5.rest_0_), channel_id=1, source_target_pairs={{0,4},{4,0},{1,5},{5,1},{2,6},{6,2},{3,7},{7,3},{8,12},{12,8},{9,1... | collective-permute-start | bytes 2654216 | tf_op jit(solution)/shard_map/ppermute | solution.py:46
  50.2 22.5 %collective-permute-start.10 = (bf16[8,144,384]{2,1,0:T(8,128)(2,1)S(1)}, bf16[8,144,384]{2,1,0:T(8,128)(2,1)}, u32[]{:S(2)}, u32[]{:S(2)}) collective-permute-start(bf16[8,144,384]{2,1,0:T(8,128)(2,1)S(1)} %constant_dynamic-update-slice_fusion.10.rest_4_), channel_id=1, source_target_pairs={{0,4},{4,0},{1,5},{5,1},{2,6},{6,2},{3,7},{7,3},{8,12},{12,8},{9,1... | collective-permute-start | bytes 2654216 | tf_op jit(solution)/shard_map/ppermute | solution.py:46
  50.8 21.9 %collective-permute-start.11 = (bf16[2,96,768]{2,1,0:T(8,128)(2,1)S(1)}, bf16[2,96,768]{2,1,0:T(8,128)(2,1)S(1)}, u32[]{:S(2)}, u32[]{:S(2)}) collective-permute-start(bf16[2,96,768]{2,1,0:T(8,128)(2,1)S(1)} %get-tuple-element.455), channel_id=1, source_target_pairs={{0,2},{1,3},{2,0},{3,1},{4,6},{5,7},{6,4},{7,5},{8,10},{9,11},{10,... | collective-permute-start | bytes 884744 | tf_op jit(solution)/shard_map/ppermute | solution.py:51
  73.4 17.5 %collective-permute-start.14 = (bf16[4,96,768]{2,1,0:T(8,128)(2,1)S(1)}, bf16[4,96,768]{2,1,0:T(8,128)(2,1)S(1)}, u32[]{:S(2)}, u32[]{:S(2)}) collective-permute-start(bf16[4,96,768]{2,1,0:T(8,128)(2,1)S(1)} %pad_maximum_fusion.7), channel_id=1, source_target_pairs={{0,16},{16,0},{1,17},{17,1},{2,18},{18,2},{3,19},{19,3},{4,20},{20... | collective-permute-start | bytes 1769480 | tf_op jit(solution)/shard_map/ppermute | solution.py:46
  74.9 15.9 %collective-permute-start.6 = (bf16[2,96,768]{2,1,0:T(8,128)(2,1)S(1)}, bf16[2,96,768]{2,1,0:T(8,128)(2,1)S(1)}, u32[]{:S(2)}, u32[]{:S(2)}) collective-permute-start(bf16[2,96,768]{2,1,0:T(8,128)(2,1)S(1)} %get-tuple-element.454), channel_id=1, source_target_pairs={{0,2},{1,3},{2,0},{3,1},{4,6},{5,7},{6,4},{7,5},{8,10},{9,11},{10,... | collective-permute-start | bytes 884744 | tf_op jit(solution)/shard_map/ppermute | solution.py:51
  90.8 7.8 %collective-permute-start.15 = (bf16[2,128,192]{2,1,0:T(8,128)(2,1)S(1)}, bf16[2,128,192]{2,1,0:T(8,128)(2,1)S(1)}, u32[]{:S(2)}, u32[]{:S(2)}) collective-permute-start(bf16[2,128,192]{2,1,0:T(8,128)(2,1)S(1)} %get-tuple-element.218), channel_id=1, source_target_pairs={{0,2},{1,3},{2,0},{3,1},{4,6},{5,7},{6,4},{7,5},{8,10},{9,11},{10,... | collective-permute-start | bytes 294920 | tf_op jit(solution)/shard_map/ppermute | solution.py:51
  91.4 19.0 %collective-permute-start.17 = (bf16[4,96,768]{2,1,0:T(8,128)(2,1)S(1)}, bf16[4,96,768]{2,1,0:T(8,128)(2,1)S(1)}, u32[]{:S(2)}, u32[]{:S(2)}) collective-permute-start(bf16[4,96,768]{2,1,0:T(8,128)(2,1)S(1)} %pad_maximum_fusion.8), channel_id=1, source_target_pairs={{0,8},{8,0},{1,9},{9,1},{2,10},{10,2},{3,11},{11,3},{4,12},{12,4},... | collective-permute-start | bytes 1769480 | tf_op jit(solution)/shard_map/ppermute | solution.py:46
  98.7 5.5 %collective-permute-start.16 = (bf16[2,128,192]{2,1,0:T(8,128)(2,1)S(1)}, bf16[2,128,192]{2,1,0:T(8,128)(2,1)S(1)}, u32[]{:S(2)}, u32[]{:S(2)}) collective-permute-start(bf16[2,128,192]{2,1,0:T(8,128)(2,1)S(1)} %pad_maximum_fusion.20), channel_id=1, source_target_pairs={{0,1},{1,0},{2,3},{3,2},{4,5},{5,4},{6,7},{7,6},{8,9},{9,8},{10,11... | collective-permute-start | bytes 294920 | tf_op jit(solution)/shard_map/ppermute | solution.py:51
  98.7 25.6 %collective-permute-start.20 = (bf16[4,96,768]{2,1,0:T(8,128)(2,1)S(1)}, bf16[4,96,768]{2,1,0:T(8,128)(2,1)S(1)}, u32[]{:S(2)}, u32[]{:S(2)}) collective-permute-start(bf16[4,96,768]{2,1,0:T(8,128)(2,1)S(1)} %pad_maximum_fusion.7), channel_id=1, source_target_pairs={{0,8},{8,0},{1,9},{9,1},{2,10},{10,2},{3,11},{11,3},{4,12},{12,4},... | collective-permute-start | bytes 1769480 | tf_op jit(solution)/shard_map/ppermute | solution.py:46
  99.4 25.0 %collective-permute-start.21 = (bf16[4,96,768]{2,1,0:T(8,128)(2,1)S(1)}, bf16[4,96,768]{2,1,0:T(8,128)(2,1)S(1)}, u32[]{:S(2)}, u32[]{:S(2)}) collective-permute-start(bf16[4,96,768]{2,1,0:T(8,128)(2,1)S(1)} %pad_maximum_fusion.8), channel_id=1, source_target_pairs={{0,16},{16,0},{1,17},{17,1},{2,18},{18,2},{3,19},{19,3},{4,20},{20... | collective-permute-start | bytes 1769480 | tf_op jit(solution)/shard_map/ppermute | solution.py:46
  110.4 8.3 %collective-permute-start.18 = (bf16[2,128,192]{2,1,0:T(8,128)(2,1)S(1)}, bf16[2,128,192]{2,1,0:T(8,128)(2,1)S(1)}, u32[]{:S(2)}, u32[]{:S(2)}) collective-permute-start(bf16[2,128,192]{2,1,0:T(8,128)(2,1)S(1)} %get-tuple-element.229), channel_id=1, source_target_pairs={{0,2},{1,3},{2,0},{3,1},{4,6},{5,7},{6,4},{7,5},{8,10},{9,11},{10,... | collective-permute-start | bytes 294920 | tf_op jit(solution)/shard_map/ppermute | solution.py:51
  124.3 16.5 %collective-permute-start.24 = (bf16[8,96,768]{2,1,0:T(8,128)(2,1)S(1)}, bf16[8,96,768]{2,1,0:T(8,128)(2,1)S(1)}, u32[]{:S(2)}, u32[]{:S(2)}) collective-permute-start(bf16[8,96,768]{2,1,0:T(8,128)(2,1)S(1)} %pad_maximum_fusion.1.rest_0_), channel_id=1, source_target_pairs={{0,4},{4,0},{1,5},{5,1},{2,6},{6,2},{3,7},{7,3},{8,12},{12,8},{9,1... | collective-permute-start | bytes 3538952 | tf_op jit(solution)/shard_map/ppermute | solution.py:46
  124.4 16.5 %collective-permute-start.25 = (bf16[8,96,768]{2,1,0:T(8,128)(2,1)S(1)}, bf16[8,96,768]{2,1,0:T(8,128)(2,1)S(1)}, u32[]{:S(2)}, u32[]{:S(2)}) collective-permute-start(bf16[8,96,768]{2,1,0:T(8,128)(2,1)S(1)} %pad_maximum_fusion.rest_4_), channel_id=1, source_target_pairs={{0,4},{4,0},{1,5},{5,1},{2,6},{6,2},{3,7},{7,3},{8,12},{12,8},{9,1... | collective-permute-start | bytes 3538952 | tf_op jit(solution)/shard_map/ppermute | solution.py:46
  125.0 15.4 %collective-permute-start.22 = (bf16[4,96,768]{2,1,0:T(8,128)(2,1)S(1)}, bf16[4,96,768]{2,1,0:T(8,128)(2,1)S(1)}, u32[]{:S(2)}, u32[]{:S(2)}) collective-permute-start(bf16[4,96,768]{2,1,0:T(8,128)(2,1)S(1)} %slice.485), channel_id=1, source_target_pairs={{0,8},{8,0},{1,9},{9,1},{2,10},{10,2},{3,11},{11,3},{4,12},{12,4},... | collective-permute-start | bytes 1769480 | tf_op jit(solution)/shard_map/ppermute | solution.py:46
  125.6 15.1 %collective-permute-start.23 = (bf16[4,96,768]{2,1,0:T(8,128)(2,1)S(1)}, bf16[4,96,768]{2,1,0:T(8,128)(2,1)S(1)}, u32[]{:S(2)}, u32[]{:S(2)}) collective-permute-start(bf16[4,96,768]{2,1,0:T(8,128)(2,1)S(1)} %slice.486), channel_id=1, source_target_pairs={{0,16},{16,0},{1,17},{17,1},{2,18},{18,2},{3,19},{19,3},{4,20},{20... | collective-permute-start | bytes 1769480 | tf_op jit(solution)/shard_map/ppermute | solution.py:46
  128.6 12.3 %collective-permute-start.26 = (bf16[128,768]{1,0:T(8,128)(2,1)S(1)}, bf16[128,768]{1,0:T(8,128)(2,1)S(1)}, u32[]{:S(2)}, u32[]{:S(2)}) collective-permute-start(bf16[128,768]{1,0:T(8,128)(2,1)S(1)} %get-tuple-element.243), channel_id=1, source_target_pairs={{0,1},{1,0},{2,3},{3,2},{4,5},{5,4},{6,7},{7,6},{8,9},{9,8},{10,11... | collective-permute-start | bytes 589832 | tf_op jit(solution)/shard_map/ppermute | solution.py:51
  160.1 7.5 %collective-permute-start.30 = (bf16[16,96,768]{2,1,0:T(8,128)(2,1)}, bf16[16,96,768]{2,1,0:T(8,128)(2,1)S(1)}, u32[]{:S(2)}, u32[]{:S(2)}) collective-permute-start(bf16[16,96,768]{2,1,0:T(8,128)(2,1)} %get-tuple-element.256), channel_id=1, source_target_pairs={{0,4},{4,0},{1,5},{5,1},{2,6},{6,2},{3,7},{7,3},{8,12},{12,8},{9,1... | collective-permute-start | bytes 7077896 | tf_op jit(solution)/shard_map/ppermute | solution.py:46
  160.3 8.0 %collective-permute-start.31 = (bf16[16,96,768]{2,1,0:T(8,128)(2,1)}, bf16[16,96,768]{2,1,0:T(8,128)(2,1)S(1)}, u32[]{:S(2)}, u32[]{:S(2)}) collective-permute-start(bf16[16,96,768]{2,1,0:T(8,128)(2,1)} %get-tuple-element.257), channel_id=1, source_target_pairs={{0,4},{4,0},{1,5},{5,1},{2,6},{6,2},{3,7},{7,3},{8,12},{12,8},{9,1... | collective-permute-start | bytes 7077896 | tf_op jit(solution)/shard_map/ppermute | solution.py:46
  160.7 6.9 %collective-permute-start.29 = (bf16[128,768]{1,0:T(8,128)(2,1)S(1)}, bf16[128,768]{1,0:T(8,128)(2,1)S(1)}, u32[]{:S(2)}, u32[]{:S(2)}) collective-permute-start(bf16[128,768]{1,0:T(8,128)(2,1)S(1)} %get-tuple-element.255), channel_id=1, source_target_pairs={{0,1},{1,0},{2,3},{3,2},{4,5},{5,4},{6,7},{7,6},{8,9},{9,8},{10,11... | collective-permute-start | bytes 589832 | tf_op jit(solution)/shard_map/ppermute | solution.py:51
  170.8 39.5 %collective-permute-start.35 = (bf16[8,96,768]{2,1,0:T(8,128)(2,1)S(1)}, bf16[8,96,768]{2,1,0:T(8,128)(2,1)S(1)}, u32[]{:S(2)}, u32[]{:S(2)}) collective-permute-start(bf16[8,96,768]{2,1,0:T(8,128)(2,1)S(1)} %get-tuple-element.419), channel_id=1, source_target_pairs={{0,8},{8,0},{1,9},{9,1},{2,10},{10,2},{3,11},{11,3},{4,12},{12,4},... | collective-permute-start | bytes 3538952 | tf_op jit(solution)/shard_map/ppermute | solution.py:46
  173.0 37.3 %collective-permute-start.36 = (bf16[8,96,768]{2,1,0:T(8,128)(2,1)S(1)}, bf16[8,96,768]{2,1,0:T(8,128)(2,1)S(1)}, u32[]{:S(2)}, u32[]{:S(2)}) collective-permute-start(bf16[8,96,768]{2,1,0:T(8,128)(2,1)S(1)} %get-tuple-element.417), channel_id=1, source_target_pairs={{0,16},{16,0},{1,17},{17,1},{2,18},{18,2},{3,19},{19,3},{4,20},{20... | collective-permute-start | bytes 3538952 | tf_op jit(solution)/shard_map/ppermute | solution.py:46
  174.7 8.5 %collective-permute-start.32 = (bf16[2,128,192]{2,1,0:T(8,128)(2,1)S(1)}, bf16[2,128,192]{2,1,0:T(8,128)(2,1)S(1)}, u32[]{:S(2)}, u32[]{:S(2)}) collective-permute-start(bf16[2,128,192]{2,1,0:T(8,128)(2,1)S(1)} %get-tuple-element.269), channel_id=1, source_target_pairs={{0,2},{1,3},{2,0},{3,1},{4,6},{5,7},{6,4},{7,5},{8,10},{9,11},{10,... | collective-permute-start | bytes 294920 | tf_op jit(solution)/shard_map/ppermute | solution.py:51
  183.3 6.4 %collective-permute-start.33 = (bf16[2,128,192]{2,1,0:T(8,128)(2,1)S(1)}, bf16[2,128,192]{2,1,0:T(8,128)(2,1)S(1)}, u32[]{:S(2)}, u32[]{:S(2)}) collective-permute-start(bf16[2,128,192]{2,1,0:T(8,128)(2,1)S(1)} %pad_maximum_fusion.24), channel_id=1, source_target_pairs={{0,1},{1,0},{2,3},{3,2},{4,5},{5,4},{6,7},{7,6},{8,9},{9,8},{10,11... | collective-permute-start | bytes 294920 | tf_op jit(solution)/shard_map/ppermute | solution.py:51
  183.4 13.8 %collective-permute-start.34 = (bf16[2,4,32,768]{3,2,1,0:T(8,128)(2,1)S(1)}, bf16[2,4,32,768]{3,2,1,0:T(8,128)(2,1)S(1)}, u32[]{:S(2)}, u32[]{:S(2)}) collective-permute-start(bf16[2,4,32,768]{3,2,1,0:T(8,128)(2,1)S(1)} %get-tuple-element.260), channel_id=1, source_target_pairs={{0,1},{1,0},{2,3},{3,2},{4,5},{5,4},{6,7},{7,6},{8,9},{9,8},{10,11... | collective-permute-start | bytes 1179656 | tf_op jit(solution)/shard_map/ppermute | solution.py:51
  197.3 31.3 %collective-permute-start.41 = (bf16[2,2,4,32,768]{4,3,2,1,0:T(8,128)(2,1)S(1)}, bf16[2,2,4,32,768]{4,3,2,1,0:T(8,128)(2,1)S(1)}, u32[]{:S(2)}, u32[]{:S(2)}) collective-permute-start(bf16[2,2,4,32,768]{4,3,2,1,0:T(8,128)(2,1)S(1)} %pad_maximum_fusion.4.two), channel_id=1, source_target_pairs={{1,2},{2,1},{5,6},{6,5},{9,10},{10,9},{13,14},{14,13},{17,18},{18,... | collective-permute-start | bytes 2359304 | tf_op jit(solution)/shard_map/ppermute | solution.py:134
  210.3 13.2 %collective-permute-start.37 = (bf16[2,128,192]{2,1,0:T(8,128)(2,1)S(1)}, bf16[2,128,192]{2,1,0:T(8,128)(2,1)S(1)}, u32[]{:S(2)}, u32[]{:S(2)}) collective-permute-start(bf16[2,128,192]{2,1,0:T(8,128)(2,1)S(1)} %get-tuple-element.283), channel_id=1, source_target_pairs={{0,2},{1,3},{2,0},{3,1},{4,6},{5,7},{6,4},{7,5},{8,10},{9,11},{10,... | collective-permute-start | bytes 294920 | tf_op jit(solution)/shard_map/ppermute | solution.py:51
  213.5 15.1 %collective-permute-start.39 = (bf16[4,96,768]{2,1,0:T(8,128)(2,1)S(1)}, bf16[4,96,768]{2,1,0:T(8,128)(2,1)S(1)}, u32[]{:S(2)}, u32[]{:S(2)}) collective-permute-start(bf16[4,96,768]{2,1,0:T(8,128)(2,1)S(1)} %get-tuple-element.425), channel_id=1, source_target_pairs={{0,16},{16,0},{1,17},{17,1},{2,18},{18,2},{3,19},{19,3},{4,20},{20... | collective-permute-start | bytes 1769480 | tf_op jit(solution)/shard_map/ppermute | solution.py:46
  215.4 13.9 %collective-permute-start.40 = (bf16[4,96,768]{2,1,0:T(8,128)(2,1)S(1)}, bf16[4,96,768]{2,1,0:T(8,128)(2,1)S(1)}, u32[]{:S(2)}, u32[]{:S(2)}) collective-permute-start(bf16[4,96,768]{2,1,0:T(8,128)(2,1)S(1)} %get-tuple-element.427), channel_id=1, source_target_pairs={{0,8},{8,0},{1,9},{9,1},{2,10},{10,2},{3,11},{11,3},{4,12},{12,4},... | collective-permute-start | bytes 1769480 | tf_op jit(solution)/shard_map/ppermute | solution.py:46
  233.5 22.1 %collective-permute-start.43 = (bf16[16,48,384]{2,1,0:T(8,128)(2,1)S(1)}, bf16[16,48,384]{2,1,0:T(8,128)(2,1)S(1)}, u32[]{:S(2)}, u32[]{:S(2)}) collective-permute-start(bf16[16,48,384]{2,1,0:T(8,128)(2,1)S(1)} %get-tuple-element.315), channel_id=1, source_target_pairs={{0,4},{4,0},{1,5},{5,1},{2,6},{6,2},{3,7},{7,3},{8,12},{12,8},{9,1... | collective-permute-start | bytes 1769480 | tf_op jit(solution)/shard_map/ppermute | solution.py:46
  233.6 22.0 %collective-permute-start.44 = (bf16[16,48,384]{2,1,0:T(8,128)(2,1)S(1)}, bf16[16,48,384]{2,1,0:T(8,128)(2,1)S(1)}, u32[]{:S(2)}, u32[]{:S(2)}) collective-permute-start(bf16[16,48,384]{2,1,0:T(8,128)(2,1)S(1)} %get-tuple-element.316), channel_id=1, source_target_pairs={{0,4},{4,0},{1,5},{5,1},{2,6},{6,2},{3,7},{7,3},{8,12},{12,8},{9,1... | collective-permute-start | bytes 1769480 | tf_op jit(solution)/shard_map/ppermute | solution.py:46
  234.1 21.5 %collective-permute-start.42 = (bf16[2,96,768]{2,1,0:T(8,128)(2,1)S(1)}, bf16[2,96,768]{2,1,0:T(8,128)(2,1)S(1)}, u32[]{:S(2)}, u32[]{:S(2)}) collective-permute-start(bf16[2,96,768]{2,1,0:T(8,128)(2,1)S(1)} %get-tuple-element.453), channel_id=1, source_target_pairs={{0,2},{1,3},{2,0},{3,1},{4,6},{5,7},{6,4},{7,5},{8,10},{9,11},{10,... | collective-permute-start | bytes 884744 | tf_op jit(solution)/shard_map/ppermute | solution.py:51
  234.5 34.9 %collective-permute-start.46 = (bf16[2,2,4,32,768]{4,3,2,1,0:T(8,128)(2,1)S(1)}, bf16[2,2,4,32,768]{4,3,2,1,0:T(8,128)(2,1)S(1)}, u32[]{:S(2)}, u32[]{:S(2)}) collective-permute-start(bf16[2,2,4,32,768]{4,3,2,1,0:T(8,128)(2,1)S(1)} %collective-permute-done.41.across), channel_id=1, source_target_pairs={{1,0},{2,3},{5,4},{6,7},{9,8},{10,11},{13,12},{14,15},{17,16},{18,... | collective-permute-start | bytes 2359304 | tf_op jit(solution)/shard_map/ppermute | solution.py:140
  236.0 25.9 %collective-permute-start.47 = (bf16[2,96,768]{2,1,0:T(8,128)(2,1)S(1)}, bf16[2,96,768]{2,1,0:T(8,128)(2,1)S(1)}, u32[]{:S(2)}, u32[]{:S(2)}) collective-permute-start(bf16[2,96,768]{2,1,0:T(8,128)(2,1)S(1)} %get-tuple-element.452), channel_id=1, source_target_pairs={{0,2},{1,3},{2,0},{3,1},{4,6},{5,7},{6,4},{7,5},{8,10},{9,11},{10,... | collective-permute-start | bytes 884744 | tf_op jit(solution)/shard_map/ppermute | solution.py:51
  255.6 21.0 %collective-permute-start.45 = (bf16[256,768]{1,0:T(8,128)(2,1)S(1)}, bf16[256,768]{1,0:T(8,128)(2,1)S(1)}, u32[]{:S(2)}, u32[]{:S(2)}) collective-permute-start(bf16[256,768]{1,0:T(8,128)(2,1)S(1)} %get-tuple-element.317), channel_id=1, source_target_pairs={{0,1},{1,0},{2,3},{3,2},{4,5},{5,4},{6,7},{7,6},{8,9},{9,8},{10,11... | collective-permute-start | bytes 1179656 | tf_op jit(solution)/shard_map/ppermute | solution.py:51
  255.8 13.5 %collective-permute-start.48 = (bf16[8,48,384]{2,1,0:T(8,128)(2,1)S(1)}, bf16[8,48,384]{2,1,0:T(8,128)(2,1)S(1)}, u32[]{:S(2)}, u32[]{:S(2)}) collective-permute-start(bf16[8,48,384]{2,1,0:T(8,128)(2,1)S(1)} %get-tuple-element.439), channel_id=1, source_target_pairs={{0,8},{8,0},{1,9},{9,1},{2,10},{10,2},{3,11},{11,3},{4,12},{12,4},... | collective-permute-start | bytes 884744 | tf_op jit(solution)/shard_map/ppermute | solution.py:46
  257.4 11.9 %collective-permute-start.49 = (bf16[8,48,384]{2,1,0:T(8,128)(2,1)S(1)}, bf16[8,48,384]{2,1,0:T(8,128)(2,1)S(1)}, u32[]{:S(2)}, u32[]{:S(2)}) collective-permute-start(bf16[8,48,384]{2,1,0:T(8,128)(2,1)S(1)} %get-tuple-element.437), channel_id=1, source_target_pairs={{0,16},{16,0},{1,17},{17,1},{2,18},{18,2},{3,19},{19,3},{4,20},{20... | collective-permute-start | bytes 884744 | tf_op jit(solution)/shard_map/ppermute | solution.py:46
  276.6 7.7 %collective-permute-start.50 = (bf16[16,96,384]{2,1,0:T(8,128)(2,1)S(1)}, bf16[16,96,384]{2,1,0:T(8,128)(2,1)S(1)}, u32[]{:S(2)}, u32[]{:S(2)}) collective-permute-start(bf16[16,96,384]{2,1,0:T(8,128)(2,1)S(1)} %get-tuple-element.333), channel_id=1, source_target_pairs={{0,4},{4,0},{1,5},{5,1},{2,6},{6,2},{3,7},{7,3},{8,12},{12,8},{9,1... | collective-permute-start | bytes 3538952 | tf_op jit(solution)/shard_map/ppermute | solution.py:46
  276.6 7.7 %collective-permute-start.51 = (bf16[16,96,384]{2,1,0:T(8,128)(2,1)S(1)}, bf16[16,96,384]{2,1,0:T(8,128)(2,1)S(1)}, u32[]{:S(2)}, u32[]{:S(2)}) collective-permute-start(bf16[16,96,384]{2,1,0:T(8,128)(2,1)S(1)} %get-tuple-element.334), channel_id=1, source_target_pairs={{0,4},{4,0},{1,5},{5,1},{2,6},{6,2},{3,7},{7,3},{8,12},{12,8},{9,1... | collective-permute-start | bytes 3538952 | tf_op jit(solution)/shard_map/ppermute | solution.py:46
  277.3 6.3 %collective-permute-start.53 = (bf16[4,48,384]{2,1,0:T(8,128)(2,1)S(1)}, bf16[4,48,384]{2,1,0:T(8,128)(2,1)S(1)}, u32[]{:S(2)}, u32[]{:S(2)}) collective-permute-start(bf16[4,48,384]{2,1,0:T(8,128)(2,1)S(1)} %get-tuple-element.449), channel_id=1, source_target_pairs={{0,16},{16,0},{1,17},{17,1},{2,18},{18,2},{3,19},{19,3},{4,20},{20... | collective-permute-start | bytes 442376 | tf_op jit(solution)/shard_map/ppermute | solution.py:46
  278.2 6.0 %collective-permute-start.54 = (bf16[4,48,384]{2,1,0:T(8,128)(2,1)S(1)}, bf16[4,48,384]{2,1,0:T(8,128)(2,1)S(1)}, u32[]{:S(2)}, u32[]{:S(2)}) collective-permute-start(bf16[4,48,384]{2,1,0:T(8,128)(2,1)S(1)} %get-tuple-element.451), channel_id=1, source_target_pairs={{0,8},{8,0},{1,9},{9,1},{2,10},{10,2},{3,11},{11,3},{4,12},{12,4},... | collective-permute-start | bytes 442376 | tf_op jit(solution)/shard_map/ppermute | solution.py:46
  281.2 30.4 %collective-permute-start.58 = (bf16[2,256,768]{2,1,0:T(8,128)(2,1)S(1)}, bf16[2,256,768]{2,1,0:T(8,128)(2,1)S(1)}, u32[]{:S(2)}, u32[]{:S(2)}) collective-permute-start(bf16[2,256,768]{2,1,0:T(8,128)(2,1)S(1)} %pad_maximum_fusion.5.two), channel_id=1, source_target_pairs={{1,2},{2,1},{5,6},{6,5},{9,10},{10,9},{13,14},{14,13},{17,18},{18,... | collective-permute-start | bytes 2359304 | tf_op jit(solution)/shard_map/ppermute | solution.py:134
  283.6 8.7 %collective-permute-start.63 = (bf16[192,768]{1,0:T(8,128)(2,1)S(1)}, bf16[192,768]{1,0:T(8,128)(2,1)}, u32[]{:S(2)}, u32[]{:S(2)}) collective-permute-start(bf16[192,768]{1,0:T(8,128)(2,1)S(1)} %get-tuple-element.434), channel_id=1, source_target_pairs={{0,1},{1,0},{2,3},{3,2},{4,5},{5,4},{6,7},{7,6},{8,9},{9,8},{10,11... | collective-permute-start | bytes 884744 | tf_op jit(solution)/shard_map/ppermute | solution.py:51
  285.6 26.1 %collective-permute-start.55 = (bf16[8,96,384]{2,1,0:T(8,128)(2,1)}, bf16[8,96,384]{2,1,0:T(8,128)(2,1)}, u32[]{:S(2)}, u32[]{:S(2)}) collective-permute-start(bf16[8,96,384]{2,1,0:T(8,128)(2,1)} %get-tuple-element.423), channel_id=1, source_target_pairs={{0,8},{8,0},{1,9},{9,1},{2,10},{10,2},{3,11},{11,3},{4,12},{12,4},... | collective-permute-start | bytes 1769480 | tf_op jit(solution)/shard_map/ppermute | solution.py:46
  288.0 23.6 %collective-permute-start.56 = (bf16[8,96,384]{2,1,0:T(8,128)(2,1)}, bf16[8,96,384]{2,1,0:T(8,128)(2,1)}, u32[]{:S(2)}, u32[]{:S(2)}) collective-permute-start(bf16[8,96,384]{2,1,0:T(8,128)(2,1)} %get-tuple-element.421), channel_id=1, source_target_pairs={{0,16},{16,0},{1,17},{17,1},{2,18},{18,2},{3,19},{19,3},{4,20},{20... | collective-permute-start | bytes 1769480 | tf_op jit(solution)/shard_map/ppermute | solution.py:46
  289.6 22.0 %collective-permute-start.59 = (bf16[2,96,384]{2,1,0:T(8,128)(2,1)}, bf16[2,96,384]{2,1,0:T(8,128)(2,1)}, u32[]{:S(2)}, u32[]{:S(2)}) collective-permute-start(bf16[2,96,384]{2,1,0:T(8,128)(2,1)} %pad_maximum_fusion.18), channel_id=1, source_target_pairs={{0,2},{1,3},{2,0},{3,1},{4,6},{5,7},{6,4},{7,5},{8,10},{9,11},{10,... | collective-permute-start | bytes 442376 | tf_op jit(solution)/shard_map/ppermute | solution.py:51
  292.3 19.3 %collective-permute-start.57 = (f32[24,768]{1,0:T(8,128)S(1)}, f32[24,768]{1,0:T(8,128)S(1)}, u32[]{:S(2)}, u32[]{:S(2)}) collective-permute-start(f32[24,768]{1,0:T(8,128)S(1)} %add.309), channel_id=1, source_target_pairs={{0,1},{1,0},{2,3},{3,2},{4,5},{5,4},{6,7},{7,6},{8,9},{9,8},{10,11... | collective-permute-start | bytes 221192 | tf_op jit(solution)/shard_map/ppermute | solution.py:51
  313.8 30.3 %collective-permute-start.60 = (bf16[4,96,384]{2,1,0:T(8,128)(2,1)}, bf16[4,96,384]{2,1,0:T(8,128)(2,1)}, u32[]{:S(2)}, u32[]{:S(2)}) collective-permute-start(bf16[4,96,384]{2,1,0:T(8,128)(2,1)} %get-tuple-element.433), channel_id=1, source_target_pairs={{0,16},{16,0},{1,17},{17,1},{2,18},{18,2},{3,19},{19,3},{4,20},{20... | collective-permute-start | bytes 884744 | tf_op jit(solution)/shard_map/ppermute | solution.py:46
  314.9 29.2 %collective-permute-start.64 = (bf16[2,256,768]{2,1,0:T(8,128)(2,1)S(1)}, bf16[2,256,768]{2,1,0:T(8,128)(2,1)S(1)}, u32[]{:S(2)}, u32[]{:S(2)}) collective-permute-start(bf16[2,256,768]{2,1,0:T(8,128)(2,1)S(1)} %collective-permute-done.58.across), channel_id=1, source_target_pairs={{1,0},{2,3},{5,4},{6,7},{9,8},{10,11},{13,12},{14,15},{17,16},{18,... | collective-permute-start | bytes 2359304 | tf_op jit(solution)/shard_map/ppermute | solution.py:140
  317.1 20.7 %collective-permute-start.70 = (bf16[96,384]{1,0:T(8,128)(2,1)S(1)}, bf16[96,384]{1,0:T(8,128)(2,1)S(1)}, u32[]{:S(2)}, u32[]{:S(2)}) collective-permute-start(bf16[96,384]{1,0:T(8,128)(2,1)S(1)} %fusion.22), channel_id=1, source_target_pairs={{0,1},{1,0},{2,3},{3,2},{4,5},{5,4},{6,7},{7,6},{8,9},{9,8},{10,11... | collective-permute-start | bytes 221192 | tf_op jit(solution)/shard_map/ppermute | solution.py:51
  321.9 22.2 %collective-permute-start.61 = (bf16[4,96,384]{2,1,0:T(8,128)(2,1)}, bf16[4,96,384]{2,1,0:T(8,128)(2,1)}, u32[]{:S(2)}, u32[]{:S(2)}) collective-permute-start(bf16[4,96,384]{2,1,0:T(8,128)(2,1)} %get-tuple-element.431), channel_id=1, source_target_pairs={{0,8},{8,0},{1,9},{9,1},{2,10},{10,2},{3,11},{11,3},{4,12},{12,4},... | collective-permute-start | bytes 884744 | tf_op jit(solution)/shard_map/ppermute | solution.py:46
  323.3 20.8 %collective-permute-start.62 = (f32[24,768]{1,0:T(8,128)}, f32[24,768]{1,0:T(8,128)}, u32[]{:S(2)}, u32[]{:S(2)}) collective-permute-start(f32[24,768]{1,0:T(8,128)} %add.318), channel_id=1, source_target_pairs={{0,2},{1,3},{2,0},{3,1},{4,6},{5,7},{6,4},{7,5},{8,10},{9,11},{10,... | collective-permute-start | bytes 221192 | tf_op jit(solution)/shard_map/ppermute | solution.py:51
  346.4 14.3 %collective-permute-start.65 = (bf16[192,384]{1,0:T(8,128)(2,1)S(1)}, bf16[192,384]{1,0:T(8,128)(2,1)S(1)}, u32[]{:S(2)}, u32[]{:S(2)}) collective-permute-start(bf16[192,384]{1,0:T(8,128)(2,1)S(1)} %get-tuple-element.468), channel_id=1, source_target_pairs={{0,1},{1,0},{2,3},{3,2},{4,5},{5,4},{6,7},{7,6},{8,9},{9,8},{10,11... | collective-permute-start | bytes 442376 | tf_op jit(solution)/shard_map/ppermute | solution.py:51
  346.5 14.2 %collective-permute-start.66 = (bf16[192,384]{1,0:T(8,128)(2,1)S(1)}, bf16[192,384]{1,0:T(8,128)(2,1)S(1)}, u32[]{:S(2)}, u32[]{:S(2)}) collective-permute-start(bf16[192,384]{1,0:T(8,128)(2,1)S(1)} %get-tuple-element.467), channel_id=1, source_target_pairs={{0,2},{1,3},{2,0},{3,1},{4,6},{5,7},{6,4},{7,5},{8,10},{9,11},{10,... | collective-permute-start | bytes 442376 | tf_op jit(solution)/shard_map/ppermute | solution.py:51
  348.9 11.8 %collective-permute-start.67 = (bf16[192,384]{1,0:T(8,128)(2,1)S(1)}, bf16[192,384]{1,0:T(8,128)(2,1)S(1)}, u32[]{:S(2)}, u32[]{:S(2)}) collective-permute-start(bf16[192,384]{1,0:T(8,128)(2,1)S(1)} %get-tuple-element.466), channel_id=1, source_target_pairs={{0,3},{1,2},{2,1},{3,0},{4,7},{5,6},{6,5},{7,4},{8,11},{9,10},{10,... | collective-permute-start | bytes 442376 | tf_op jit(solution)/shard_map/ppermute | solution.py:51
  (82 other events, 535.6 us)
Sparse Core Ops, SparseCore 0:
  17.4 27.8 all-gather.1
  324.1 34.9 reduce-scatter.1

commit v4 on v3

--- a/solution.py
+++ b/solution.py
@@ -471,23 +471,27 @@
 
 
 def distance_shapes(plan):
-    shape = (plan.half, plan.width)
-    return [
-        jax.ShapeDtypeStruct(shape, BF),
-        jax.ShapeDtypeStruct(shape, BF),
-        jax.ShapeDtypeStruct((plan.mp - 2,) + shape, BF),
-    ]
+    both = jax.ShapeDtypeStruct((plan.half, 2 * plan.width), BF)
+    return [jax.ShapeDtypeStruct((plan.half, plan.width), BF), both, both]
 
 
 def put_distance(refs, j, values):
-    if j < 2:
-        refs[j][...] = values
+    width = values.shape[1]
+    if j == 0:
+        refs[0][...] = values
+    elif j == 1:
+        refs[1][...] = before(values, width)
     else:
-        refs[2][j - 2] = values
+        refs[2][:, (j - 2) * width : (j - 1) * width] = values
 
 
 def get_distance(refs, j, span=slice(None)):
-    return refs[j][span, :] if j < 2 else refs[2][j - 2, span, :]
+    width = refs[0].shape[1]
+    if j == 0:
+        return refs[0][span, :]
+    if j == 2:
+        return refs[2][span, :width]
+    return refs[1][span, :width] if j == 1 else refs[1][span, width:]
 
 
 def self_forward(plan, lengths, hidden, vec, heads, sets):
@@ -1047,7 +1051,7 @@
         ],
         [VMEM] * 4,
         [pltpu.VMEM((mp, D, 2 * width), BF)] * 3 + [DMA((3,))],
-        32,
+        56,
     )
 
 
@@ -1151,25 +1155,41 @@
     )[0]
 
 
-def place_gradient(plan, two, across, far):
+def place_gradient(plan, own, near, across_own, across_near, far_own, far_near):
     mp, items = plan.mp, plan.items
 
-    def kernel(two, across, far, out):
+    def kernel(own, near, across_own, across_near, far_own, far_near, out):
         me = lax.axis_index("mp")
-        for j in range(mp):
-            values = two[j] if j < 2 else from_line(plan, across, far, j)
+        end = (me == 0) | (me == mp - 1)
+        found = [
+            own[...],
+            near[...],
+            jnp.where(end, far_own[...], across_near[...]),
+            jnp.where(end, far_near[...], across_own[...]),
+        ]
+        for j, values in enumerate(found):
             values = values.astype(F32).reshape(items, 2 * NQ, D)
             out[pl.ds((me ^ j) * items, items)] = values
 
     return call(
         kernel,
-        (two, across, far),
-        [VMEM] * 3,
+        (own, near, across_own, across_near, far_own, far_near),
+        [VMEM] * 6,
         [jax.ShapeDtypeStruct((mp * items, 2 * NQ, D), F32)],
         [VMEM],
         [],
         24,
     )[0]
+
+
+RATES = {
+    "attn_in": 2.0 / math.sqrt(D),
+    "attn_out": 2.0 / math.sqrt(max(D // 8, 1)),
+    "cross_kv": 2.0 / math.sqrt(E),
+    "ffn_up": 2.0 / math.sqrt(D),
+    "ffn_down": 2.0 / math.sqrt(F),
+    "vector": 0.3,
+}
 
 
 def adam_update(weight, first, second, grad, rate):
@@ -1181,6 +1201,78 @@
         first_hat / (jnp.sqrt(second_hat) + ADAM_EPS) + WEIGHT_DECAY * weight
     )
     return (first_new, second_new, weight_new)
+
+
+def update_into(held, outs, place, grad, rate):
+    found = adam_update(held[0][place], held[1][place], held[2][place], grad, rate)
+    for out, values in zip(outs, found):
+        out[place] = values
+
+
+def bring(sources, targets, sems):
+    copies = [
+        pltpu.make_async_copy(s, t, sems.at[k]) for k, (s, t) in enumerate(zip(sources, targets))
+    ]
+    for c in copies:
+        c.start()
+    return copies
+
+
+def ffn_step(mine, theirs, up, down):
+    rows = up[0].shape[1]
+
+    def kernel(*refs):
+        mine, theirs, sources, outs = refs[0], refs[1], refs[2:8], refs[8:14]
+        held, sems = refs[14:20], refs[20]
+        copies = bring(sources, held, sems)
+        up, down = held[:3], held[3:]
+        low = (lax.axis_index("mp") & 1) == 0
+        own, other = mine[...].astype(F32), theirs[...].astype(F32)
+        for copy in copies:
+            copy.wait()
+        for g in range(2):
+            grad = jnp.where(low, own, other) if g == 0 else jnp.where(low, other, own)
+            update_into(up, outs[:3], g, grad[:rows], RATES["ffn_up"])
+            update_into(down, outs[3:], g, grad[rows:], RATES["ffn_down"])
+
+    shapes = [jax.ShapeDtypeStruct(v.shape, F32) for v in up + down]
+    return call(
+        kernel,
+        (mine, theirs, *up, *down),
+        [VMEM] * 2 + [HBM] * 6,
+        shapes,
+        [VMEM] * 6,
+        [pltpu.VMEM(v.shape, F32) for v in up + down] + [DMA((6,))],
+        32,
+    )
+
+
+def other_steps(plan, pieces, kv_total, attn_in, out_turned, kv):
+    width = plan.width
+    rows = attn_in[0].shape[1]
+    total = sum(p.astype(F32) for p in pieces)
+
+    def columns(values):
+        return jnp.stack([values[:, :width], values[:, width:]])
+
+    in_grad = jnp.concatenate([columns(total[:rows]), columns(total[rows : 2 * rows])])
+    found = adam_update(*attn_in, in_grad, RATES["attn_in"])
+    turned = adam_update(*out_turned, columns(total[2 * rows :]), RATES["attn_out"])
+    image = adam_update(*kv, columns(kv_total.astype(F32)), RATES["cross_kv"])
+    return (*found, *(v.transpose(0, 2, 1) for v in turned), *image)
+
+
+def vector_steps(plan, vectors, rep_, head, bias):
+    me = lax.axis_index("mp")
+    width, hidden_width = head[0].shape[1], bias[0].shape[1]
+    head_grad = lax.dynamic_slice_in_dim(vectors[12:16], me * width, width, 1)
+    bias_grad = lax.dynamic_slice_in_dim(
+        vectors[16:].reshape(2, -1), me * hidden_width, hidden_width, 1
+    )
+    found = []
+    for held, grad in ((rep_, vectors[:12]), (head, head_grad), (bias, bias_grad)):
+        found.extend(adam_update(*held, grad, RATES["vector"]))
+    return found
 
 
 def local(
@@ -1294,7 +1386,12 @@
     first = mp_direct(plan, first_shard, lambda j: first_shard)
     maps = lax.all_gather(low_kv, forth + ("core",), axis=0, tiled=True)
     images = with_layout_constraint(images, Layout(major_to_minor=(0, 1, 2)))
-    first, images, third_own, third_other = hold(first, images, third_own, third_other)
+    out_turned = tuple(
+        v.transpose(0, 2, 1) for v in (attn_out, attn_out_first, attn_out_second)
+    )
+    first, images, third_own, third_other, out_turned = hold(
+        first, images, third_own, third_other, out_turned
+    )
     packed_rows = packed.shape[0]
     heads = jnp.stack([p[attn_first + attn_second :].astype(F32) for p in first])
     heads = heads.reshape(mp, 3, packed_rows, heads.shape[-1]).sum(axis=1)
@@ -1339,10 +1436,9 @@
     def exchange(values):
         own, near, others = values
         got = mp_swap(others, 2)
-        for distance in plan.distances[2:]:
-            got = mp_swap(got, distance)
-        passed = mp_swap(jnp.stack([near, got[1]]), 1)
-        return own, passed[0], jnp.stack([got[0], passed[1]])
+        lane = lax.broadcasted_iota(jnp.int32, got.shape, 1)
+        passed = mp_swap(jnp.where(lane < plan.width, near, got), 1)
+        return own, passed, got
 
     far_down, cross, up_got = hold(far_down, cross, up_got)
     up = jnp.concatenate([up, up_got])
@@ -1414,8 +1510,12 @@
     query_back, got = hold(query_back, got)
     ffn_state = shrink_add(ffn_state, got)
     got = shrink_send(ffn_state, (forth[0], back[0]))
+    kv_grad = image_gradient(plan, images, kv_back)
     query_back = exchange(query_back)
-    query_back, got, layer_across = hold(query_back, got, layer_across)
+    query_back, got, layer_across, kv_grad = hold(query_back, got, layer_across, kv_grad)
+    kv_total = lax.psum_scatter(
+        kv_grad, forth + ("core",), scatter_dimension=0, tiled=True
+    )
     ffn_state = join_trees(shrink_add(ffn_state, got))
     for distance in plan.distances[:1:-1]:
         ffn_state = mp_halve(ffn_state, distance)
@@ -1439,8 +1539,8 @@
     token_back, maps_back, vectors, ffn_got_up, out_got = hold(
         token_back, maps_back, vectors, ffn_got_up, out_got
     )
+    across_own = mp_middle(plan, token_back)
     near = mp_swap(token_back, 1)
-    ffn_got_down = mp_swap(ffn_state[1][:, middle:], 2)
     out_state = shrink_add(out_state, out_got)
     for k in range(plan.bits - 1, 1, -1):
         out_state = shrink_add(out_state, shrink_send(out_state, (forth[k], back[k])))
@@ -1451,136 +1551,84 @@
         (vec_rep, z_first, maps_back, value_maps, *query_back),
         attn_gradients,
     )
-    near, layer_far, vectors, attn_halves, kv_back, ffn_got_down, out_got = hold(
-        near, layer_far, vectors, attn_halves, kv_back, ffn_got_down, out_got
+    across_own, layer_far, near, attn_halves, out_got = hold(
+        across_own, layer_far, near, attn_halves, out_got
     )
     attn_state = attn_halves["a"], attn_halves["b"]
     attn_got = shrink_send(attn_state, cores)
-    vector_got = swap(vectors, "core")
-    tokens_two = jnp.stack([token_back, near])
-    across = mp_middle(plan, tokens_two)
+    ffn_got_down = mp_swap(ffn_state[1][:, middle:], 2)
     out_state = shrink_add(out_state, out_got)
     out_got = shrink_send(out_state, (forth[0], back[0]))
-    attn_got, vector_got, kv_back, out_got = hold(attn_got, vector_got, kv_back, out_got)
-    vectors = vectors + vector_got
+    attn_got, out_got, ffn_got_down, vectors = hold(attn_got, out_got, ffn_got_down, vectors)
+    across_near = mp_middle(plan, near)
+    far_own = mp_outward(plan, across_own)
     attn_state = shrink_add(attn_state, attn_got)
     for k in range(plan.bits - 1, 1, -1):
         attn_state = shrink_add(attn_state, shrink_send(attn_state, (forth[k], back[k])))
     attn_got = shrink_send(attn_state, (forth[1], back[1]))
-    out_state = join_trees(shrink_add(out_state, out_got))
-    for distance in plan.distances[:1:-1]:
-        out_state = mp_halve(out_state, distance)
-    out_got = mp_swap(out_state[1], 2)
+    out_state = shrink_add(out_state, out_got)
     vector_got = mp_swap(vectors, 1)
-    kv_grad = image_gradient(plan, images, kv_back)
-    attn_got, kv_grad, vector_got, across, out_got = hold(
-        attn_got, kv_grad, vector_got, across, out_got
-    )
-    kv_total = lax.psum_scatter(
-        kv_grad, forth + ("core",), scatter_dimension=0, tiled=True
-    ).astype(F32)
-    vectors = vectors + vector_got
-    vector_got = mp_swap(vectors, 2)
-    tokens_far = mp_outward(plan, across)
-    attn_state = shrink_add(attn_state, attn_got)
-    attn_got = shrink_send(attn_state, (forth[0], back[0]))
-    layer_out = place_layer(plan, layer_two, layer_across, layer_far)
-
-    def add_halves(state, got):
-        half = got.shape[0] // 2
-        return add_low(state[0][:half], got[:half]), add_low(state[0][half:], got[half:])
-
-    ffn_got = jnp.concatenate([ffn_got_up, ffn_got_down], axis=1)
-    mine, theirs = mp_last(add_halves(ffn_state, ffn_got))
-    out_state = add_halves(out_state, out_got)
-    attn_got, vector_got, mine, theirs, tokens_far = hold(
-        attn_got, vector_got, mine, theirs, tokens_far
+    attn_got, across_near, far_own, vector_got = hold(
+        attn_got, across_near, far_own, vector_got
     )
     vectors = vectors + vector_got
     for distance in plan.distances[2:]:
         vectors = vectors + mp_swap(vectors, distance)
-    for axis in forth[1:]:
+    vector_got = mp_swap(vectors, 2)
+    attn_state = shrink_add(attn_state, attn_got)
+    attn_got = shrink_send(attn_state, (forth[0], back[0]))
+    far_near = mp_outward(plan, across_near)
+    ffn_got = jnp.concatenate([ffn_got_up, ffn_got_down], axis=1)
+    half = ffn_got.shape[0] // 2
+    ffn_state = (
+        add_low(ffn_state[0][:half], ffn_got[:half]),
+        add_low(ffn_state[0][half:], ffn_got[half:]),
+    )
+    theirs = mp_swap(ffn_state[1][0], 1)
+    attn_got, vector_got, theirs, far_near = hold(attn_got, vector_got, theirs, far_near)
+    attn_state = shrink_add(attn_state, attn_got)
+    pieces = mp_scatter(plan, join_trees(attn_state + out_state))
+    vectors = vectors + vector_got
+    for axis in forth:
         vectors = vectors + swap(vectors, axis)
-    attn_pieces = mp_scatter(plan, join_trees(shrink_add(attn_state, attn_got)))
-    vector_got = swap(vectors, forth[0])
-    out_total = sum(mp_last(out_state))
-    attn_pieces, vector_got = hold(attn_pieces, vector_got)
-    vectors = vectors + vector_got
-    attn_total = sum(p.astype(F32) for p in attn_pieces)
-    grad_hidden = place_gradient(plan, tokens_two, across, tokens_far)
-    reduced_rep = vectors[:12]
-    head_width = query_value_bias_rows.shape[1]
-    bias_width = bias_up.shape[1]
-    reduced_head = lax.dynamic_slice_in_dim(vectors[12:16], me * head_width, head_width, 1)
-    reduced_bias = lax.dynamic_slice_in_dim(
-        vectors[16:].reshape(2, -1), me * bias_width, bias_width, 1
-    )
-
-    def split_columns(values):
-        width = values.shape[1] // 2
-        return jnp.stack([values[:, :width], values[:, width:]])
-
-    both = jnp.stack([jnp.where(low, mine, theirs), jnp.where(low, theirs, mine)])
-    reduced_up, reduced_down = both[:, :ffn_rows], both[:, ffn_rows:].transpose(0, 2, 1)
-    reduced_out = split_columns(out_total).transpose(0, 2, 1)
-    reduced_in = jnp.concatenate(
-        [split_columns(attn_total[:attn_rows]), split_columns(attn_total[attn_rows:])]
-    )
-    reduced_kv = split_columns(kv_total)
-    rates = (
-        2.0 / math.sqrt(D),
-        2.0 / math.sqrt(max(D // 8, 1)),
-        2.0 / math.sqrt(E),
-        2.0 / math.sqrt(D),
-        2.0 / math.sqrt(F),
-        0.3,
-        0.3,
-        0.3,
-    )
-    weights = (
-        attn_in,
-        attn_out,
-        cross_key_value_maps,
-        ffn_up,
-        ffn_down,
-        vec_rep,
-        query_value_bias_rows,
-        bias_up,
-    )
-    firsts = (
-        attn_in_first,
-        attn_out_first,
-        cross_kv_first,
-        ffn_up_first,
-        ffn_down_first,
-        vec_rep_first,
-        vec_head_first,
-        bias_up_first,
-    )
-    seconds = (
-        attn_in_second,
-        attn_out_second,
-        cross_kv_second,
-        ffn_up_second,
-        ffn_down_second,
-        vec_rep_second,
-        vec_head_second,
-        bias_up_second,
-    )
-    reduced = (
-        reduced_in,
-        reduced_out,
-        reduced_kv,
-        reduced_up,
-        reduced_down,
-        reduced_rep,
-        reduced_head,
-        reduced_bias,
-    )
-    results = []
-    for weight, first, second, grad, rate in zip(weights, firsts, seconds, reduced, rates):
-        results.extend(adam_update(weight, first, second, grad, rate))
-    return (layer_out, grad_hidden, *results)
+    grad_hidden = place_gradient(
+        plan, token_back, near, across_own, across_near, far_own, far_near
+    )
+    layer_out = place_layer(plan, layer_two, layer_across, layer_far)
+    turn = (0, 2, 1)
+    ffn_results = ffn_step(
+        ffn_state[0][0],
+        theirs,
+        (ffn_up, ffn_up_first, ffn_up_second),
+        tuple(v.transpose(turn) for v in (ffn_down, ffn_down_first, ffn_down_second)),
+    )
+    vectors, grad_hidden, layer_out, ffn_results = hold(
+        vectors, grad_hidden, layer_out, ffn_results
+    )
+    vectors = vectors + swap(vectors, "core")
+    results = other_steps(
+        plan,
+        pieces,
+        kv_total,
+        (attn_in, attn_in_first, attn_in_second),
+        out_turned,
+        (cross_key_value_maps, cross_kv_first, cross_kv_second),
+    )
+    vector_results = vector_steps(
+        plan,
+        vectors,
+        (vec_rep, vec_rep_first, vec_rep_second),
+        (query_value_bias_rows, vec_head_first, vec_head_second),
+        (bias_up, bias_up_first, bias_up_second),
+    )
+    return (
+        layer_out,
+        grad_hidden,
+        *results,
+        *ffn_results[:3],
+        *(v.transpose(turn) for v in ffn_results[3:]),
+        *vector_results,
+    )
 
 
 def solution(mesh):

time: 379 us -> 367 us (0.968)
  waiting for transfers between devices: 133 us -> 97 us
  starting transfers between devices: 70.8 us -> 82.1 us
  Pallas kernels: 83.4 us -> 92.8 us
  local copies, waits for them, and re-layouts: 37.4 us -> 41.2 us
    ppermute x28 -> x26, waiting for transfers between devices: 104 us -> 65.4 us  [mp_swap(): return lax.ppermute(values, 'mp', [(i, i ^ distance) for i in range(count)])]
    pallas_call x14 -> x15, Pallas kernels: 83.4 us -> 92.8 us  [call(): pl.pallas_call(kernel, out_shape=outs, in_specs=[pl.BlockSpec(memory_spac...]
    ppermute x28 -> x26, starting transfers between devices: 36.4 us -> 45.5 us  [mp_swap(): return lax.ppermute(values, 'mp', [(i, i ^ distance) for i in range(count)])]
    convert_element_type x18, other arithmetic: 13.5 us -> 18.4 us  [add_low(): return (first.astype(F32) + second.astype(F32)).astype(BF)]
    sub x8 -> x5, other arithmetic: 8.2 us -> 4.35 us  [adam_update(): weight - rate * (first_hat / (jnp.sqrt(second_hat) + ADAM_EPS) + WEIGHT_D...]
    ppermute x39, waiting for transfers between devices: 21.6 us -> 25.5 us  [swap(): return lax.ppermute(values, axis, [(0, 1), (1, 0)])]
    unnamed x158 -> x204, local copies, waits for them, and re-layouts: 35 us -> 36 us
  transfers between devices with their start and end apart: 73 -> 73, of which waited for: 29 -> 27; matrix products, arithmetic and copies ran while one was open for 12% -> 12% of each run, Pallas kernels for 17% -> 21%
where the time goes in v4:
time: 367 us; the launch traced here: 361 us
  waiting for transfers between devices  97 us (26%)
  Pallas kernels  92.8 us (25%)
  starting transfers between devices  82.1 us (22%)
  local copies, waits for them, and re-layouts  41.2 us (11%)
  other arithmetic  31.4 us (9%)
  between operations  16.2 us (4%)
    pallas_call x15, Pallas kernels, call(): pl.pallas_call(kernel, out_shape=outs, in_specs=[pl.BlockSpec(memory_spac...  92.8 us
    ppermute x26, waiting for transfers between devices, mp_swap(): return lax.ppermute(values, 'mp', [(i, i ^ distance) for i in range(count)])  65.4 us
    ppermute x26, starting transfers between devices, mp_swap(): return lax.ppermute(values, 'mp', [(i, i ^ distance) for i in range(count)])  45.5 us
    unnamed x204, local copies, waits for them, and re-layouts  36 us
    ppermute x39, starting transfers between devices, swap(): return lax.ppermute(values, axis, [(0, 1), (1, 0)])  30.3 us
    ppermute x39, waiting for transfers between devices, swap(): return lax.ppermute(values, axis, [(0, 1), (1, 0)])  25.5 us
    convert_element_type x18, other arithmetic, add_low(): return (first.astype(F32) + second.astype(F32)).astype(BF)  18.4 us
  transfers between devices with their start and end apart: 73, of which 27 were waited for; matrix products, arithmetic and copies ran while one was open for 12% of the time, Pallas kernels for 21%

profile of v4, /device:TPU:0, one launch (start us, length us, event | category | flops | bytes accessed | tf_op | source)
XLA Modules:
  0.0 360.7 jit_solution(3709149878093889547)
XLA Ops:
  10.1 3.1 collective-permute-start
  13.2 2.6 collective-permute-start.1
  16.8 11.5 %copy.55.images = bf16[16,257,1408]{2,1,0:T(8,128)(2,1)} copy(bf16[16,257,1408]{2,0,1:T(8,128)(2,1)} %param.29) | data formatting | bytes 23158784 | tf_op args[1]
  30.0 3.2 collective-permute-done.1
  35.2 1.6 collective-permute-start.4
  36.9 1.6 collective-permute-start.3
  38.4 4.2 %collective-permute-start.5 = (bf16[192,768]{1,0:T(8,128)(2,1)S(1)}, bf16[192,768]{1,0:T(8,128)(2,1)S(1)}, u32[]{:S(2)}, u32[]{:S(2)}) collective-permute-start(bf16[192,768]{1,0:T(8,128)(2,1)S(1)} %get-tuple-element.211), channel_id=1, source_target_pairs={{0,1},{1,0},{2,3},{3,2},{4,5},{5,4},{6,7},{7,6},{8,9},{9,8},{10,11... | collective-permute-start | bytes 884744 | tf_op jit(solution)/shard_map/ppermute | solution.py:51
  43.7 4.2 %collective-permute-done.5 = bf16[192,768]{1,0:T(8,128)(2,1)S(1)} collective-permute-done((bf16[192,768]{1,0:T(8,128)(2,1)S(1)}, bf16[192,768]{1,0:T(8,128)(2,1)S(1)}, u32[]{:S(2)}, u32[]{:S(2)}) %collective-permute-start.5) | collective-permute-done | bytes 294944 | tf_op jit(solution)/shard_map/ppermute | solution.py:51
  52.1 3.7 %collective-permute-start.11 = (bf16[2,96,768]{2,1,0:T(8,128)(2,1)S(1)}, bf16[2,96,768]{2,1,0:T(8,128)(2,1)S(1)}, u32[]{:S(2)}, u32[]{:S(2)}) collective-permute-start(bf16[2,96,768]{2,1,0:T(8,128)(2,1)S(1)} %get-tuple-element.463), channel_id=1, source_target_pairs={{0,2},{1,3},{2,0},{3,1},{4,6},{5,7},{6,4},{7,5},{8,10},{9,11},{10,... | collective-permute-start | bytes 884744 | tf_op jit(solution)/shard_map/ppermute | solution.py:51
  55.8 4.4 %copy-done = bf16[16,257,1408]{2,1,0:T(8,128)(2,1)S(1)} copy-done((bf16[16,257,1408]{2,1,0:T(8,128)(2,1)S(1)}, bf16[16,257,1408]{2,1,0:T(8,128)(2,1)}, u32[]{:S(2)}) %copy-start) | copy-done | bytes 11579416
  61.4 11.1 %shard_map.467.refs_3_.refs_6_ = bf16[16,384,384]{2,1,0:T(8,128)(2,1)S(1)} custom-call(bf16[16,257,1408]{2,1,0:T(8,128)(2,1)S(1)} %copy-done, f32[8,384]{1,0:T(8,128)S(1)} %concatenate.84.bias, bf16[1408,384]{1,0:T(8,128)(2,1)S(1)} %copy-done.22), custom_call_target="tpu_custom_call" | custom-call | flops 1000 | bytes 1000 | tf_op jit(solution)/shard_map/pallas_call | solution.py:440
  74.5 3.0 collective-permute-start.6
  81.4 10.3 %shard_map.468 = (bf16[4,256,384]{2,1,0:T(8,128)(2,1)S(1)}, bf16[4,256,192]{2,1,0:T(8,128)(2,1)S(1)}, bf16[4,256,192]{2,1,0:T(8,128)(2,1)S(1)}, f32[256,768]{1,0...) custom-call(s32[16]{0:T(128)S(1)} %copy-done.51, ...), custom_call_target="tpu_custom_call" | custom-call | flops 1000 | bytes 1000 | tf_op jit(solution)/shard_map/pallas_call | solution.py:440
  97.8 6.0 %collective-permute-done.15.refs_2_ = bf16[128,384]{1,0:T(8,128)(2,1)S(1)} collective-permute-done((bf16[128,384]{1,0:T(8,128)(2,1)S(1)}, bf16[128,384]{1,0:T(8,128)(2,1)S(1)}, u32[]{:S(2)}, u32[]{:S(2)}) %collective-permute-start.15) | collective-permute-done | bytes 98336 | tf_op jit(solution)/shard_map/ppermute | solution.py:51
  106.0 2.6 collective-permute-done.16.refs_1_
  108.6 6.2 %shard_map.469 = (bf16[128,192]{1,0:T(8,128)(2,1)S(1)}, bf16[128,384]{1,0:T(8,128)(2,1)S(1)}, bf16[128,384]{1,0:T(8,128)(2,1)S(1)}) custom-call(bf16[128,192]{1,0:T(8,128)(2,1)S(1)} %get-tuple-element.229.refs_0_, bf16[128,384]{1,0:T(8,128)(2,1)S(1)} %collective-permute-done.16.refs_1_, bf16[128,384]{1,0:T(8,128)(2,1)S(1)} %collective-permute-done.15.refs_2_, ...), custom_call_target="tpu_custom_call" | custom-call | flops 1000 | bytes 1000 | tf_op jit(solution)/shard_map/pallas_call | solution.py:440
  115.2 6.6 %collective-permute-done.18.rest_2_ = bf16[128,384]{1,0:T(8,128)(2,1)S(1)} collective-permute-done((bf16[128,384]{1,0:T(8,128)(2,1)S(1)}, bf16[128,384]{1,0:T(8,128)(2,1)S(1)}, u32[]{:S(2)}, u32[]{:S(2)}) %collective-permute-start.18) | collective-permute-done | bytes 98336 | tf_op jit(solution)/shard_map/ppermute | solution.py:51
  123.3 3.2 collective-permute-done.19.rest_1_
  128.6 1.5 shard_map.470
  130.2 12.1 %collective-permute-done.23 = bf16[4,96,768]{2,1,0:T(8,128)(2,1)S(1)} collective-permute-done((bf16[4,96,768]{2,1,0:T(8,128)(2,1)S(1)}, bf16[4,96,768]{2,1,0:T(8,128)(2,1)S(1)}, u32[]{:S(2)}, u32[]{:S(2)}) %collective-permute-start.23) | collective-permute-done | bytes 589856 | tf_op jit(solution)/shard_map/ppermute | solution.py:46
  144.1 3.1 collective-permute-done.27.rest_3_
  148.2 14.3 %shard_map.471 = (bf16[2,4,32,768]{3,2,1,0:T(8,128)(2,1)S(1)}, f32[128,768]{1,0:T(8,128)S(1)}, bf16[128,768]{1,0:T(8,128)(2,1)S(1)}, f32[3,768]{1,0:T(4,128)S(1)...) custom-call(f32[12,768]{1,0:T(8,128)S(1)} %copy-done.6, ...), custom_call_target="tpu_custom_call" | custom-call | flops 1000 | bytes 1000 | tf_op jit(solution)/shard_map/pallas_call | solution.py:440
  163.2 6.9 %collective-permute-done.29.got = bf16[128,768]{1,0:T(8,128)(2,1)S(1)} collective-permute-done((bf16[128,768]{1,0:T(8,128)(2,1)S(1)}, bf16[128,768]{1,0:T(8,128)(2,1)S(1)}, u32[]{:S(2)}, u32[]{:S(2)}) %collective-permute-start.29) | collective-permute-done | bytes 196640 | tf_op jit(solution)/shard_map/ppermute | solution.py:51
  170.8 2.5 add_convert_fusion.3
  176.8 2.0 collective-permute-start.34
  178.8 4.5 %collective-permute-done.32.refs_5_ = bf16[128,384]{1,0:T(8,128)(2,1)S(1)} collective-permute-done((bf16[128,384]{1,0:T(8,128)(2,1)S(1)}, bf16[128,384]{1,0:T(8,128)(2,1)S(1)}, u32[]{:S(2)}, u32[]{:S(2)}) %collective-permute-start.32) | collective-permute-done | bytes 98336 | tf_op jit(solution)/shard_map/ppermute | solution.py:51
  183.5 8.2 %collective-permute-done.33.refs_4_ = bf16[128,384]{1,0:T(8,128)(2,1)S(1)} collective-permute-done((bf16[128,384]{1,0:T(8,128)(2,1)S(1)}, bf16[128,384]{1,0:T(8,128)(2,1)S(1)}, u32[]{:S(2)}, u32[]{:S(2)}) %collective-permute-start.33) | collective-permute-done | bytes 98336 | tf_op jit(solution)/shard_map/ppermute | solution.py:51
  192.6 9.8 %shard_map.473 = (bf16[16,384,384]{2,1,0:T(8,128)(2,1)S(1)}, f32[1,192]{1,0:T(1,128)S(1)}, bf16[128,192]{1,0:T(8,128)(2,1)S(1)}, bf16[128,384]{1,0:T(8,128)(2,1)S(1)}, bf16[128,384]{1,0:T(8,128)(2,1)S(1)}) custom-call(bf16[128,192]{1,0:T(8,128)(2,1)S(1)} %get-tuple-element.229.refs_0_, bf16[128,384]{1,0:T(8,128)(2,1)S(1)} %collective-permute-done.16.refs_1_, ...), custom_call_target="tpu_custom_call" | custom-call | flops 1000 | bytes 1000 | tf_op jit(solution)/shard_map/pallas_call | solution.py:440
  206.2 1.5 collective-permute-start.40
  207.8 2.9 collective-permute-start.37
  210.7 5.6 %collective-permute-done.37.rest_2_.rest_6_ = bf16[128,384]{1,0:T(8,128)(2,1)S(1)} collective-permute-done((bf16[128,384]{1,0:T(8,128)(2,1)S(1)}, bf16[128,384]{1,0:T(8,128)(2,1)S(1)}, u32[]{:S(2)}, u32[]{:S(2)}) %collective-permute-start.37) | collective-permute-done | bytes 98336 | tf_op jit(solution)/shard_map/ppermute | solution.py:51
  216.4 8.9 %shard_map.474 = bf16[1408,384]{1,0:T(8,128)(2,1)} custom-call(bf16[16,257,1408]{2,1,0:T(8,128)(2,1)} %copy.55.images, bf16[16,384,384]{2,1,0:T(8,128)(2,1)S(1)} %get-tuple-element.296.kv_back), custom_call_target="tpu_custom_call" | custom-call | flops 1000 | bytes 1000 | tf_op jit(solution)/shard_map/pallas_call | solution.py:440
  225.4 1.9 add_convert_fusion.23
  230.5 1.5 shard_map.475
  232.5 2.6 shard_map.476
  236.6 2.6 collective-permute-start.42
  240.5 13.7 %shard_map.477 = (bf16[256,768]{1,0:T(8,128)(2,1)}, f32[24,768]{1,0:T(8,128)}, bf16[4,256,384]{2,1,0:T(8,128)(2,1)}, bf16[4,256,192]{2,1,0:T(8,128)(2,1)}) custom-call(s32[16]{0:T(128)} %lengths.3, f32[12,768]{1,0:T(8,128)} %rest_0_.3, f32[256,768]{1,0:T(8,128)} %copy-done.8, bf16[4,256,384]{2,1,0:T(8,128)(2,1)} %copy-done.25, ...), custom_call_target="tpu_custom_call" | custom-call | flops 1000 | bytes 1000 | tf_op jit(solution)/shard_map/pallas_call | solution.py:440
  255.2 5.7 %collective-permute-start.47 = (bf16[256,768]{1,0:T(8,128)(2,1)}, bf16[256,768]{1,0:T(8,128)(2,1)S(1)}, u32[]{:S(2)}, u32[]{:S(2)}) collective-permute-start(bf16[256,768]{1,0:T(8,128)(2,1)} %get-tuple-element.327.own), channel_id=1, source_target_pairs={{0,1},{1,0},{2,3},{3,2},{4,5},{5,4},{6,7},{7,6},{8,9},{9,8},{10,11... | collective-permute-start | bytes 1179656 | tf_op jit(solution)/shard_map/ppermute | solution.py:51
  264.5 1.5 collective-permute-start.48
  266.0 4.1 %shard_map.478 = (bf16[16,96,384]{2,1,0:T(8,128)(2,1)S(1)}, bf16[16,96,384]{2,1,0:T(8,128)(2,1)}, bf16[16,96,384]{2,1,0:T(8,128)(2,1)S(1)}, bf16[16,96,384]{2,1,0:T(8,128)(2,1)}) custom-call(bf16[16,64,768]{2,1,0:T(8,128)(2,1)S(1)} %copy-done.5, f32[12,768]{1,0:T(8,128)S(1)} %copy-done.7, f32[256,768]{1,0:T(8,128)S(1)} %get-tuple-element.246.z_first.rest_1_, ...), custom_call_target="tpu_custom_call" | custom-call | flops 1000 | bytes 1000 | tf_op jit(solution)/shard_map/pallas_call | solution.py:440
  271.2 1.7 collective-permute-done.49
  274.0 1.9 collective-permute-start.54
  278.0 1.5 collective-permute-start.52
  281.4 2.5 shard_map.480
  284.8 5.7 %collective-permute-done.54 = bf16[2,96,768]{2,1,0:T(8,128)(2,1)} collective-permute-done((bf16[2,96,768]{2,1,0:T(8,128)(2,1)}, bf16[2,96,768]{2,1,0:T(8,128)(2,1)}, u32[]{:S(2)}, u32[]{:S(2)}) %collective-permute-start.54) | collective-permute-done | bytes 294944 | tf_op jit(solution)/shard_map/ppermute | solution.py:51
  292.5 1.5 add_convert_fusion.4
  295.2 1.5 add_convert_fusion.5
  296.8 1.5 collective-permute-start.55
  298.3 2.7 collective-permute-start.59
  302.2 1.4 collective-permute-start.63
  303.6 1.7 collective-permute-done.58.far_own
  305.3 1.6 collective-permute-done.59
  306.9 2.0 collective-permute-done.56
  308.9 2.5 collective-permute-done.55
  311.6 1.8 collective-permute-start.61
  316.5 3.7 %collective-permute-start.62 = (f32[24,768]{1,0:T(8,128)S(1)}, f32[24,768]{1,0:T(8,128)S(1)}, u32[]{:S(2)}, u32[]{:S(2)}) collective-permute-start(f32[24,768]{1,0:T(8,128)S(1)} %add.270), channel_id=1, source_target_pairs={{0,2},{1,3},{2,0},{3,1},{4,6},{5,7},{6,4},{7,5},{8,10},{9,11},{10,... | collective-permute-start | bytes 221192 | tf_op jit(solution)/shard_map/ppermute | solution.py:51
  321.1 1.5 collective-permute-done.62
  322.6 4.4 %collective-permute-done.64.far_near = bf16[256,768]{1,0:T(8,128)(2,1)S(1)} collective-permute-done((bf16[256,768]{1,0:T(8,128)(2,1)S(1)}, bf16[256,768]{1,0:T(8,128)(2,1)S(1)}, u32[]{:S(2)}, u32[]{:S(2)}) %collective-permute-start.64) | collective-permute-done | bytes 393248 | tf_op jit(solution)/shard_map/ppermute | solution.py:140
  327.0 1.5 collective-permute-start.65
  329.0 3.0 collective-permute-start.68
  332.0 1.4 collective-permute-start.69
  335.5 1.9 shard_map.479
  338.6 3.2 shard_map.481
  341.9 5.1 %collective-permute-done.68 = bf16[288,384]{1,0:T(8,128)(2,1)S(1)} collective-permute-done((bf16[288,384]{1,0:T(8,128)(2,1)S(1)}, bf16[288,384]{1,0:T(8,128)(2,1)S(1)}, u32[]{:S(2)}, u32[]{:S(2)}) %collective-permute-start.68) | collective-permute-done | bytes 221216 | tf_op jit(solution)/shard_map/ppermute | solution.py:51
  (399 shorter events, 80.9 us)
Async XLA Ops:
  7.2 48.6 %all-gather.2.cloned.1.call-start = ((), (), s32[]{:S(2)}) async-start(), calls=%async_computation.1 | async-start | bytes 1216512 | tf_op jit(solution)/shard_map/all_gather | solution.py:1387
  10.1 19.8 %collective-permute-start = (bf16[312,384]{1,0:T(8,128)(2,1)S(1)}, bf16[312,384]{1,0:T(8,128)(2,1)}, u32[]{:S(2)}, u32[]{:S(2)}) collective-permute-start(bf16[312,384]{1,0:T(8,128)(2,1)S(1)} %constant_dynamic-update-slice_fusion), channel_id=1, source_target_pairs={{0,1},{1,0},{2,3},{3,2},{4,5},{5,4},{6,7},{7,6},{8,9},{9,8},{10,11... | collective-permute-start | bytes 718856 | tf_op jit(solution)/shard_map/ppermute | solution.py:51
  13.2 19.9 %collective-permute-start.1 = (bf16[312,384]{1,0:T(8,128)(2,1)S(1)}, bf16[312,384]{1,0:T(8,128)(2,1)S(1)}, u32[]{:S(2)}, u32[]{:S(2)}) collective-permute-start(bf16[312,384]{1,0:T(8,128)(2,1)S(1)} %constant_dynamic-update-slice_fusion), channel_id=1, source_target_pairs={{0,2},{1,3},{2,0},{3,1},{4,6},{5,7},{6,4},{7,5},{8,10},{9,11},{10,... | collective-permute-start | bytes 718856 | tf_op jit(solution)/shard_map/ppermute | solution.py:51
  15.8 17.3 %collective-permute-start.2 = (bf16[312,384]{1,0:T(8,128)(2,1)S(1)}, bf16[312,384]{1,0:T(8,128)(2,1)S(1)}, u32[]{:S(2)}, u32[]{:S(2)}) collective-permute-start(bf16[312,384]{1,0:T(8,128)(2,1)S(1)} %constant_dynamic-update-slice_fusion), channel_id=1, source_target_pairs={{0,3},{1,2},{2,1},{3,0},{4,7},{5,6},{6,5},{7,4},{8,11},{9,10},{10,... | collective-permute-start | bytes 718856 | tf_op jit(solution)/shard_map/ppermute | solution.py:51
  16.7 267.2 %reduce-scatter.2.cloned.1.call-start = ((), (), s32[]{:S(2)}) async-start(), calls=%async_computation.2 | async-start | bytes 1216512 | tf_op jit(solution)/shard_map/reduce_scatter | solution.py:1516
  35.2 12.7 %collective-permute-start.4 = (bf16[4,144,384]{2,1,0:T(8,128)(2,1)S(1)}, bf16[4,144,384]{2,1,0:T(8,128)(2,1)S(1)}, u32[]{:S(2)}, u32[]{:S(2)}) collective-permute-start(bf16[4,144,384]{2,1,0:T(8,128)(2,1)S(1)} %pad_maximum_fusion.10), channel_id=1, source_target_pairs={{0,8},{8,0},{1,9},{9,1},{2,10},{10,2},{3,11},{11,3},{4,12},{12,4},... | collective-permute-start | bytes 1327112 | tf_op jit(solution)/shard_map/ppermute | solution.py:46
  36.9 12.0 %collective-permute-start.3 = (bf16[4,144,384]{2,1,0:T(8,128)(2,1)S(1)}, bf16[4,144,384]{2,1,0:T(8,128)(2,1)S(1)}, u32[]{:S(2)}, u32[]{:S(2)}) collective-permute-start(bf16[4,144,384]{2,1,0:T(8,128)(2,1)S(1)} %pad_maximum_fusion.9), channel_id=1, source_target_pairs={{0,16},{16,0},{1,17},{17,1},{2,18},{18,2},{3,19},{19,3},{4,20},{20... | collective-permute-start | bytes 1327112 | tf_op jit(solution)/shard_map/ppermute | solution.py:46
  38.4 9.5 %collective-permute-start.5 = (bf16[192,768]{1,0:T(8,128)(2,1)S(1)}, bf16[192,768]{1,0:T(8,128)(2,1)S(1)}, u32[]{:S(2)}, u32[]{:S(2)}) collective-permute-start(bf16[192,768]{1,0:T(8,128)(2,1)S(1)} %get-tuple-element.211), channel_id=1, source_target_pairs={{0,1},{1,0},{2,3},{3,2},{4,5},{5,4},{6,7},{7,6},{8,9},{9,8},{10,11... | collective-permute-start | bytes 884744 | tf_op jit(solution)/shard_map/ppermute | solution.py:51
  49.0 23.7 %collective-permute-start.10 = (bf16[8,144,384]{2,1,0:T(8,128)(2,1)S(1)}, bf16[8,144,384]{2,1,0:T(8,128)(2,1)S(1)}, u32[]{:S(2)}, u32[]{:S(2)}) collective-permute-start(bf16[8,144,384]{2,1,0:T(8,128)(2,1)S(1)} %constant_dynamic-update-slice_fusion.10.rest_4_), channel_id=1, source_target_pairs={{0,4},{4,0},{1,5},{5,1},{2,6},{6,2},{3,7},{7,3},{8,12},{12,8},{9,1... | collective-permute-start | bytes 2654216 | tf_op jit(solution)/shard_map/ppermute | solution.py:46
  49.1 23.6 %collective-permute-start.8 = (bf16[8,144,384]{2,1,0:T(8,128)(2,1)S(1)}, bf16[8,144,384]{2,1,0:T(8,128)(2,1)}, u32[]{:S(2)}, u32[]{:S(2)}) collective-permute-start(bf16[8,144,384]{2,1,0:T(8,128)(2,1)S(1)} %constant_dynamic-update-slice_fusion.10.rest_4_), channel_id=1, source_target_pairs={{0,16},{16,0},{1,17},{17,1},{2,18},{18,2},{3,19},{19,3},{4,20},{20... | collective-permute-start | bytes 2654216 | tf_op jit(solution)/shard_map/ppermute | solution.py:46
  50.5 22.2 %collective-permute-start.7 = (bf16[8,144,384]{2,1,0:T(8,128)(2,1)S(1)}, bf16[8,144,384]{2,1,0:T(8,128)(2,1)}, u32[]{:S(2)}, u32[]{:S(2)}) collective-permute-start(bf16[8,144,384]{2,1,0:T(8,128)(2,1)S(1)} %constant_dynamic-update-slice_fusion.5.rest_0_), channel_id=1, source_target_pairs={{0,8},{8,0},{1,9},{9,1},{2,10},{10,2},{3,11},{11,3},{4,12},{12,4},... | collective-permute-start | bytes 2654216 | tf_op jit(solution)/shard_map/ppermute | solution.py:46
  51.3 21.4 %collective-permute-start.9 = (bf16[8,144,384]{2,1,0:T(8,128)(2,1)S(1)}, bf16[8,144,384]{2,1,0:T(8,128)(2,1)}, u32[]{:S(2)}, u32[]{:S(2)}) collective-permute-start(bf16[8,144,384]{2,1,0:T(8,128)(2,1)S(1)} %constant_dynamic-update-slice_fusion.5.rest_0_), channel_id=1, source_target_pairs={{0,4},{4,0},{1,5},{5,1},{2,6},{6,2},{3,7},{7,3},{8,12},{12,8},{9,1... | collective-permute-start | bytes 2654216 | tf_op jit(solution)/shard_map/ppermute | solution.py:46
  52.1 20.5 %collective-permute-start.11 = (bf16[2,96,768]{2,1,0:T(8,128)(2,1)S(1)}, bf16[2,96,768]{2,1,0:T(8,128)(2,1)S(1)}, u32[]{:S(2)}, u32[]{:S(2)}) collective-permute-start(bf16[2,96,768]{2,1,0:T(8,128)(2,1)S(1)} %get-tuple-element.463), channel_id=1, source_target_pairs={{0,2},{1,3},{2,0},{3,1},{4,6},{5,7},{6,4},{7,5},{8,10},{9,11},{10,... | collective-permute-start | bytes 884744 | tf_op jit(solution)/shard_map/ppermute | solution.py:51
  73.3 21.4 %collective-permute-start.14 = (bf16[4,96,768]{2,1,0:T(8,128)(2,1)S(1)}, bf16[4,96,768]{2,1,0:T(8,128)(2,1)S(1)}, u32[]{:S(2)}, u32[]{:S(2)}) collective-permute-start(bf16[4,96,768]{2,1,0:T(8,128)(2,1)S(1)} %pad_maximum_fusion.5), channel_id=1, source_target_pairs={{0,16},{16,0},{1,17},{17,1},{2,18},{18,2},{3,19},{19,3},{4,20},{20... | collective-permute-start | bytes 1769480 | tf_op jit(solution)/shard_map/ppermute | solution.py:46
  74.5 20.2 %collective-permute-start.6 = (bf16[2,96,768]{2,1,0:T(8,128)(2,1)}, bf16[2,96,768]{2,1,0:T(8,128)(2,1)S(1)}, u32[]{:S(2)}, u32[]{:S(2)}) collective-permute-start(bf16[2,96,768]{2,1,0:T(8,128)(2,1)} %get-tuple-element.464), channel_id=1, source_target_pairs={{0,2},{1,3},{2,0},{3,1},{4,6},{5,7},{6,4},{7,5},{8,10},{9,11},{10,... | collective-permute-start | bytes 884744 | tf_op jit(solution)/shard_map/ppermute | solution.py:51
  96.0 18.9 %collective-permute-start.17 = (bf16[4,96,768]{2,1,0:T(8,128)(2,1)S(1)}, bf16[4,96,768]{2,1,0:T(8,128)(2,1)S(1)}, u32[]{:S(2)}, u32[]{:S(2)}) collective-permute-start(bf16[4,96,768]{2,1,0:T(8,128)(2,1)S(1)} %pad_maximum_fusion.6), channel_id=1, source_target_pairs={{0,8},{8,0},{1,9},{9,1},{2,10},{10,2},{3,11},{11,3},{4,12},{12,4},... | collective-permute-start | bytes 1769480 | tf_op jit(solution)/shard_map/ppermute | solution.py:46
  103.9 19.4 %collective-permute-start.20 = (bf16[4,96,768]{2,1,0:T(8,128)(2,1)S(1)}, bf16[4,96,768]{2,1,0:T(8,128)(2,1)S(1)}, u32[]{:S(2)}, u32[]{:S(2)}) collective-permute-start(bf16[4,96,768]{2,1,0:T(8,128)(2,1)S(1)} %pad_maximum_fusion.5), channel_id=1, source_target_pairs={{0,8},{8,0},{1,9},{9,1},{2,10},{10,2},{3,11},{11,3},{4,12},{12,4},... | collective-permute-start | bytes 1769480 | tf_op jit(solution)/shard_map/ppermute | solution.py:46
  105.1 18.2 %collective-permute-start.21 = (bf16[4,96,768]{2,1,0:T(8,128)(2,1)S(1)}, bf16[4,96,768]{2,1,0:T(8,128)(2,1)S(1)}, u32[]{:S(2)}, u32[]{:S(2)}) collective-permute-start(bf16[4,96,768]{2,1,0:T(8,128)(2,1)S(1)} %pad_maximum_fusion.6), channel_id=1, source_target_pairs={{0,16},{16,0},{1,17},{17,1},{2,18},{18,2},{3,19},{19,3},{4,20},{20... | collective-permute-start | bytes 1769480 | tf_op jit(solution)/shard_map/ppermute | solution.py:46
  114.8 6.9 %collective-permute-start.18 = (bf16[128,384]{1,0:T(8,128)(2,1)S(1)}, bf16[128,384]{1,0:T(8,128)(2,1)S(1)}, u32[]{:S(2)}, u32[]{:S(2)}) collective-permute-start(bf16[128,384]{1,0:T(8,128)(2,1)S(1)} %get-tuple-element.239), channel_id=1, source_target_pairs={{0,2},{1,3},{2,0},{3,1},{4,6},{5,7},{6,4},{7,5},{8,10},{9,11},{10,... | collective-permute-start | bytes 294920 | tf_op jit(solution)/shard_map/ppermute | solution.py:51
  126.5 17.0 %collective-permute-start.24 = (bf16[8,96,768]{2,1,0:T(8,128)(2,1)S(1)}, bf16[8,96,768]{2,1,0:T(8,128)(2,1)S(1)}, u32[]{:S(2)}, u32[]{:S(2)}) collective-permute-start(bf16[8,96,768]{2,1,0:T(8,128)(2,1)S(1)} %pad_maximum_fusion.1.rest_0_), channel_id=1, source_target_pairs={{0,4},{4,0},{1,5},{5,1},{2,6},{6,2},{3,7},{7,3},{8,12},{12,8},{9,1... | collective-permute-start | bytes 3538952 | tf_op jit(solution)/shard_map/ppermute | solution.py:46
  126.5 17.0 %collective-permute-start.25 = (bf16[8,96,768]{2,1,0:T(8,128)(2,1)S(1)}, bf16[8,96,768]{2,1,0:T(8,128)(2,1)S(1)}, u32[]{:S(2)}, u32[]{:S(2)}) collective-permute-start(bf16[8,96,768]{2,1,0:T(8,128)(2,1)S(1)} %pad_maximum_fusion.rest_4_), channel_id=1, source_target_pairs={{0,4},{4,0},{1,5},{5,1},{2,6},{6,2},{3,7},{7,3},{8,12},{12,8},{9,1... | collective-permute-start | bytes 3538952 | tf_op jit(solution)/shard_map/ppermute | solution.py:46
  127.0 15.3 %collective-permute-start.23 = (bf16[4,96,768]{2,1,0:T(8,128)(2,1)S(1)}, bf16[4,96,768]{2,1,0:T(8,128)(2,1)S(1)}, u32[]{:S(2)}, u32[]{:S(2)}) collective-permute-start(bf16[4,96,768]{2,1,0:T(8,128)(2,1)S(1)} %slice.415), channel_id=1, source_target_pairs={{0,16},{16,0},{1,17},{17,1},{2,18},{18,2},{3,19},{19,3},{4,20},{20... | collective-permute-start | bytes 1769480 | tf_op jit(solution)/shard_map/ppermute | solution.py:46
  128.3 15.0 %collective-permute-start.22 = (bf16[4,96,768]{2,1,0:T(8,128)(2,1)S(1)}, bf16[4,96,768]{2,1,0:T(8,128)(2,1)S(1)}, u32[]{:S(2)}, u32[]{:S(2)}) collective-permute-start(bf16[4,96,768]{2,1,0:T(8,128)(2,1)S(1)} %slice.414), channel_id=1, source_target_pairs={{0,8},{8,0},{1,9},{9,1},{2,10},{10,2},{3,11},{11,3},{4,12},{12,4},... | collective-permute-start | bytes 1769480 | tf_op jit(solution)/shard_map/ppermute | solution.py:46
  130.1 13.3 %collective-permute-start.26 = (bf16[128,768]{1,0:T(8,128)(2,1)S(1)}, bf16[128,768]{1,0:T(8,128)(2,1)S(1)}, u32[]{:S(2)}, u32[]{:S(2)}) collective-permute-start(bf16[128,768]{1,0:T(8,128)(2,1)S(1)} %get-tuple-element.253), channel_id=1, source_target_pairs={{0,1},{1,0},{2,3},{3,2},{4,5},{5,4},{6,7},{7,6},{8,9},{9,8},{10,11... | collective-permute-start | bytes 589832 | tf_op jit(solution)/shard_map/ppermute | solution.py:51
  162.6 7.5 %collective-permute-start.30 = (bf16[16,96,768]{2,1,0:T(8,128)(2,1)}, bf16[16,96,768]{2,1,0:T(8,128)(2,1)S(1)}, u32[]{:S(2)}, u32[]{:S(2)}) collective-permute-start(bf16[16,96,768]{2,1,0:T(8,128)(2,1)} %get-tuple-element.267), channel_id=1, source_target_pairs={{0,4},{4,0},{1,5},{5,1},{2,6},{6,2},{3,7},{7,3},{8,12},{12,8},{9,1... | collective-permute-start | bytes 7077896 | tf_op jit(solution)/shard_map/ppermute | solution.py:46
  162.8 8.0 %collective-permute-start.31 = (bf16[16,96,768]{2,1,0:T(8,128)(2,1)}, bf16[16,96,768]{2,1,0:T(8,128)(2,1)S(1)}, u32[]{:S(2)}, u32[]{:S(2)}) collective-permute-start(bf16[16,96,768]{2,1,0:T(8,128)(2,1)} %get-tuple-element.268), channel_id=1, source_target_pairs={{0,4},{4,0},{1,5},{5,1},{2,6},{6,2},{3,7},{7,3},{8,12},{12,8},{9,1... | collective-permute-start | bytes 7077896 | tf_op jit(solution)/shard_map/ppermute | solution.py:46
  163.2 6.9 %collective-permute-start.29 = (bf16[128,768]{1,0:T(8,128)(2,1)S(1)}, bf16[128,768]{1,0:T(8,128)(2,1)S(1)}, u32[]{:S(2)}, u32[]{:S(2)}) collective-permute-start(bf16[128,768]{1,0:T(8,128)(2,1)S(1)} %get-tuple-element.266), channel_id=1, source_target_pairs={{0,1},{1,0},{2,3},{3,2},{4,5},{5,4},{6,7},{7,6},{8,9},{9,8},{10,11... | collective-permute-start | bytes 589832 | tf_op jit(solution)/shard_map/ppermute | solution.py:51
  173.3 29.2 %collective-permute-start.35 = (bf16[8,96,768]{2,1,0:T(8,128)(2,1)S(1)}, bf16[8,96,768]{2,1,0:T(8,128)(2,1)S(1)}, u32[]{:S(2)}, u32[]{:S(2)}) collective-permute-start(bf16[8,96,768]{2,1,0:T(8,128)(2,1)S(1)} %get-tuple-element.428), channel_id=1, source_target_pairs={{0,8},{8,0},{1,9},{9,1},{2,10},{10,2},{3,11},{11,3},{4,12},{12,4},... | collective-permute-start | bytes 3538952 | tf_op jit(solution)/shard_map/ppermute | solution.py:46
  174.3 28.2 %collective-permute-start.36 = (bf16[8,96,768]{2,1,0:T(8,128)(2,1)S(1)}, bf16[8,96,768]{2,1,0:T(8,128)(2,1)S(1)}, u32[]{:S(2)}, u32[]{:S(2)}) collective-permute-start(bf16[8,96,768]{2,1,0:T(8,128)(2,1)S(1)} %get-tuple-element.429), channel_id=1, source_target_pairs={{0,16},{16,0},{1,17},{17,1},{2,18},{18,2},{3,19},{19,3},{4,20},{20... | collective-permute-start | bytes 3538952 | tf_op jit(solution)/shard_map/ppermute | solution.py:46
  176.5 6.9 %collective-permute-start.32 = (bf16[128,384]{1,0:T(8,128)(2,1)S(1)}, bf16[128,384]{1,0:T(8,128)(2,1)S(1)}, u32[]{:S(2)}, u32[]{:S(2)}) collective-permute-start(bf16[128,384]{1,0:T(8,128)(2,1)S(1)} %get-tuple-element.280), channel_id=1, source_target_pairs={{0,2},{1,3},{2,0},{3,1},{4,6},{5,7},{6,4},{7,5},{8,10},{9,11},{10,... | collective-permute-start | bytes 294920 | tf_op jit(solution)/shard_map/ppermute | solution.py:51
  176.8 14.8 %collective-permute-start.34 = (bf16[2,4,32,768]{3,2,1,0:T(8,128)(2,1)S(1)}, bf16[2,4,32,768]{3,2,1,0:T(8,128)(2,1)S(1)}, u32[]{:S(2)}, u32[]{:S(2)}) collective-permute-start(bf16[2,4,32,768]{3,2,1,0:T(8,128)(2,1)S(1)} %get-tuple-element.281), channel_id=1, source_target_pairs={{0,1},{1,0},{2,3},{3,2},{4,5},{5,4},{6,7},{7,6},{8,9},{9,8},{10,11... | collective-permute-start | bytes 1179656 | tf_op jit(solution)/shard_map/ppermute | solution.py:51
  183.4 8.2 %collective-permute-start.33 = (bf16[128,384]{1,0:T(8,128)(2,1)S(1)}, bf16[128,384]{1,0:T(8,128)(2,1)S(1)}, u32[]{:S(2)}, u32[]{:S(2)}) collective-permute-start(bf16[128,384]{1,0:T(8,128)(2,1)S(1)} %broadcast_select_fusion.1), channel_id=1, source_target_pairs={{0,1},{1,0},{2,3},{3,2},{4,5},{5,4},{6,7},{7,6},{8,9},{9,8},{10,11... | collective-permute-start | bytes 294920 | tf_op jit(solution)/shard_map/ppermute | solution.py:51
  191.8 33.6 %collective-permute-start.41 = (bf16[2,2,4,32,768]{4,3,2,1,0:T(8,128)(2,1)S(1)}, bf16[2,2,4,32,768]{4,3,2,1,0:T(8,128)(2,1)S(1)}, u32[]{:S(2)}, u32[]{:S(2)}) collective-permute-start(bf16[2,2,4,32,768]{4,3,2,1,0:T(8,128)(2,1)S(1)} %pad_maximum_fusion.4.two), channel_id=1, source_target_pairs={{1,2},{2,1},{5,6},{6,5},{9,10},{10,9},{13,14},{14,13},{17,18},{18,... | collective-permute-start | bytes 2359304 | tf_op jit(solution)/shard_map/ppermute | solution.py:134
  203.8 21.6 %collective-permute-start.39 = (bf16[4,96,768]{2,1,0:T(8,128)(2,1)}, bf16[4,96,768]{2,1,0:T(8,128)(2,1)}, u32[]{:S(2)}, u32[]{:S(2)}) collective-permute-start(bf16[4,96,768]{2,1,0:T(8,128)(2,1)} %get-tuple-element.436), channel_id=1, source_target_pairs={{0,16},{16,0},{1,17},{17,1},{2,18},{18,2},{3,19},{19,3},{4,20},{20... | collective-permute-start | bytes 1769480 | tf_op jit(solution)/shard_map/ppermute | solution.py:46
  206.2 19.1 %collective-permute-start.40 = (bf16[4,96,768]{2,1,0:T(8,128)(2,1)}, bf16[4,96,768]{2,1,0:T(8,128)(2,1)}, u32[]{:S(2)}, u32[]{:S(2)}) collective-permute-start(bf16[4,96,768]{2,1,0:T(8,128)(2,1)} %get-tuple-element.437), channel_id=1, source_target_pairs={{0,8},{8,0},{1,9},{9,1},{2,10},{10,2},{3,11},{11,3},{4,12},{12,4},... | collective-permute-start | bytes 1769480 | tf_op jit(solution)/shard_map/ppermute | solution.py:46
  207.8 8.5 %collective-permute-start.37 = (bf16[128,384]{1,0:T(8,128)(2,1)S(1)}, bf16[128,384]{1,0:T(8,128)(2,1)S(1)}, u32[]{:S(2)}, u32[]{:S(2)}) collective-permute-start(bf16[128,384]{1,0:T(8,128)(2,1)S(1)} %get-tuple-element.293), channel_id=1, source_target_pairs={{0,2},{1,3},{2,0},{3,1},{4,6},{5,7},{6,4},{7,5},{8,10},{9,11},{10,... | collective-permute-start | bytes 294920 | tf_op jit(solution)/shard_map/ppermute | solution.py:51
  216.3 9.1 %collective-permute-start.38 = (bf16[128,384]{1,0:T(8,128)(2,1)S(1)}, bf16[128,384]{1,0:T(8,128)(2,1)S(1)}, u32[]{:S(2)}, u32[]{:S(2)}) collective-permute-start(bf16[128,384]{1,0:T(8,128)(2,1)S(1)} %broadcast_select_fusion), channel_id=1, source_target_pairs={{0,1},{1,0},{2,3},{3,2},{4,5},{5,4},{6,7},{7,6},{8,9},{9,8},{10,11... | collective-permute-start | bytes 294920 | tf_op jit(solution)/shard_map/ppermute | solution.py:51
  235.1 19.1 %collective-permute-start.43 = (bf16[16,48,384]{2,1,0:T(8,128)(2,1)}, bf16[16,48,384]{2,1,0:T(8,128)(2,1)}, u32[]{:S(2)}, u32[]{:S(2)}) collective-permute-start(bf16[16,48,384]{2,1,0:T(8,128)(2,1)} %get-tuple-element.325), channel_id=1, source_target_pairs={{0,4},{4,0},{1,5},{5,1},{2,6},{6,2},{3,7},{7,3},{8,12},{12,8},{9,1... | collective-permute-start | bytes 1769480 | tf_op jit(solution)/shard_map/ppermute | solution.py:46
  235.2 19.0 %collective-permute-start.44 = (bf16[16,48,384]{2,1,0:T(8,128)(2,1)}, bf16[16,48,384]{2,1,0:T(8,128)(2,1)}, u32[]{:S(2)}, u32[]{:S(2)}) collective-permute-start(bf16[16,48,384]{2,1,0:T(8,128)(2,1)} %get-tuple-element.326), channel_id=1, source_target_pairs={{0,4},{4,0},{1,5},{5,1},{2,6},{6,2},{3,7},{7,3},{8,12},{12,8},{9,1... | collective-permute-start | bytes 1769480 | tf_op jit(solution)/shard_map/ppermute | solution.py:46
  236.6 17.6 %collective-permute-start.42 = (bf16[2,96,768]{2,1,0:T(8,128)(2,1)}, bf16[2,96,768]{2,1,0:T(8,128)(2,1)S(1)}, u32[]{:S(2)}, u32[]{:S(2)}) collective-permute-start(bf16[2,96,768]{2,1,0:T(8,128)(2,1)} %get-tuple-element.462), channel_id=1, source_target_pairs={{0,2},{1,3},{2,0},{3,1},{4,6},{5,7},{6,4},{7,5},{8,10},{9,11},{10,... | collective-permute-start | bytes 884744 | tf_op jit(solution)/shard_map/ppermute | solution.py:51
  239.1 32.1 %collective-permute-start.46 = (bf16[2,2,4,32,768]{4,3,2,1,0:T(8,128)(2,1)S(1)}, bf16[2,2,4,32,768]{4,3,2,1,0:T(8,128)(2,1)}, u32[]{:S(2)}, u32[]{:S(2)}) collective-permute-start(bf16[2,2,4,32,768]{4,3,2,1,0:T(8,128)(2,1)S(1)} %copy-done.27), channel_id=1, source_target_pairs={{1,0},{2,3},{5,4},{6,7},{9,8},{10,11},{13,12},{14,15},{17,16},{18,... | collective-permute-start | bytes 2359304 | tf_op jit(solution)/shard_map/ppermute | solution.py:140
  254.2 18.7 %collective-permute-start.45 = (bf16[256,768]{1,0:T(8,128)(2,1)}, bf16[256,768]{1,0:T(8,128)(2,1)S(1)}, u32[]{:S(2)}, u32[]{:S(2)}) collective-permute-start(bf16[256,768]{1,0:T(8,128)(2,1)} %get-tuple-element.327.own), channel_id=1, source_target_pairs={{1,2},{2,1},{5,6},{6,5},{9,10},{10,9},{13,14},{14,13},{17,18},{18,... | collective-permute-start | bytes 1179656 | tf_op jit(solution)/shard_map/ppermute | solution.py:134
  255.2 18.3 %collective-permute-start.47 = (bf16[256,768]{1,0:T(8,128)(2,1)}, bf16[256,768]{1,0:T(8,128)(2,1)S(1)}, u32[]{:S(2)}, u32[]{:S(2)}) collective-permute-start(bf16[256,768]{1,0:T(8,128)(2,1)} %get-tuple-element.327.own), channel_id=1, source_target_pairs={{0,1},{1,0},{2,3},{3,2},{4,5},{5,4},{6,7},{7,6},{8,9},{9,8},{10,11... | collective-permute-start | bytes 1179656 | tf_op jit(solution)/shard_map/ppermute | solution.py:51
  262.3 10.6 %collective-permute-start.49 = (bf16[8,48,384]{2,1,0:T(8,128)(2,1)S(1)}, bf16[8,48,384]{2,1,0:T(8,128)(2,1)S(1)}, u32[]{:S(2)}, u32[]{:S(2)}) collective-permute-start(bf16[8,48,384]{2,1,0:T(8,128)(2,1)S(1)} %get-tuple-element.446), channel_id=1, source_target_pairs={{0,16},{16,0},{1,17},{17,1},{2,18},{18,2},{3,19},{19,3},{4,20},{20... | collective-permute-start | bytes 884744 | tf_op jit(solution)/shard_map/ppermute | solution.py:46
  264.5 8.4 %collective-permute-start.48 = (bf16[8,48,384]{2,1,0:T(8,128)(2,1)S(1)}, bf16[8,48,384]{2,1,0:T(8,128)(2,1)S(1)}, u32[]{:S(2)}, u32[]{:S(2)}) collective-permute-start(bf16[8,48,384]{2,1,0:T(8,128)(2,1)S(1)} %get-tuple-element.448), channel_id=1, source_target_pairs={{0,8},{8,0},{1,9},{9,1},{2,10},{10,2},{3,11},{11,3},{4,12},{12,4},... | collective-permute-start | bytes 884744 | tf_op jit(solution)/shard_map/ppermute | solution.py:46
  273.5 19.0 %collective-permute-start.50 = (bf16[16,96,384]{2,1,0:T(8,128)(2,1)}, bf16[16,96,384]{2,1,0:T(8,128)(2,1)}, u32[]{:S(2)}, u32[]{:S(2)}) collective-permute-start(bf16[16,96,384]{2,1,0:T(8,128)(2,1)} %get-tuple-element.339), channel_id=1, source_target_pairs={{0,4},{4,0},{1,5},{5,1},{2,6},{6,2},{3,7},{7,3},{8,12},{12,8},{9,1... | collective-permute-start | bytes 3538952 | tf_op jit(solution)/shard_map/ppermute | solution.py:46
  273.5 19.0 %collective-permute-start.51 = (bf16[16,96,384]{2,1,0:T(8,128)(2,1)}, bf16[16,96,384]{2,1,0:T(8,128)(2,1)}, u32[]{:S(2)}, u32[]{:S(2)}) collective-permute-start(bf16[16,96,384]{2,1,0:T(8,128)(2,1)} %get-tuple-element.340), channel_id=1, source_target_pairs={{0,4},{4,0},{1,5},{5,1},{2,6},{6,2},{3,7},{7,3},{8,12},{12,8},{9,1... | collective-permute-start | bytes 3538952 | tf_op jit(solution)/shard_map/ppermute | solution.py:46
  274.0 16.5 %collective-permute-start.54 = (bf16[2,96,768]{2,1,0:T(8,128)(2,1)}, bf16[2,96,768]{2,1,0:T(8,128)(2,1)}, u32[]{:S(2)}, u32[]{:S(2)}) collective-permute-start(bf16[2,96,768]{2,1,0:T(8,128)(2,1)} %get-tuple-element.461), channel_id=1, source_target_pairs={{0,2},{1,3},{2,0},{3,1},{4,6},{5,7},{6,4},{7,5},{8,10},{9,11},{10,... | collective-permute-start | bytes 884744 | tf_op jit(solution)/shard_map/ppermute | solution.py:51
  276.7 14.5 %collective-permute-start.53 = (bf16[4,48,384]{2,1,0:T(8,128)(2,1)}, bf16[4,48,384]{2,1,0:T(8,128)(2,1)}, u32[]{:S(2)}, u32[]{:S(2)}) collective-permute-start(bf16[4,48,384]{2,1,0:T(8,128)(2,1)} %get-tuple-element.460), channel_id=1, source_target_pairs={{0,8},{8,0},{1,9},{9,1},{2,10},{10,2},{3,11},{11,3},{4,12},{12,4},... | collective-permute-start | bytes 442376 | tf_op jit(solution)/shard_map/ppermute | solution.py:46
  278.0 14.5 %collective-permute-start.52 = (bf16[4,48,384]{2,1,0:T(8,128)(2,1)}, bf16[4,48,384]{2,1,0:T(8,128)(2,1)}, u32[]{:S(2)}, u32[]{:S(2)}) collective-permute-start(bf16[4,48,384]{2,1,0:T(8,128)(2,1)} %get-tuple-element.458), channel_id=1, source_target_pairs={{0,16},{16,0},{1,17},{17,1},{2,18},{18,2},{3,19},{19,3},{4,20},{20... | collective-permute-start | bytes 442376 | tf_op jit(solution)/shard_map/ppermute | solution.py:46
  290.5 11.7 %collective-permute-start.57 = (bf16[256,768]{1,0:T(8,128)(2,1)}, bf16[256,768]{1,0:T(8,128)(2,1)S(1)}, u32[]{:S(2)}, u32[]{:S(2)}) collective-permute-start(bf16[256,768]{1,0:T(8,128)(2,1)} %copy-done.45), channel_id=1, source_target_pairs={{1,2},{2,1},{5,6},{6,5},{9,10},{10,9},{13,14},{14,13},{17,18},{18,... | collective-permute-start | bytes 1179656 | tf_op jit(solution)/shard_map/ppermute | solution.py:134
  291.2 14.1 %collective-permute-start.58 = (bf16[256,768]{1,0:T(8,128)(2,1)}, bf16[256,768]{1,0:T(8,128)(2,1)S(1)}, u32[]{:S(2)}, u32[]{:S(2)}) collective-permute-start(bf16[256,768]{1,0:T(8,128)(2,1)} %copy-done.43), channel_id=1, source_target_pairs={{1,0},{2,3},{5,4},{6,7},{9,8},{10,11},{13,12},{14,15},{17,16},{18,... | collective-permute-start | bytes 1179656 | tf_op jit(solution)/shard_map/ppermute | solution.py:140
  294.1 14.9 %collective-permute-start.56 = (bf16[8,96,384]{2,1,0:T(8,128)(2,1)S(1)}, bf16[8,96,384]{2,1,0:T(8,128)(2,1)S(1)}, u32[]{:S(2)}, u32[]{:S(2)}) collective-permute-start(bf16[8,96,384]{2,1,0:T(8,128)(2,1)S(1)} %get-tuple-element.432), channel_id=1, source_target_pairs={{0,16},{16,0},{1,17},{17,1},{2,18},{18,2},{3,19},{19,3},{4,20},{20... | collective-permute-start | bytes 1769480 | tf_op jit(solution)/shard_map/ppermute | solution.py:46
  296.8 14.7 %collective-permute-start.55 = (bf16[8,96,384]{2,1,0:T(8,128)(2,1)S(1)}, bf16[8,96,384]{2,1,0:T(8,128)(2,1)S(1)}, u32[]{:S(2)}, u32[]{:S(2)}) collective-permute-start(bf16[8,96,384]{2,1,0:T(8,128)(2,1)S(1)} %get-tuple-element.434), channel_id=1, source_target_pairs={{0,8},{8,0},{1,9},{9,1},{2,10},{10,2},{3,11},{11,3},{4,12},{12,4},... | collective-permute-start | bytes 1769480 | tf_op jit(solution)/shard_map/ppermute | solution.py:46
  298.3 8.5 %collective-permute-start.59 = (f32[24,768]{1,0:T(8,128)S(1)}, f32[24,768]{1,0:T(8,128)S(1)}, u32[]{:S(2)}, u32[]{:S(2)}) collective-permute-start(f32[24,768]{1,0:T(8,128)S(1)} %copy-done.85), channel_id=1, source_target_pairs={{0,1},{1,0},{2,3},{3,2},{4,5},{5,4},{6,7},{7,6},{8,9},{9,8},{10,11... | collective-permute-start | bytes 221192 | tf_op jit(solution)/shard_map/ppermute | solution.py:51
  302.2 18.9 %collective-permute-start.63 = (bf16[192,768]{1,0:T(8,128)(2,1)S(1)}, bf16[192,768]{1,0:T(8,128)(2,1)S(1)}, u32[]{:S(2)}, u32[]{:S(2)}) collective-permute-start(bf16[192,768]{1,0:T(8,128)(2,1)S(1)} %get-tuple-element.444), channel_id=1, source_target_pairs={{0,1},{1,0},{2,3},{3,2},{4,5},{5,4},{6,7},{7,6},{8,9},{9,8},{10,11... | collective-permute-start | bytes 884744 | tf_op jit(solution)/shard_map/ppermute | solution.py:51
  311.6 11.0 %collective-permute-start.61 = (bf16[4,96,384]{2,1,0:T(8,128)(2,1)S(1)}, bf16[4,96,384]{2,1,0:T(8,128)(2,1)S(1)}, u32[]{:S(2)}, u32[]{:S(2)}) collective-permute-start(bf16[4,96,384]{2,1,0:T(8,128)(2,1)S(1)} %get-tuple-element.442), channel_id=1, source_target_pairs={{0,8},{8,0},{1,9},{9,1},{2,10},{10,2},{3,11},{11,3},{4,12},{12,4},... | collective-permute-start | bytes 884744 | tf_op jit(solution)/shard_map/ppermute | solution.py:46
  313.6 9.0 %collective-permute-start.60 = (bf16[4,96,384]{2,1,0:T(8,128)(2,1)S(1)}, bf16[4,96,384]{2,1,0:T(8,128)(2,1)S(1)}, u32[]{:S(2)}, u32[]{:S(2)}) collective-permute-start(bf16[4,96,384]{2,1,0:T(8,128)(2,1)S(1)} %get-tuple-element.440), channel_id=1, source_target_pairs={{0,16},{16,0},{1,17},{17,1},{2,18},{18,2},{3,19},{19,3},{4,20},{20... | collective-permute-start | bytes 884744 | tf_op jit(solution)/shard_map/ppermute | solution.py:46
  314.2 12.8 %collective-permute-start.64 = (bf16[256,768]{1,0:T(8,128)(2,1)S(1)}, bf16[256,768]{1,0:T(8,128)(2,1)S(1)}, u32[]{:S(2)}, u32[]{:S(2)}) collective-permute-start(bf16[256,768]{1,0:T(8,128)(2,1)S(1)} %collective-permute-done.57.across_near), channel_id=1, source_target_pairs={{1,0},{2,3},{5,4},{6,7},{9,8},{10,11},{13,12},{14,15},{17,16},{18,... | collective-permute-start | bytes 1179656 | tf_op jit(solution)/shard_map/ppermute | solution.py:140
  328.8 13.1 %collective-permute-start.67 = (bf16[288,384]{1,0:T(8,128)(2,1)S(1)}, bf16[288,384]{1,0:T(8,128)(2,1)S(1)}, u32[]{:S(2)}, u32[]{:S(2)}) collective-permute-start(bf16[288,384]{1,0:T(8,128)(2,1)S(1)} %slice_bitcast_fusion.2), channel_id=1, source_target_pairs={{0,1},{1,0},{2,3},{3,2},{4,5},{5,4},{6,7},{7,6},{8,9},{9,8},{10,11... | collective-permute-start | bytes 663560 | tf_op jit(solution)/shard_map/ppermute | solution.py:51
  329.0 18.0 %collective-permute-start.68 = (bf16[288,384]{1,0:T(8,128)(2,1)S(1)}, bf16[288,384]{1,0:T(8,128)(2,1)S(1)}, u32[]{:S(2)}, u32[]{:S(2)}) collective-permute-start(bf16[288,384]{1,0:T(8,128)(2,1)S(1)} %get-tuple-element.473), channel_id=1, source_target_pairs={{0,2},{1,3},{2,0},{3,1},{4,6},{5,7},{6,4},{7,5},{8,10},{9,11},{10,... | collective-permute-start | bytes 663560 | tf_op jit(solution)/shard_map/ppermute | solution.py:51
  332.0 15.0 %collective-permute-start.69 = (bf16[288,384]{1,0:T(8,128)(2,1)S(1)}, bf16[288,384]{1,0:T(8,128)(2,1)S(1)}, u32[]{:S(2)}, u32[]{:S(2)}) collective-permute-start(bf16[288,384]{1,0:T(8,128)(2,1)S(1)} %get-tuple-element.474), channel_id=1, source_target_pairs={{0,3},{1,2},{2,1},{3,0},{4,7},{5,6},{6,5},{7,4},{8,11},{9,10},{10,... | collective-permute-start | bytes 663560 | tf_op jit(solution)/shard_map/ppermute | solution.py:51
  333.5 8.3 %collective-permute-start.66 = (f32[24,768]{1,0:T(8,128)S(1)}, f32[24,768]{1,0:T(8,128)S(1)}, u32[]{:S(2)}, u32[]{:S(2)}) collective-permute-start(f32[24,768]{1,0:T(8,128)S(1)} %add.277), channel_id=1, source_target_pairs={{0,8},{8,0},{1,9},{9,1},{2,10},{10,2},{3,11},{11,3},{4,12},{12,4},... | collective-permute-start | bytes 221192 | tf_op jit(solution)/shard_map/ppermute | solution.py:46
  341.8 9.5 %collective-permute-start.70 = (f32[24,768]{1,0:T(8,128)S(1)}, f32[24,768]{1,0:T(8,128)S(1)}, u32[]{:S(2)}, u32[]{:S(2)}) collective-permute-start(f32[24,768]{1,0:T(8,128)S(1)} %add.278), channel_id=1, source_target_pairs={{0,4},{4,0},{1,5},{5,1},{2,6},{6,2},{3,7},{7,3},{8,12},{12,8},{9,1... | collective-permute-start | bytes 221192 | tf_op jit(solution)/shard_map/ppermute | solution.py:46
  (105 other events, 673.9 us)
Sparse Core Ops, SparseCore 0:
  16.8 27.7 all-gather.1
  240.6 39.6 reduce-scatter.1

commit v5 on v4

--- a/solution.py
+++ b/solution.py
@@ -1434,8 +1434,10 @@
     whole_qk, whole_vc, whole_oo = wholes
 
     def exchange(values):
-        own, near, others = values
-        got = mp_swap(others, 2)
+        return exchange_rest(values, mp_swap(values[2], 2))
+
+    def exchange_rest(values, got):
+        own, near, _ = values
         lane = lax.broadcasted_iota(jnp.int32, got.shape, 1)
         passed = mp_swap(jnp.where(lane < plan.width, near, got), 1)
         return own, passed, got
@@ -1450,10 +1452,14 @@
     down = jnp.concatenate([down, down_got])
     half = up.shape[0] // 2
     up_last, down_last = swap(up[:half], forth[-1]), swap(down[:half], back[-1])
-    contexts = exchange(contexts)
-    contexts, down, up, up_last, down_last = hold(contexts, down, up, up_last, down_last)
+    context_got = mp_swap(contexts[2], 2)
+    contexts, context_got, down, up, up_last, down_last = hold(
+        contexts, context_got, down, up, up_last, down_last
+    )
+    contexts = exchange_rest(contexts, context_got)
     up_last = jnp.concatenate([up_last, swap(up[half:], forth[-1])])
     down_last = jnp.concatenate([down_last, swap(down[half:], back[-1])])
+    (contexts,) = hold(contexts)
     up_core, down_core = send_cores((up, down))
     z_second, kept, given = cross_output(plan, vec_rep, z_first, contexts, whole_oo)
     kept, given = hold(kept, given)
@@ -1536,9 +1542,11 @@
         (first_sums, cross_sums, third_sums, bias_sums, value_sum),
         wholes,
     )
-    token_back, maps_back, vectors, ffn_got_up, out_got = hold(
-        token_back, maps_back, vectors, ffn_got_up, out_got
-    )
+    token_back, maps_back, vectors, ffn_got_up, out_got, layer_far = hold(
+        token_back, maps_back, vectors, ffn_got_up, out_got, layer_far
+    )
+    middle_down = (ffn_state[1].shape[1] + middle) // 2
+    ffn_got_down = mp_swap(ffn_state[1][:, middle:middle_down], 2)
     across_own = mp_middle(plan, token_back)
     near = mp_swap(token_back, 1)
     out_state = shrink_add(out_state, out_got)
@@ -1551,15 +1559,15 @@
         (vec_rep, z_first, maps_back, value_maps, *query_back),
         attn_gradients,
     )
-    across_own, layer_far, near, attn_halves, out_got = hold(
-        across_own, layer_far, near, attn_halves, out_got
+    across_own, near, attn_halves, out_got, ffn_got_down = hold(
+        across_own, near, attn_halves, out_got, ffn_got_down
     )
     attn_state = attn_halves["a"], attn_halves["b"]
     attn_got = shrink_send(attn_state, cores)
-    ffn_got_down = mp_swap(ffn_state[1][:, middle:], 2)
+    ffn_got_rest = mp_swap(ffn_state[1][:, middle_down:], 2)
     out_state = shrink_add(out_state, out_got)
     out_got = shrink_send(out_state, (forth[0], back[0]))
-    attn_got, out_got, ffn_got_down, vectors = hold(attn_got, out_got, ffn_got_down, vectors)
+    attn_got, out_got, ffn_got_rest, vectors = hold(attn_got, out_got, ffn_got_rest, vectors)
     across_near = mp_middle(plan, near)
     far_own = mp_outward(plan, across_own)
     attn_state = shrink_add(attn_state, attn_got)
@@ -1578,7 +1586,7 @@
     attn_state = shrink_add(attn_state, attn_got)
     attn_got = shrink_send(attn_state, (forth[0], back[0]))
     far_near = mp_outward(plan, across_near)
-    ffn_got = jnp.concatenate([ffn_got_up, ffn_got_down], axis=1)
+    ffn_got = jnp.concatenate([ffn_got_up, ffn_got_down, ffn_got_rest], axis=1)
     half = ffn_got.shape[0] // 2
     ffn_state = (
         add_low(ffn_state[0][:half], ffn_got[:half]),

time: 367 us -> 358 us (0.975)
  waiting for transfers between devices: 97 us -> 86.8 us
  local copies, waits for them, and re-layouts: 41.2 us -> 36.8 us
    ppermute x26 -> x27, waiting for transfers between devices: 65.4 us -> 57.8 us  [mp_swap(): return lax.ppermute(values, 'mp', [(i, i ^ distance) for i in range(count)])]
    unnamed x204 -> x221, local copies, waits for them, and re-layouts: 36 us -> 32.1 us
    ppermute x26 -> x27, starting transfers between devices: 45.5 us -> 45.3 us  [mp_swap(): return lax.ppermute(values, 'mp', [(i, i ^ distance) for i in range(count)])]
  transfers between devices with their start and end apart: 73 -> 74, of which waited for: 27 -> 24; matrix products, arithmetic and copies ran while one was open for 12% -> 14% of each run, Pallas kernels for 21% -> 23%
where the time goes in v5:
time: 358 us; the launch traced here: 352 us
  Pallas kernels  94.1 us (26%)
  waiting for transfers between devices  86.8 us (24%)
  starting transfers between devices  83.7 us (23%)
  local copies, waits for them, and re-layouts  36.8 us (10%)
  other arithmetic  34.1 us (10%)
  between operations  16.4 us (5%)
    pallas_call x15, Pallas kernels, call(): pl.pallas_call(kernel, out_shape=outs, in_specs=[pl.BlockSpec(memory_spac...  94.1 us
    ppermute x27, waiting for transfers between devices, mp_swap(): return lax.ppermute(values, 'mp', [(i, i ^ distance) for i in range(count)])  57.8 us
    ppermute x27, starting transfers between devices, mp_swap(): return lax.ppermute(values, 'mp', [(i, i ^ distance) for i in range(count)])  45.3 us
    unnamed x221, local copies, waits for them, and re-layouts  32.1 us
    ppermute x39, starting transfers between devices, swap(): return lax.ppermute(values, axis, [(0, 1), (1, 0)])  30.9 us
    ppermute x39, waiting for transfers between devices, swap(): return lax.ppermute(values, axis, [(0, 1), (1, 0)])  22.8 us
    convert_element_type x18, other arithmetic, add_low(): return (first.astype(F32) + second.astype(F32)).astype(BF)  22 us
  transfers between devices with their start and end apart: 74, of which 24 were waited for; matrix products, arithmetic and copies ran while one was open for 14% of the time, Pallas kernels for 23%

profile of v5, /device:TPU:0, one launch (start us, length us, event | category | flops | bytes accessed | tf_op | source)
XLA Modules:
  0.0 351.8 jit_solution(16506974890371414165)
XLA Ops:
  10.1 3.1 collective-permute-start
  13.2 2.6 collective-permute-start.1
  16.8 11.5 %copy.55.images = bf16[16,257,1408]{2,1,0:T(8,128)(2,1)} copy(bf16[16,257,1408]{2,0,1:T(8,128)(2,1)} %param.29) | data formatting | bytes 23158784 | tf_op args[1]
  30.0 3.2 collective-permute-done.1
  33.4 1.6 collective-permute-start.4
  35.0 1.6 collective-permute-start.3
  36.6 4.3 %collective-permute-start.5 = (bf16[192,768]{1,0:T(8,128)(2,1)S(1)}, bf16[192,768]{1,0:T(8,128)(2,1)S(1)}, u32[]{:S(2)}, u32[]{:S(2)}) collective-permute-start(bf16[192,768]{1,0:T(8,128)(2,1)S(1)} %get-tuple-element.215), channel_id=1, source_target_pairs={{0,1},{1,0},{2,3},{3,2},{4,5},{5,4},{6,7},{7,6},{8,9},{9,8},{10,11... | collective-permute-start | bytes 884744 | tf_op jit(solution)/shard_map/ppermute | solution.py:51
  41.0 5.1 %collective-permute-done.5 = bf16[192,768]{1,0:T(8,128)(2,1)S(1)} collective-permute-done((bf16[192,768]{1,0:T(8,128)(2,1)S(1)}, bf16[192,768]{1,0:T(8,128)(2,1)S(1)}, u32[]{:S(2)}, u32[]{:S(2)}) %collective-permute-start.5) | collective-permute-done | bytes 294944 | tf_op jit(solution)/shard_map/ppermute | solution.py:51
  47.3 1.6 collective-permute-start.8
  49.7 5.2 %collective-permute-start.11 = (bf16[2,96,768]{2,1,0:T(8,128)(2,1)S(1)}, bf16[2,96,768]{2,1,0:T(8,128)(2,1)}, u32[]{:S(2)}, u32[]{:S(2)}) collective-permute-start(bf16[2,96,768]{2,1,0:T(8,128)(2,1)S(1)} %get-tuple-element.471), channel_id=1, source_target_pairs={{0,2},{1,3},{2,0},{3,1},{4,6},{5,7},{6,4},{7,5},{8,10},{9,11},{10,... | collective-permute-start | bytes 884744 | tf_op jit(solution)/shard_map/ppermute | solution.py:51
  54.8 4.4 %copy-done = bf16[16,257,1408]{2,1,0:T(8,128)(2,1)S(1)} copy-done((bf16[16,257,1408]{2,1,0:T(8,128)(2,1)S(1)}, bf16[16,257,1408]{2,1,0:T(8,128)(2,1)}, u32[]{:S(2)}) %copy-start) | copy-done | bytes 11579416
  60.5 11.1 %shard_map.467.refs_3_.refs_6_ = bf16[16,384,384]{2,1,0:T(8,128)(2,1)S(1)} custom-call(bf16[16,257,1408]{2,1,0:T(8,128)(2,1)S(1)} %copy-done, f32[8,384]{1,0:T(8,128)S(1)} %concatenate.84.bias, bf16[1408,384]{1,0:T(8,128)(2,1)S(1)} %copy-done.22), custom_call_target="tpu_custom_call" | custom-call | flops 1000 | bytes 1000 | tf_op jit(solution)/shard_map/pallas_call | solution.py:440
  73.3 1.5 collective-permute-start.14
  74.8 3.3 collective-permute-start.6
  82.0 10.3 %shard_map.468 = (bf16[4,256,384]{2,1,0:T(8,128)(2,1)S(1)}, bf16[4,256,192]{2,1,0:T(8,128)(2,1)S(1)}, bf16[4,256,192]{2,1,0:T(8,128)(2,1)S(1)}, f32[256,768]{1,0...) custom-call(s32[16]{0:T(128)S(1)} %copy-done.53, ...), custom_call_target="tpu_custom_call" | custom-call | flops 1000 | bytes 1000 | tf_op jit(solution)/shard_map/pallas_call | solution.py:440
  96.0 1.5 collective-permute-start.17
  99.6 5.5 %collective-permute-done.15.refs_2_ = bf16[128,384]{1,0:T(8,128)(2,1)S(1)} collective-permute-done((bf16[128,384]{1,0:T(8,128)(2,1)S(1)}, bf16[128,384]{1,0:T(8,128)(2,1)S(1)}, u32[]{:S(2)}, u32[]{:S(2)}) %collective-permute-start.15) | collective-permute-done | bytes 98336 | tf_op jit(solution)/shard_map/ppermute | solution.py:51
  106.3 3.5 collective-permute-done.16.refs_1_
  109.8 6.2 %shard_map.469 = (bf16[128,192]{1,0:T(8,128)(2,1)S(1)}, bf16[128,384]{1,0:T(8,128)(2,1)S(1)}, bf16[128,384]{1,0:T(8,128)(2,1)S(1)}) custom-call(bf16[128,192]{1,0:T(8,128)(2,1)S(1)} %get-tuple-element.233.refs_0_, bf16[128,384]{1,0:T(8,128)(2,1)S(1)} %collective-permute-done.16.refs_1_, bf16[128,384]{1,0:T(8,128)(2,1)S(1)} %collective-permute-done.15.refs_2_, ...), custom_call_target="tpu_custom_call" | custom-call | flops 1000 | bytes 1000 | tf_op jit(solution)/shard_map/pallas_call | solution.py:440
  116.7 6.6 %collective-permute-done.19 = bf16[4,96,768]{2,1,0:T(8,128)(2,1)S(1)} collective-permute-done((bf16[4,96,768]{2,1,0:T(8,128)(2,1)S(1)}, bf16[4,96,768]{2,1,0:T(8,128)(2,1)S(1)}, u32[]{:S(2)}, u32[]{:S(2)}) %collective-permute-start.19) | collective-permute-done | bytes 589856 | tf_op jit(solution)/shard_map/ppermute | solution.py:46
  123.9 1.5 collective-permute-start.22
  126.2 4.6 %collective-permute-done.25.rest_1_ = bf16[128,384]{1,0:T(8,128)(2,1)S(1)} collective-permute-done((bf16[128,384]{1,0:T(8,128)(2,1)S(1)}, bf16[128,384]{1,0:T(8,128)(2,1)S(1)}, u32[]{:S(2)}, u32[]{:S(2)}) %collective-permute-start.25) | collective-permute-done | bytes 98336 | tf_op jit(solution)/shard_map/ppermute | solution.py:51
  130.9 1.5 shard_map.470
  132.5 6.8 %collective-permute-done.22 = bf16[4,96,768]{2,1,0:T(8,128)(2,1)S(1)} collective-permute-done((bf16[4,96,768]{2,1,0:T(8,128)(2,1)S(1)}, bf16[4,96,768]{2,1,0:T(8,128)(2,1)S(1)}, u32[]{:S(2)}, u32[]{:S(2)}) %collective-permute-start.22) | collective-permute-done | bytes 589856 | tf_op jit(solution)/shard_map/ppermute | solution.py:46
  141.3 3.1 collective-permute-done.27.rest_3_
  145.5 14.3 %shard_map.471 = (bf16[2,4,32,768]{3,2,1,0:T(8,128)(2,1)S(1)}, f32[128,768]{1,0:T(8,128)S(1)}, bf16[128,768]{1,0:T(8,128)(2,1)S(1)}, f32[3,768]{1,0:T(4,128)S(1)...) custom-call(f32[12,768]{1,0:T(8,128)S(1)} %copy-done.6, ...), custom_call_target="tpu_custom_call" | custom-call | flops 1000 | bytes 1000 | tf_op jit(solution)/shard_map/pallas_call | solution.py:440
  160.5 6.9 %collective-permute-done.29.got = bf16[128,768]{1,0:T(8,128)(2,1)S(1)} collective-permute-done((bf16[128,768]{1,0:T(8,128)(2,1)S(1)}, bf16[128,768]{1,0:T(8,128)(2,1)S(1)}, u32[]{:S(2)}, u32[]{:S(2)}) %collective-permute-start.29) | collective-permute-done | bytes 196640 | tf_op jit(solution)/shard_map/ppermute | solution.py:51
  168.1 2.5 add_convert_fusion.3
  175.0 1.7 collective-permute-start.34
  176.7 4.3 %collective-permute-done.32.refs_5_ = bf16[128,384]{1,0:T(8,128)(2,1)S(1)} collective-permute-done((bf16[128,384]{1,0:T(8,128)(2,1)S(1)}, bf16[128,384]{1,0:T(8,128)(2,1)S(1)}, u32[]{:S(2)}, u32[]{:S(2)}) %collective-permute-start.32) | collective-permute-done | bytes 98336 | tf_op jit(solution)/shard_map/ppermute | solution.py:51
  181.1 8.5 %collective-permute-done.33.refs_4_ = bf16[128,384]{1,0:T(8,128)(2,1)S(1)} collective-permute-done((bf16[128,384]{1,0:T(8,128)(2,1)S(1)}, bf16[128,384]{1,0:T(8,128)(2,1)S(1)}, u32[]{:S(2)}, u32[]{:S(2)}) %collective-permute-start.33) | collective-permute-done | bytes 98336 | tf_op jit(solution)/shard_map/ppermute | solution.py:51
  189.7 1.7 collective-permute-start.41
  191.4 9.8 %shard_map.473 = (bf16[16,384,384]{2,1,0:T(8,128)(2,1)S(1)}, f32[1,192]{1,0:T(1,128)S(1)}, bf16[128,192]{1,0:T(8,128)(2,1)S(1)}, bf16[128,384]{1,0:T(8,128)(2,1)S(1)}, bf16[128,384]{1,0:T(8,128)(2,1)S(1)}) custom-call(bf16[128,192]{1,0:T(8,128)(2,1)S(1)} %get-tuple-element.233.refs_0_, bf16[128,384]{1,0:T(8,128)(2,1)S(1)} %collective-permute-done.16.refs_1_, ...), custom_call_target="tpu_custom_call" | custom-call | flops 1000 | bytes 1000 | tf_op jit(solution)/shard_map/pallas_call | solution.py:440
  206.0 2.4 collective-permute-start.37
  208.4 6.0 %collective-permute-done.37.rest_2_.rest_6_ = bf16[128,384]{1,0:T(8,128)(2,1)S(1)} collective-permute-done((bf16[128,384]{1,0:T(8,128)(2,1)S(1)}, bf16[128,384]{1,0:T(8,128)(2,1)S(1)}, u32[]{:S(2)}, u32[]{:S(2)}) %collective-permute-start.37) | collective-permute-done | bytes 98336 | tf_op jit(solution)/shard_map/ppermute | solution.py:51
  214.5 8.9 %shard_map.474 = bf16[1408,384]{1,0:T(8,128)(2,1)} custom-call(bf16[16,257,1408]{2,1,0:T(8,128)(2,1)} %copy.55.images, bf16[16,384,384]{2,1,0:T(8,128)(2,1)S(1)} %get-tuple-element.303.kv_back), custom_call_target="tpu_custom_call" | custom-call | flops 1000 | bytes 1000 | tf_op jit(solution)/shard_map/pallas_call | solution.py:440
  225.6 1.5 add_convert_fusion.23
  230.3 2.4 shard_map.476
  234.9 3.4 collective-permute-start.42
  238.3 13.7 %shard_map.477 = (bf16[256,768]{1,0:T(8,128)(2,1)}, f32[24,768]{1,0:T(8,128)}, bf16[4,256,384]{2,1,0:T(8,128)(2,1)}, bf16[4,256,192]{2,1,0:T(8,128)(2,1)}) custom-call(s32[16]{0:T(128)} %lengths.3, f32[12,768]{1,0:T(8,128)} %rest_0_.3, f32[256,768]{1,0:T(8,128)} %copy-done.8, bf16[4,256,384]{2,1,0:T(8,128)(2,1)} %copy-done.25, ...), custom_call_target="tpu_custom_call" | custom-call | flops 1000 | bytes 1000 | tf_op jit(solution)/shard_map/pallas_call | solution.py:440
  253.7 1.9 collective-permute-start.47
  255.6 2.0 add_convert_fusion.18
  258.9 1.9 add_convert_fusion.19
  263.8 4.1 %shard_map.478 = (bf16[16,96,384]{2,1,0:T(8,128)(2,1)S(1)}, bf16[16,96,384]{2,1,0:T(8,128)(2,1)}, bf16[16,96,384]{2,1,0:T(8,128)(2,1)S(1)}, bf16[16,96,384]{2,1,0:T(8,128)(2,1)}) custom-call(bf16[16,64,768]{2,1,0:T(8,128)(2,1)S(1)} %copy-done.5, f32[12,768]{1,0:T(8,128)S(1)} %copy-done.7, f32[256,768]{1,0:T(8,128)S(1)} %get-tuple-element.250.z_first.rest_1_, ...), custom_call_target="tpu_custom_call" | custom-call | flops 1000 | bytes 1000 | tf_op jit(solution)/shard_map/pallas_call | solution.py:440
  268.9 2.9 collective-permute-done.50
  273.2 1.9 add_convert_fusion.28
  275.6 1.9 add_convert_fusion.29
  277.6 1.6 collective-permute-start.53
  279.2 2.8 shard_map.480
  285.0 1.5 add_convert_fusion.4
  287.1 1.5 add_convert_fusion.5
  288.6 1.6 collective-permute-start.56
  290.4 4.8 %collective-permute-start.60 = (f32[24,768]{1,0:T(8,128)S(1)}, f32[24,768]{1,0:T(8,128)S(1)}, u32[]{:S(2)}, u32[]{:S(2)}) collective-permute-start(f32[24,768]{1,0:T(8,128)S(1)} %copy-done.93), channel_id=1, source_target_pairs={{0,1},{1,0},{2,3},{3,2},{4,5},{5,4},{6,7},{7,6},{8,9},{9,8},{10,11... | collective-permute-start | bytes 221192 | tf_op jit(solution)/shard_map/ppermute | solution.py:51
  297.5 2.2 collective-permute-done.59.far_own
  299.7 1.6 collective-permute-done.60
  301.4 2.1 collective-permute-done.56
  308.3 4.4 %collective-permute-start.63 = (f32[24,768]{1,0:T(8,128)S(1)}, f32[24,768]{1,0:T(8,128)S(1)}, u32[]{:S(2)}, u32[]{:S(2)}) collective-permute-start(f32[24,768]{1,0:T(8,128)S(1)} %add.270), channel_id=1, source_target_pairs={{0,2},{1,3},{2,0},{3,1},{4,6},{5,7},{6,4},{7,5},{8,10},{9,11},{10,... | collective-permute-start | bytes 221192 | tf_op jit(solution)/shard_map/ppermute | solution.py:51
  315.1 3.9 %collective-permute-done.65.far_near = bf16[256,768]{1,0:T(8,128)(2,1)S(1)} collective-permute-done((bf16[256,768]{1,0:T(8,128)(2,1)S(1)}, bf16[256,768]{1,0:T(8,128)(2,1)S(1)}, u32[]{:S(2)}, u32[]{:S(2)}) %collective-permute-start.65) | collective-permute-done | bytes 393248 | tf_op jit(solution)/shard_map/ppermute | solution.py:140
  319.1 1.6 collective-permute-start.66
  321.2 2.2 collective-permute-start.69
  323.4 2.2 collective-permute-start.70
  327.4 3.0 shard_map.479
  330.5 3.2 shard_map.481
  333.9 4.2 %collective-permute-done.69 = bf16[288,384]{1,0:T(8,128)(2,1)S(1)} collective-permute-done((bf16[288,384]{1,0:T(8,128)(2,1)S(1)}, bf16[288,384]{1,0:T(8,128)(2,1)S(1)}, u32[]{:S(2)}, u32[]{:S(2)}) %collective-permute-start.69) | collective-permute-done | bytes 221216 | tf_op jit(solution)/shard_map/ppermute | solution.py:51
  (419 shorter events, 74.9 us)
Async XLA Ops:
  7.2 47.6 %all-gather.2.cloned.1.call-start = ((), (), s32[]{:S(2)}) async-start(), calls=%async_computation.1 | async-start | bytes 1216512 | tf_op jit(solution)/shard_map/all_gather | solution.py:1387
  10.1 19.8 %collective-permute-start = (bf16[312,384]{1,0:T(8,128)(2,1)S(1)}, bf16[312,384]{1,0:T(8,128)(2,1)S(1)}, u32[]{:S(2)}, u32[]{:S(2)}) collective-permute-start(bf16[312,384]{1,0:T(8,128)(2,1)S(1)} %constant_dynamic-update-slice_fusion), channel_id=1, source_target_pairs={{0,1},{1,0},{2,3},{3,2},{4,5},{5,4},{6,7},{7,6},{8,9},{9,8},{10,11... | collective-permute-start | bytes 718856 | tf_op jit(solution)/shard_map/ppermute | solution.py:51
  13.2 19.9 %collective-permute-start.1 = (bf16[312,384]{1,0:T(8,128)(2,1)S(1)}, bf16[312,384]{1,0:T(8,128)(2,1)S(1)}, u32[]{:S(2)}, u32[]{:S(2)}) collective-permute-start(bf16[312,384]{1,0:T(8,128)(2,1)S(1)} %constant_dynamic-update-slice_fusion), channel_id=1, source_target_pairs={{0,2},{1,3},{2,0},{3,1},{4,6},{5,7},{6,4},{7,5},{8,10},{9,11},{10,... | collective-permute-start | bytes 718856 | tf_op jit(solution)/shard_map/ppermute | solution.py:51
  15.8 17.3 %collective-permute-start.2 = (bf16[312,384]{1,0:T(8,128)(2,1)S(1)}, bf16[312,384]{1,0:T(8,128)(2,1)S(1)}, u32[]{:S(2)}, u32[]{:S(2)}) collective-permute-start(bf16[312,384]{1,0:T(8,128)(2,1)S(1)} %constant_dynamic-update-slice_fusion), channel_id=1, source_target_pairs={{0,3},{1,2},{2,1},{3,0},{4,7},{5,6},{6,5},{7,4},{8,11},{9,10},{10,... | collective-permute-start | bytes 718856 | tf_op jit(solution)/shard_map/ppermute | solution.py:51
  16.7 265.4 %reduce-scatter.2.cloned.1.call-start = ((), (), s32[]{:S(2)}) async-start(), calls=%async_computation.2 | async-start | bytes 1216512 | tf_op jit(solution)/shard_map/reduce_scatter | solution.py:1522
  33.4 12.8 %collective-permute-start.4 = (bf16[4,144,384]{2,1,0:T(8,128)(2,1)S(1)}, bf16[4,144,384]{2,1,0:T(8,128)(2,1)S(1)}, u32[]{:S(2)}, u32[]{:S(2)}) collective-permute-start(bf16[4,144,384]{2,1,0:T(8,128)(2,1)S(1)} %pad_maximum_fusion.10), channel_id=1, source_target_pairs={{0,8},{8,0},{1,9},{9,1},{2,10},{10,2},{3,11},{11,3},{4,12},{12,4},... | collective-permute-start | bytes 1327112 | tf_op jit(solution)/shard_map/ppermute | solution.py:46
  35.0 12.1 %collective-permute-start.3 = (bf16[4,144,384]{2,1,0:T(8,128)(2,1)S(1)}, bf16[4,144,384]{2,1,0:T(8,128)(2,1)S(1)}, u32[]{:S(2)}, u32[]{:S(2)}) collective-permute-start(bf16[4,144,384]{2,1,0:T(8,128)(2,1)S(1)} %pad_maximum_fusion.9), channel_id=1, source_target_pairs={{0,16},{16,0},{1,17},{17,1},{2,18},{18,2},{3,19},{19,3},{4,20},{20... | collective-permute-start | bytes 1327112 | tf_op jit(solution)/shard_map/ppermute | solution.py:46
  36.6 9.6 %collective-permute-start.5 = (bf16[192,768]{1,0:T(8,128)(2,1)S(1)}, bf16[192,768]{1,0:T(8,128)(2,1)S(1)}, u32[]{:S(2)}, u32[]{:S(2)}) collective-permute-start(bf16[192,768]{1,0:T(8,128)(2,1)S(1)} %get-tuple-element.215), channel_id=1, source_target_pairs={{0,1},{1,0},{2,3},{3,2},{4,5},{5,4},{6,7},{7,6},{8,9},{9,8},{10,11... | collective-permute-start | bytes 884744 | tf_op jit(solution)/shard_map/ppermute | solution.py:51
  47.2 24.4 %collective-permute-start.10 = (bf16[8,144,384]{2,1,0:T(8,128)(2,1)S(1)}, bf16[8,144,384]{2,1,0:T(8,128)(2,1)S(1)}, u32[]{:S(2)}, u32[]{:S(2)}) collective-permute-start(bf16[8,144,384]{2,1,0:T(8,128)(2,1)S(1)} %constant_dynamic-update-slice_fusion.10.rest_4_), channel_id=1, source_target_pairs={{0,4},{4,0},{1,5},{5,1},{2,6},{6,2},{3,7},{7,3},{8,12},{12,8},{9,1... | collective-permute-start | bytes 2654216 | tf_op jit(solution)/shard_map/ppermute | solution.py:46
  47.3 24.4 %collective-permute-start.8 = (bf16[8,144,384]{2,1,0:T(8,128)(2,1)S(1)}, bf16[8,144,384]{2,1,0:T(8,128)(2,1)}, u32[]{:S(2)}, u32[]{:S(2)}) collective-permute-start(bf16[8,144,384]{2,1,0:T(8,128)(2,1)S(1)} %constant_dynamic-update-slice_fusion.10.rest_4_), channel_id=1, source_target_pairs={{0,16},{16,0},{1,17},{17,1},{2,18},{18,2},{3,19},{19,3},{4,20},{20... | collective-permute-start | bytes 2654216 | tf_op jit(solution)/shard_map/ppermute | solution.py:46
  49.0 22.7 %collective-permute-start.7 = (bf16[8,144,384]{2,1,0:T(8,128)(2,1)S(1)}, bf16[8,144,384]{2,1,0:T(8,128)(2,1)}, u32[]{:S(2)}, u32[]{:S(2)}) collective-permute-start(bf16[8,144,384]{2,1,0:T(8,128)(2,1)S(1)} %constant_dynamic-update-slice_fusion.5.rest_0_), channel_id=1, source_target_pairs={{0,8},{8,0},{1,9},{9,1},{2,10},{10,2},{3,11},{11,3},{4,12},{12,4},... | collective-permute-start | bytes 2654216 | tf_op jit(solution)/shard_map/ppermute | solution.py:46
  49.6 22.1 %collective-permute-start.9 = (bf16[8,144,384]{2,1,0:T(8,128)(2,1)S(1)}, bf16[8,144,384]{2,1,0:T(8,128)(2,1)}, u32[]{:S(2)}, u32[]{:S(2)}) collective-permute-start(bf16[8,144,384]{2,1,0:T(8,128)(2,1)S(1)} %constant_dynamic-update-slice_fusion.5.rest_0_), channel_id=1, source_target_pairs={{0,4},{4,0},{1,5},{5,1},{2,6},{6,2},{3,7},{7,3},{8,12},{12,8},{9,1... | collective-permute-start | bytes 2654216 | tf_op jit(solution)/shard_map/ppermute | solution.py:46
  49.7 22.0 %collective-permute-start.11 = (bf16[2,96,768]{2,1,0:T(8,128)(2,1)S(1)}, bf16[2,96,768]{2,1,0:T(8,128)(2,1)}, u32[]{:S(2)}, u32[]{:S(2)}) collective-permute-start(bf16[2,96,768]{2,1,0:T(8,128)(2,1)S(1)} %get-tuple-element.471), channel_id=1, source_target_pairs={{0,2},{1,3},{2,0},{3,1},{4,6},{5,7},{6,4},{7,5},{8,10},{9,11},{10,... | collective-permute-start | bytes 884744 | tf_op jit(solution)/shard_map/ppermute | solution.py:51
  71.7 7.9 %collective-permute-start.12 = (bf16[8,144,384]{2,1,0:T(8,128)(2,1)}, bf16[8,144,384]{2,1,0:T(8,128)(2,1)S(1)}, u32[]{:S(2)}, u32[]{:S(2)}) collective-permute-start(bf16[8,144,384]{2,1,0:T(8,128)(2,1)} %collective-permute-done.7.rest_1_), channel_id=1, source_target_pairs={{0,4},{4,0},{1,5},{5,1},{2,6},{6,2},{3,7},{7,3},{8,12},{12,8},{9,1... | collective-permute-start | bytes 2654216 | tf_op jit(solution)/shard_map/ppermute | solution.py:46
  72.0 7.6 %collective-permute-start.13 = (bf16[8,144,384]{2,1,0:T(8,128)(2,1)}, bf16[8,144,384]{2,1,0:T(8,128)(2,1)S(1)}, u32[]{:S(2)}, u32[]{:S(2)}) collective-permute-start(bf16[8,144,384]{2,1,0:T(8,128)(2,1)} %collective-permute-done.8.rest_5_), channel_id=1, source_target_pairs={{0,4},{4,0},{1,5},{5,1},{2,6},{6,2},{3,7},{7,3},{8,12},{12,8},{9,1... | collective-permute-start | bytes 2654216 | tf_op jit(solution)/shard_map/ppermute | solution.py:46
  73.3 22.6 %collective-permute-start.14 = (bf16[4,96,768]{2,1,0:T(8,128)(2,1)S(1)}, bf16[4,96,768]{2,1,0:T(8,128)(2,1)S(1)}, u32[]{:S(2)}, u32[]{:S(2)}) collective-permute-start(bf16[4,96,768]{2,1,0:T(8,128)(2,1)S(1)} %pad_maximum_fusion.5), channel_id=1, source_target_pairs={{0,16},{16,0},{1,17},{17,1},{2,18},{18,2},{3,19},{19,3},{4,20},{20... | collective-permute-start | bytes 1769480 | tf_op jit(solution)/shard_map/ppermute | solution.py:46
  74.8 21.1 %collective-permute-start.6 = (bf16[2,96,768]{2,1,0:T(8,128)(2,1)S(1)}, bf16[2,96,768]{2,1,0:T(8,128)(2,1)S(1)}, u32[]{:S(2)}, u32[]{:S(2)}) collective-permute-start(bf16[2,96,768]{2,1,0:T(8,128)(2,1)S(1)} %get-tuple-element.472), channel_id=1, source_target_pairs={{0,2},{1,3},{2,0},{3,1},{4,6},{5,7},{6,4},{7,5},{8,10},{9,11},{10,... | collective-permute-start | bytes 884744 | tf_op jit(solution)/shard_map/ppermute | solution.py:51
  96.0 20.0 %collective-permute-start.17 = (bf16[4,96,768]{2,1,0:T(8,128)(2,1)S(1)}, bf16[4,96,768]{2,1,0:T(8,128)(2,1)S(1)}, u32[]{:S(2)}, u32[]{:S(2)}) collective-permute-start(bf16[4,96,768]{2,1,0:T(8,128)(2,1)S(1)} %pad_maximum_fusion.6), channel_id=1, source_target_pairs={{0,8},{8,0},{1,9},{9,1},{2,10},{10,2},{3,11},{11,3},{4,12},{12,4},... | collective-permute-start | bytes 1769480 | tf_op jit(solution)/shard_map/ppermute | solution.py:46
  97.5 25.9 %collective-permute-start.19 = (bf16[4,96,768]{2,1,0:T(8,128)(2,1)S(1)}, bf16[4,96,768]{2,1,0:T(8,128)(2,1)S(1)}, u32[]{:S(2)}, u32[]{:S(2)}) collective-permute-start(bf16[4,96,768]{2,1,0:T(8,128)(2,1)S(1)} %pad_maximum_fusion.5), channel_id=1, source_target_pairs={{0,8},{8,0},{1,9},{9,1},{2,10},{10,2},{3,11},{11,3},{4,12},{12,4},... | collective-permute-start | bytes 1769480 | tf_op jit(solution)/shard_map/ppermute | solution.py:46
  98.1 25.3 %collective-permute-start.20 = (bf16[4,96,768]{2,1,0:T(8,128)(2,1)S(1)}, bf16[4,96,768]{2,1,0:T(8,128)(2,1)S(1)}, u32[]{:S(2)}, u32[]{:S(2)}) collective-permute-start(bf16[4,96,768]{2,1,0:T(8,128)(2,1)S(1)} %pad_maximum_fusion.6), channel_id=1, source_target_pairs={{0,16},{16,0},{1,17},{17,1},{2,18},{18,2},{3,19},{19,3},{4,20},{20... | collective-permute-start | bytes 1769480 | tf_op jit(solution)/shard_map/ppermute | solution.py:46
  123.4 17.4 %collective-permute-start.23 = (bf16[8,96,768]{2,1,0:T(8,128)(2,1)S(1)}, bf16[8,96,768]{2,1,0:T(8,128)(2,1)S(1)}, u32[]{:S(2)}, u32[]{:S(2)}) collective-permute-start(bf16[8,96,768]{2,1,0:T(8,128)(2,1)S(1)} %pad_maximum_fusion.1.rest_0_), channel_id=1, source_target_pairs={{0,4},{4,0},{1,5},{5,1},{2,6},{6,2},{3,7},{7,3},{8,12},{12,8},{9,1... | collective-permute-start | bytes 3538952 | tf_op jit(solution)/shard_map/ppermute | solution.py:46
  123.4 17.4 %collective-permute-start.24 = (bf16[8,96,768]{2,1,0:T(8,128)(2,1)S(1)}, bf16[8,96,768]{2,1,0:T(8,128)(2,1)S(1)}, u32[]{:S(2)}, u32[]{:S(2)}) collective-permute-start(bf16[8,96,768]{2,1,0:T(8,128)(2,1)S(1)} %pad_maximum_fusion.rest_4_), channel_id=1, source_target_pairs={{0,4},{4,0},{1,5},{5,1},{2,6},{6,2},{3,7},{7,3},{8,12},{12,8},{9,1... | collective-permute-start | bytes 3538952 | tf_op jit(solution)/shard_map/ppermute | solution.py:46
  123.9 15.4 %collective-permute-start.22 = (bf16[4,96,768]{2,1,0:T(8,128)(2,1)S(1)}, bf16[4,96,768]{2,1,0:T(8,128)(2,1)S(1)}, u32[]{:S(2)}, u32[]{:S(2)}) collective-permute-start(bf16[4,96,768]{2,1,0:T(8,128)(2,1)S(1)} %slice.418), channel_id=1, source_target_pairs={{0,16},{16,0},{1,17},{17,1},{2,18},{18,2},{3,19},{19,3},{4,20},{20... | collective-permute-start | bytes 1769480 | tf_op jit(solution)/shard_map/ppermute | solution.py:46
  125.5 15.1 %collective-permute-start.21 = (bf16[4,96,768]{2,1,0:T(8,128)(2,1)S(1)}, bf16[4,96,768]{2,1,0:T(8,128)(2,1)S(1)}, u32[]{:S(2)}, u32[]{:S(2)}) collective-permute-start(bf16[4,96,768]{2,1,0:T(8,128)(2,1)S(1)} %slice.417), channel_id=1, source_target_pairs={{0,8},{8,0},{1,9},{9,1},{2,10},{10,2},{3,11},{11,3},{4,12},{12,4},... | collective-permute-start | bytes 1769480 | tf_op jit(solution)/shard_map/ppermute | solution.py:46
  132.4 8.3 %collective-permute-start.26 = (bf16[128,768]{1,0:T(8,128)(2,1)S(1)}, bf16[128,768]{1,0:T(8,128)(2,1)S(1)}, u32[]{:S(2)}, u32[]{:S(2)}) collective-permute-start(bf16[128,768]{1,0:T(8,128)(2,1)S(1)} %get-tuple-element.260), channel_id=1, source_target_pairs={{0,1},{1,0},{2,3},{3,2},{4,5},{5,4},{6,7},{7,6},{8,9},{9,8},{10,11... | collective-permute-start | bytes 589832 | tf_op jit(solution)/shard_map/ppermute | solution.py:51
  159.9 7.5 %collective-permute-start.30 = (bf16[16,96,768]{2,1,0:T(8,128)(2,1)}, bf16[16,96,768]{2,1,0:T(8,128)(2,1)S(1)}, u32[]{:S(2)}, u32[]{:S(2)}) collective-permute-start(bf16[16,96,768]{2,1,0:T(8,128)(2,1)} %get-tuple-element.274), channel_id=1, source_target_pairs={{0,4},{4,0},{1,5},{5,1},{2,6},{6,2},{3,7},{7,3},{8,12},{12,8},{9,1... | collective-permute-start | bytes 7077896 | tf_op jit(solution)/shard_map/ppermute | solution.py:46
  160.1 8.0 %collective-permute-start.31 = (bf16[16,96,768]{2,1,0:T(8,128)(2,1)}, bf16[16,96,768]{2,1,0:T(8,128)(2,1)S(1)}, u32[]{:S(2)}, u32[]{:S(2)}) collective-permute-start(bf16[16,96,768]{2,1,0:T(8,128)(2,1)} %get-tuple-element.275), channel_id=1, source_target_pairs={{0,4},{4,0},{1,5},{5,1},{2,6},{6,2},{3,7},{7,3},{8,12},{12,8},{9,1... | collective-permute-start | bytes 7077896 | tf_op jit(solution)/shard_map/ppermute | solution.py:46
  170.6 30.7 %collective-permute-start.35 = (bf16[8,96,768]{2,1,0:T(8,128)(2,1)S(1)}, bf16[8,96,768]{2,1,0:T(8,128)(2,1)S(1)}, u32[]{:S(2)}, u32[]{:S(2)}) collective-permute-start(bf16[8,96,768]{2,1,0:T(8,128)(2,1)S(1)} %get-tuple-element.436), channel_id=1, source_target_pairs={{0,8},{8,0},{1,9},{9,1},{2,10},{10,2},{3,11},{11,3},{4,12},{12,4},... | collective-permute-start | bytes 3538952 | tf_op jit(solution)/shard_map/ppermute | solution.py:46
  171.9 29.4 %collective-permute-start.36 = (bf16[8,96,768]{2,1,0:T(8,128)(2,1)S(1)}, bf16[8,96,768]{2,1,0:T(8,128)(2,1)S(1)}, u32[]{:S(2)}, u32[]{:S(2)}) collective-permute-start(bf16[8,96,768]{2,1,0:T(8,128)(2,1)S(1)} %get-tuple-element.437), channel_id=1, source_target_pairs={{0,16},{16,0},{1,17},{17,1},{2,18},{18,2},{3,19},{19,3},{4,20},{20... | collective-permute-start | bytes 3538952 | tf_op jit(solution)/shard_map/ppermute | solution.py:46
  175.0 14.6 %collective-permute-start.34 = (bf16[2,4,32,768]{3,2,1,0:T(8,128)(2,1)S(1)}, bf16[2,4,32,768]{3,2,1,0:T(8,128)(2,1)S(1)}, u32[]{:S(2)}, u32[]{:S(2)}) collective-permute-start(bf16[2,4,32,768]{3,2,1,0:T(8,128)(2,1)S(1)} %get-tuple-element.288), channel_id=1, source_target_pairs={{0,1},{1,0},{2,3},{3,2},{4,5},{5,4},{6,7},{7,6},{8,9},{9,8},{10,11... | collective-permute-start | bytes 1179656 | tf_op jit(solution)/shard_map/ppermute | solution.py:51
  181.1 8.5 %collective-permute-start.33 = (bf16[128,384]{1,0:T(8,128)(2,1)S(1)}, bf16[128,384]{1,0:T(8,128)(2,1)S(1)}, u32[]{:S(2)}, u32[]{:S(2)}) collective-permute-start(bf16[128,384]{1,0:T(8,128)(2,1)S(1)} %broadcast_select_fusion.1), channel_id=1, source_target_pairs={{0,1},{1,0},{2,3},{3,2},{4,5},{5,4},{6,7},{7,6},{8,9},{9,8},{10,11... | collective-permute-start | bytes 294920 | tf_op jit(solution)/shard_map/ppermute | solution.py:51
  189.7 33.7 %collective-permute-start.41 = (bf16[2,2,4,32,768]{4,3,2,1,0:T(8,128)(2,1)S(1)}, bf16[2,2,4,32,768]{4,3,2,1,0:T(8,128)(2,1)}, u32[]{:S(2)}, u32[]{:S(2)}) collective-permute-start(bf16[2,2,4,32,768]{4,3,2,1,0:T(8,128)(2,1)S(1)} %pad_maximum_fusion.4.two), channel_id=1, source_target_pairs={{1,2},{2,1},{5,6},{6,5},{9,10},{10,9},{13,14},{14,13},{17,18},{18,... | collective-permute-start | bytes 2359304 | tf_op jit(solution)/shard_map/ppermute | solution.py:134
  202.6 21.4 %collective-permute-start.39 = (bf16[4,96,768]{2,1,0:T(8,128)(2,1)}, bf16[4,96,768]{2,1,0:T(8,128)(2,1)S(1)}, u32[]{:S(2)}, u32[]{:S(2)}) collective-permute-start(bf16[4,96,768]{2,1,0:T(8,128)(2,1)} %get-tuple-element.444), channel_id=1, source_target_pairs={{0,16},{16,0},{1,17},{17,1},{2,18},{18,2},{3,19},{19,3},{4,20},{20... | collective-permute-start | bytes 1769480 | tf_op jit(solution)/shard_map/ppermute | solution.py:46
  205.1 19.0 %collective-permute-start.40 = (bf16[4,96,768]{2,1,0:T(8,128)(2,1)}, bf16[4,96,768]{2,1,0:T(8,128)(2,1)S(1)}, u32[]{:S(2)}, u32[]{:S(2)}) collective-permute-start(bf16[4,96,768]{2,1,0:T(8,128)(2,1)} %get-tuple-element.445), channel_id=1, source_target_pairs={{0,8},{8,0},{1,9},{9,1},{2,10},{10,2},{3,11},{11,3},{4,12},{12,4},... | collective-permute-start | bytes 1769480 | tf_op jit(solution)/shard_map/ppermute | solution.py:46
  206.0 8.4 %collective-permute-start.37 = (bf16[128,384]{1,0:T(8,128)(2,1)S(1)}, bf16[128,384]{1,0:T(8,128)(2,1)S(1)}, u32[]{:S(2)}, u32[]{:S(2)}) collective-permute-start(bf16[128,384]{1,0:T(8,128)(2,1)S(1)} %get-tuple-element.300), channel_id=1, source_target_pairs={{0,2},{1,3},{2,0},{3,1},{4,6},{5,7},{6,4},{7,5},{8,10},{9,11},{10,... | collective-permute-start | bytes 294920 | tf_op jit(solution)/shard_map/ppermute | solution.py:51
  214.4 9.0 %collective-permute-start.38 = (bf16[128,384]{1,0:T(8,128)(2,1)S(1)}, bf16[128,384]{1,0:T(8,128)(2,1)S(1)}, u32[]{:S(2)}, u32[]{:S(2)}) collective-permute-start(bf16[128,384]{1,0:T(8,128)(2,1)S(1)} %broadcast_select_fusion), channel_id=1, source_target_pairs={{0,1},{1,0},{2,3},{3,2},{4,5},{5,4},{6,7},{7,6},{8,9},{9,8},{10,11... | collective-permute-start | bytes 294920 | tf_op jit(solution)/shard_map/ppermute | solution.py:51
  224.1 28.0 %collective-permute-start.45 = (bf16[2,2,4,32,768]{4,3,2,1,0:T(8,128)(2,1)}, bf16[2,2,4,32,768]{4,3,2,1,0:T(8,128)(2,1)}, u32[]{:S(2)}, u32[]{:S(2)}) collective-permute-start(bf16[2,2,4,32,768]{4,3,2,1,0:T(8,128)(2,1)} %collective-permute-done.41.across), channel_id=1, source_target_pairs={{1,0},{2,3},{5,4},{6,7},{9,8},{10,11},{13,12},{14,15},{17,16},{18,... | collective-permute-start | bytes 2359304 | tf_op jit(solution)/shard_map/ppermute | solution.py:140
  233.7 18.4 %collective-permute-start.43 = (bf16[16,48,384]{2,1,0:T(8,128)(2,1)}, bf16[16,48,384]{2,1,0:T(8,128)(2,1)}, u32[]{:S(2)}, u32[]{:S(2)}) collective-permute-start(bf16[16,48,384]{2,1,0:T(8,128)(2,1)} %get-tuple-element.332), channel_id=1, source_target_pairs={{0,4},{4,0},{1,5},{5,1},{2,6},{6,2},{3,7},{7,3},{8,12},{12,8},{9,1... | collective-permute-start | bytes 1769480 | tf_op jit(solution)/shard_map/ppermute | solution.py:46
  233.7 18.4 %collective-permute-start.44 = (bf16[16,48,384]{2,1,0:T(8,128)(2,1)S(1)}, bf16[16,48,384]{2,1,0:T(8,128)(2,1)}, u32[]{:S(2)}, u32[]{:S(2)}) collective-permute-start(bf16[16,48,384]{2,1,0:T(8,128)(2,1)S(1)} %get-tuple-element.333), channel_id=1, source_target_pairs={{0,4},{4,0},{1,5},{5,1},{2,6},{6,2},{3,7},{7,3},{8,12},{12,8},{9,1... | collective-permute-start | bytes 1769480 | tf_op jit(solution)/shard_map/ppermute | solution.py:46
  234.9 17.1 %collective-permute-start.42 = (bf16[2,96,768]{2,1,0:T(8,128)(2,1)}, bf16[2,96,768]{2,1,0:T(8,128)(2,1)S(1)}, u32[]{:S(2)}, u32[]{:S(2)}) collective-permute-start(bf16[2,96,768]{2,1,0:T(8,128)(2,1)} %slice.443), channel_id=1, source_target_pairs={{0,2},{1,3},{2,0},{3,1},{4,6},{5,7},{6,4},{7,5},{8,10},{9,11},{10,... | collective-permute-start | bytes 884744 | tf_op jit(solution)/shard_map/ppermute | solution.py:51
  252.8 19.1 %collective-permute-start.46 = (bf16[256,768]{1,0:T(8,128)(2,1)}, bf16[256,768]{1,0:T(8,128)(2,1)S(1)}, u32[]{:S(2)}, u32[]{:S(2)}) collective-permute-start(bf16[256,768]{1,0:T(8,128)(2,1)} %get-tuple-element.335.own), channel_id=1, source_target_pairs={{1,2},{2,1},{5,6},{6,5},{9,10},{10,9},{13,14},{14,13},{17,18},{18,... | collective-permute-start | bytes 1179656 | tf_op jit(solution)/shard_map/ppermute | solution.py:134
  253.7 18.9 %collective-permute-start.47 = (bf16[256,768]{1,0:T(8,128)(2,1)}, bf16[256,768]{1,0:T(8,128)(2,1)}, u32[]{:S(2)}, u32[]{:S(2)}) collective-permute-start(bf16[256,768]{1,0:T(8,128)(2,1)} %get-tuple-element.335.own), channel_id=1, source_target_pairs={{0,1},{1,0},{2,3},{3,2},{4,5},{5,4},{6,7},{7,6},{8,9},{9,8},{10,11... | collective-permute-start | bytes 1179656 | tf_op jit(solution)/shard_map/ppermute | solution.py:51
  257.6 14.3 %collective-permute-start.49 = (bf16[8,48,384]{2,1,0:T(8,128)(2,1)S(1)}, bf16[8,48,384]{2,1,0:T(8,128)(2,1)S(1)}, u32[]{:S(2)}, u32[]{:S(2)}) collective-permute-start(bf16[8,48,384]{2,1,0:T(8,128)(2,1)S(1)} %get-tuple-element.454), channel_id=1, source_target_pairs={{0,16},{16,0},{1,17},{17,1},{2,18},{18,2},{3,19},{19,3},{4,20},{20... | collective-permute-start | bytes 884744 | tf_op jit(solution)/shard_map/ppermute | solution.py:46
  260.8 11.1 %collective-permute-start.48 = (bf16[8,48,384]{2,1,0:T(8,128)(2,1)S(1)}, bf16[8,48,384]{2,1,0:T(8,128)(2,1)S(1)}, u32[]{:S(2)}, u32[]{:S(2)}) collective-permute-start(bf16[8,48,384]{2,1,0:T(8,128)(2,1)S(1)} %get-tuple-element.456), channel_id=1, source_target_pairs={{0,8},{8,0},{1,9},{9,1},{2,10},{10,2},{3,11},{11,3},{4,12},{12,4},... | collective-permute-start | bytes 884744 | tf_op jit(solution)/shard_map/ppermute | solution.py:46
  262.3 9.5 %collective-permute-start.50 = (bf16[2,48,768]{2,1,0:T(8,128)(2,1)S(1)}, bf16[2,48,768]{2,1,0:T(8,128)(2,1)S(1)}, u32[]{:S(2)}, u32[]{:S(2)}) collective-permute-start(bf16[2,48,768]{2,1,0:T(8,128)(2,1)S(1)} %get-tuple-element.470), channel_id=1, source_target_pairs={{0,2},{1,3},{2,0},{3,1},{4,6},{5,7},{6,4},{7,5},{8,10},{9,11},{10,... | collective-permute-start | bytes 442376 | tf_op jit(solution)/shard_map/ppermute | solution.py:51
  272.7 12.3 %collective-permute-start.51 = (bf16[16,96,384]{2,1,0:T(8,128)(2,1)}, bf16[16,96,384]{2,1,0:T(8,128)(2,1)}, u32[]{:S(2)}, u32[]{:S(2)}) collective-permute-start(bf16[16,96,384]{2,1,0:T(8,128)(2,1)} %get-tuple-element.346), channel_id=1, source_target_pairs={{0,4},{4,0},{1,5},{5,1},{2,6},{6,2},{3,7},{7,3},{8,12},{12,8},{9,1... | collective-permute-start | bytes 3538952 | tf_op jit(solution)/shard_map/ppermute | solution.py:46
  272.7 12.3 %collective-permute-start.52 = (bf16[16,96,384]{2,1,0:T(8,128)(2,1)}, bf16[16,96,384]{2,1,0:T(8,128)(2,1)}, u32[]{:S(2)}, u32[]{:S(2)}) collective-permute-start(bf16[16,96,384]{2,1,0:T(8,128)(2,1)} %get-tuple-element.347), channel_id=1, source_target_pairs={{0,4},{4,0},{1,5},{5,1},{2,6},{6,2},{3,7},{7,3},{8,12},{12,8},{9,1... | collective-permute-start | bytes 3538952 | tf_op jit(solution)/shard_map/ppermute | solution.py:46
  273.2 9.7 %collective-permute-start.55 = (bf16[2,48,768]{2,1,0:T(8,128)(2,1)}, bf16[2,48,768]{2,1,0:T(8,128)(2,1)}, u32[]{:S(2)}, u32[]{:S(2)}) collective-permute-start(bf16[2,48,768]{2,1,0:T(8,128)(2,1)} %get-tuple-element.469), channel_id=1, source_target_pairs={{0,2},{1,3},{2,0},{3,1},{4,6},{5,7},{6,4},{7,5},{8,10},{9,11},{10,... | collective-permute-start | bytes 442376 | tf_op jit(solution)/shard_map/ppermute | solution.py:51
  275.1 8.5 %collective-permute-start.54 = (bf16[4,48,384]{2,1,0:T(8,128)(2,1)}, bf16[4,48,384]{2,1,0:T(8,128)(2,1)}, u32[]{:S(2)}, u32[]{:S(2)}) collective-permute-start(bf16[4,48,384]{2,1,0:T(8,128)(2,1)} %get-tuple-element.468), channel_id=1, source_target_pairs={{0,8},{8,0},{1,9},{9,1},{2,10},{10,2},{3,11},{11,3},{4,12},{12,4},... | collective-permute-start | bytes 442376 | tf_op jit(solution)/shard_map/ppermute | solution.py:46
  277.6 7.4 %collective-permute-start.53 = (bf16[4,48,384]{2,1,0:T(8,128)(2,1)}, bf16[4,48,384]{2,1,0:T(8,128)(2,1)}, u32[]{:S(2)}, u32[]{:S(2)}) collective-permute-start(bf16[4,48,384]{2,1,0:T(8,128)(2,1)} %get-tuple-element.466), channel_id=1, source_target_pairs={{0,16},{16,0},{1,17},{17,1},{2,18},{18,2},{3,19},{19,3},{4,20},{20... | collective-permute-start | bytes 442376 | tf_op jit(solution)/shard_map/ppermute | solution.py:46
  283.0 13.3 %collective-permute-start.58 = (bf16[256,768]{1,0:T(8,128)(2,1)}, bf16[256,768]{1,0:T(8,128)(2,1)S(1)}, u32[]{:S(2)}, u32[]{:S(2)}) collective-permute-start(bf16[256,768]{1,0:T(8,128)(2,1)} %collective-permute-done.47.near), channel_id=1, source_target_pairs={{1,2},{2,1},{5,6},{6,5},{9,10},{10,9},{13,14},{14,13},{17,18},{18,... | collective-permute-start | bytes 1179656 | tf_op jit(solution)/shard_map/ppermute | solution.py:134
  283.7 16.0 %collective-permute-start.59 = (bf16[256,768]{1,0:T(8,128)(2,1)S(1)}, bf16[256,768]{1,0:T(8,128)(2,1)S(1)}, u32[]{:S(2)}, u32[]{:S(2)}) collective-permute-start(bf16[256,768]{1,0:T(8,128)(2,1)S(1)} %copy-done.41), channel_id=1, source_target_pairs={{1,0},{2,3},{5,4},{6,7},{9,8},{10,11},{13,12},{14,15},{17,16},{18,... | collective-permute-start | bytes 1179656 | tf_op jit(solution)/shard_map/ppermute | solution.py:140
  286.6 14.8 %collective-permute-start.57 = (bf16[8,96,384]{2,1,0:T(8,128)(2,1)S(1)}, bf16[8,96,384]{2,1,0:T(8,128)(2,1)S(1)}, u32[]{:S(2)}, u32[]{:S(2)}) collective-permute-start(bf16[8,96,384]{2,1,0:T(8,128)(2,1)S(1)} %get-tuple-element.440), channel_id=1, source_target_pairs={{0,16},{16,0},{1,17},{17,1},{2,18},{18,2},{3,19},{19,3},{4,20},{20... | collective-permute-start | bytes 1769480 | tf_op jit(solution)/shard_map/ppermute | solution.py:46
  288.6 14.9 %collective-permute-start.56 = (bf16[8,96,384]{2,1,0:T(8,128)(2,1)S(1)}, bf16[8,96,384]{2,1,0:T(8,128)(2,1)S(1)}, u32[]{:S(2)}, u32[]{:S(2)}) collective-permute-start(bf16[8,96,384]{2,1,0:T(8,128)(2,1)S(1)} %get-tuple-element.442), channel_id=1, source_target_pairs={{0,8},{8,0},{1,9},{9,1},{2,10},{10,2},{3,11},{11,3},{4,12},{12,4},... | collective-permute-start | bytes 1769480 | tf_op jit(solution)/shard_map/ppermute | solution.py:46
  290.4 10.9 %collective-permute-start.60 = (f32[24,768]{1,0:T(8,128)S(1)}, f32[24,768]{1,0:T(8,128)S(1)}, u32[]{:S(2)}, u32[]{:S(2)}) collective-permute-start(f32[24,768]{1,0:T(8,128)S(1)} %copy-done.93), channel_id=1, source_target_pairs={{0,1},{1,0},{2,3},{3,2},{4,5},{5,4},{6,7},{7,6},{8,9},{9,8},{10,11... | collective-permute-start | bytes 221192 | tf_op jit(solution)/shard_map/ppermute | solution.py:51
  296.2 17.4 %collective-permute-start.64 = (bf16[192,768]{1,0:T(8,128)(2,1)S(1)}, bf16[192,768]{1,0:T(8,128)(2,1)S(1)}, u32[]{:S(2)}, u32[]{:S(2)}) collective-permute-start(bf16[192,768]{1,0:T(8,128)(2,1)S(1)} %get-tuple-element.452), channel_id=1, source_target_pairs={{0,1},{1,0},{2,3},{3,2},{4,5},{5,4},{6,7},{7,6},{8,9},{9,8},{10,11... | collective-permute-start | bytes 884744 | tf_op jit(solution)/shard_map/ppermute | solution.py:51
  303.7 11.5 %collective-permute-start.62 = (bf16[4,96,384]{2,1,0:T(8,128)(2,1)S(1)}, bf16[4,96,384]{2,1,0:T(8,128)(2,1)S(1)}, u32[]{:S(2)}, u32[]{:S(2)}) collective-permute-start(bf16[4,96,384]{2,1,0:T(8,128)(2,1)S(1)} %get-tuple-element.450), channel_id=1, source_target_pairs={{0,8},{8,0},{1,9},{9,1},{2,10},{10,2},{3,11},{11,3},{4,12},{12,4},... | collective-permute-start | bytes 884744 | tf_op jit(solution)/shard_map/ppermute | solution.py:46
  305.1 10.1 %collective-permute-start.61 = (bf16[4,96,384]{2,1,0:T(8,128)(2,1)S(1)}, bf16[4,96,384]{2,1,0:T(8,128)(2,1)S(1)}, u32[]{:S(2)}, u32[]{:S(2)}) collective-permute-start(bf16[4,96,384]{2,1,0:T(8,128)(2,1)S(1)} %get-tuple-element.448), channel_id=1, source_target_pairs={{0,16},{16,0},{1,17},{17,1},{2,18},{18,2},{3,19},{19,3},{4,20},{20... | collective-permute-start | bytes 884744 | tf_op jit(solution)/shard_map/ppermute | solution.py:46
  306.0 13.0 %collective-permute-start.65 = (bf16[256,768]{1,0:T(8,128)(2,1)S(1)}, bf16[256,768]{1,0:T(8,128)(2,1)S(1)}, u32[]{:S(2)}, u32[]{:S(2)}) collective-permute-start(bf16[256,768]{1,0:T(8,128)(2,1)S(1)} %collective-permute-done.58.across_near), channel_id=1, source_target_pairs={{1,0},{2,3},{5,4},{6,7},{9,8},{10,11},{13,12},{14,15},{17,16},{18,... | collective-permute-start | bytes 1179656 | tf_op jit(solution)/shard_map/ppermute | solution.py:140
  321.0 12.8 %collective-permute-start.68 = (bf16[288,384]{1,0:T(8,128)(2,1)S(1)}, bf16[288,384]{1,0:T(8,128)(2,1)S(1)}, u32[]{:S(2)}, u32[]{:S(2)}) collective-permute-start(bf16[288,384]{1,0:T(8,128)(2,1)S(1)} %slice_bitcast_fusion.2), channel_id=1, source_target_pairs={{0,1},{1,0},{2,3},{3,2},{4,5},{5,4},{6,7},{7,6},{8,9},{9,8},{10,11... | collective-permute-start | bytes 663560 | tf_op jit(solution)/shard_map/ppermute | solution.py:51
  321.2 16.9 %collective-permute-start.69 = (bf16[288,384]{1,0:T(8,128)(2,1)S(1)}, bf16[288,384]{1,0:T(8,128)(2,1)S(1)}, u32[]{:S(2)}, u32[]{:S(2)}) collective-permute-start(bf16[288,384]{1,0:T(8,128)(2,1)S(1)} %get-tuple-element.481), channel_id=1, source_target_pairs={{0,2},{1,3},{2,0},{3,1},{4,6},{5,7},{6,4},{7,5},{8,10},{9,11},{10,... | collective-permute-start | bytes 663560 | tf_op jit(solution)/shard_map/ppermute | solution.py:51
  323.4 14.6 %collective-permute-start.70 = (bf16[288,384]{1,0:T(8,128)(2,1)S(1)}, bf16[288,384]{1,0:T(8,128)(2,1)S(1)}, u32[]{:S(2)}, u32[]{:S(2)}) collective-permute-start(bf16[288,384]{1,0:T(8,128)(2,1)S(1)} %get-tuple-element.482), channel_id=1, source_target_pairs={{0,3},{1,2},{2,1},{3,0},{4,7},{5,6},{6,5},{7,4},{8,11},{9,10},{10,... | collective-permute-start | bytes 663560 | tf_op jit(solution)/shard_map/ppermute | solution.py:51
  325.7 8.1 %collective-permute-start.67 = (f32[24,768]{1,0:T(8,128)S(1)}, f32[24,768]{1,0:T(8,128)S(1)}, u32[]{:S(2)}, u32[]{:S(2)}) collective-permute-start(f32[24,768]{1,0:T(8,128)S(1)} %add.277), channel_id=1, source_target_pairs={{0,8},{8,0},{1,9},{9,1},{2,10},{10,2},{3,11},{11,3},{4,12},{12,4},... | collective-permute-start | bytes 221192 | tf_op jit(solution)/shard_map/ppermute | solution.py:46
  333.8 8.7 %collective-permute-start.71 = (f32[24,768]{1,0:T(8,128)S(1)}, f32[24,768]{1,0:T(8,128)S(1)}, u32[]{:S(2)}, u32[]{:S(2)}) collective-permute-start(f32[24,768]{1,0:T(8,128)S(1)} %add.278), channel_id=1, source_target_pairs={{0,4},{4,0},{1,5},{5,1},{2,6},{6,2},{3,7},{7,3},{8,12},{12,8},{9,1... | collective-permute-start | bytes 221192 | tf_op jit(solution)/shard_map/ppermute | solution.py:46
  (114 other events, 804.0 us)
Sparse Core Ops, SparseCore 0:
  16.8 27.8 all-gather.1
  238.5 38.0 reduce-scatter.1

commit v6 on v5

--- a/solution.py
+++ b/solution.py
@@ -517,14 +517,19 @@
         x = tokens[...].reshape(rows, D)
         total = x.astype(F32) + vec[0:1, :]
         kept = []
-        for k, matrix in enumerate((w_qk, w_vc, w_oo)):
+
+        def arrive(k, matrix):
             settle(matrix, sems.at[1 + k])
             kept.append(pltpu.make_async_copy(matrix, wholes[k], sems.at[4 + k]))
             kept[-1].start()
+
+        arrive(0, w_qk)
         for j in range(mp):
             both = (dot(x, w_qk[j]) + heads[j, 0:1, :]).astype(BF)
             qk_out[j] = both
             q, k = both[:, :width], both[:, width:]
+            if j == 0:
+                arrive(1, w_vc)
             v = (dot(x, w_vc[j]) + heads[j, 1:2, :]).astype(BF)[:, :width]
             v_out[j] = v
             context = jnp.zeros((rows, width), F32)
@@ -533,6 +538,8 @@
                 context = context + only(dot(probs.astype(BF), v), lane)
             context = context.astype(BF)
             context_out[j] = context
+            if j == 0:
+                arrive(2, w_oo)
             total = total + dot_t(before(context, width), w_oo[j])
         z_out[...] = total
         normed, _ = norm_parts(total)
@@ -743,9 +750,9 @@
             value = (pre * cdf).astype(BF)
             act[z] = value
             slope[z] = cdf + pre * jnp.exp(-0.5 * pre * pre) * (1.0 / math.sqrt(2.0 * math.pi))
-            if z == 0:
-                settle(w_down, w_sems.at[1])
-            total = total + dot_t(value, w_down[z])
+        settle(w_down, w_sems.at[1])
+        for z in range(mp):
+            total = total + dot_t(act[z], w_down[z])
         normed, inverse = norm_parts(total)
         gain = vec[pl.ds(8 + 2 * group, 1), :]
         third = normed * gain + vec[pl.ds(9 + 2 * group, 1), :]
@@ -984,7 +991,7 @@
         token_back, vectors, maps_back, value_maps = rest[:4]
         w_qk, w_vc, w_oo, w_sems = rest[4:]
         me = lax.axis_index("mp")
-        for k, target in enumerate((w_qk, w_vc, w_oo)):
+        for k, target in ((2, w_oo), (0, w_qk), (1, w_vc)):
             fetch_whole(wholes[k], target, w_sems.at[k])
         mask = self_mask(plan, lengths, me)
         lanes = head_lanes(width)

time: 358 us -> 358 us (level)
  transfers between devices with their start and end apart: 74 -> 74, of which waited for: 24 -> 25; matrix products, arithmetic and copies ran while one was open for 14% -> 14% of each run, Pallas kernels for 23% -> 22%
where the time goes in v6:
time: 358 us; the launch traced here: 351 us
  Pallas kernels  92.7 us (26%)
  waiting for transfers between devices  87.5 us (24%)
  starting transfers between devices  83.5 us (23%)
  local copies, waits for them, and re-layouts  36.8 us (10%)
  other arithmetic  34.1 us (10%)
  between operations  16.4 us (5%)
    pallas_call x15, Pallas kernels, call(): pl.pallas_call(kernel, out_shape=outs, in_specs=[pl.BlockSpec(memory_spac...  92.7 us
    ppermute x27, waiting for transfers between devices, mp_swap(): return lax.ppermute(values, 'mp', [(i, i ^ distance) for i in range(count)])  58.3 us
    ppermute x27, starting transfers between devices, mp_swap(): return lax.ppermute(values, 'mp', [(i, i ^ distance) for i in range(count)])  45 us
    unnamed x221, local copies, waits for them, and re-layouts  32.1 us
    ppermute x39, starting transfers between devices, swap(): return lax.ppermute(values, axis, [(0, 1), (1, 0)])  31 us
    ppermute x39, waiting for transfers between devices, swap(): return lax.ppermute(values, axis, [(0, 1), (1, 0)])  23.4 us
    convert_element_type x18, other arithmetic, add_low(): return (first.astype(F32) + second.astype(F32)).astype(BF)  22 us
  transfers between devices with their start and end apart: 74, of which 25 were waited for; matrix products, arithmetic and copies ran while one was open for 14% of the time, Pallas kernels for 22%

profile of v6, /device:TPU:0, one launch (start us, length us, event | category | flops | bytes accessed | tf_op | source)
XLA Modules:
  0.0 351.0 jit_solution(18411332873174390556)
XLA Ops:
  10.1 3.1 collective-permute-start
  13.2 2.6 collective-permute-start.1
  16.8 11.5 %copy.55.images = bf16[16,257,1408]{2,1,0:T(8,128)(2,1)} copy(bf16[16,257,1408]{2,0,1:T(8,128)(2,1)} %param.29) | data formatting | bytes 23158784 | tf_op args[1]
  30.0 3.2 collective-permute-done.1
  33.4 1.6 collective-permute-start.4
  35.0 1.6 collective-permute-start.3
  36.6 4.3 %collective-permute-start.5 = (bf16[192,768]{1,0:T(8,128)(2,1)S(1)}, bf16[192,768]{1,0:T(8,128)(2,1)S(1)}, u32[]{:S(2)}, u32[]{:S(2)}) collective-permute-start(bf16[192,768]{1,0:T(8,128)(2,1)S(1)} %get-tuple-element.215), channel_id=1, source_target_pairs={{0,1},{1,0},{2,3},{3,2},{4,5},{5,4},{6,7},{7,6},{8,9},{9,8},{10,11... | collective-permute-start | bytes 884744 | tf_op jit(solution)/shard_map/ppermute | solution.py:51
  41.0 5.1 %collective-permute-done.5 = bf16[192,768]{1,0:T(8,128)(2,1)S(1)} collective-permute-done((bf16[192,768]{1,0:T(8,128)(2,1)S(1)}, bf16[192,768]{1,0:T(8,128)(2,1)S(1)}, u32[]{:S(2)}, u32[]{:S(2)}) %collective-permute-start.5) | collective-permute-done | bytes 294944 | tf_op jit(solution)/shard_map/ppermute | solution.py:51
  47.3 1.6 collective-permute-start.8
  49.7 5.2 %collective-permute-start.11 = (bf16[2,96,768]{2,1,0:T(8,128)(2,1)S(1)}, bf16[2,96,768]{2,1,0:T(8,128)(2,1)}, u32[]{:S(2)}, u32[]{:S(2)}) collective-permute-start(bf16[2,96,768]{2,1,0:T(8,128)(2,1)S(1)} %get-tuple-element.471), channel_id=1, source_target_pairs={{0,2},{1,3},{2,0},{3,1},{4,6},{5,7},{6,4},{7,5},{8,10},{9,11},{10,... | collective-permute-start | bytes 884744 | tf_op jit(solution)/shard_map/ppermute | solution.py:51
  54.8 4.4 %copy-done = bf16[16,257,1408]{2,1,0:T(8,128)(2,1)S(1)} copy-done((bf16[16,257,1408]{2,1,0:T(8,128)(2,1)S(1)}, bf16[16,257,1408]{2,1,0:T(8,128)(2,1)}, u32[]{:S(2)}) %copy-start) | copy-done | bytes 11579416
  60.5 11.1 %shard_map.467.refs_3_.refs_6_ = bf16[16,384,384]{2,1,0:T(8,128)(2,1)S(1)} custom-call(bf16[16,257,1408]{2,1,0:T(8,128)(2,1)S(1)} %copy-done, f32[8,384]{1,0:T(8,128)S(1)} %concatenate.84.bias, bf16[1408,384]{1,0:T(8,128)(2,1)S(1)} %copy-done.22), custom_call_target="tpu_custom_call" | custom-call | flops 1000 | bytes 1000 | tf_op jit(solution)/shard_map/pallas_call | solution.py:440
  74.8 3.3 collective-permute-start.6
  82.0 10.2 %shard_map.468 = (bf16[4,256,384]{2,1,0:T(8,128)(2,1)S(1)}, bf16[4,256,192]{2,1,0:T(8,128)(2,1)S(1)}, bf16[4,256,192]{2,1,0:T(8,128)(2,1)S(1)}, f32[256,768]{1,0...) custom-call(s32[16]{0:T(128)S(1)} %copy-done.53, ...), custom_call_target="tpu_custom_call" | custom-call | flops 1000 | bytes 1000 | tf_op jit(solution)/shard_map/pallas_call | solution.py:440
  95.9 1.5 collective-permute-start.17
  99.5 5.5 %collective-permute-done.15.refs_2_ = bf16[128,384]{1,0:T(8,128)(2,1)S(1)} collective-permute-done((bf16[128,384]{1,0:T(8,128)(2,1)S(1)}, bf16[128,384]{1,0:T(8,128)(2,1)S(1)}, u32[]{:S(2)}, u32[]{:S(2)}) %collective-permute-start.15) | collective-permute-done | bytes 98336 | tf_op jit(solution)/shard_map/ppermute | solution.py:51
  106.2 3.5 collective-permute-done.16.refs_1_
  109.7 6.2 %shard_map.469 = (bf16[128,192]{1,0:T(8,128)(2,1)S(1)}, bf16[128,384]{1,0:T(8,128)(2,1)S(1)}, bf16[128,384]{1,0:T(8,128)(2,1)S(1)}) custom-call(bf16[128,192]{1,0:T(8,128)(2,1)S(1)} %get-tuple-element.233.refs_0_, bf16[128,384]{1,0:T(8,128)(2,1)S(1)} %collective-permute-done.16.refs_1_, bf16[128,384]{1,0:T(8,128)(2,1)S(1)} %collective-permute-done.15.refs_2_, ...), custom_call_target="tpu_custom_call" | custom-call | flops 1000 | bytes 1000 | tf_op jit(solution)/shard_map/pallas_call | solution.py:440
  116.7 6.6 %collective-permute-done.19 = bf16[4,96,768]{2,1,0:T(8,128)(2,1)S(1)} collective-permute-done((bf16[4,96,768]{2,1,0:T(8,128)(2,1)S(1)}, bf16[4,96,768]{2,1,0:T(8,128)(2,1)S(1)}, u32[]{:S(2)}, u32[]{:S(2)}) %collective-permute-start.19) | collective-permute-done | bytes 589856 | tf_op jit(solution)/shard_map/ppermute | solution.py:46
  123.9 1.5 collective-permute-start.22
  126.2 4.6 %collective-permute-done.25.rest_1_ = bf16[128,384]{1,0:T(8,128)(2,1)S(1)} collective-permute-done((bf16[128,384]{1,0:T(8,128)(2,1)S(1)}, bf16[128,384]{1,0:T(8,128)(2,1)S(1)}, u32[]{:S(2)}, u32[]{:S(2)}) %collective-permute-start.25) | collective-permute-done | bytes 98336 | tf_op jit(solution)/shard_map/ppermute | solution.py:51
  130.8 1.5 shard_map.470
  132.4 6.8 %collective-permute-done.22 = bf16[4,96,768]{2,1,0:T(8,128)(2,1)S(1)} collective-permute-done((bf16[4,96,768]{2,1,0:T(8,128)(2,1)S(1)}, bf16[4,96,768]{2,1,0:T(8,128)(2,1)S(1)}, u32[]{:S(2)}, u32[]{:S(2)}) %collective-permute-start.22) | collective-permute-done | bytes 589856 | tf_op jit(solution)/shard_map/ppermute | solution.py:46
  141.3 3.1 collective-permute-done.27.rest_3_
  145.5 14.5 %shard_map.471 = (bf16[2,4,32,768]{3,2,1,0:T(8,128)(2,1)S(1)}, f32[128,768]{1,0:T(8,128)S(1)}, bf16[128,768]{1,0:T(8,128)(2,1)S(1)}, f32[3,768]{1,0:T(4,128)S(1)...) custom-call(f32[12,768]{1,0:T(8,128)S(1)} %copy-done.6, ...), custom_call_target="tpu_custom_call" | custom-call | flops 1000 | bytes 1000 | tf_op jit(solution)/shard_map/pallas_call | solution.py:440
  160.6 6.9 %collective-permute-done.29.got = bf16[128,768]{1,0:T(8,128)(2,1)S(1)} collective-permute-done((bf16[128,768]{1,0:T(8,128)(2,1)S(1)}, bf16[128,768]{1,0:T(8,128)(2,1)S(1)}, u32[]{:S(2)}, u32[]{:S(2)}) %collective-permute-start.29) | collective-permute-done | bytes 196640 | tf_op jit(solution)/shard_map/ppermute | solution.py:51
  168.2 2.5 add_convert_fusion.3
  172.0 1.5 collective-permute-start.36
  175.1 1.7 collective-permute-start.34
  176.8 4.3 %collective-permute-done.32.refs_5_ = bf16[128,384]{1,0:T(8,128)(2,1)S(1)} collective-permute-done((bf16[128,384]{1,0:T(8,128)(2,1)S(1)}, bf16[128,384]{1,0:T(8,128)(2,1)S(1)}, u32[]{:S(2)}, u32[]{:S(2)}) %collective-permute-start.32) | collective-permute-done | bytes 98336 | tf_op jit(solution)/shard_map/ppermute | solution.py:51
  181.2 8.5 %collective-permute-done.33.refs_4_ = bf16[128,384]{1,0:T(8,128)(2,1)S(1)} collective-permute-done((bf16[128,384]{1,0:T(8,128)(2,1)S(1)}, bf16[128,384]{1,0:T(8,128)(2,1)S(1)}, u32[]{:S(2)}, u32[]{:S(2)}) %collective-permute-start.33) | collective-permute-done | bytes 98336 | tf_op jit(solution)/shard_map/ppermute | solution.py:51
  189.8 1.7 collective-permute-start.41
  191.5 9.8 %shard_map.473 = (bf16[16,384,384]{2,1,0:T(8,128)(2,1)S(1)}, f32[1,192]{1,0:T(1,128)S(1)}, bf16[128,192]{1,0:T(8,128)(2,1)S(1)}, bf16[128,384]{1,0:T(8,128)(2,1)S(1)}, bf16[128,384]{1,0:T(8,128)(2,1)S(1)}) custom-call(bf16[128,192]{1,0:T(8,128)(2,1)S(1)} %get-tuple-element.233.refs_0_, bf16[128,384]{1,0:T(8,128)(2,1)S(1)} %collective-permute-done.16.refs_1_, ...), custom_call_target="tpu_custom_call" | custom-call | flops 1000 | bytes 1000 | tf_op jit(solution)/shard_map/pallas_call | solution.py:440
  206.1 2.4 collective-permute-start.37
  208.5 6.0 %collective-permute-done.37.rest_2_.rest_6_ = bf16[128,384]{1,0:T(8,128)(2,1)S(1)} collective-permute-done((bf16[128,384]{1,0:T(8,128)(2,1)S(1)}, bf16[128,384]{1,0:T(8,128)(2,1)S(1)}, u32[]{:S(2)}, u32[]{:S(2)}) %collective-permute-start.37) | collective-permute-done | bytes 98336 | tf_op jit(solution)/shard_map/ppermute | solution.py:51
  214.6 8.9 %shard_map.474 = bf16[1408,384]{1,0:T(8,128)(2,1)} custom-call(bf16[16,257,1408]{2,1,0:T(8,128)(2,1)} %copy.55.images, bf16[16,384,384]{2,1,0:T(8,128)(2,1)S(1)} %get-tuple-element.303.kv_back), custom_call_target="tpu_custom_call" | custom-call | flops 1000 | bytes 1000 | tf_op jit(solution)/shard_map/pallas_call | solution.py:440
  225.7 1.5 add_convert_fusion.23
  230.4 2.4 shard_map.476
  235.1 3.4 collective-permute-start.42
  238.4 12.3 %shard_map.477 = (bf16[256,768]{1,0:T(8,128)(2,1)}, f32[24,768]{1,0:T(8,128)}, bf16[4,256,384]{2,1,0:T(8,128)(2,1)}, bf16[4,256,192]{2,1,0:T(8,128)(2,1)}) custom-call(s32[16]{0:T(128)} %lengths.3, f32[12,768]{1,0:T(8,128)} %rest_0_.3, f32[256,768]{1,0:T(8,128)} %copy-done.8, bf16[4,256,384]{2,1,0:T(8,128)(2,1)} %copy-done.25, ...), custom_call_target="tpu_custom_call" | custom-call | flops 1000 | bytes 1000 | tf_op jit(solution)/shard_map/pallas_call | solution.py:440
  255.3 2.0 add_convert_fusion.18
  258.6 1.9 add_convert_fusion.19
  262.1 1.6 collective-permute-start.50
  263.7 4.1 %shard_map.478 = (bf16[16,96,384]{2,1,0:T(8,128)(2,1)S(1)}, bf16[16,96,384]{2,1,0:T(8,128)(2,1)}, bf16[16,96,384]{2,1,0:T(8,128)(2,1)S(1)}, bf16[16,96,384]{2,1,0:T(8,128)(2,1)}) custom-call(bf16[16,64,768]{2,1,0:T(8,128)(2,1)S(1)} %copy-done.5, f32[12,768]{1,0:T(8,128)S(1)} %copy-done.7, f32[256,768]{1,0:T(8,128)S(1)} %get-tuple-element.250.z_first.rest_1_, ...), custom_call_target="tpu_custom_call" | custom-call | flops 1000 | bytes 1000 | tf_op jit(solution)/shard_map/pallas_call | solution.py:440
  268.9 2.1 collective-permute-done.50
  272.8 1.9 add_convert_fusion.28
  275.3 1.9 add_convert_fusion.29
  278.8 2.8 shard_map.480
  284.6 1.5 add_convert_fusion.4
  286.8 1.5 add_convert_fusion.5
  288.3 1.5 collective-permute-start.56
  290.0 4.4 %collective-permute-start.60 = (f32[24,768]{1,0:T(8,128)S(1)}, f32[24,768]{1,0:T(8,128)S(1)}, u32[]{:S(2)}, u32[]{:S(2)}) collective-permute-start(f32[24,768]{1,0:T(8,128)S(1)} %copy-done.93), channel_id=1, source_target_pairs={{0,1},{1,0},{2,3},{3,2},{4,5},{5,4},{6,7},{7,6},{8,9},{9,8},{10,11... | collective-permute-start | bytes 221192 | tf_op jit(solution)/shard_map/ppermute | solution.py:51
  296.7 2.1 collective-permute-done.59.far_own
  298.8 1.6 collective-permute-done.60
  300.7 2.5 collective-permute-done.56
  304.4 1.5 collective-permute-start.61
  308.2 4.0 %collective-permute-start.63 = (f32[24,768]{1,0:T(8,128)S(1)}, f32[24,768]{1,0:T(8,128)S(1)}, u32[]{:S(2)}, u32[]{:S(2)}) collective-permute-start(f32[24,768]{1,0:T(8,128)S(1)} %add.270), channel_id=1, source_target_pairs={{0,2},{1,3},{2,0},{3,1},{4,6},{5,7},{6,4},{7,5},{8,10},{9,11},{10,... | collective-permute-start | bytes 221192 | tf_op jit(solution)/shard_map/ppermute | solution.py:51
  314.7 3.7 %collective-permute-done.65.far_near = bf16[256,768]{1,0:T(8,128)(2,1)S(1)} collective-permute-done((bf16[256,768]{1,0:T(8,128)(2,1)S(1)}, bf16[256,768]{1,0:T(8,128)(2,1)S(1)}, u32[]{:S(2)}, u32[]{:S(2)}) %collective-permute-start.65) | collective-permute-done | bytes 393248 | tf_op jit(solution)/shard_map/ppermute | solution.py:140
  318.4 1.5 collective-permute-start.66
  320.4 2.3 collective-permute-start.69
  322.7 2.1 collective-permute-start.70
  326.7 3.0 shard_map.479
  329.8 3.2 shard_map.481
  333.2 4.1 %collective-permute-done.69 = bf16[288,384]{1,0:T(8,128)(2,1)S(1)} collective-permute-done((bf16[288,384]{1,0:T(8,128)(2,1)S(1)}, bf16[288,384]{1,0:T(8,128)(2,1)S(1)}, u32[]{:S(2)}, u32[]{:S(2)}) %collective-permute-start.69) | collective-permute-done | bytes 221216 | tf_op jit(solution)/shard_map/ppermute | solution.py:51
  (419 shorter events, 77.6 us)
Async XLA Ops:
  7.2 47.6 %all-gather.2.cloned.1.call-start = ((), (), s32[]{:S(2)}) async-start(), calls=%async_computation.1 | async-start | bytes 1216512 | tf_op jit(solution)/shard_map/all_gather | solution.py:1394
  10.1 19.8 %collective-permute-start = (bf16[312,384]{1,0:T(8,128)(2,1)S(1)}, bf16[312,384]{1,0:T(8,128)(2,1)S(1)}, u32[]{:S(2)}, u32[]{:S(2)}) collective-permute-start(bf16[312,384]{1,0:T(8,128)(2,1)S(1)} %constant_dynamic-update-slice_fusion), channel_id=1, source_target_pairs={{0,1},{1,0},{2,3},{3,2},{4,5},{5,4},{6,7},{7,6},{8,9},{9,8},{10,11... | collective-permute-start | bytes 718856 | tf_op jit(solution)/shard_map/ppermute | solution.py:51
  13.2 19.9 %collective-permute-start.1 = (bf16[312,384]{1,0:T(8,128)(2,1)S(1)}, bf16[312,384]{1,0:T(8,128)(2,1)S(1)}, u32[]{:S(2)}, u32[]{:S(2)}) collective-permute-start(bf16[312,384]{1,0:T(8,128)(2,1)S(1)} %constant_dynamic-update-slice_fusion), channel_id=1, source_target_pairs={{0,2},{1,3},{2,0},{3,1},{4,6},{5,7},{6,4},{7,5},{8,10},{9,11},{10,... | collective-permute-start | bytes 718856 | tf_op jit(solution)/shard_map/ppermute | solution.py:51
  15.8 17.3 %collective-permute-start.2 = (bf16[312,384]{1,0:T(8,128)(2,1)S(1)}, bf16[312,384]{1,0:T(8,128)(2,1)S(1)}, u32[]{:S(2)}, u32[]{:S(2)}) collective-permute-start(bf16[312,384]{1,0:T(8,128)(2,1)S(1)} %constant_dynamic-update-slice_fusion), channel_id=1, source_target_pairs={{0,3},{1,2},{2,1},{3,0},{4,7},{5,6},{6,5},{7,4},{8,11},{9,10},{10,... | collective-permute-start | bytes 718856 | tf_op jit(solution)/shard_map/ppermute | solution.py:51
  16.7 264.9 %reduce-scatter.2.cloned.1.call-start = ((), (), s32[]{:S(2)}) async-start(), calls=%async_computation.2 | async-start | bytes 1216512 | tf_op jit(solution)/shard_map/reduce_scatter | solution.py:1529
  33.4 12.8 %collective-permute-start.4 = (bf16[4,144,384]{2,1,0:T(8,128)(2,1)S(1)}, bf16[4,144,384]{2,1,0:T(8,128)(2,1)S(1)}, u32[]{:S(2)}, u32[]{:S(2)}) collective-permute-start(bf16[4,144,384]{2,1,0:T(8,128)(2,1)S(1)} %pad_maximum_fusion.10), channel_id=1, source_target_pairs={{0,8},{8,0},{1,9},{9,1},{2,10},{10,2},{3,11},{11,3},{4,12},{12,4},... | collective-permute-start | bytes 1327112 | tf_op jit(solution)/shard_map/ppermute | solution.py:46
  35.0 12.1 %collective-permute-start.3 = (bf16[4,144,384]{2,1,0:T(8,128)(2,1)S(1)}, bf16[4,144,384]{2,1,0:T(8,128)(2,1)S(1)}, u32[]{:S(2)}, u32[]{:S(2)}) collective-permute-start(bf16[4,144,384]{2,1,0:T(8,128)(2,1)S(1)} %pad_maximum_fusion.9), channel_id=1, source_target_pairs={{0,16},{16,0},{1,17},{17,1},{2,18},{18,2},{3,19},{19,3},{4,20},{20... | collective-permute-start | bytes 1327112 | tf_op jit(solution)/shard_map/ppermute | solution.py:46
  36.6 9.6 %collective-permute-start.5 = (bf16[192,768]{1,0:T(8,128)(2,1)S(1)}, bf16[192,768]{1,0:T(8,128)(2,1)S(1)}, u32[]{:S(2)}, u32[]{:S(2)}) collective-permute-start(bf16[192,768]{1,0:T(8,128)(2,1)S(1)} %get-tuple-element.215), channel_id=1, source_target_pairs={{0,1},{1,0},{2,3},{3,2},{4,5},{5,4},{6,7},{7,6},{8,9},{9,8},{10,11... | collective-permute-start | bytes 884744 | tf_op jit(solution)/shard_map/ppermute | solution.py:51
  47.2 24.4 %collective-permute-start.10 = (bf16[8,144,384]{2,1,0:T(8,128)(2,1)S(1)}, bf16[8,144,384]{2,1,0:T(8,128)(2,1)S(1)}, u32[]{:S(2)}, u32[]{:S(2)}) collective-permute-start(bf16[8,144,384]{2,1,0:T(8,128)(2,1)S(1)} %constant_dynamic-update-slice_fusion.10.rest_4_), channel_id=1, source_target_pairs={{0,4},{4,0},{1,5},{5,1},{2,6},{6,2},{3,7},{7,3},{8,12},{12,8},{9,1... | collective-permute-start | bytes 2654216 | tf_op jit(solution)/shard_map/ppermute | solution.py:46
  47.3 24.4 %collective-permute-start.8 = (bf16[8,144,384]{2,1,0:T(8,128)(2,1)S(1)}, bf16[8,144,384]{2,1,0:T(8,128)(2,1)}, u32[]{:S(2)}, u32[]{:S(2)}) collective-permute-start(bf16[8,144,384]{2,1,0:T(8,128)(2,1)S(1)} %constant_dynamic-update-slice_fusion.10.rest_4_), channel_id=1, source_target_pairs={{0,16},{16,0},{1,17},{17,1},{2,18},{18,2},{3,19},{19,3},{4,20},{20... | collective-permute-start | bytes 2654216 | tf_op jit(solution)/shard_map/ppermute | solution.py:46
  49.0 22.7 %collective-permute-start.7 = (bf16[8,144,384]{2,1,0:T(8,128)(2,1)S(1)}, bf16[8,144,384]{2,1,0:T(8,128)(2,1)}, u32[]{:S(2)}, u32[]{:S(2)}) collective-permute-start(bf16[8,144,384]{2,1,0:T(8,128)(2,1)S(1)} %constant_dynamic-update-slice_fusion.5.rest_0_), channel_id=1, source_target_pairs={{0,8},{8,0},{1,9},{9,1},{2,10},{10,2},{3,11},{11,3},{4,12},{12,4},... | collective-permute-start | bytes 2654216 | tf_op jit(solution)/shard_map/ppermute | solution.py:46
  49.6 22.1 %collective-permute-start.9 = (bf16[8,144,384]{2,1,0:T(8,128)(2,1)S(1)}, bf16[8,144,384]{2,1,0:T(8,128)(2,1)}, u32[]{:S(2)}, u32[]{:S(2)}) collective-permute-start(bf16[8,144,384]{2,1,0:T(8,128)(2,1)S(1)} %constant_dynamic-update-slice_fusion.5.rest_0_), channel_id=1, source_target_pairs={{0,4},{4,0},{1,5},{5,1},{2,6},{6,2},{3,7},{7,3},{8,12},{12,8},{9,1... | collective-permute-start | bytes 2654216 | tf_op jit(solution)/shard_map/ppermute | solution.py:46
  49.7 22.0 %collective-permute-start.11 = (bf16[2,96,768]{2,1,0:T(8,128)(2,1)S(1)}, bf16[2,96,768]{2,1,0:T(8,128)(2,1)}, u32[]{:S(2)}, u32[]{:S(2)}) collective-permute-start(bf16[2,96,768]{2,1,0:T(8,128)(2,1)S(1)} %get-tuple-element.471), channel_id=1, source_target_pairs={{0,2},{1,3},{2,0},{3,1},{4,6},{5,7},{6,4},{7,5},{8,10},{9,11},{10,... | collective-permute-start | bytes 884744 | tf_op jit(solution)/shard_map/ppermute | solution.py:51
  71.7 7.9 %collective-permute-start.12 = (bf16[8,144,384]{2,1,0:T(8,128)(2,1)}, bf16[8,144,384]{2,1,0:T(8,128)(2,1)S(1)}, u32[]{:S(2)}, u32[]{:S(2)}) collective-permute-start(bf16[8,144,384]{2,1,0:T(8,128)(2,1)} %collective-permute-done.7.rest_1_), channel_id=1, source_target_pairs={{0,4},{4,0},{1,5},{5,1},{2,6},{6,2},{3,7},{7,3},{8,12},{12,8},{9,1... | collective-permute-start | bytes 2654216 | tf_op jit(solution)/shard_map/ppermute | solution.py:46
  72.0 7.6 %collective-permute-start.13 = (bf16[8,144,384]{2,1,0:T(8,128)(2,1)}, bf16[8,144,384]{2,1,0:T(8,128)(2,1)S(1)}, u32[]{:S(2)}, u32[]{:S(2)}) collective-permute-start(bf16[8,144,384]{2,1,0:T(8,128)(2,1)} %collective-permute-done.8.rest_5_), channel_id=1, source_target_pairs={{0,4},{4,0},{1,5},{5,1},{2,6},{6,2},{3,7},{7,3},{8,12},{12,8},{9,1... | collective-permute-start | bytes 2654216 | tf_op jit(solution)/shard_map/ppermute | solution.py:46
  73.3 22.5 %collective-permute-start.14 = (bf16[4,96,768]{2,1,0:T(8,128)(2,1)S(1)}, bf16[4,96,768]{2,1,0:T(8,128)(2,1)S(1)}, u32[]{:S(2)}, u32[]{:S(2)}) collective-permute-start(bf16[4,96,768]{2,1,0:T(8,128)(2,1)S(1)} %pad_maximum_fusion.5), channel_id=1, source_target_pairs={{0,16},{16,0},{1,17},{17,1},{2,18},{18,2},{3,19},{19,3},{4,20},{20... | collective-permute-start | bytes 1769480 | tf_op jit(solution)/shard_map/ppermute | solution.py:46
  74.8 21.0 %collective-permute-start.6 = (bf16[2,96,768]{2,1,0:T(8,128)(2,1)S(1)}, bf16[2,96,768]{2,1,0:T(8,128)(2,1)S(1)}, u32[]{:S(2)}, u32[]{:S(2)}) collective-permute-start(bf16[2,96,768]{2,1,0:T(8,128)(2,1)S(1)} %get-tuple-element.472), channel_id=1, source_target_pairs={{0,2},{1,3},{2,0},{3,1},{4,6},{5,7},{6,4},{7,5},{8,10},{9,11},{10,... | collective-permute-start | bytes 884744 | tf_op jit(solution)/shard_map/ppermute | solution.py:51
  95.9 20.0 %collective-permute-start.17 = (bf16[4,96,768]{2,1,0:T(8,128)(2,1)S(1)}, bf16[4,96,768]{2,1,0:T(8,128)(2,1)S(1)}, u32[]{:S(2)}, u32[]{:S(2)}) collective-permute-start(bf16[4,96,768]{2,1,0:T(8,128)(2,1)S(1)} %pad_maximum_fusion.6), channel_id=1, source_target_pairs={{0,8},{8,0},{1,9},{9,1},{2,10},{10,2},{3,11},{11,3},{4,12},{12,4},... | collective-permute-start | bytes 1769480 | tf_op jit(solution)/shard_map/ppermute | solution.py:46
  97.5 25.9 %collective-permute-start.19 = (bf16[4,96,768]{2,1,0:T(8,128)(2,1)S(1)}, bf16[4,96,768]{2,1,0:T(8,128)(2,1)S(1)}, u32[]{:S(2)}, u32[]{:S(2)}) collective-permute-start(bf16[4,96,768]{2,1,0:T(8,128)(2,1)S(1)} %pad_maximum_fusion.5), channel_id=1, source_target_pairs={{0,8},{8,0},{1,9},{9,1},{2,10},{10,2},{3,11},{11,3},{4,12},{12,4},... | collective-permute-start | bytes 1769480 | tf_op jit(solution)/shard_map/ppermute | solution.py:46
  98.0 25.3 %collective-permute-start.20 = (bf16[4,96,768]{2,1,0:T(8,128)(2,1)S(1)}, bf16[4,96,768]{2,1,0:T(8,128)(2,1)S(1)}, u32[]{:S(2)}, u32[]{:S(2)}) collective-permute-start(bf16[4,96,768]{2,1,0:T(8,128)(2,1)S(1)} %pad_maximum_fusion.6), channel_id=1, source_target_pairs={{0,16},{16,0},{1,17},{17,1},{2,18},{18,2},{3,19},{19,3},{4,20},{20... | collective-permute-start | bytes 1769480 | tf_op jit(solution)/shard_map/ppermute | solution.py:46
  116.0 7.4 %collective-permute-start.18 = (bf16[128,384]{1,0:T(8,128)(2,1)S(1)}, bf16[128,384]{1,0:T(8,128)(2,1)S(1)}, u32[]{:S(2)}, u32[]{:S(2)}) collective-permute-start(bf16[128,384]{1,0:T(8,128)(2,1)S(1)} %get-tuple-element.243), channel_id=1, source_target_pairs={{0,2},{1,3},{2,0},{3,1},{4,6},{5,7},{6,4},{7,5},{8,10},{9,11},{10,... | collective-permute-start | bytes 294920 | tf_op jit(solution)/shard_map/ppermute | solution.py:51
  123.3 17.4 %collective-permute-start.23 = (bf16[8,96,768]{2,1,0:T(8,128)(2,1)S(1)}, bf16[8,96,768]{2,1,0:T(8,128)(2,1)S(1)}, u32[]{:S(2)}, u32[]{:S(2)}) collective-permute-start(bf16[8,96,768]{2,1,0:T(8,128)(2,1)S(1)} %pad_maximum_fusion.1.rest_0_), channel_id=1, source_target_pairs={{0,4},{4,0},{1,5},{5,1},{2,6},{6,2},{3,7},{7,3},{8,12},{12,8},{9,1... | collective-permute-start | bytes 3538952 | tf_op jit(solution)/shard_map/ppermute | solution.py:46
  123.3 17.4 %collective-permute-start.24 = (bf16[8,96,768]{2,1,0:T(8,128)(2,1)S(1)}, bf16[8,96,768]{2,1,0:T(8,128)(2,1)S(1)}, u32[]{:S(2)}, u32[]{:S(2)}) collective-permute-start(bf16[8,96,768]{2,1,0:T(8,128)(2,1)S(1)} %pad_maximum_fusion.rest_4_), channel_id=1, source_target_pairs={{0,4},{4,0},{1,5},{5,1},{2,6},{6,2},{3,7},{7,3},{8,12},{12,8},{9,1... | collective-permute-start | bytes 3538952 | tf_op jit(solution)/shard_map/ppermute | solution.py:46
  123.9 15.4 %collective-permute-start.22 = (bf16[4,96,768]{2,1,0:T(8,128)(2,1)S(1)}, bf16[4,96,768]{2,1,0:T(8,128)(2,1)S(1)}, u32[]{:S(2)}, u32[]{:S(2)}) collective-permute-start(bf16[4,96,768]{2,1,0:T(8,128)(2,1)S(1)} %slice.418), channel_id=1, source_target_pairs={{0,16},{16,0},{1,17},{17,1},{2,18},{18,2},{3,19},{19,3},{4,20},{20... | collective-permute-start | bytes 1769480 | tf_op jit(solution)/shard_map/ppermute | solution.py:46
  125.5 15.1 %collective-permute-start.21 = (bf16[4,96,768]{2,1,0:T(8,128)(2,1)S(1)}, bf16[4,96,768]{2,1,0:T(8,128)(2,1)S(1)}, u32[]{:S(2)}, u32[]{:S(2)}) collective-permute-start(bf16[4,96,768]{2,1,0:T(8,128)(2,1)S(1)} %slice.417), channel_id=1, source_target_pairs={{0,8},{8,0},{1,9},{9,1},{2,10},{10,2},{3,11},{11,3},{4,12},{12,4},... | collective-permute-start | bytes 1769480 | tf_op jit(solution)/shard_map/ppermute | solution.py:46
  132.3 8.3 %collective-permute-start.26 = (bf16[128,768]{1,0:T(8,128)(2,1)S(1)}, bf16[128,768]{1,0:T(8,128)(2,1)S(1)}, u32[]{:S(2)}, u32[]{:S(2)}) collective-permute-start(bf16[128,768]{1,0:T(8,128)(2,1)S(1)} %get-tuple-element.260), channel_id=1, source_target_pairs={{0,1},{1,0},{2,3},{3,2},{4,5},{5,4},{6,7},{7,6},{8,9},{9,8},{10,11... | collective-permute-start | bytes 589832 | tf_op jit(solution)/shard_map/ppermute | solution.py:51
  160.0 7.5 %collective-permute-start.30 = (bf16[16,96,768]{2,1,0:T(8,128)(2,1)}, bf16[16,96,768]{2,1,0:T(8,128)(2,1)S(1)}, u32[]{:S(2)}, u32[]{:S(2)}) collective-permute-start(bf16[16,96,768]{2,1,0:T(8,128)(2,1)} %get-tuple-element.274), channel_id=1, source_target_pairs={{0,4},{4,0},{1,5},{5,1},{2,6},{6,2},{3,7},{7,3},{8,12},{12,8},{9,1... | collective-permute-start | bytes 7077896 | tf_op jit(solution)/shard_map/ppermute | solution.py:46
  160.2 8.0 %collective-permute-start.31 = (bf16[16,96,768]{2,1,0:T(8,128)(2,1)}, bf16[16,96,768]{2,1,0:T(8,128)(2,1)S(1)}, u32[]{:S(2)}, u32[]{:S(2)}) collective-permute-start(bf16[16,96,768]{2,1,0:T(8,128)(2,1)} %get-tuple-element.275), channel_id=1, source_target_pairs={{0,4},{4,0},{1,5},{5,1},{2,6},{6,2},{3,7},{7,3},{8,12},{12,8},{9,1... | collective-permute-start | bytes 7077896 | tf_op jit(solution)/shard_map/ppermute | solution.py:46
  170.7 30.7 %collective-permute-start.35 = (bf16[8,96,768]{2,1,0:T(8,128)(2,1)S(1)}, bf16[8,96,768]{2,1,0:T(8,128)(2,1)S(1)}, u32[]{:S(2)}, u32[]{:S(2)}) collective-permute-start(bf16[8,96,768]{2,1,0:T(8,128)(2,1)S(1)} %get-tuple-element.436), channel_id=1, source_target_pairs={{0,8},{8,0},{1,9},{9,1},{2,10},{10,2},{3,11},{11,3},{4,12},{12,4},... | collective-permute-start | bytes 3538952 | tf_op jit(solution)/shard_map/ppermute | solution.py:46
  172.0 29.4 %collective-permute-start.36 = (bf16[8,96,768]{2,1,0:T(8,128)(2,1)S(1)}, bf16[8,96,768]{2,1,0:T(8,128)(2,1)S(1)}, u32[]{:S(2)}, u32[]{:S(2)}) collective-permute-start(bf16[8,96,768]{2,1,0:T(8,128)(2,1)S(1)} %get-tuple-element.437), channel_id=1, source_target_pairs={{0,16},{16,0},{1,17},{17,1},{2,18},{18,2},{3,19},{19,3},{4,20},{20... | collective-permute-start | bytes 3538952 | tf_op jit(solution)/shard_map/ppermute | solution.py:46
  175.1 14.6 %collective-permute-start.34 = (bf16[2,4,32,768]{3,2,1,0:T(8,128)(2,1)S(1)}, bf16[2,4,32,768]{3,2,1,0:T(8,128)(2,1)S(1)}, u32[]{:S(2)}, u32[]{:S(2)}) collective-permute-start(bf16[2,4,32,768]{3,2,1,0:T(8,128)(2,1)S(1)} %get-tuple-element.288), channel_id=1, source_target_pairs={{0,1},{1,0},{2,3},{3,2},{4,5},{5,4},{6,7},{7,6},{8,9},{9,8},{10,11... | collective-permute-start | bytes 1179656 | tf_op jit(solution)/shard_map/ppermute | solution.py:51
  181.2 8.5 %collective-permute-start.33 = (bf16[128,384]{1,0:T(8,128)(2,1)S(1)}, bf16[128,384]{1,0:T(8,128)(2,1)S(1)}, u32[]{:S(2)}, u32[]{:S(2)}) collective-permute-start(bf16[128,384]{1,0:T(8,128)(2,1)S(1)} %broadcast_select_fusion.1), channel_id=1, source_target_pairs={{0,1},{1,0},{2,3},{3,2},{4,5},{5,4},{6,7},{7,6},{8,9},{9,8},{10,11... | collective-permute-start | bytes 294920 | tf_op jit(solution)/shard_map/ppermute | solution.py:51
  189.8 33.7 %collective-permute-start.41 = (bf16[2,2,4,32,768]{4,3,2,1,0:T(8,128)(2,1)S(1)}, bf16[2,2,4,32,768]{4,3,2,1,0:T(8,128)(2,1)}, u32[]{:S(2)}, u32[]{:S(2)}) collective-permute-start(bf16[2,2,4,32,768]{4,3,2,1,0:T(8,128)(2,1)S(1)} %pad_maximum_fusion.4.two), channel_id=1, source_target_pairs={{1,2},{2,1},{5,6},{6,5},{9,10},{10,9},{13,14},{14,13},{17,18},{18,... | collective-permute-start | bytes 2359304 | tf_op jit(solution)/shard_map/ppermute | solution.py:134
  202.8 21.4 %collective-permute-start.39 = (bf16[4,96,768]{2,1,0:T(8,128)(2,1)}, bf16[4,96,768]{2,1,0:T(8,128)(2,1)S(1)}, u32[]{:S(2)}, u32[]{:S(2)}) collective-permute-start(bf16[4,96,768]{2,1,0:T(8,128)(2,1)} %get-tuple-element.444), channel_id=1, source_target_pairs={{0,16},{16,0},{1,17},{17,1},{2,18},{18,2},{3,19},{19,3},{4,20},{20... | collective-permute-start | bytes 1769480 | tf_op jit(solution)/shard_map/ppermute | solution.py:46
  205.2 19.0 %collective-permute-start.40 = (bf16[4,96,768]{2,1,0:T(8,128)(2,1)}, bf16[4,96,768]{2,1,0:T(8,128)(2,1)S(1)}, u32[]{:S(2)}, u32[]{:S(2)}) collective-permute-start(bf16[4,96,768]{2,1,0:T(8,128)(2,1)} %get-tuple-element.445), channel_id=1, source_target_pairs={{0,8},{8,0},{1,9},{9,1},{2,10},{10,2},{3,11},{11,3},{4,12},{12,4},... | collective-permute-start | bytes 1769480 | tf_op jit(solution)/shard_map/ppermute | solution.py:46
  206.1 8.4 %collective-permute-start.37 = (bf16[128,384]{1,0:T(8,128)(2,1)S(1)}, bf16[128,384]{1,0:T(8,128)(2,1)S(1)}, u32[]{:S(2)}, u32[]{:S(2)}) collective-permute-start(bf16[128,384]{1,0:T(8,128)(2,1)S(1)} %get-tuple-element.300), channel_id=1, source_target_pairs={{0,2},{1,3},{2,0},{3,1},{4,6},{5,7},{6,4},{7,5},{8,10},{9,11},{10,... | collective-permute-start | bytes 294920 | tf_op jit(solution)/shard_map/ppermute | solution.py:51
  214.5 9.0 %collective-permute-start.38 = (bf16[128,384]{1,0:T(8,128)(2,1)S(1)}, bf16[128,384]{1,0:T(8,128)(2,1)S(1)}, u32[]{:S(2)}, u32[]{:S(2)}) collective-permute-start(bf16[128,384]{1,0:T(8,128)(2,1)S(1)} %broadcast_select_fusion), channel_id=1, source_target_pairs={{0,1},{1,0},{2,3},{3,2},{4,5},{5,4},{6,7},{7,6},{8,9},{9,8},{10,11... | collective-permute-start | bytes 294920 | tf_op jit(solution)/shard_map/ppermute | solution.py:51
  224.2 28.0 %collective-permute-start.45 = (bf16[2,2,4,32,768]{4,3,2,1,0:T(8,128)(2,1)}, bf16[2,2,4,32,768]{4,3,2,1,0:T(8,128)(2,1)}, u32[]{:S(2)}, u32[]{:S(2)}) collective-permute-start(bf16[2,2,4,32,768]{4,3,2,1,0:T(8,128)(2,1)} %collective-permute-done.41.across), channel_id=1, source_target_pairs={{1,0},{2,3},{5,4},{6,7},{9,8},{10,11},{13,12},{14,15},{17,16},{18,... | collective-permute-start | bytes 2359304 | tf_op jit(solution)/shard_map/ppermute | solution.py:140
  233.8 18.4 %collective-permute-start.43 = (bf16[16,48,384]{2,1,0:T(8,128)(2,1)}, bf16[16,48,384]{2,1,0:T(8,128)(2,1)}, u32[]{:S(2)}, u32[]{:S(2)}) collective-permute-start(bf16[16,48,384]{2,1,0:T(8,128)(2,1)} %get-tuple-element.332), channel_id=1, source_target_pairs={{0,4},{4,0},{1,5},{5,1},{2,6},{6,2},{3,7},{7,3},{8,12},{12,8},{9,1... | collective-permute-start | bytes 1769480 | tf_op jit(solution)/shard_map/ppermute | solution.py:46
  233.8 18.4 %collective-permute-start.44 = (bf16[16,48,384]{2,1,0:T(8,128)(2,1)S(1)}, bf16[16,48,384]{2,1,0:T(8,128)(2,1)}, u32[]{:S(2)}, u32[]{:S(2)}) collective-permute-start(bf16[16,48,384]{2,1,0:T(8,128)(2,1)S(1)} %get-tuple-element.333), channel_id=1, source_target_pairs={{0,4},{4,0},{1,5},{5,1},{2,6},{6,2},{3,7},{7,3},{8,12},{12,8},{9,1... | collective-permute-start | bytes 1769480 | tf_op jit(solution)/shard_map/ppermute | solution.py:46
  235.1 17.1 %collective-permute-start.42 = (bf16[2,96,768]{2,1,0:T(8,128)(2,1)}, bf16[2,96,768]{2,1,0:T(8,128)(2,1)S(1)}, u32[]{:S(2)}, u32[]{:S(2)}) collective-permute-start(bf16[2,96,768]{2,1,0:T(8,128)(2,1)} %slice.443), channel_id=1, source_target_pairs={{0,2},{1,3},{2,0},{3,1},{4,6},{5,7},{6,4},{7,5},{8,10},{9,11},{10,... | collective-permute-start | bytes 884744 | tf_op jit(solution)/shard_map/ppermute | solution.py:51
  252.9 18.2 %collective-permute-start.46 = (bf16[256,768]{1,0:T(8,128)(2,1)}, bf16[256,768]{1,0:T(8,128)(2,1)S(1)}, u32[]{:S(2)}, u32[]{:S(2)}) collective-permute-start(bf16[256,768]{1,0:T(8,128)(2,1)} %get-tuple-element.335.own), channel_id=1, source_target_pairs={{1,2},{2,1},{5,6},{6,5},{9,10},{10,9},{13,14},{14,13},{17,18},{18,... | collective-permute-start | bytes 1179656 | tf_op jit(solution)/shard_map/ppermute | solution.py:134
  253.8 18.0 %collective-permute-start.47 = (bf16[256,768]{1,0:T(8,128)(2,1)}, bf16[256,768]{1,0:T(8,128)(2,1)}, u32[]{:S(2)}, u32[]{:S(2)}) collective-permute-start(bf16[256,768]{1,0:T(8,128)(2,1)} %get-tuple-element.335.own), channel_id=1, source_target_pairs={{0,1},{1,0},{2,3},{3,2},{4,5},{5,4},{6,7},{7,6},{8,9},{9,8},{10,11... | collective-permute-start | bytes 1179656 | tf_op jit(solution)/shard_map/ppermute | solution.py:51
  257.3 13.7 %collective-permute-start.49 = (bf16[8,48,384]{2,1,0:T(8,128)(2,1)S(1)}, bf16[8,48,384]{2,1,0:T(8,128)(2,1)S(1)}, u32[]{:S(2)}, u32[]{:S(2)}) collective-permute-start(bf16[8,48,384]{2,1,0:T(8,128)(2,1)S(1)} %get-tuple-element.454), channel_id=1, source_target_pairs={{0,16},{16,0},{1,17},{17,1},{2,18},{18,2},{3,19},{19,3},{4,20},{20... | collective-permute-start | bytes 884744 | tf_op jit(solution)/shard_map/ppermute | solution.py:46
  260.5 10.5 %collective-permute-start.48 = (bf16[8,48,384]{2,1,0:T(8,128)(2,1)S(1)}, bf16[8,48,384]{2,1,0:T(8,128)(2,1)S(1)}, u32[]{:S(2)}, u32[]{:S(2)}) collective-permute-start(bf16[8,48,384]{2,1,0:T(8,128)(2,1)S(1)} %get-tuple-element.456), channel_id=1, source_target_pairs={{0,8},{8,0},{1,9},{9,1},{2,10},{10,2},{3,11},{11,3},{4,12},{12,4},... | collective-permute-start | bytes 884744 | tf_op jit(solution)/shard_map/ppermute | solution.py:46
  262.1 9.0 %collective-permute-start.50 = (bf16[2,48,768]{2,1,0:T(8,128)(2,1)S(1)}, bf16[2,48,768]{2,1,0:T(8,128)(2,1)S(1)}, u32[]{:S(2)}, u32[]{:S(2)}) collective-permute-start(bf16[2,48,768]{2,1,0:T(8,128)(2,1)S(1)} %get-tuple-element.470), channel_id=1, source_target_pairs={{0,2},{1,3},{2,0},{3,1},{4,6},{5,7},{6,4},{7,5},{8,10},{9,11},{10,... | collective-permute-start | bytes 442376 | tf_op jit(solution)/shard_map/ppermute | solution.py:51
  271.9 12.7 %collective-permute-start.51 = (bf16[16,96,384]{2,1,0:T(8,128)(2,1)}, bf16[16,96,384]{2,1,0:T(8,128)(2,1)}, u32[]{:S(2)}, u32[]{:S(2)}) collective-permute-start(bf16[16,96,384]{2,1,0:T(8,128)(2,1)} %get-tuple-element.346), channel_id=1, source_target_pairs={{0,4},{4,0},{1,5},{5,1},{2,6},{6,2},{3,7},{7,3},{8,12},{12,8},{9,1... | collective-permute-start | bytes 3538952 | tf_op jit(solution)/shard_map/ppermute | solution.py:46
  271.9 12.7 %collective-permute-start.52 = (bf16[16,96,384]{2,1,0:T(8,128)(2,1)}, bf16[16,96,384]{2,1,0:T(8,128)(2,1)}, u32[]{:S(2)}, u32[]{:S(2)}) collective-permute-start(bf16[16,96,384]{2,1,0:T(8,128)(2,1)} %get-tuple-element.347), channel_id=1, source_target_pairs={{0,4},{4,0},{1,5},{5,1},{2,6},{6,2},{3,7},{7,3},{8,12},{12,8},{9,1... | collective-permute-start | bytes 3538952 | tf_op jit(solution)/shard_map/ppermute | solution.py:46
  272.4 10.2 %collective-permute-start.55 = (bf16[2,48,768]{2,1,0:T(8,128)(2,1)}, bf16[2,48,768]{2,1,0:T(8,128)(2,1)}, u32[]{:S(2)}, u32[]{:S(2)}) collective-permute-start(bf16[2,48,768]{2,1,0:T(8,128)(2,1)} %get-tuple-element.469), channel_id=1, source_target_pairs={{0,2},{1,3},{2,0},{3,1},{4,6},{5,7},{6,4},{7,5},{8,10},{9,11},{10,... | collective-permute-start | bytes 442376 | tf_op jit(solution)/shard_map/ppermute | solution.py:51
  274.8 8.5 %collective-permute-start.54 = (bf16[4,48,384]{2,1,0:T(8,128)(2,1)}, bf16[4,48,384]{2,1,0:T(8,128)(2,1)}, u32[]{:S(2)}, u32[]{:S(2)}) collective-permute-start(bf16[4,48,384]{2,1,0:T(8,128)(2,1)} %get-tuple-element.468), channel_id=1, source_target_pairs={{0,8},{8,0},{1,9},{9,1},{2,10},{10,2},{3,11},{11,3},{4,12},{12,4},... | collective-permute-start | bytes 442376 | tf_op jit(solution)/shard_map/ppermute | solution.py:46
  282.6 12.8 %collective-permute-start.58 = (bf16[256,768]{1,0:T(8,128)(2,1)}, bf16[256,768]{1,0:T(8,128)(2,1)S(1)}, u32[]{:S(2)}, u32[]{:S(2)}) collective-permute-start(bf16[256,768]{1,0:T(8,128)(2,1)} %collective-permute-done.47.near), channel_id=1, source_target_pairs={{1,2},{2,1},{5,6},{6,5},{9,10},{10,9},{13,14},{14,13},{17,18},{18,... | collective-permute-start | bytes 1179656 | tf_op jit(solution)/shard_map/ppermute | solution.py:134
  283.3 15.6 %collective-permute-start.59 = (bf16[256,768]{1,0:T(8,128)(2,1)S(1)}, bf16[256,768]{1,0:T(8,128)(2,1)S(1)}, u32[]{:S(2)}, u32[]{:S(2)}) collective-permute-start(bf16[256,768]{1,0:T(8,128)(2,1)S(1)} %copy-done.41), channel_id=1, source_target_pairs={{1,0},{2,3},{5,4},{6,7},{9,8},{10,11},{13,12},{14,15},{17,16},{18,... | collective-permute-start | bytes 1179656 | tf_op jit(solution)/shard_map/ppermute | solution.py:140
  286.2 14.6 %collective-permute-start.57 = (bf16[8,96,384]{2,1,0:T(8,128)(2,1)S(1)}, bf16[8,96,384]{2,1,0:T(8,128)(2,1)S(1)}, u32[]{:S(2)}, u32[]{:S(2)}) collective-permute-start(bf16[8,96,384]{2,1,0:T(8,128)(2,1)S(1)} %get-tuple-element.440), channel_id=1, source_target_pairs={{0,16},{16,0},{1,17},{17,1},{2,18},{18,2},{3,19},{19,3},{4,20},{20... | collective-permute-start | bytes 1769480 | tf_op jit(solution)/shard_map/ppermute | solution.py:46
  288.3 14.9 %collective-permute-start.56 = (bf16[8,96,384]{2,1,0:T(8,128)(2,1)S(1)}, bf16[8,96,384]{2,1,0:T(8,128)(2,1)S(1)}, u32[]{:S(2)}, u32[]{:S(2)}) collective-permute-start(bf16[8,96,384]{2,1,0:T(8,128)(2,1)S(1)} %get-tuple-element.442), channel_id=1, source_target_pairs={{0,8},{8,0},{1,9},{9,1},{2,10},{10,2},{3,11},{11,3},{4,12},{12,4},... | collective-permute-start | bytes 1769480 | tf_op jit(solution)/shard_map/ppermute | solution.py:46
  290.0 10.5 %collective-permute-start.60 = (f32[24,768]{1,0:T(8,128)S(1)}, f32[24,768]{1,0:T(8,128)S(1)}, u32[]{:S(2)}, u32[]{:S(2)}) collective-permute-start(f32[24,768]{1,0:T(8,128)S(1)} %copy-done.93), channel_id=1, source_target_pairs={{0,1},{1,0},{2,3},{3,2},{4,5},{5,4},{6,7},{7,6},{8,9},{9,8},{10,11... | collective-permute-start | bytes 221192 | tf_op jit(solution)/shard_map/ppermute | solution.py:51
  295.4 17.8 %collective-permute-start.64 = (bf16[192,768]{1,0:T(8,128)(2,1)S(1)}, bf16[192,768]{1,0:T(8,128)(2,1)S(1)}, u32[]{:S(2)}, u32[]{:S(2)}) collective-permute-start(bf16[192,768]{1,0:T(8,128)(2,1)S(1)} %get-tuple-element.452), channel_id=1, source_target_pairs={{0,1},{1,0},{2,3},{3,2},{4,5},{5,4},{6,7},{7,6},{8,9},{9,8},{10,11... | collective-permute-start | bytes 884744 | tf_op jit(solution)/shard_map/ppermute | solution.py:51
  303.4 11.2 %collective-permute-start.62 = (bf16[4,96,384]{2,1,0:T(8,128)(2,1)S(1)}, bf16[4,96,384]{2,1,0:T(8,128)(2,1)S(1)}, u32[]{:S(2)}, u32[]{:S(2)}) collective-permute-start(bf16[4,96,384]{2,1,0:T(8,128)(2,1)S(1)} %get-tuple-element.450), channel_id=1, source_target_pairs={{0,8},{8,0},{1,9},{9,1},{2,10},{10,2},{3,11},{11,3},{4,12},{12,4},... | collective-permute-start | bytes 884744 | tf_op jit(solution)/shard_map/ppermute | solution.py:46
  304.4 10.3 %collective-permute-start.61 = (bf16[4,96,384]{2,1,0:T(8,128)(2,1)S(1)}, bf16[4,96,384]{2,1,0:T(8,128)(2,1)S(1)}, u32[]{:S(2)}, u32[]{:S(2)}) collective-permute-start(bf16[4,96,384]{2,1,0:T(8,128)(2,1)S(1)} %get-tuple-element.448), channel_id=1, source_target_pairs={{0,16},{16,0},{1,17},{17,1},{2,18},{18,2},{3,19},{19,3},{4,20},{20... | collective-permute-start | bytes 884744 | tf_op jit(solution)/shard_map/ppermute | solution.py:46
  305.9 12.4 %collective-permute-start.65 = (bf16[256,768]{1,0:T(8,128)(2,1)S(1)}, bf16[256,768]{1,0:T(8,128)(2,1)S(1)}, u32[]{:S(2)}, u32[]{:S(2)}) collective-permute-start(bf16[256,768]{1,0:T(8,128)(2,1)S(1)} %collective-permute-done.58.across_near), channel_id=1, source_target_pairs={{1,0},{2,3},{5,4},{6,7},{9,8},{10,11},{13,12},{14,15},{17,16},{18,... | collective-permute-start | bytes 1179656 | tf_op jit(solution)/shard_map/ppermute | solution.py:140
  320.2 13.0 %collective-permute-start.68 = (bf16[288,384]{1,0:T(8,128)(2,1)S(1)}, bf16[288,384]{1,0:T(8,128)(2,1)S(1)}, u32[]{:S(2)}, u32[]{:S(2)}) collective-permute-start(bf16[288,384]{1,0:T(8,128)(2,1)S(1)} %slice_bitcast_fusion.2), channel_id=1, source_target_pairs={{0,1},{1,0},{2,3},{3,2},{4,5},{5,4},{6,7},{7,6},{8,9},{9,8},{10,11... | collective-permute-start | bytes 663560 | tf_op jit(solution)/shard_map/ppermute | solution.py:51
  320.4 16.9 %collective-permute-start.69 = (bf16[288,384]{1,0:T(8,128)(2,1)S(1)}, bf16[288,384]{1,0:T(8,128)(2,1)S(1)}, u32[]{:S(2)}, u32[]{:S(2)}) collective-permute-start(bf16[288,384]{1,0:T(8,128)(2,1)S(1)} %get-tuple-element.481), channel_id=1, source_target_pairs={{0,2},{1,3},{2,0},{3,1},{4,6},{5,7},{6,4},{7,5},{8,10},{9,11},{10,... | collective-permute-start | bytes 663560 | tf_op jit(solution)/shard_map/ppermute | solution.py:51
  322.7 14.6 %collective-permute-start.70 = (bf16[288,384]{1,0:T(8,128)(2,1)S(1)}, bf16[288,384]{1,0:T(8,128)(2,1)S(1)}, u32[]{:S(2)}, u32[]{:S(2)}) collective-permute-start(bf16[288,384]{1,0:T(8,128)(2,1)S(1)} %get-tuple-element.482), channel_id=1, source_target_pairs={{0,3},{1,2},{2,1},{3,0},{4,7},{5,6},{6,5},{7,4},{8,11},{9,10},{10,... | collective-permute-start | bytes 663560 | tf_op jit(solution)/shard_map/ppermute | solution.py:51
  324.8 8.2 %collective-permute-start.67 = (f32[24,768]{1,0:T(8,128)S(1)}, f32[24,768]{1,0:T(8,128)S(1)}, u32[]{:S(2)}, u32[]{:S(2)}) collective-permute-start(f32[24,768]{1,0:T(8,128)S(1)} %add.277), channel_id=1, source_target_pairs={{0,8},{8,0},{1,9},{9,1},{2,10},{10,2},{3,11},{11,3},{4,12},{12,4},... | collective-permute-start | bytes 221192 | tf_op jit(solution)/shard_map/ppermute | solution.py:46
  333.1 8.6 %collective-permute-start.71 = (f32[24,768]{1,0:T(8,128)S(1)}, f32[24,768]{1,0:T(8,128)S(1)}, u32[]{:S(2)}, u32[]{:S(2)}) collective-permute-start(f32[24,768]{1,0:T(8,128)S(1)} %add.278), channel_id=1, source_target_pairs={{0,4},{4,0},{1,5},{5,1},{2,6},{6,2},{3,7},{7,3},{8,12},{12,8},{9,1... | collective-permute-start | bytes 221192 | tf_op jit(solution)/shard_map/ppermute | solution.py:46
  (114 other events, 805.0 us)
Sparse Core Ops, SparseCore 0:
  16.8 27.8 all-gather.1
  238.6 37.9 reduce-scatter.1
